TPU v7x, 32 devices: a whole 2x2x4 slice. The times are simulated.
32 devices in a mesh: fsdp: 8 (over z, x), dp: 4 (over y, core).
Axes of the slice: x: 2, y: 2, z: 4, core: 2. Of those that a mesh axis runs over, the one named last changes fastest.
Arguments:
- features: bfloat16 [512, 256, 1024], P(('fsdp', 'dp')), may hold values from -11 to 11
- half_sides: int32 [512], P(('fsdp', 'dp')), may hold values from 6 to 8
- cotangent: bfloat16 [512, 256, 1024], P(('fsdp', 'dp')), may hold values from -6 to 6
- conv_in: bfloat16 [1024, 256], P('fsdp'), may hold values from -0.1875 to 0.1875
- conv_mid: bfloat16 [2, 9, 128, 256], P(None, None, None, 'fsdp'), may hold values from -0.1875 to 0.1875
- attn_down: bfloat16 [256, 128], P('fsdp'), may hold values from -0.375 to 0.375
- attn_up: bfloat16 [128, 512], P(None, 'fsdp'), may hold values from -0.5 to 0.5
- attn_bias: bfloat16 [512], P('fsdp'), may hold values from -3 to 3
- conv_out: bfloat16 [256, 1024], P(None, 'fsdp'), may hold values from -0.375 to 0.375
- gain_in: bfloat16 [256], P('fsdp'), may hold values from 0.5 to 1.5
- shift_in: bfloat16 [256], P('fsdp'), may hold values from -3 to 3
- gain_mid: bfloat16 [512], P('fsdp'), may hold values from 0.5 to 1.5
- shift_mid: bfloat16 [512], P('fsdp'), may hold values from -3 to 3
- gain_attn: bfloat16 [128], P('fsdp'), may hold values from 0.5 to 1.5
- shift_attn: bfloat16 [128], P('fsdp'), may hold values from -3 to 3
- gain_out: bfloat16 [1024], P('fsdp'), may hold values from 0.5 to 1.5
- shift_out: bfloat16 [1024], P('fsdp'), may hold values from -3 to 3
Outputs:
- block_out: bfloat16 [512, 256, 1024], P(('fsdp', 'dp'))
- grad_features: float32 [512, 256, 1024], P(('fsdp', 'dp'))
- norms: float32 [4], replicated
- grad_conv_in: float32 [1024, 256], P('fsdp')
- grad_conv_mid: float32 [2, 9, 128, 256], P(None, None, None, 'fsdp')
- grad_attn_down: float32 [256, 128], P('fsdp')
- grad_attn_up: float32 [128, 512], P(None, 'fsdp')
- grad_attn_bias: float32 [512], P('fsdp')
- grad_conv_out: float32 [256, 1024], P(None, 'fsdp')
- grad_gain_in: float32 [256], P('fsdp')
- grad_shift_in: float32 [256], P('fsdp')
- grad_gain_mid: float32 [512], P('fsdp')
- grad_shift_mid: float32 [512], P('fsdp')
- grad_gain_attn: float32 [128], P('fsdp')
- grad_shift_attn: float32 [128], P('fsdp')
- grad_gain_out: float32 [1024], P('fsdp')
- grad_shift_out: float32 [1024], P('fsdp')
Inputs may be any that keep to these rules, and one draw needn't show every extreme that they name: Half the side of image i's feature map; its valid pixels are the top-left square of side 2 half_sides[i] in its 16 x 16 grid.
All inputs are finite; a program needn't handle non-finite values.
Results may differ from a plain program's by a relative error of at most 0.033.
The roundings to bfloat16 on the way count: a program that leaves them out, or rounds other values in their place, can miss the bound.
Values may be sent and summed in bfloat16 or wider, within the bound.
No kernel may reach another device: no remote copies, remote signals or barrier semaphores. Data moves between devices by JAX's collectives and lax.ppermute only.
A program may use at most 256 MiB of HBM per device.

v0:
```python
import jax
import jax.numpy as jnp
from jax import lax
from jax.sharding import PartitionSpec as P

RADIX = 2
SIDE = 16


epsilon = 1e-05


def silu_slope(values):
    sigmoid = jax.nn.sigmoid(values)
    return sigmoid * (1.0 + values * (1.0 - sigmoid))


def pixel_mask(half_sides, extent):
    places = jnp.arange(extent * extent, dtype=jnp.int32)
    limits = (2 * half_sides)[:, None]
    inside = ((places // extent)[None, :] < limits) & ((places % extent)[None, :] < limits)
    return inside.astype(jnp.float32)


def patches(planes):
    images, extent = (planes.shape[0], planes.shape[1])
    padded = jnp.pad(planes, ((0, 0), (1, 1), (1, 1), (0, 0)))
    shifted = [
        padded[:, row_shift : row_shift + extent, col_shift : col_shift + extent, :]
        for row_shift in range(3)
        for col_shift in range(3)
    ]
    return jnp.concatenate(shifted, axis=-1).reshape(images * extent * extent, -1)


def unpatch(columns, images, extent, channels):
    columns = columns.reshape(images, extent, extent, 9, channels)
    summed = jnp.zeros((images, extent + 2, extent + 2, channels), jnp.float32)
    for position in range(9):
        row_shift, col_shift = (position // 3, position % 3)
        summed = summed.at[
            :, row_shift : row_shift + extent, col_shift : col_shift + extent, :
        ].add(columns[:, :, :, position, :])
    return summed[:, 1 : extent + 1, 1 : extent + 1, :]


def contract_lead(left, right):
    return lax.dot_general(
        left, right, (((0,), (0,)), ((), ())), preferred_element_type=jnp.float32
    )


def contract_last(left, right):
    return lax.dot_general(
        left, right, (((1,), (1,)), ((), ())), preferred_element_type=jnp.float32
    )


def moments_of(values, weight):
    summed, square, counted = lax.psum(
        (
            jnp.sum(weight * values, axis=0),
            jnp.sum(weight * values * values, axis=0),
            jnp.sum(weight),
        ),
        ("fsdp", "dp"),
    )
    center = summed / counted
    spread = square / counted - center * center
    inv_std = lax.rsqrt(spread + epsilon)
    return ((values - center) * inv_std, inv_std, counted)


def norm_back(grad_norm, normed, scales, weight, counted, inv_std):
    shift_sum, scale_sum = lax.psum(
        (jnp.sum(grad_norm, axis=0), jnp.sum(grad_norm * normed, axis=0)), ("fsdp", "dp")
    )
    grad_input = (
        scales * inv_std * (grad_norm - weight * (shift_sum + normed * scale_sum) / counted)
    )
    return (grad_input, scale_sum, shift_sum)


def own_part(whole, pieces):
    piece_len = whole.shape[0] // pieces
    return lax.dynamic_slice_in_dim(whole, lax.axis_index("fsdp") * piece_len, piece_len, 0)


def local(
    features,
    half_sides,
    cotangent,
    conv_in,
    conv_mid,
    attn_down,
    attn_up,
    attn_bias,
    conv_out,
    gain_in,
    shift_in,
    gain_mid,
    shift_mid,
    gain_attn,
    shift_attn,
    gain_out,
    shift_out,
):
    images = features.shape[0]
    pixels = features.shape[1]
    model_width = features.shape[2]
    pieces = lax.axis_size("fsdp")
    gathered = (
        lax.all_gather(conv_in, "fsdp", axis=0, tiled=True),
        lax.all_gather(conv_mid, "fsdp", axis=3, tiled=True),
        lax.all_gather(attn_down, "fsdp", axis=0, tiled=True),
        lax.all_gather(attn_up, "fsdp", axis=1, tiled=True),
        lax.all_gather(attn_bias, "fsdp", axis=0, tiled=True),
        lax.all_gather(conv_out, "fsdp", axis=1, tiled=True),
        lax.all_gather(gain_in, "fsdp", axis=0, tiled=True),
        lax.all_gather(shift_in, "fsdp", axis=0, tiled=True),
        lax.all_gather(gain_mid, "fsdp", axis=0, tiled=True),
        lax.all_gather(shift_mid, "fsdp", axis=0, tiled=True),
        lax.all_gather(gain_attn, "fsdp", axis=0, tiled=True),
        lax.all_gather(shift_attn, "fsdp", axis=0, tiled=True),
        lax.all_gather(gain_out, "fsdp", axis=0, tiled=True),
        lax.all_gather(shift_out, "fsdp", axis=0, tiled=True),
    )
    whole_in, whole_mid, whole_down, whole_up, whole_bias, whole_out = gathered[0:6]
    scale_in, offset_in, scale_mid, offset_mid, scale_attn, offset_attn, scale_out, offset_out = [
        item.astype(jnp.float32) for item in gathered[6:]
    ]
    bottleneck = whole_in.shape[1]
    half_width = bottleneck // RADIX
    inside = pixel_mask(half_sides, SIDE).reshape(-1, 1)
    per_image = jnp.square(2.0 * half_sides.astype(jnp.float32))
    rows = features.reshape(-1, model_width)
    rows_float = rows.astype(jnp.float32)
    masked = rows * inside.astype(jnp.bfloat16)
    first = jnp.dot(masked, whole_in, preferred_element_type=jnp.float32)
    normed_in, inv_in, counted = moments_of(first, inside)
    pre_in = scale_in * normed_in + offset_in
    act_in = jax.nn.silu(pre_in) * inside
    planes = act_in.astype(jnp.bfloat16).reshape(images, SIDE, SIDE, bottleneck)
    columns_all = []
    outputs_mid = []
    for branch in range(RADIX):
        columns = patches(planes[..., branch * half_width : (branch + 1) * half_width])
        columns_all.append(columns)
        outputs_mid.append(
            jnp.dot(
                columns,
                whole_mid[branch].reshape(9 * half_width, bottleneck),
                preferred_element_type=jnp.float32,
            )
        )
    second = jnp.concatenate(outputs_mid, axis=1)
    normed_mid, inv_mid, counted_mid = moments_of(second, inside)
    pre_mid = scale_mid * normed_mid + offset_mid
    act_mid = jax.nn.silu(pre_mid) * inside
    split = act_mid.reshape(images, pixels, RADIX, bottleneck)
    pooled = jnp.sum(jnp.sum(split, axis=2), axis=1) / per_image[:, None]
    pooled_low = pooled.astype(jnp.bfloat16)
    squeeze = jnp.dot(pooled_low, whole_down, preferred_element_type=jnp.float32)
    every_image = jnp.ones((images, 1), jnp.float32)
    normed_attn, inv_attn, counted_attn = moments_of(squeeze, every_image)
    pre_attn = scale_attn * normed_attn + offset_attn
    excite_low = jax.nn.silu(pre_attn).astype(jnp.bfloat16)
    logits = jnp.dot(excite_low, whole_up, preferred_element_type=jnp.float32) + whole_bias.astype(
        jnp.float32
    )
    weights = jax.nn.softmax(logits.reshape(images, RADIX, bottleneck), axis=1)
    mixed = jnp.sum(weights[:, None, :, :] * split, axis=2).reshape(-1, bottleneck)
    mixed_low = mixed.astype(jnp.bfloat16)
    third = jnp.dot(mixed_low, whole_out, preferred_element_type=jnp.float32)
    normed_out, inv_out, counted_out = moments_of(third, inside)
    branch_out = scale_out * normed_out + offset_out
    total = rows_float + branch_out
    output = jax.nn.silu(total) * inside
    local_sums = jnp.stack(
        [
            jnp.sum(inside * rows_float * rows_float),
            jnp.sum(mixed * mixed),
            jnp.sum(inside * branch_out * branch_out),
            jnp.sum(output * output),
        ]
    )
    global_sums = lax.psum(local_sums, ("fsdp", "dp"))
    widths = jnp.array([model_width, bottleneck, model_width, model_width], jnp.float32)
    norms = jnp.sqrt(global_sums / (counted * widths))
    block_out = output.astype(jnp.bfloat16).reshape(images, pixels, model_width)
    regathered = (
        lax.all_gather(conv_in, "fsdp", axis=0, tiled=True),
        lax.all_gather(conv_mid, "fsdp", axis=3, tiled=True),
        lax.all_gather(attn_down, "fsdp", axis=0, tiled=True),
        lax.all_gather(attn_up, "fsdp", axis=1, tiled=True),
        lax.all_gather(conv_out, "fsdp", axis=1, tiled=True),
        lax.all_gather(gain_in, "fsdp", axis=0, tiled=True),
        lax.all_gather(gain_mid, "fsdp", axis=0, tiled=True),
        lax.all_gather(gain_attn, "fsdp", axis=0, tiled=True),
        lax.all_gather(gain_out, "fsdp", axis=0, tiled=True),
    )
    back_in, back_mid, back_down, back_up, back_out = regathered[0:5]
    back_scale_in, back_scale_mid, back_scale_attn, back_scale_out = [
        item.astype(jnp.float32) for item in regathered[5:]
    ]
    d_total = cotangent.astype(jnp.float32).reshape(-1, model_width) * inside * silu_slope(total)
    d_third, grad_gain_out, grad_shift_out = norm_back(
        d_total, normed_out, back_scale_out, inside, counted_out, inv_out
    )
    d_third_low = d_third.astype(jnp.bfloat16)
    grad_conv_out = contract_lead(mixed_low, d_third_low)
    d_mixed = contract_last(d_third_low, back_out).reshape(images, pixels, 1, bottleneck)
    d_weights = jnp.sum(split * d_mixed, axis=1)
    d_logits = weights * (d_weights - jnp.sum(weights * d_weights, axis=1, keepdims=True))
    d_logits = d_logits.reshape(images, RADIX * bottleneck)
    grad_attn_bias = jnp.sum(d_logits, axis=0)
    d_logits_low = d_logits.astype(jnp.bfloat16)
    grad_attn_up = contract_lead(excite_low, d_logits_low)
    d_excite = contract_last(d_logits_low, back_up)
    d_squeeze, grad_gain_attn, grad_shift_attn = norm_back(
        d_excite * silu_slope(pre_attn),
        normed_attn,
        back_scale_attn,
        every_image,
        counted_attn,
        inv_attn,
    )
    d_squeeze_low = d_squeeze.astype(jnp.bfloat16)
    grad_attn_down = contract_lead(pooled_low, d_squeeze_low)
    d_pooled = contract_last(d_squeeze_low, back_down) / per_image[:, None]
    d_split = weights[:, None, :, :] * d_mixed + d_pooled[:, None, None, :]
    d_act_mid = d_split.reshape(-1, RADIX * bottleneck)
    d_second, grad_gain_mid, grad_shift_mid = norm_back(
        d_act_mid * inside * silu_slope(pre_mid),
        normed_mid,
        back_scale_mid,
        inside,
        counted_mid,
        inv_mid,
    )
    d_second_low = d_second.astype(jnp.bfloat16)
    grads_mid = []
    d_planes = []
    for branch in range(RADIX):
        d_part = d_second_low[:, branch * bottleneck : (branch + 1) * bottleneck]
        grads_mid.append(
            contract_lead(columns_all[branch], d_part).reshape(9, half_width, bottleneck)
        )
        d_columns = contract_last(d_part, back_mid[branch].reshape(9 * half_width, bottleneck))
        d_planes.append(unpatch(d_columns, images, SIDE, half_width))
    grad_conv_mid = jnp.stack(grads_mid, axis=0)
    d_act_in = jnp.concatenate(d_planes, axis=-1).reshape(-1, bottleneck)
    d_first, grad_gain_in, grad_shift_in = norm_back(
        d_act_in * inside * silu_slope(pre_in), normed_in, back_scale_in, inside, counted, inv_in
    )
    d_first_low = d_first.astype(jnp.bfloat16)
    grad_conv_in = contract_lead(masked, d_first_low)
    grad_features = (d_total + inside * contract_last(d_first_low, back_in)).reshape(
        images, pixels, model_width
    )
    shards = (
        lax.psum_scatter(grad_conv_in, "fsdp", scatter_dimension=0, tiled=True),
        lax.psum_scatter(grad_conv_mid, "fsdp", scatter_dimension=3, tiled=True),
        lax.psum_scatter(grad_attn_down, "fsdp", scatter_dimension=0, tiled=True),
        lax.psum_scatter(grad_attn_up, "fsdp", scatter_dimension=1, tiled=True),
        lax.psum_scatter(grad_attn_bias, "fsdp", scatter_dimension=0, tiled=True),
        lax.psum_scatter(grad_conv_out, "fsdp", scatter_dimension=1, tiled=True),
    )
    shards = (
        lax.psum(shards[0].astype(jnp.bfloat16), "dp").astype(jnp.float32),
        lax.psum(shards[1].astype(jnp.bfloat16), "dp").astype(jnp.float32),
        lax.psum(shards[2].astype(jnp.bfloat16), "dp").astype(jnp.float32),
        lax.psum(shards[3].astype(jnp.bfloat16), "dp").astype(jnp.float32),
        lax.psum(shards[4].astype(jnp.bfloat16), "dp").astype(jnp.float32),
        lax.psum(shards[5].astype(jnp.bfloat16), "dp").astype(jnp.float32),
    )
    shard_in, shard_mid, shard_down, shard_up, shard_bias, shard_out = (
        shards[0],
        shards[1],
        shards[2],
        shards[3],
        shards[4],
        shards[5],
    )
    return (
        block_out,
        grad_features,
        norms,
        shard_in,
        shard_mid,
        shard_down,
        shard_up,
        shard_bias,
        shard_out,
        own_part(grad_gain_in, pieces),
        own_part(grad_shift_in, pieces),
        own_part(grad_gain_mid, pieces),
        own_part(grad_shift_mid, pieces),
        own_part(grad_gain_attn, pieces),
        own_part(grad_shift_attn, pieces),
        own_part(grad_gain_out, pieces),
        own_part(grad_shift_out, pieces),
    )


def solution(mesh):
    return jax.shard_map(
        local,
        mesh=mesh,
        in_specs=(
            P(("fsdp", "dp"), None, None),
            P(("fsdp", "dp")),
            P(("fsdp", "dp"), None, None),
            P("fsdp", None),
            P(None, None, None, "fsdp"),
            P("fsdp", None),
            P(None, "fsdp"),
            P("fsdp"),
            P(None, "fsdp"),
            P("fsdp"),
            P("fsdp"),
            P("fsdp"),
            P("fsdp"),
            P("fsdp"),
            P("fsdp"),
            P("fsdp"),
            P("fsdp"),
        ),
        out_specs=(
            P(("fsdp", "dp"), None, None),
            P(("fsdp", "dp"), None, None),
            P(),
            P("fsdp", None),
            P(None, None, None, "fsdp"),
            P("fsdp", None),
            P(None, "fsdp"),
            P("fsdp"),
            P(None, "fsdp"),
            P("fsdp"),
            P("fsdp"),
            P("fsdp"),
            P("fsdp"),
            P("fsdp"),
            P("fsdp"),
            P("fsdp"),
            P("fsdp"),
        ),
        check_vma=False,
    )
```

profile of v0, /device:TPU:0, one launch (start us, length us, event | category | flops | bytes accessed | tf_op | source)
XLA Modules:
  0.0 1235.8 jit_solution(13849766958602305238)
XLA Ops:
  19.6 23.5 %all-reduce.22 = (bf16[256]{0:T(256)(128)(2,1)S(1)}, bf16[256]{0:T(256)(128)(2,1)S(1)}, bf16[512]{0:T(512)(128)(2,1)S(1)}, bf16[512]{0:T(512)(128)(2,1)S(1)}, bf...) all-reduce(bf16[256]{0:T(256)(128)(2,1)S(1)} %dynamic-update-slice., ...), channel_id=1, replica_groups=mesh['fsdp'=8,'dp'=4] {'fsdp'}, use_global_device_ids=true, to_apply=%add.7 | all-reduce | flops 2304 | bytes 9216
  45.5 31.8 %all_gather.55 = bf16[1024,256]{1,0:T(8,128)(2,1)S(1)} all-gather(bf16[128,256]{1,0:T(8,128)(2,1)} %param.57), channel_id=1, replica_groups=mesh['fsdp'=8,'dp'=4] {'fsdp'}, dimensions={0}, use_global_device_ids=true | all-gather | bytes 589824 | tf_op jit(solution)/shard_map/all_gather | solution.py:113
  92.7 37.4 %all-reduce.20 = (f32[256]{0:T(256)S(1)}, f32[]{:T(128)}, f32[256]{0:T(256)S(1)}) all-reduce(f32[256]{0:T(256)S(1)} %get-tuple-element.311, f32[]{:T(128)} %fusion.57, f32[256]{0:T(256)S(1)} %get-tuple-element.310), channel_id=1, replica_groups=mesh['fsdp'=8,'dp'=4] {'fsdp','dp'}, use_global_device_ids=true, to_apply=%region_1.2 | all-reduce | flops 513 | bytes 4104 | tf_op jit(solution)/shard_map/psum | solution.py:60
  141.0 32.6 %all_gather.59 = bf16[256,128]{1,0:T(8,128)(2,1)} all-gather(bf16[32,128]{1,0:T(8,128)(2,1)S(1)} %copy-done.49), channel_id=1, replica_groups=mesh['fsdp'=8,'dp'=4] {'fsdp'}, dimensions={0}, use_global_device_ids=true | all-gather | bytes 73728 | tf_op jit(solution)/shard_map/all_gather | solution.py:115
  175.2 20.1 %all-gather = bf16[8,1,128]{2,1,0:T(2,128)(2,1)S(1)} all-gather(bf16[1,1,128]{2,1,0:T(2,128)(2,1)S(1)} %bitcast.268), channel_id=1, replica_groups=mesh['fsdp'=8,'dp'=4] {'fsdp'}, dimensions={0}, use_global_device_ids=true | all-gather | bytes 2304 | tf_op jit(solution)/shard_map/all_gather | solution.py:125
  195.9 16.1 %all-gather.1 = bf16[8,1,128]{2,1,0:T(2,128)(2,1)S(1)} all-gather(bf16[1,1,128]{2,1,0:T(2,128)(2,1)S(1)} %bitcast.269), channel_id=1, replica_groups=mesh['fsdp'=8,'dp'=4] {'fsdp'}, dimensions={0}, use_global_device_ids=true | all-gather | bytes 2304 | tf_op jit(solution)/shard_map/all_gather | solution.py:126
  214.7 30.7 %all_gather.61 = bf16[128,512]{0,1:T(8,128)(2,1)S(1)} all-gather(bf16[128,64]{0,1:T(8,128)(2,1)S(1)} %copy-done.31), channel_id=1, replica_groups=mesh['fsdp'=8,'dp'=4] {'fsdp'}, dimensions={1}, use_global_device_ids=true | all-gather | bytes 147456 | tf_op jit(solution)/shard_map/all_gather | solution.py:116
  253.9 28.5 %all_gather.63 = bf16[256,1024]{1,0:T(8,128)(2,1)} all-gather(bf16[256,128]{1,0:T(8,128)(2,1)S(1)} %copy-done.25), channel_id=1, replica_groups=mesh['fsdp'=8,'dp'=4] {'fsdp'}, dimensions={1}, use_global_device_ids=true | all-gather | bytes 589824 | tf_op jit(solution)/shard_map/all_gather | solution.py:118
  315.1 38.4 %all-reduce.19 = (f32[512]{0:T(512)S(1)}, f32[512]{0:T(512)S(1)}) all-reduce(f32[512]{0:T(512)S(1)} %get-tuple-element.307, f32[512]{0:T(512)S(1)} %get-tuple-element.306), channel_id=1, replica_groups=mesh['fsdp'=8,'dp'=4] {'fsdp','dp'}, use_global_device_ids=true, to_apply=%region_9.10 | all-reduce | flops 1024 | bytes 8192 | tf_op jit(solution)/shard_map/psum | solution.py:60
  366.1 41.7 %all-reduce.18 = (f32[128]{0:T(128)S(1)}, f32[]{:T(128)}, f32[128]{0:T(128)S(1)}) all-reduce(f32[128]{0:T(128)S(1)} %get-tuple-element.317, f32[]{:T(128)} %constant.523.clone.1, f32[128]{0:T(128)S(1)} %get-tuple-element.316), channel_id=1, replica_groups=mesh['fsdp'=8,'dp'=4] {'fsdp','dp'}, use_global_device_ids=true, to_apply=%region_12.13 | all-reduce | flops 257 | bytes 2056 | tf_op jit(solution)/shard_map/psum | solution.py:60
  423.9 39.5 %all-reduce.17 = (f32[1024]{0:T(1024)S(1)}, f32[1024]{0:T(1024)S(1)}) all-reduce(f32[1024]{0:T(1024)S(1)} %get-tuple-element.302, f32[1024]{0:T(1024)S(1)} %get-tuple-element.301), channel_id=1, replica_groups=mesh['fsdp'=8,'dp'=4] {'fsdp','dp'}, use_global_device_ids=true, to_apply=%region_20.21 | all-reduce | flops 2048 | bytes 16384 | tf_op jit(solution)/shard_map/psum | solution.py:60
  464.8 27.5 %fusion.2 = (f32[]{:T(128)}, f32[1024]{0:T(1024)S(1)}, f32[1024]{0:T(1024)S(1)}, f32[4096,1024]{1,0:T(8,128)}, f32[]{:T(128)}, /*index=5*/bf16[4096,1024]{1,0:T(8,128)(2,1)}) fusion(f32[4096,1024]{1,0:T(8,128)} %get-tuple-element.395, f32[1024]{0:T(1024)S(1)} %bitcast.267, f32[1024]{0:T(1024)S(1)} %add_rsqrt_fusion, f32[1024]{0:T(1024)S(1)} %get-tuple-element.367, ...), kind=kLoop, calls=%fused_computation.6 | loop fusion | flops 113244160 | bytes 58761224 | tf_op jit(solution)/shard_map/reduce_sum | solution.py:183
  492.3 41.0 %all-reduce.16 = (f32[1024]{0:T(1024)S(1)}, f32[1024]{0:T(1024)S(1)}) all-reduce(f32[1024]{0:T(1024)S(1)} %get-tuple-element.304, f32[1024]{0:T(1024)S(1)} %get-tuple-element.305), channel_id=1, replica_groups=mesh['fsdp'=8,'dp'=4] {'fsdp','dp'}, use_global_device_ids=true, to_apply=%region_26.27 | all-reduce | flops 2048 | bytes 16384 | tf_op jit(solution)/shard_map/psum | solution.py:75
  533.3 12.7 %multiply_convert_fusion = bf16[4096,1024]{1,0:T(8,128)(2,1)S(1)} fusion(f32[4096,1024]{1,0:T(8,128)} %get-tuple-element.368, f32[4096,1024]{1,0:T(8,128)} %get-tuple-element.395, f32[]{:T(128)} %get-tuple-element.335, f32[1024]{0:T(1024)S(1)} %get-tuple-element.325, f32[1024]{0:T(1024)S(1)} %get-tuple-element.326, f32[1024]{0:T(1024)S(1)} %get-tuple-element.366, ...), kind=kLoop, calls=%fused_computation.11 | loop fusion | flops 37748736 | bytes 41979908 | tf_op jit(solution)/shard_map/convert_element_type | solution.py:210
  566.4 39.5 %all-reduce.15 = (f32[128]{0:T(128)S(1)}, f32[128]{0:T(128)S(1)}) all-reduce(f32[128]{0:T(128)S(1)} %get-tuple-element.315, f32[128]{0:T(128)S(1)} %get-tuple-element.314), channel_id=1, replica_groups=mesh['fsdp'=8,'dp'=4] {'fsdp','dp'}, use_global_device_ids=true, to_apply=%region_32.33 | all-reduce | flops 256 | bytes 2048 | tf_op jit(solution)/shard_map/psum | solution.py:75
  613.5 11.7 copy.186
  633.4 41.1 %all-reduce.14 = (f32[512]{0:T(512)S(1)}, f32[512]{0:T(512)S(1)}) all-reduce(f32[512]{0:T(512)S(1)} %get-tuple-element.309, f32[512]{0:T(512)S(1)} %get-tuple-element.308), channel_id=1, replica_groups=mesh['fsdp'=8,'dp'=4] {'fsdp','dp'}, use_global_device_ids=true, to_apply=%region_36.37 | all-reduce | flops 1024 | bytes 8192 | tf_op jit(solution)/shard_map/psum | solution.py:75
  674.5 13.0 %multiply_convert_fusion.1 = bf16[4096,512]{0,1:T(8,128)(2,1)S(1)} fusion(f32[4096,512]{0,1:T(8,128)} %get-tuple-element.362, f32[]{:T(128)} %get-tuple-element.335, f32[512]{0:T(512)S(1)} %get-tuple-element.321, f32[512]{0:T(512)S(1)} %get-tuple-element.322, f32[512]{0:T(512)S(1)} %get-tuple-element.361, f32[512]{0:T(512)S(1)} %get-tuple-element.386, ...), kind=kLoop, calls=%fused_computation.23 | loop fusion | flops 20971520 | bytes 20998148 | tf_op jit(solution)/shard_map/convert_element_type | solution.py:241
  724.7 14.5 %scatter-add.61 = f32[16,18,18,128]{3,2,1,0:T(8,128)} dynamic-update-slice(f32[16,18,18,128]{3,2,1,0:T(8,128)} %scatter-add.60, f32[16,16,16,128]{3,2,1,0:T(8,128)} %fusion.24, s32[]{:T(128)} %constant.513.clone.1, s32[]{:T(128)} %bitcast.26, s32[]{:T(128)} %bitcast.27, s32[]{:T(128)} %constant.513.clone.1) | dynamic-update-slice | bytes 4194308 | tf_op jit(solution)/shard_map/scatter-add | solution.py:43
  745.3 14.2 %scatter-add.64 = f32[16,18,18,128]{3,2,1,0:T(8,128)} dynamic-update-slice(f32[16,18,18,128]{3,2,1,0:T(8,128)} %scatter-add.61, f32[16,16,16,128]{3,2,1,0:T(8,128)} %add_select_fusion.1, s32[]{:T(128)} %constant.513.clone.1, s32[]{:T(128)} %bitcast.29, s32[]{:T(128)} %bitcast.30, s32[]{:T(128)} %constant.513.clone.1) | dynamic-update-slice | bytes 4194308 | tf_op jit(solution)/shard_map/scatter-add | solution.py:43
  767.7 12.9 %scatter-add.66 = f32[16,18,18,128]{3,2,1,0:T(8,128)} dynamic-update-slice(f32[16,18,18,128]{3,2,1,0:T(8,128)} %fusion.23, f32[16,16,16,128]{3,2,1,0:T(8,128)} %fusion.21, s32[]{:T(128)} %constant.513.clone.1, s32[]{:T(128)} %constant.511.clone.1, s32[]{:T(128)} %constant.511.clone.1, s32[]{:T(128)} %constant.513.clone.1) | dynamic-update-slice | bytes 4194308 | tf_op jit(solution)/shard_map/scatter-add | solution.py:43
  784.8 12.9 %scatter-add.69 = f32[16,18,18,128]{3,2,1,0:T(8,128)} dynamic-update-slice(f32[16,18,18,128]{3,2,1,0:T(8,128)} %scatter-add.66, f32[16,16,16,128]{3,2,1,0:T(8,128)} %fusion.20, s32[]{:T(128)} %constant.513.clone.1, s32[]{:T(128)} %constant.511.clone.1, s32[]{:T(128)} %constant.516.clone.1, s32[]{:T(128)} %constant.513.clone.1) | dynamic-update-slice | bytes 4194308 | tf_op jit(solution)/shard_map/scatter-add | solution.py:43
  805.8 12.9 %scatter-add.71 = f32[16,18,18,128]{3,2,1,0:T(8,128)} dynamic-update-slice(f32[16,18,18,128]{3,2,1,0:T(8,128)} %fusion.19, f32[16,16,16,128]{3,2,1,0:T(8,128)} %fusion.17, s32[]{:T(128)} %constant.513.clone.1, s32[]{:T(128)} %constant.516.clone.1, s32[]{:T(128)} %constant.511.clone.1, s32[]{:T(128)} %constant.513.clone.1) | dynamic-update-slice | bytes 4194308 | tf_op jit(solution)/shard_map/scatter-add | solution.py:43
  822.9 12.9 %scatter-add.74 = f32[16,18,18,128]{3,2,1,0:T(8,128)} dynamic-update-slice(f32[16,18,18,128]{3,2,1,0:T(8,128)} %scatter-add.71, f32[16,16,16,128]{3,2,1,0:T(8,128)} %fusion.16, s32[]{:T(128)} %constant.513.clone.1, s32[]{:T(128)} %constant.516.clone.1, s32[]{:T(128)} %constant.516.clone.1, s32[]{:T(128)} %constant.513.clone.1) | dynamic-update-slice | bytes 4194308 | tf_op jit(solution)/shard_map/scatter-add | solution.py:43
  839.2 12.4 scatter-add.76
  856.7 12.3 scatter-add.79
  940.7 39.3 %all-reduce.13 = (f32[256]{0:T(256)S(1)}, f32[256]{0:T(256)S(1)}, f32[4]{0:T(128)S(1)}) all-reduce(f32[256]{0:T(256)S(1)} %get-tuple-element.313, f32[256]{0:T(256)S(1)} %get-tuple-element.312, f32[4]{0:T(128)S(1)} %pad_maximum_fusion.3), channel_id=1, replica_groups=mesh['fsdp'=8,'dp'=4] {'fsdp','dp'}, use_global_device_ids=true, to_apply=%region_41.42 | all-reduce | flops 516 | bytes 4128 | tf_op jit(solution)/shard_map/psum | solution.py:75
  991.5 12.8 %copy.156 = bf16[4096,1152]{0,1:T(8,128)(2,1)} copy(bf16[4096,1152]{1,0:T(8,128)(2,1)} %bitcast.239) | data formatting | bytes 18874368 | tf_op jit(solution)/shard_map/reshape | solution.py:33
  1004.3 12.7 %copy.158 = bf16[4096,1152]{0,1:T(8,128)(2,1)} copy(bf16[4096,1152]{1,0:T(8,128)(2,1)} %bitcast.234) | data formatting | bytes 18874368 | tf_op jit(solution)/shard_map/reshape | solution.py:33
  1040.6 101.0 %all-reduce.29 = (bf16[2,9,128,256]{2,0,1,3:T(2,128)(2,1)}, bf16[512]{0:T(512)(128)(2,1)S(1)}) all-reduce(f32[2,9,128,256]{2,0,1,3:T(2,128)} %copy.160, f32[512]{0:T(512)S(1)} %copy-done.50), channel_id=3, replica_groups=mesh['fsdp'=8,'dp'=4] {'fsdp'}, use_global_device_ids=true, to_apply=%region_49.50.clone | all-reduce | flops 590336 | bytes 3542016
  1166.5 23.4 %reduce-scatter.9.cloned.1.call-done = f32[128,64]{0,1:T(8,128)} async-done(((f32[128,512]{0,1:T(8,128)}), f32[128,64]{0,1:T(8,128)}) %reduce-scatter.9.cloned.1.call-update) | async-done | bytes 32784 | tf_op jit(solution)/shard_map/reduce_scatter | solution.py:265
  1203.1 20.8 %all-reduce.28.cloned.1.call-done = (bf16[2,9,128,32]{2,0,1,3:T(2,128)(2,1)}, bf16[128,256]{1,0:T(8,128)(2,1)}, bf16[256,128]{1,0:T(8,128)(2,1)}) async-done(((bf16[2,9,128,32]{2,0,1,3:T(2,128)(2,1)}, bf16[128,256]{1,0:T(8,128)(2,1)}, bf16[256,128]{1,0:T(8,128)(2,1)}), (bf16[2,9,128,32]{2,0,1,3:T(2,128)(2,1)}, bf16[128,256]{1,0:T(8,128)(2,1)}, bf16[256,128]{1,0:T(8,128)(2,1)})) %all-reduce.28.cloned.1.call-update) | async-done | bytes 278544 | tf_op jit(solution)/shard_map/psum | solution.py:271
  (354 shorter events, 374.8 us)
Async XLA Ops:
  7.2 281.5 %all-gather.4.cloned.1.call-start = ((), (), s32[]{:S(2)}) async-start(), calls=%async_computation.4 | async-start | bytes 1327104 | tf_op jit(solution)/shard_map/all_gather | solution.py:114
  8.9 1152.5 %reduce-scatter.11.cloned.1.call-start = ((), (), s32[]{:S(2)}) async-start(), calls=%async_computation.8 | async-start | bytes 1179648 | tf_op jit(solution)/shard_map/reduce_scatter | solution.py:267
  9.7 272.7 %copy-start.19 = (f32[16,256]{1,0:T(8,128)}, f32[16,256]{1,0:T(8,128)S(1)}, u32[]{:S(2)}) copy-start(f32[16,256]{1,0:T(8,128)S(1)} %get-tuple-element.384) | copy-start | bytes 49156
  43.2 130.4 %copy-start.72 = (bf16[128]{0:T(256)(128)(2,1)}, bf16[128]{0:T(256)(128)(2,1)S(1)}, u32[]{:S(2)}) copy-start(bf16[128]{0:T(256)(128)(2,1)S(1)} %get-tuple-element.345) | copy-start | bytes 772
  77.3 53.9 %copy-start.57 = (f32[256]{0:T(256)}, f32[256]{0:T(256)S(1)}, u32[]{:S(2)}) copy-start(f32[256]{0:T(256)S(1)} %convert_element_type.145) | copy-start | bytes 3076
  77.4 53.9 %copy-start.59 = (f32[256]{0:T(256)}, f32[256]{0:T(256)S(1)}, u32[]{:S(2)}) copy-start(f32[256]{0:T(256)S(1)} %convert_element_type.150) | copy-start | bytes 3076
  138.8 36.5 %copy-start.66 = (bf16[128]{0:T(256)(128)(2,1)S(1)}, bf16[128]{0:T(256)(128)(2,1)}, u32[]{:S(2)}) copy-start(bf16[128]{0:T(256)(128)(2,1)} %param.69) | copy-start | bytes 772
  138.8 57.2 %copy-start.67 = (bf16[128]{0:T(256)(128)(2,1)S(1)}, bf16[128]{0:T(256)(128)(2,1)}, u32[]{:S(2)}) copy-start(bf16[128]{0:T(256)(128)(2,1)} %param.70) | copy-start | bytes 772
  138.8 75.2 %copy-start.75 = (s32[4]{0:T(128)S(1)}, s32[4]{0:T(128)}, u32[]{:S(2)}) copy-start(s32[4]{0:T(128)} %constant.526.clone.1) | copy-start | bytes 52
  138.8 75.9 %copy-start.31 = (bf16[128,64]{0,1:T(8,128)(2,1)S(1)}, bf16[128,64]{0,1:T(8,128)(2,1)}, u32[]{:S(2)}) copy-start(bf16[128,64]{0,1:T(8,128)(2,1)} %param.60) | copy-start | bytes 49156
  140.4 142.0 %slice-start = ((s8[8388608]{0:T(1024)(128)(4,1)}), s8[4194304]{0:T(1024)(128)(4,1)S(1)}, s32[]{:S(2)}) async-start(s8[8388608]{0:T(1024)(128)(4,1)} %bitcast.224), calls=%async_computation.10 | async-start | bytes 8388608
  307.7 45.7 %copy-start.43 = (bf16[512]{0:T(512)(128)(2,1)S(1)}, bf16[512]{0:T(512)(128)(2,1)}, u32[]{:S(2)}) copy-start(bf16[512]{0:T(512)(128)(2,1)} %copy-done.42) | copy-start | bytes 3076
  307.7 46.4 %copy-start.20 = (f32[16,256]{1,0:T(8,128)S(1)}, f32[16,256]{1,0:T(8,128)}, u32[]{:S(2)}) copy-start(f32[16,256]{1,0:T(8,128)} %copy-done.19) | copy-start | bytes 49156
  307.7 46.4 %copy-start.46 = (f32[2,256]{1,0:T(2,128)S(1)}, f32[2,256]{1,0:T(2,128)}, u32[]{:S(2)}) copy-start(f32[2,256]{1,0:T(2,128)} %mul.513) | copy-start | bytes 6148
  307.7 46.4 %copy-start.47 = (f32[2,256]{1,0:T(2,128)S(1)}, f32[2,256]{1,0:T(2,128)}, u32[]{:S(2)}) copy-start(f32[2,256]{1,0:T(2,128)} %add.426) | copy-start | bytes 6148
  354.2 53.6 %copy-start.73 = (bf16[128]{0:T(256)(128)(2,1)S(1)}, bf16[128]{0:T(256)(128)(2,1)}, u32[]{:S(2)}) copy-start(bf16[128]{0:T(256)(128)(2,1)} %copy-done.72) | copy-start | bytes 772
  354.2 54.3 %copy-start.48 = (f32[512]{0:T(512)S(1)}, f32[512]{0:T(512)}, u32[]{:S(2)}) copy-start(f32[512]{0:T(512)} %convert_element_type.157) | copy-start | bytes 6148
  354.2 54.3 %copy-start.51 = (f32[128]{0:T(128)S(1)}, f32[128]{0:T(128)}, u32[]{:S(2)}) copy-start(f32[128]{0:T(128)} %convert_element_type.143) | copy-start | bytes 1540
  354.2 54.3 %copy-start.53 = (f32[128]{0:T(128)S(1)}, f32[128]{0:T(128)}, u32[]{:S(2)}) copy-start(f32[128]{0:T(128)} %convert_element_type.155) | copy-start | bytes 1540
  365.9 47.6 %copy-start.26 = (f32[16,256]{1,0:T(8,128)}, f32[16,256]{1,0:T(8,128)S(1)}, u32[]{:S(2)}) copy-start(f32[16,256]{1,0:T(8,128)S(1)} %copy.129) | copy-start | bytes 49156
  366.1 239.8 %copy-start.23 = (f32[16,128]{1,0:T(8,128)}, f32[16,128]{1,0:T(8,128)S(1)}, u32[]{:S(2)}) copy-start(f32[16,128]{1,0:T(8,128)S(1)} %get-tuple-element.394) | copy-start | bytes 24580
  408.5 197.5 %copy-start.38 = (f32[128]{0:T(128)}, f32[128]{0:T(128)S(1)}, u32[]{:S(2)}) copy-start(f32[128]{0:T(128)S(1)} %get-tuple-element.364) | copy-start | bytes 1540
  408.5 197.5 %copy-start.40 = (f32[128]{0:T(128)}, f32[128]{0:T(128)S(1)}, u32[]{:S(2)}) copy-start(f32[128]{0:T(128)S(1)} %get-tuple-element.365) | copy-start | bytes 1540
  416.1 47.3 %copy-start.29 = (f32[8,1,128]{2,1,0:T(1,128)S(1)}, f32[8,1,128]{2,1,0:T(1,128)}, u32[]{:S(2)}) copy-start(f32[8,1,128]{2,1,0:T(1,128)} %convert_element_type.181) | copy-start | bytes 12292
  416.1 48.6 %copy-start.30 = (f32[8,1,128]{2,1,0:T(1,128)S(1)}, f32[8,1,128]{2,1,0:T(1,128)}, u32[]{:S(2)}) copy-start(f32[8,1,128]{2,1,0:T(1,128)} %convert_element_type.182) | copy-start | bytes 12292
  566.3 47.2 %copy-start.21 = (bf16[16,512]{1,0:T(8,128)(2,1)}, bf16[16,512]{1,0:T(8,128)(2,1)S(1)}, u32[]{:S(2)}) copy-start(bf16[16,512]{1,0:T(8,128)(2,1)S(1)} %get-tuple-element.353) | copy-start | bytes 49156
  724.7 438.3 %reduce-scatter.5.cloned.1.call-start = ((), (), s32[]{:S(2)}) async-start(), calls=%async_computation.5 | async-start | bytes 1179648 | tf_op jit(solution)/shard_map/reduce_scatter | solution.py:262
  933.8 46.1 %copy-start.61 = (f32[256]{0:T(256)S(1)}, f32[256]{0:T(256)}, u32[]{:S(2)}) copy-start(f32[256]{0:T(256)} %get-tuple-element.354) | copy-start | bytes 3076
  991.4 174.3 %reduce-scatter.7.cloned.1.call-start = ((), (), s32[]{:S(2)}) async-start(), calls=%async_computation.6 | async-start | bytes 147456 | tf_op jit(solution)/shard_map/reduce_scatter | solution.py:264
  1031.5 158.4 %reduce-scatter.9.cloned.1.call-start = ((), (), s32[]{:S(2)}) async-start(), calls=%async_computation.7 | async-start | bytes 294912 | tf_op jit(solution)/shard_map/reduce_scatter | solution.py:265
  1034.4 107.2 %copy-start.15 = (bf16[1024,256]{1,0:T(8,128)(2,1)S(1)}, bf16[1024,256]{1,0:T(8,128)(2,1)}, u32[]{:S(2)}) copy-start(bf16[1024,256]{1,0:T(8,128)(2,1)} %copy-done.14) | copy-start | bytes 1572868
  1040.5 183.4 %all-reduce.28.cloned.1.call-start = ((), (), s32[]{:S(2)}) async-start(), calls=%async_computation.9 | async-start | bytes 557056 | tf_op jit(solution)/shard_map/psum | solution.py:271
  (56 other events, 467.1 us)
Sparse Core Ops, SparseCore 0:
  10.8 46.5 all-gather.3
  724.8 62.9 reduce-scatter.10
  991.6 67.0 reduce-scatter.4
  1062.4 62.2 reduce-scatter.6
  1128.5 61.3 reduce-scatter.8
  1192.8 31.0 all-reduce.27
where the time goes:
time: 1250 us; the launch traced here: 1240 us
  blocking collectives  613 us (49%)
  local copies, waits for them, and re-layouts  279 us (22%)
  other arithmetic  210 us (17%)
  matrix products  70.5 us (6%)
  waiting for transfers between devices  44.3 us (4%)
  between operations  19.2 us (2%)
    psum x4, blocking collectives, norm_back(): lax.psum((jnp.sum(grad_norm, axis=0), jnp.sum(grad_norm * normed, axis=0)...  161 us
    psum x4, blocking collectives, moments_of(): lax.psum((jnp.sum(weight * values, axis=0), jnp.sum(weight * values * val...  157 us
    scatter-add x14, local copies, waits for them, and re-layouts, unpatch(): summed = summed.at[:, row_shift:row_shift + extent, col_shift:col_shift +...  152 us
    unnamed x2, blocking collectives  125 us
    unnamed x203, local copies, waits for them, and re-layouts  59.5 us
    add x10, other arithmetic, unpatch(): summed = summed.at[:, row_shift:row_shift + extent, col_shift:col_shift +...  39.1 us
    all_gather x1, blocking collectives, local(): lax.all_gather(attn_down, 'fsdp', axis=0, tiled=True)  32.6 us
    all_gather x1, blocking collectives, local(): lax.all_gather(conv_in, 'fsdp', axis=0, tiled=True)  31.8 us
  transfers between devices with their start and end apart: 6, of which 2 were waited for; matrix products, arithmetic and copies ran while one was open for 28% of the time, Pallas kernels for 0%

commit v1 on v0

v1 whole, which is shorter than its diff:
```python
import jax
import jax.numpy as jnp
from jax import lax
from jax.experimental import pallas as pl
from jax.experimental.pallas import tpu as pltpu
from jax.sharding import PartitionSpec as P

RADIX = 2
SIDE = 16
TAPS = 9
STEP = 2

epsilon = 1e-05
AXES = ("fsdp", "dp")
f32 = jnp.float32
bf16 = jnp.bfloat16
HIGH = lax.Precision.HIGHEST


def swap_all(values, axes):
    return lax.all_to_all(values, axes, 0, 0)


def all_sum(values):
    devices = lax.axis_size("fsdp") * lax.axis_size("dp")
    copies = jnp.broadcast_to(values[None], (devices,) + values.shape)
    return jnp.sum(swap_all(copies, AXES), axis=0)


def spread_dp(values):
    count = lax.axis_size("dp")
    return swap_all(jnp.broadcast_to(values[None], (count,) + values.shape), "dp")


def gather_rows(shard):
    pieces = lax.axis_size("fsdp")
    count = lax.axis_size("dp")
    rows, lanes = shard.shape
    odd = lax.rem(lax.axis_index("dp"), 2)
    half = lax.dynamic_slice_in_dim(shard, odd * (rows // 2), rows // 2, 0)
    mine = swap_all(jnp.broadcast_to(half[None], (pieces,) + half.shape), "fsdp")
    other = lax.ppermute(mine, "dp", [(i, i ^ 1) for i in range(count)])
    low = jnp.where(odd == 0, mine, other)
    high = jnp.where(odd == 0, other, mine)
    return jnp.stack([low, high], axis=1).reshape(pieces * rows, lanes)


def scatter_sum(parts):
    summed = jnp.sum(swap_all(parts, AXES).astype(f32), axis=0).astype(bf16)
    return spread_dp(summed)


def sigmoid(values):
    return 0.5 * jnp.tanh(0.5 * values) + 0.5


def fold(values):
    return values[:8] + values[8:]


def wide(mask, lanes):
    return jnp.concatenate([mask] * (lanes // mask.shape[1]), axis=1)


def places():
    return lax.broadcasted_iota(jnp.int32, (SIDE, 128), 0)


def row_mask(place, row, limit):
    return jnp.where((place < limit) & (row < limit), 1.0, 0.0).astype(f32)


def chunk(image, row):
    return pl.ds(pl.multiple_of(image * 256 + row * SIDE, SIDE), SIDE)


def rows_of(carry, body, unroll=2):
    return lax.fori_loop(0, SIDE, body, carry, unroll=unroll)


def contract_lead(left, right):
    return lax.dot_general(left, right, (((0,), (0,)), ((), ())), preferred_element_type=f32)


def contract_last(left, right):
    return lax.dot_general(left, right, (((1,), (1,)), ((), ())), preferred_element_type=f32)


def zeros_at_start(*refs):
    @pl.when(pl.program_id(0) == 0)
    def _():
        for ref in refs:
            ref[...] = jnp.zeros(ref.shape, ref.dtype)


def last_step():
    return pl.program_id(0) == pl.num_programs(0) - 1


def column_total(values):
    return jnp.sum(values, axis=0, keepdims=True)


def first_kernel(sides, x_ref, w_ref, first_ref, stat_ref, acc_ref):
    step = pl.program_id(0)
    zeros_at_start(acc_ref)
    first_ref[...] = jnp.dot(x_ref[...], w_ref[...], preferred_element_type=f32)
    place = places()
    lanes = first_ref.shape[1]
    for image in range(STEP):
        limit = 2 * sides[step * STEP + image]

        def body(row, carry):
            total, square = carry
            here = chunk(image, row)
            values = first_ref[here, :] * wide(row_mask(place, row, limit), lanes)
            first_ref[here, :] = values
            return (total + fold(values), square + fold(values * values))

        total, square = rows_of((acc_ref[0], acc_ref[1]), body)
        acc_ref[0] = total
        acc_ref[1] = square

    @pl.when(last_step())
    def _():
        stat_ref[...] = jnp.zeros(stat_ref.shape, f32)
        stat_ref[0:1, :] = column_total(acc_ref[0])
        stat_ref[1:2, :] = column_total(acc_ref[1])


def cross_kernel(sides, x_ref, first_ref, cross_ref, square_ref, ones_ref):
    step = pl.program_id(0)
    zeros_at_start(cross_ref, square_ref, ones_ref)
    cross_ref[...] += contract_lead(first_ref[...].astype(bf16), x_ref[...])
    place = places()
    lanes = x_ref.shape[1]
    for image in range(STEP):
        limit = 2 * sides[step * STEP + image]

        def body(row, carry):
            square, total = carry
            values = x_ref[chunk(image, row), :].astype(f32) * wide(
                row_mask(place, row, limit), lanes
            )
            return (square + fold(values * values), total + fold(values))

        square, total = rows_of((square_ref[...], ones_ref[...]), body)
        square_ref[...] = square
        ones_ref[...] = total


def write_patches(patch_ref, image, row, low, place):
    values = low.astype(f32)
    lanes = values.shape[1]
    inner = wide(place, lanes)
    left = jnp.where(inner == 0, 0.0, pltpu.roll(values, 1, 0)).astype(bf16)
    right = jnp.where(inner == SIDE - 1, 0.0, pltpu.roll(values, SIDE - 1, 0)).astype(bf16)
    half = lanes // RADIX
    for tap in range(TAPS):
        up, side = tap // 3, tap % 3
        source = (left, low, right)[side]
        here = pl.ds(pl.multiple_of((row + 2 - up) * SIDE, SIDE), SIDE)
        for group in range(RADIX):
            at = group * TAPS * half + tap * half
            patch_ref[image, here, at : at + half] = source[:, group * half : (group + 1) * half]


def second_kernel(sides, first_ref, ab_ref, w_ref, act_ref, second_ref, stat_ref, patch_ref, acc_ref):
    step = pl.program_id(0)
    zeros_at_start(acc_ref, patch_ref)
    place = places()
    lanes = first_ref.shape[1]
    columns = TAPS * lanes // RADIX
    for image in range(STEP):
        limit = 2 * sides[step * STEP + image]

        def body(row, carry):
            here = chunk(image, row)
            pre = first_ref[here, :] * ab_ref[0:1, :] + ab_ref[1:2, :]
            act = pre * (sigmoid(pre) * wide(row_mask(place, row, limit), lanes))
            low = act.astype(bf16)
            act_ref[here, :] = low
            write_patches(patch_ref, image, row, low, place)
            return carry

        rows_of(0, body)
    for image in range(STEP):
        for group in range(RADIX):
            second_ref[image * 256 : image * 256 + 256, group * lanes : (group + 1) * lanes] = (
                contract_last(
                    patch_ref[image, SIDE : SIDE + 256, group * columns : (group + 1) * columns],
                    w_ref[:, group * columns : (group + 1) * columns],
                )
            )
    for image in range(STEP):
        limit = 2 * sides[step * STEP + image]

        def body(row, carry):
            total, square = carry
            values = second_ref[chunk(image, row), :]
            values = values * wide(row_mask(place, row, limit), values.shape[1])
            return (total + fold(values), square + fold(values * values))

        total, square = rows_of((acc_ref[0], acc_ref[1]), body)
        acc_ref[0] = total
        acc_ref[1] = square

    @pl.when(last_step())
    def _():
        stat_ref[...] = jnp.zeros(stat_ref.shape, f32)
        stat_ref[0:1, :] = column_total(acc_ref[0])
        stat_ref[1:2, :] = column_total(acc_ref[1])


def pool_kernel(sides, second_ref, ab_ref, down_ref, pooled_ref, squeeze_ref, stat_ref, pool_ref):
    step = pl.program_id(0)
    place = places()
    lanes = second_ref.shape[1]
    for image in range(STEP):
        limit = 2 * sides[step * STEP + image]

        def body(row, total):
            pre = second_ref[chunk(image, row), :] * ab_ref[0:1, :] + ab_ref[1:2, :]
            act = pre * (sigmoid(pre) * wide(row_mask(place, row, limit), lanes))
            return total + fold(act)

        total = column_total(rows_of(jnp.zeros((8, lanes), f32), body))
        both = total[:, : lanes // 2] + total[:, lanes // 2 :]
        area = jnp.full(both.shape, limit * limit, jnp.int32).astype(f32)
        pool_ref[pl.ds(step * STEP + image, 1), :] = both / area

    @pl.when(last_step())
    def _():
        low = pool_ref[...].astype(bf16)
        pooled_ref[...] = low
        squeeze = jnp.dot(low, down_ref[...], preferred_element_type=f32)
        squeeze_ref[...] = squeeze
        stat_ref[...] = jnp.zeros(stat_ref.shape, f32)
        stat_ref[0:1, :] = column_total(squeeze)
        stat_ref[1:2, :] = column_total(squeeze * squeeze)


def mix_kernel(
    sides,
    second_ref,
    ab_ref,
    squeeze_ref,
    gate_ref,
    up_ref,
    bias_ref,
    out_ref,
    mixed_ref,
    weights_ref,
    excite_ref,
    gram_ref,
    gw_ref,
    stat_ref,
    colsum_ref,
    power_ref,
    acc_ref,
):
    step = pl.program_id(0)
    zeros_at_start(acc_ref, gram_ref)
    place = places()
    lanes = second_ref.shape[1]
    half = lanes // 2

    @pl.when(step == 0)
    def _():
        pre = squeeze_ref[...] * gate_ref[0:1, :] + gate_ref[1:2, :]
        excite = (pre * sigmoid(pre)).astype(bf16)
        excite_ref[...] = excite
        logits = contract_last(excite, up_ref[...]) + bias_ref[0:1, :]
        one, two = logits[:, :half], logits[:, half:]
        top = jnp.maximum(one, two)
        one, two = jnp.exp(one - top), jnp.exp(two - top)
        weights_ref[:, :half] = one / (one + two)
        weights_ref[:, half:] = two / (one + two)

    for image in range(STEP):
        limit = 2 * sides[step * STEP + image]
        weights = weights_ref[pl.ds(step * STEP + image, 1), :]

        def body(row, carry):
            total, square = carry
            here = chunk(image, row)
            pre = second_ref[here, :] * ab_ref[0:1, :] + ab_ref[1:2, :]
            act = pre * (sigmoid(pre) * wide(row_mask(place, row, limit), lanes))
            act = act * weights
            mixed = act[:, :half] + act[:, half:]
            low = mixed.astype(bf16)
            mixed_ref[here, :] = low
            return (total + fold(low.astype(f32)), square + fold(mixed * mixed))

        total, square = rows_of((acc_ref[0], acc_ref[1]), body)
        acc_ref[0] = total
        acc_ref[1] = square
    gram_ref[...] += contract_lead(mixed_ref[...], mixed_ref[...])

    @pl.when(last_step())
    def _():
        whole = out_ref[...].astype(f32)
        total = column_total(acc_ref[0])
        colsum_ref[...] = jnp.broadcast_to(total, colsum_ref.shape)
        power_ref[...] = acc_ref[1]
        gw = jnp.dot(gram_ref[...], whole, precision=HIGH, preferred_element_type=f32)
        gw_ref[...] = gw
        stat_ref[...] = jnp.zeros(stat_ref.shape, f32)
        sums = jnp.dot(
            jnp.broadcast_to(total, (8, half)), whole, precision=HIGH, preferred_element_type=f32
        )
        stat_ref[0:1, :] = sums[0:1, :]
        stat_ref[1:2, :] = column_total(gw * whole)


def out_kernel(
    sides,
    mixed_ref,
    x_ref,
    cot_ref,
    ab_ref,
    w_ref,
    wt_ref,
    block_ref,
    slope_ref,
    back_ref,
    grad_ref,
    stat_ref,
    power_ref,
    third_ref,
    acc_ref,
    square_ref,
):
    step = pl.program_id(0)
    zeros_at_start(acc_ref, square_ref, grad_ref)
    place = places()
    lanes = x_ref.shape[1]
    part = 512 if lanes % 512 == 0 else lanes
    third_ref[...] = jnp.dot(mixed_ref[...], w_ref[...], preferred_element_type=f32)
    for image in range(STEP):
        limit = 2 * sides[step * STEP + image]

        def body(row, square):
            here = chunk(image, row)
            mask = wide(row_mask(place, row, limit), part)
            for at in range(0, lanes, part):
                cut = slice(at, at + part)
                total = (
                    x_ref[here, cut].astype(f32)
                    + third_ref[here, cut] * ab_ref[0:1, cut]
                    + ab_ref[1:2, cut]
                )
                plain = sigmoid(total)
                gate = plain * mask
                output = total * gate
                block_ref[here, cut] = output.astype(bf16)
                slope = gate + output * (1.0 - plain)
                grad = cot_ref[here, cut].astype(f32) * (slope * ab_ref[0:1, cut])
                slope_ref[here, cut] = grad.astype(bf16)
                acc_ref[:, cut] += fold(grad)
                power = fold(output * output)
                for lane in range(0, part, 128):
                    square = square + power[:, lane : lane + 128]
            return square

        square_ref[...] = rows_of(square_ref[...], body, 1)
    back_ref[...] = jnp.dot(slope_ref[...], wt_ref[...], preferred_element_type=f32)
    grad_ref[...] += contract_lead(mixed_ref[...], slope_ref[...])

    @pl.when(last_step())
    def _():
        stat_ref[...] = jnp.zeros(stat_ref.shape, f32)
        stat_ref[0:1, :] = column_total(acc_ref[...])
        stat_ref[1:2, :] = column_total(grad_ref[...] * w_ref[...].astype(f32))
        power_ref[...] = square_ref[...]


def mid_terms(second_ref, ab_ref, here, mask):
    pre = second_ref[here, :] * ab_ref[0:1, :] + ab_ref[1:2, :]
    plain = sigmoid(pre)
    gate = plain * mask
    act = pre * gate
    return pre, act, gate + act * (1.0 - plain)


def gate_kernel(
    sides,
    second_ref,
    ab_ref,
    back_ref,
    mixed_ref,
    turn_ref,
    row_ref,
    weights_ref,
    excite_ref,
    squeeze_ref,
    gate_ref,
    up_ref,
    dmixed_ref,
    sums_ref,
    dup_ref,
    dbias_ref,
    dq_ref,
    stat_ref,
):
    step = pl.program_id(0)
    place = places()
    lanes = second_ref.shape[1]
    half = lanes // 2
    dmixed_ref[...] = back_ref[...] - jnp.dot(
        mixed_ref[...], turn_ref[...], preferred_element_type=f32
    )
    for image in range(STEP):
        limit = 2 * sides[step * STEP + image]

        def body(row, carry):
            here = chunk(image, row)
            mask = row_mask(place, row, limit)
            dmixed = (dmixed_ref[here, :] - row_ref[0:1, :]) * wide(mask, half)
            dmixed_ref[here, :] = dmixed
            both = jnp.concatenate([dmixed, dmixed], axis=1)
            pre, act, slope = mid_terms(second_ref, ab_ref, here, wide(mask, lanes))
            along = slope * both
            terms = (act * both, along, along * pre, slope, slope * pre)
            return tuple(old + fold(new) for old, new in zip(carry, terms))

        start = tuple(jnp.zeros((8, lanes), f32) for _ in range(5))
        totals = rows_of(start, body, 1)
        for index in range(5):
            sums_ref[index, pl.ds(step * STEP + image, 1), :] = column_total(totals[index])

    @pl.when(last_step())
    def _():
        weights = weights_ref[...]
        grads = sums_ref[0]
        mean = weights * grads
        mean = mean[:, :half] + mean[:, half:]
        dlogits = weights * (grads - jnp.concatenate([mean, mean], axis=1))
        dbias_ref[...] = jnp.broadcast_to(column_total(dlogits), dbias_ref.shape)
        low = dlogits.astype(bf16)
        dup_ref[...] = contract_lead(low, excite_ref[...])
        dexcite = jnp.dot(low, up_ref[...], preferred_element_type=f32)
        squeeze = squeeze_ref[...]
        pre = squeeze * gate_ref[0:1, :] + gate_ref[1:2, :]
        normed = squeeze * gate_ref[2:3, :] + gate_ref[3:4, :]
        plain = sigmoid(pre)
        dq = dexcite * (plain * (1.0 + pre * (1.0 - plain)))
        dq_ref[...] = dq
        stat_ref[...] = jnp.zeros(stat_ref.shape, f32)
        stat_ref[0:1, :] = column_total(dq)
        stat_ref[1:2, :] = column_total(dq * normed)


def squeeze_kernel(
    dq_ref,
    squeeze_ref,
    gate_ref,
    grads_ref,
    pooled_ref,
    down_ref,
    area_ref,
    weights_ref,
    sums_ref,
    ddown_ref,
    dpool_ref,
    stat_ref,
):
    normed = squeeze_ref[...] * gate_ref[2:3, :] + gate_ref[3:4, :]
    dsqueeze = gate_ref[0:1, :] * (
        dq_ref[...] - (grads_ref[0:1, :] + normed * grads_ref[1:2, :])
    )
    low = dsqueeze.astype(bf16)
    ddown_ref[...] = contract_lead(pooled_ref[...], low)
    dpool = contract_last(low, down_ref[...]) / area_ref[...]
    dpool_ref[...] = dpool
    both = jnp.concatenate([dpool, dpool], axis=1)
    weights = weights_ref[...]
    stat_ref[...] = jnp.zeros(stat_ref.shape, f32)
    stat_ref[0:1, :] = column_total(weights * sums_ref[1] + both * sums_ref[3])
    stat_ref[1:2, :] = column_total(weights * sums_ref[2] + both * sums_ref[4])


def conv_back_kernel(
    sides,
    second_ref,
    ab_ref,
    dmixed_ref,
    weights_ref,
    dpool_ref,
    first_ref,
    ab_in_ref,
    w_ref,
    dsecond_ref,
    dfirst_ref,
    stat_ref,
    column_ref,
    acc_ref,
):
    step = pl.program_id(0)
    zeros_at_start(acc_ref, column_ref)
    place = places()
    lanes = second_ref.shape[1]
    half = lanes // 2
    quarter = half // RADIX
    columns = TAPS * quarter
    for image in range(STEP):
        limit = 2 * sides[step * STEP + image]
        weights = weights_ref[pl.ds(step * STEP + image, 1), :]
        dpool = dpool_ref[pl.ds(step * STEP + image, 1), :]
        dpool = jnp.concatenate([dpool, dpool], axis=1)

        def body(row, carry):
            here = chunk(image, row)
            mask = wide(row_mask(place, row, limit), lanes)
            dmixed = dmixed_ref[here, :]
            both = jnp.concatenate([dmixed, dmixed], axis=1)
            pre, _, slope = mid_terms(second_ref, ab_ref, here, mask)
            grad = slope * (weights * both + dpool) * ab_ref[0:1, :]
            grad = grad - mask * (pre * ab_ref[2:3, :] + ab_ref[3:4, :])
            dsecond_ref[here, :] = grad.astype(bf16)
            return carry

        rows_of(0, body)
    for image in range(STEP):
        for group in range(RADIX):
            column_ref[image, SIDE : SIDE + 256, group * columns : (group + 1) * columns] = jnp.dot(
                dsecond_ref[image * 256 : image * 256 + 256, group * half : (group + 1) * half],
                w_ref[:, group * columns : (group + 1) * columns],
                preferred_element_type=f32,
            )
    for image in range(STEP):
        limit = 2 * sides[step * STEP + image]

        def body(row, carry):
            total, product = carry
            here = chunk(image, row)
            mask = row_mask(place, row, limit)
            parts = []
            for group in range(RADIX):
                sides_sum = []
                for side in range(3):
                    summed = None
                    for up in range(3):
                        at = group * columns + (up * 3 + side) * quarter
                        rows = pl.ds(pl.multiple_of((row + 2 - up) * SIDE, SIDE), SIDE)
                        piece = column_ref[image, rows, at : at + quarter]
                        summed = piece if summed is None else summed + piece
                    sides_sum.append(summed)
                inner = wide(place, quarter)
                low = jnp.where(inner == SIDE - 1, 0.0, pltpu.roll(sides_sum[0], SIDE - 1, 0))
                high = jnp.where(inner == 0, 0.0, pltpu.roll(sides_sum[2], 1, 0))
                parts.append(sides_sum[1] + low + high)
            dact = jnp.concatenate(parts, axis=1)
            first = first_ref[here, :]
            pre = first * ab_in_ref[0:1, :] + ab_in_ref[1:2, :]
            normed = first * ab_in_ref[2:3, :] + ab_in_ref[3:4, :]
            plain = sigmoid(pre)
            grad = dact * (plain * (1.0 + pre * (1.0 - plain)) * wide(mask, half))
            dfirst_ref[here, :] = grad
            return (total + fold(grad), product + fold(grad * normed))

        total, product = rows_of((acc_ref[0], acc_ref[1]), body, 1)
        acc_ref[0] = total
        acc_ref[1] = product

    @pl.when(last_step())
    def _():
        stat_ref[...] = jnp.zeros(stat_ref.shape, f32)
        stat_ref[0:1, :] = column_total(acc_ref[0])
        stat_ref[1:2, :] = column_total(acc_ref[1])


def conv_grad_kernel(act_ref, dsecond_ref, x_ref, dfirst_ref, conv_ref, in_ref, patch_ref):
    zeros_at_start(conv_ref, in_ref, patch_ref)
    place = places()
    lanes = act_ref.shape[1]
    columns = TAPS * lanes // RADIX
    for image in range(STEP):

        def body(row, carry):
            write_patches(patch_ref, image, row, act_ref[chunk(image, row), :], place)
            return carry

        rows_of(0, body)
    for image in range(STEP):
        for group in range(RADIX):
            conv_ref[:, group * columns : (group + 1) * columns] += contract_lead(
                dsecond_ref[image * 256 : image * 256 + 256, group * lanes : (group + 1) * lanes],
                patch_ref[image, SIDE : SIDE + 256, group * columns : (group + 1) * columns],
            )
    in_ref[...] += contract_lead(dfirst_ref[...].astype(bf16), x_ref[...])


def last_kernel(sides, dfirst_ref, first_ref, ab_ref, w_ref, slope_ref, scale_ref, out_ref, low_ref):
    step = pl.program_id(0)
    place = places()
    lanes = first_ref.shape[1]
    width = out_ref.shape[1]
    part = 512 if width % 512 == 0 else width
    for image in range(STEP):
        limit = 2 * sides[step * STEP + image]

        def body(row, carry):
            here = chunk(image, row)
            mask = wide(row_mask(place, row, limit), lanes)
            grad = dfirst_ref[here, :] * ab_ref[0:1, :]
            grad = grad - mask * (first_ref[here, :] * ab_ref[1:2, :] + ab_ref[2:3, :])
            low_ref[here, :] = grad.astype(bf16)
            return carry

        rows_of(0, body)
    out_ref[...] = contract_last(low_ref[...], w_ref[...])
    for image in range(STEP):

        def body(row, carry):
            here = chunk(image, row)
            for at in range(0, width, part):
                cut = slice(at, at + part)
                out_ref[here, cut] += slope_ref[here, cut].astype(f32) * scale_ref[0:1, cut]
            return carry

        rows_of(0, body)


def tiles(lanes):
    return pl.BlockSpec((STEP * 256, lanes), lambda i: (i, 0))


def held(*shape):
    return pl.BlockSpec(shape, lambda i: (0,) * len(shape))


def scalars():
    return pl.BlockSpec(memory_space=pltpu.SMEM)


def shaped(shape, dtype=f32):
    return jax.ShapeDtypeStruct(shape, dtype)


def call(kernel, steps, ins, outs, out_shapes, scratch=(), limit=48, name=None):
    return pl.pallas_call(
        kernel,
        grid=(steps,),
        in_specs=ins,
        out_specs=outs,
        out_shape=out_shapes,
        scratch_shapes=scratch,
        compiler_params=pltpu.CompilerParams(
            dimension_semantics=("arbitrary",), vmem_limit_bytes=limit * 1024 * 1024
        ),
        name=name,
    )


def rows8(*vectors):
    stacked = jnp.stack(vectors, axis=0)
    return jnp.pad(stacked, ((0, 8 - len(vectors)), (0, 0)))


def norm_terms(sums, squares, counted, gain, shift):
    center = sums / counted
    spread = squares / counted - center * center
    inv = lax.rsqrt(spread + epsilon)
    scale = gain * inv
    return center, spread, inv, scale, shift - center * scale


def local(
    features,
    half_sides,
    cotangent,
    conv_in,
    conv_mid,
    attn_down,
    attn_up,
    attn_bias,
    conv_out,
    gain_in,
    shift_in,
    gain_mid,
    shift_mid,
    gain_attn,
    shift_attn,
    gain_out,
    shift_out,
):
    images, pixels, width = features.shape
    rows = images * pixels
    steps = images // STEP
    pieces = lax.axis_size("fsdp")
    groups = lax.axis_size("dp")
    devices = pieces * groups
    bottleneck = conv_in.shape[1]
    att = attn_down.shape[1]
    mid = RADIX * bottleneck
    columns = RADIX * TAPS * conv_mid.shape[2]

    whole_in = gather_rows(conv_in)
    small = [gain_in, shift_in, gain_mid, shift_mid, gain_attn, shift_attn, gain_out, shift_out, attn_bias]
    lengths = [item.shape[0] for item in small]
    flat = jnp.concatenate(small)
    vector_rows = -(-flat.shape[0] // (4 * 128)) * 4
    flat = jnp.pad(flat, (0, vector_rows * 128 - flat.shape[0])).reshape(vector_rows, 128)
    out_cut = conv_out.T.reshape(-1, 128)
    packed = jnp.concatenate([out_cut, attn_down, attn_up.T, flat], axis=0)
    marks = [out_cut.shape[0], attn_down.shape[0], attn_up.shape[1]]
    packed = gather_rows(packed).reshape(pieces, -1, 128)
    whole_mid = gather_rows(conv_mid.transpose(3, 0, 1, 2).reshape(conv_mid.shape[3], columns))
    whole_out_t = packed[:, : marks[0]].reshape(width, bottleneck)
    whole_out = whole_out_t.T
    whole_down = packed[:, marks[0] : marks[0] + marks[1]].reshape(bottleneck, att)
    whole_up = packed[:, marks[0] + marks[1] : sum(marks)].reshape(mid, att)
    vectors = packed[:, sum(marks) :].reshape(pieces, -1)
    found = []
    at = 0
    for length in lengths:
        found.append(vectors[:, at : at + length].reshape(-1).astype(f32))
        at += length
    g_in, s_in, g_mid, s_mid, g_attn, s_attn, g_out, s_out, bias = found

    x = features.reshape(rows, width)
    cot = cotangent.reshape(rows, width)
    sides_float = 2.0 * half_sides.astype(f32)
    areas = sides_float * sides_float

    first, stat = call(
        first_kernel,
        steps,
        [scalars(), tiles(width), held(width, bottleneck)],
        [tiles(bottleneck), held(8, bottleneck)],
        [shaped((rows, bottleneck)), shaped((8, bottleneck))],
        [pltpu.VMEM((2, 8, bottleneck), f32)],
        name="first",
    )(half_sides, x, whole_in)
    stat = jnp.concatenate([stat[:2], jnp.full((1, bottleneck), jnp.sum(areas))], axis=0)
    stat = all_sum(stat)
    counted = stat[2, 0]
    c_in, _, i_in, a_in, b_in = norm_terms(stat[0], stat[1], counted, g_in, s_in)
    cross, x_square, x_sum = call(
        cross_kernel,
        steps,
        [scalars(), tiles(width), tiles(bottleneck)],
        [held(bottleneck, width), held(8, width), held(8, width)],
        [shaped((bottleneck, width)), shaped((8, width)), shaped((8, width))],
        name="cross",
    )(half_sides, x, first)

    act_low, second, stat = call(
        second_kernel,
        steps,
        [scalars(), tiles(bottleneck), held(8, bottleneck), held(bottleneck, columns)],
        [tiles(bottleneck), tiles(mid), held(8, mid)],
        [shaped((rows, bottleneck), bf16), shaped((rows, mid)), shaped((8, mid))],
        [pltpu.VMEM((STEP, 256 + 2 * SIDE, columns), bf16), pltpu.VMEM((2, 8, mid), f32)],
        name="second",
    )(half_sides, first, rows8(a_in, b_in), whole_mid)
    stat = all_sum(stat[:2])
    c_mid, _, i_mid, a_mid, b_mid = norm_terms(stat[0], stat[1], counted, g_mid, s_mid)
    ab_mid = rows8(a_mid, b_mid)

    pooled, squeeze, stat = call(
        pool_kernel,
        steps,
        [scalars(), tiles(mid), held(8, mid), held(bottleneck, att)],
        [held(images, bottleneck), held(images, att), held(8, att)],
        [shaped((images, bottleneck), bf16), shaped((images, att)), shaped((8, att))],
        [pltpu.VMEM((images, bottleneck), f32)],
        name="pool",
    )(half_sides, second, ab_mid, whole_down)
    stat = all_sum(stat[:2])
    counted_attn = jnp.float32(images * devices)
    c_attn, _, i_attn, a_attn, b_attn = norm_terms(stat[0], stat[1], counted_attn, g_attn, s_attn)
    gate = rows8(a_attn, b_attn, i_attn, -c_attn * i_attn)

    mixed, weights, excite, gram, gram_out, stat, colsum, power = call(
        mix_kernel,
        steps,
        [
            scalars(),
            tiles(mid),
            held(8, mid),
            held(images, att),
            held(8, att),
            held(mid, att),
            held(8, mid),
            held(bottleneck, width),
        ],
        [
            tiles(bottleneck),
            held(images, mid),
            held(images, att),
            held(bottleneck, bottleneck),
            held(bottleneck, width),
            held(8, width),
            held(8, bottleneck),
            held(8, bottleneck),
        ],
        [
            shaped((rows, bottleneck), bf16),
            shaped((images, mid)),
            shaped((images, att), bf16),
            shaped((bottleneck, bottleneck)),
            shaped((bottleneck, width)),
            shaped((8, width)),
            shaped((8, bottleneck)),
            shaped((8, bottleneck)),
        ],
        [pltpu.VMEM((2, 8, bottleneck), f32)],
        name="mix",
    )(half_sides, second, ab_mid, squeeze, gate, whole_up, rows8(bias), whole_out)
    sums_x = jnp.sum(x_square)
    sums_mixed = jnp.sum(power)
    lane = lax.broadcasted_iota(jnp.int32, (1, width), 1)
    extra = jnp.where(lane == 0, sums_x, jnp.where(lane == 1, sums_mixed, 0.0))
    stat = all_sum(jnp.concatenate([stat[:2], extra, column_total(x_sum)], axis=0))
    x_sum_all = stat[3]
    power_x, power_mixed = stat[2, 0], stat[2, 1]
    c_out, v_out, i_out, a_out, b_out = norm_terms(stat[0], stat[1], counted, g_out, s_out)
    power_branch = counted * jnp.sum(g_out * g_out * v_out * i_out * i_out + s_out * s_out)

    block, slope, back, grad_out, stat, power = call(
        out_kernel,
        steps,
        [
            scalars(),
            tiles(bottleneck),
            tiles(width),
            tiles(width),
            held(8, width),
            held(bottleneck, width),
            held(width, bottleneck),
        ],
        [
            tiles(width),
            tiles(width),
            tiles(bottleneck),
            held(bottleneck, width),
            held(8, width),
            held(8, 128),
        ],
        [
            shaped((rows, width), bf16),
            shaped((rows, width), bf16),
            shaped((rows, bottleneck)),
            shaped((bottleneck, width)),
            shaped((8, width)),
            shaped((8, 128)),
        ],
        [
            pltpu.VMEM((STEP * 256, width), f32),
            pltpu.VMEM((8, width), f32),
            pltpu.VMEM((8, 128), f32),
        ],
        name="output",
    )(half_sides, mixed, x, cot, rows8(a_out, b_out), whole_out, whole_out_t)
    extra = jnp.full((1, width), jnp.sum(power))
    stat = all_sum(jnp.concatenate([stat[:2], extra], axis=0))
    power_output = stat[2, 0]
    shift_out_grad = stat[0] / a_out
    gain_out_grad = (stat[1] - c_out * stat[0]) / g_out
    slant = a_out * i_out * gain_out_grad / counted
    level = stat[0] / counted - c_out * slant
    global_sums = jnp.stack([power_x, power_mixed, power_branch, power_output])
    widths = jnp.array([width, bottleneck, width, width], f32)
    norms = jnp.sqrt(global_sums / (counted * widths))
    out_float = whole_out.astype(f32)
    turn = jnp.dot((out_float * slant).astype(bf16), whole_out_t, preferred_element_type=f32)
    row = jnp.sum(out_float * level, axis=1)
    grad_conv_out = grad_out - colsum[0][:, None] * level - gram_out * slant

    dmixed, sums, dup, dbias, dq, stat = call(
        gate_kernel,
        steps,
        [
            scalars(),
            tiles(mid),
            held(8, mid),
            tiles(bottleneck),
            tiles(bottleneck),
            held(bottleneck, bottleneck),
            held(8, bottleneck),
            held(images, mid),
            held(images, att),
            held(images, att),
            held(8, att),
            held(mid, att),
        ],
        [
            tiles(bottleneck),
            held(5, images, mid),
            held(mid, att),
            held(8, mid),
            held(images, att),
            held(8, att),
        ],
        [
            shaped((rows, bottleneck)),
            shaped((5, images, mid)),
            shaped((mid, att)),
            shaped((8, mid)),
            shaped((images, att)),
            shaped((8, att)),
        ],
        name="gate",
    )(
        half_sides,
        second,
        ab_mid,
        back,
        mixed,
        turn.astype(bf16),
        rows8(row),
        weights,
        excite,
        squeeze,
        gate,
        whole_up,
    )
    stat = all_sum(stat[:2])
    shift_attn_grad, gain_attn_grad = stat[0], stat[1]
    ddown, dpool, stat = call(
        squeeze_kernel,
        1,
        [
            held(images, att),
            held(images, att),
            held(8, att),
            held(8, att),
            held(images, bottleneck),
            held(bottleneck, att),
            held(images, bottleneck),
            held(images, mid),
            held(5, images, mid),
        ],
        [held(bottleneck, att), held(images, bottleneck), held(8, mid)],
        [shaped((bottleneck, att)), shaped((images, bottleneck)), shaped((8, mid))],
        name="squeeze",
    )(
        dq,
        squeeze,
        gate,
        rows8(shift_attn_grad / counted_attn, gain_attn_grad / counted_attn),
        pooled,
        whole_down,
        jnp.broadcast_to(areas[:, None], (images, bottleneck)),
        weights,
        sums,
    )
    stat = all_sum(stat[:2])
    shift_mid_grad = stat[0]
    gain_mid_grad = (stat[1] - s_mid * stat[0]) / g_mid
    slant = a_mid * gain_mid_grad / (counted * g_mid)
    level = a_mid * shift_mid_grad / counted - s_mid * slant

    dsecond, dfirst, stat = call(
        conv_back_kernel,
        steps,
        [
            scalars(),
            tiles(mid),
            held(8, mid),
            tiles(bottleneck),
            held(images, mid),
            held(images, bottleneck),
            tiles(bottleneck),
            held(8, bottleneck),
            held(bottleneck, columns),
        ],
        [tiles(mid), tiles(bottleneck), held(8, bottleneck)],
        [shaped((rows, mid), bf16), shaped((rows, bottleneck)), shaped((8, bottleneck))],
        [pltpu.VMEM((STEP, 256 + 2 * SIDE, columns), f32), pltpu.VMEM((2, 8, bottleneck), f32)],
        name="conv_back",
    )(
        half_sides,
        second,
        rows8(a_mid, b_mid, slant, level),
        dmixed,
        weights,
        dpool,
        first,
        rows8(a_in, b_in, i_in, -c_in * i_in),
        whole_mid,
    )
    stat = all_sum(stat[:2])
    shift_in_grad, gain_in_grad = stat[0], stat[1]
    slant = a_in * i_in * gain_in_grad / counted
    level = a_in * shift_in_grad / counted - c_in * slant
    conv_grad, in_grad = call(
        conv_grad_kernel,
        steps,
        [tiles(bottleneck), tiles(mid), tiles(width), tiles(bottleneck)],
        [held(bottleneck, columns), held(bottleneck, width)],
        [shaped((bottleneck, columns)), shaped((bottleneck, width))],
        [pltpu.VMEM((STEP, 256 + 2 * SIDE, columns), bf16)],
        name="conv_grad",
    )(act_low, dsecond, x, dfirst)
    grad_features = call(
        last_kernel,
        steps,
        [
            scalars(),
            tiles(bottleneck),
            tiles(bottleneck),
            held(8, bottleneck),
            held(width, bottleneck),
            tiles(width),
            held(8, width),
        ],
        tiles(width),
        shaped((rows, width)),
        [pltpu.VMEM((STEP * 256, bottleneck), bf16)],
        name="last",
    )(half_sides, dfirst, first, rows8(a_in, slant, level), whole_in, slope, rows8(1.0 / a_out))

    def lanes_out(grad):
        cut = grad.astype(bf16).reshape(bottleneck, pieces, -1).transpose(1, 0, 2)
        cut = cut.reshape(devices, bottleneck // groups, -1)
        return scatter_sum(cut).reshape(bottleneck, -1).astype(f32)

    shard_out = lanes_out(grad_conv_out)
    shard_in = lanes_out(
        in_grad * a_in[:, None]
        - cross * slant[:, None]
        - column_total(x_sum) * level[:, None]
    ).T
    shard_mid = scatter_sum(conv_grad.astype(bf16).reshape(devices, -1, columns))
    shard_mid = shard_mid.reshape(-1, columns).astype(f32).T.reshape(RADIX, TAPS, -1, conv_mid.shape[3])
    up_rows = mid // pieces
    down_rows = bottleneck // pieces
    bias_rows = jnp.pad(
        dbias[0].reshape(pieces, 1, up_rows), ((0, 0), (0, groups - 1), (0, att - up_rows))
    )
    gates = jnp.concatenate(
        [dup.reshape(pieces, up_rows, att), ddown.reshape(pieces, down_rows, att), bias_rows], axis=1
    )
    gates = scatter_sum(gates.astype(bf16).reshape(devices, -1, att))
    gates = gates.reshape(-1, att).astype(f32)
    shard_up = gates[:up_rows].T
    shard_down = gates[up_rows : up_rows + down_rows]
    shard_bias = gates[up_rows + down_rows, :up_rows]

    def own_part(whole):
        length = whole.shape[0] // pieces
        return lax.dynamic_slice_in_dim(whole, lax.axis_index("fsdp") * length, length, 0)

    return (
        block.reshape(images, pixels, width),
        grad_features.reshape(images, pixels, width),
        norms,
        shard_in,
        shard_mid,
        shard_down,
        shard_up,
        shard_bias,
        shard_out,
        own_part(gain_in_grad),
        own_part(shift_in_grad),
        own_part(gain_mid_grad),
        own_part(shift_mid_grad),
        own_part(gain_attn_grad),
        own_part(shift_attn_grad),
        own_part(gain_out_grad),
        own_part(shift_out_grad),
    )


def solution(mesh):
    return jax.shard_map(
        local,
        mesh=mesh,
        in_specs=(
            P(("fsdp", "dp"), None, None),
            P(("fsdp", "dp")),
            P(("fsdp", "dp"), None, None),
            P("fsdp", None),
            P(None, None, None, "fsdp"),
            P("fsdp", None),
            P(None, "fsdp"),
            P("fsdp"),
            P(None, "fsdp"),
            P("fsdp"),
            P("fsdp"),
            P("fsdp"),
            P("fsdp"),
            P("fsdp"),
            P("fsdp"),
            P("fsdp"),
            P("fsdp"),
        ),
        out_specs=(
            P(("fsdp", "dp"), None, None),
            P(("fsdp", "dp"), None, None),
            P(),
            P("fsdp", None),
            P(None, None, None, "fsdp"),
            P("fsdp", None),
            P(None, "fsdp"),
            P("fsdp"),
            P(None, "fsdp"),
            P("fsdp"),
            P("fsdp"),
            P("fsdp"),
            P("fsdp"),
            P("fsdp"),
            P("fsdp"),
            P("fsdp"),
            P("fsdp"),
        ),
        check_vma=False,
    )
```

time: 1250 us -> 429 us (0.34)
  blocking collectives: 613 us -> 20 us
  local copies, waits for them, and re-layouts: 279 us -> 60.3 us
  other arithmetic: 210 us -> 35.5 us
  Pallas kernels: 0 us -> 150 us
  matrix products: 70.5 us -> 0.54 us
  starting transfers between devices: 0.25 us -> 64.5 us
  waiting for transfers between devices: 44.3 us -> 91.6 us
  between operations: 19.2 us -> 3.08 us
    psum x9 -> x0, blocking collectives: 328 us -> none  [the longest x4 161 us: norm_back(): lax.psum((jnp.sum(grad_norm, axis=0), jnp.sum(grad_norm * normed, axis=0)...]
    all_gather x6 -> x0, blocking collectives: 160 us -> none  [the longest x1 32.6 us: local(): lax.all_gather(attn_down, 'fsdp', axis=0, tiled=True)]
    scatter-add x14 -> x0, local copies, waits for them, and re-layouts: 152 us -> none  [unpatch(): summed = summed.at[:, row_shift:row_shift + extent, col_shift:col_shift +...]
    pallas_call x0 -> x11, Pallas kernels: none -> 150 us  [the longest x1 27.4 us: local(): call(out_kernel, steps, [scalars(), tiles(bottleneck), tiles(width), tile...]
    unnamed x2 -> x0, blocking collectives: 125 us -> none
    all_to_all x0 -> x17, waiting for transfers between devices: none -> 90.4 us  [swap_all(): return lax.all_to_all(values, axes, 0, 0)]
    dot_general x18 -> x1, matrix products: 70.5 us -> 0.54 us  [local(): jnp.dot((out_float * slant).astype(bf16), whole_out_t, preferred_element_...]
    reduce_sum x13 -> x17, other arithmetic: 73.2 us -> 7.18 us  [the longest x8 2.57 us: all_sum(): return jnp.sum(swap_all(copies, AXES), axis=0)]
  transfers between devices with their start and end apart: 6 -> 20, of which waited for: 2 -> 15; matrix products, arithmetic and copies ran while one was open for 28% -> 12% of each run, Pallas kernels for 0% -> 11%
where the time goes in v1:
time: 429 us; the launch traced here: 426 us
  Pallas kernels  150 us (35%)
  waiting for transfers between devices  91.6 us (21%)
  starting transfers between devices  64.5 us (15%)
  local copies, waits for them, and re-layouts  60.3 us (14%)
  other arithmetic  35.5 us (8%)
  blocking collectives  20 us (5%)
    all_to_all x17, waiting for transfers between devices, swap_all(): return lax.all_to_all(values, axes, 0, 0)  90.4 us
    all_to_all x17, starting transfers between devices, swap_all(): return lax.all_to_all(values, axes, 0, 0)  64.2 us
    pallas_call x1, Pallas kernels, local(): call(out_kernel, steps, [scalars(), tiles(bottleneck), tiles(width), tile...  27.4 us
    unnamed x154, local copies, waits for them, and re-layouts  23.4 us
    pallas_call x1, Pallas kernels, local(): call(conv_back_kernel, steps, [scalars(), tiles(mid), held(8, mid), tiles...  23.4 us
    all_to_all x2, blocking collectives, swap_all(): return lax.all_to_all(values, axes, 0, 0)  20 us
    pallas_call x1, Pallas kernels, local(): call(second_kernel, steps, [scalars(), tiles(bottleneck), held(8, bottlen...  16.7 us
    pallas_call x1, Pallas kernels, local(): call(last_kernel, steps, [scalars(), tiles(bottleneck), tiles(bottleneck)...  15.5 us
  transfers between devices with their start and end apart: 20, of which 15 were waited for; matrix products, arithmetic and copies ran while one was open for 12% of the time, Pallas kernels for 11%

profile of v1, /device:TPU:0, one launch (start us, length us, event | category | flops | bytes accessed | tf_op | source)
XLA Modules:
  0.0 425.8 jit_solution(17558351527333945729)
XLA Ops:
  2.2 7.3 %all-to-all-start = ((bf16[8,64,256]{2,1,0:T(8,128)(2,1)}), bf16[8,64,256]{2,1,0:T(8,128)(2,1)S(1)}, u32[]{:S(2)}, u32[]{:S(2)}) async-start(bf16[8,64,256]{2,1,0:T(8,128)(2,1)} %broadcast_in_dim.46), calls=%async_computation | async-start | bytes 524288 | tf_op jit(solution)/shard_map/all_to_all | solution.py:21
  10.5 6.1 %concatenate.19 = bf16[544]{0:T(1024)(128)(2,1)S(1)} concatenate(bf16[32]{0:T(256)(128)(2,1)} %param.27, bf16[32]{0:T(256)(128)(2,1)} %param.28, bf16[64]{0:T(256)(128)(2,1)} %param.29, bf16[64]{0:T(256)(128)(2,1)} %param.30, bf16[16]{0:T(256)(128)(2,1)} %param.31, bf16[16]{0:T(256)(128)(2,1)} %param.32, bf16[128]{0:T(256)(128)(2,1)} %param.33, bf16[128]{0:T(256)(128)(2,1)} %param.34, ...), dimensions={0} | concatenate | bytes 2176 | tf_op jit(solution)/shard_map/concatenate | solution.py:702
  19.3 4.3 %all-to-all-start.1 = ((bf16[8,180,128]{2,1,0:T(8,128)(2,1)}), bf16[8,180,128]{2,1,0:T(8,128)(2,1)S(1)}, u32[]{:S(2)}, u32[]{:S(2)}) async-start(bf16[8,180,128]{2,1,0:T(8,128)(2,1)} %broadcast_in_dim.47), calls=%async_computation.1 | async-start | bytes 753664 | tf_op jit(solution)/shard_map/all_to_all | solution.py:21
  26.6 8.8 %first.1 = (f32[4096,256]{1,0:T(8,128)S(1)}, f32[8,256]{1,0:T(8,128)S(1)}) custom-call(s32[16]{0:T(128)S(1)} %copy-done.23, bf16[4096,1024]{1,0:T(8,128)(2,1)} %bitcast.121, bf16[1024,256]{1,0:T(8,128)(2,1)S(1)} %bitcast.115), custom_call_target="tpu_custom_call" | custom-call | tf_op jit(solution)/shard_map/first/pallas_call | solution.py:727
  38.8 6.3 %all-to-all-start.2 = ((f32[32,3,256]{2,1,0:T(4,128)}), f32[32,3,256]{2,1,0:T(4,128)S(1)}, u32[]{:S(2)}, u32[]{:S(2)}) async-start(f32[32,3,256]{2,1,0:T(4,128)} %broadcast_in_dim.48), calls=%async_computation.2 | async-start | bytes 262144 | tf_op jit(solution)/shard_map/all_to_all | solution.py:21
  45.2 8.2 %all-to-all-done.2 = f32[32,3,256]{2,1,0:T(4,128)S(1)} async-done(((f32[32,3,256]{2,1,0:T(4,128)}), f32[32,3,256]{2,1,0:T(4,128)S(1)}, u32[]{:S(2)}, u32[]{:S(2)}) %all-to-all-start.2) | async-done | bytes 98336 | tf_op jit(solution)/shard_map/all_to_all | solution.py:21
  54.2 3.5 all-to-all-start.3
  60.3 9.8 %cross.1 = (f32[256,1024]{1,0:T(8,128)S(1)}, f32[8,1024]{1,0:T(8,128)S(1)}, f32[8,1024]{1,0:T(8,128)S(1)}) custom-call(s32[16]{0:T(128)S(1)} %copy-done.23, bf16[4096,1024]{1,0:T(8,128)(2,1)} %bitcast.122, f32[4096,256]{1,0:T(8,128)S(1)} %copy-done.3), custom_call_target="tpu_custom_call" | custom-call | tf_op jit(solution)/shard_map/cross/pallas_call | solution.py:740
  77.7 16.7 %second.1 = (bf16[4096,256]{1,0:T(8,128)(2,1)S(1)}, f32[4096,512]{1,0:T(8,128)}, f32[8,512]{1,0:T(8,128)S(1)}) custom-call(s32[16]{0:T(128)S(1)} %copy-done.23, f32[4096,256]{1,0:T(8,128)} %copy-done.2, f32[8,256]{1,0:T(8,128)S(1)} %get-tuple-element.214.ab_ref, bf16[256,2304]{1,0:T(8,128)(2,1)S(1)} %bitcast.112), custom_call_target="tpu_custom_call" | custom-call | tf_op jit(solution)/shard_map/second/pallas_call | solution.py:749
  96.4 4.6 %all-to-all-start.4 = ((f32[32,2,512]{2,1,0:T(2,128)}), f32[32,2,512]{2,1,0:T(2,128)S(1)}, u32[]{:S(2)}, u32[]{:S(2)}) async-start(f32[32,2,512]{2,1,0:T(2,128)} %broadcast_in_dim.50), calls=%async_computation.4 | async-start | bytes 262144 | tf_op jit(solution)/shard_map/all_to_all | solution.py:21
  104.0 5.2 %all-to-all-done.4 = f32[32,2,512]{2,1,0:T(2,128)S(1)} async-done(((f32[32,2,512]{2,1,0:T(2,128)}), f32[32,2,512]{2,1,0:T(2,128)S(1)}, u32[]{:S(2)}, u32[]{:S(2)}) %all-to-all-start.4) | async-done | bytes 131104 | tf_op jit(solution)/shard_map/all_to_all | solution.py:21
  110.5 7.7 %pool.1 = (bf16[16,256]{1,0:T(8,128)(2,1)S(1)}, f32[16,128]{1,0:T(8,128)S(1)}, f32[8,128]{1,0:T(8,128)S(1)}) custom-call(s32[16]{0:T(128)S(1)} %copy-done.23, f32[4096,512]{1,0:T(8,128)} %get-tuple-element.57.second_ref, f32[8,512]{1,0:T(8,128)S(1)} %fusion.10.ab_ref, bf16[256,128]{1,0:T(8,128)(2,1)S(1)} %bitcast.119), custom_call_target="tpu_custom_call" | custom-call | tf_op jit(solution)/shard_map/pool/pallas_call | solution.py:762
  121.4 7.2 %all-to-all-done.5 = f32[32,2,128]{2,1,0:T(2,128)S(1)} async-done(((f32[32,2,128]{2,1,0:T(2,128)}), f32[32,2,128]{2,1,0:T(2,128)S(1)}, u32[]{:S(2)}, u32[]{:S(2)}) %all-to-all-start.5) | async-done | bytes 32800 | tf_op jit(solution)/shard_map/all_to_all | solution.py:21
  128.8 11.6 %mix.1 = (bf16[4096,256]{1,0:T(8,128)(2,1)S(1)}, f32[16,512]{1,0:T(8,128)S(1)}, bf16[16,128]{1,0:T(8,128)(2,1)S(1)}, f32[256,256]{1,0:T(8,128)}, f32[256,1024]{1...) custom-call(s32[16]{0:T(128)S(1)} %copy-done.23, ...), custom_call_target="tpu_custom_call" | custom-call | tf_op jit(solution)/shard_map/mix/pallas_call | solution.py:776
  146.7 3.3 all-to-all-start.6
  150.2 15.4 %all-to-all-done.6 = f32[32,4,1024]{2,1,0:T(4,128)} async-done(((f32[32,4,1024]{2,1,0:T(4,128)}), f32[32,4,1024]{2,1,0:T(4,128)}, u32[]{:S(2)}, u32[]{:S(2)}) %all-to-all-start.6) | async-done | bytes 524320 | tf_op jit(solution)/shard_map/all_to_all | solution.py:21
  169.7 27.4 %output.1 = (bf16[4096,1024]{1,0:T(8,128)(2,1)}, bf16[4096,1024]{1,0:T(8,128)(2,1)}, f32[4096,256]{1,0:T(8,128)}, f32[256,1024]{1,0:T(8,128)S(1)}, f32[8,1024]{1,0:T(8,128)S(1)}, /*index=5*/f32[8,128]{1,0:T(8,128)S(1)}) custom-call(s32[16]{0:T(128)S(1)} %copy-done.23, bf16[4096,256]{1,0:T(8,128)(2,1)S(1)} %copy-done.6, bf16[4096,1024]{1,0:T(8,128)(2,1)} %bitcast.123, ...), custom_call_target="tpu_custom_call" | custom-call | tf_op jit(solution)/shard_map/output/pallas_call | solution.py:822
  201.0 3.3 all-to-all-start.7
  209.5 10.4 %all-to-all-done.7 = f32[32,3,1024]{2,1,0:T(4,128)} async-done(((f32[32,3,1024]{2,1,0:T(4,128)}), f32[32,3,1024]{2,1,0:T(4,128)}, u32[]{:S(2)}, u32[]{:S(2)}) %all-to-all-start.7) | async-done | bytes 393248 | tf_op jit(solution)/shard_map/all_to_all | solution.py:21
  225.7 14.3 %gate.1 = (f32[4096,256]{1,0:T(8,128)}, f32[5,16,512]{2,1,0:T(8,128)S(1)}, f32[512,128]{1,0:T(8,128)S(1)}, f32[8,512]{1,0:T(8,128)S(1)}, f32[16,128]{1,0:T(8,128)S(1)}, /*index=5*/f32[8,128]{1,0:T(8,128)S(1)}) custom-call(s32[16]{0:T(128)S(1)} %copy-done.24, f32[4096,512]{1,0:T(8,128)} %get-tuple-element.57.second_ref, f32[8,512]{1,0:T(8,128)S(1)} %fusion.10.ab_ref, ...), custom_call_target="tpu_custom_call" | custom-call | tf_op jit(solution)/shard_map/gate/pallas_call | solution.py:872
  240.1 10.1 %all_to_all.95 = f32[32,2,128]{2,1,0:T(2,128)S(1)} all-to-all(f32[32,2,128]{2,1,0:T(2,128)S(1)} %broadcast_in_dim.58), channel_id=1, replica_groups=mesh['fsdp'=8,'dp'=4] {'fsdp','dp'}, dimensions={0} | all-to-all | bytes 65536 | tf_op jit(solution)/shard_map/all_to_all | solution.py:21
  251.0 9.9 %all_to_all.96 = f32[32,2,512]{2,1,0:T(2,128)S(1)} all-to-all(f32[32,2,512]{2,1,0:T(2,128)S(1)} %broadcast_in_dim.60), channel_id=1, replica_groups=mesh['fsdp'=8,'dp'=4] {'fsdp','dp'}, dimensions={0} | all-to-all | bytes 262144 | tf_op jit(solution)/shard_map/all_to_all | solution.py:21
  262.3 23.4 %conv_back.1 = (bf16[4096,512]{1,0:T(8,128)(2,1)S(1)}, f32[4096,256]{1,0:T(8,128)}, f32[8,256]{1,0:T(8,128)S(1)}) custom-call(s32[16]{0:T(128)S(1)} %copy-done.25, f32[4096,512]{1,0:T(8,128)} %get-tuple-element.57.second_ref, f32[8,512]{1,0:T(8,128)S(1)} %fusion.13.ab_ref, f32[4096,256]{1,0:T(8,128)} %get-tuple-element.77.dmixed_ref, ...), custom_call_target="tpu_custom_call" | custom-call | tf_op jit(solution)/shard_map/conv_back/pallas_call | solution.py:956
  291.9 6.5 %all-to-all-done.10 = f32[32,2,256]{2,1,0:T(2,128)S(1)} async-done(((f32[32,2,256]{2,1,0:T(2,128)}), f32[32,2,256]{2,1,0:T(2,128)S(1)}, u32[]{:S(2)}, u32[]{:S(2)}) %all-to-all-start.10) | async-done | bytes 65568 | tf_op jit(solution)/shard_map/all_to_all | solution.py:21
  302.0 9.6 %all-to-all-done.15 = bf16[32,25,128]{2,1,0:T(8,128)(2,1)S(1)} async-done(((bf16[32,25,128]{2,1,0:T(8,128)(2,1)}), bf16[32,25,128]{2,1,0:T(8,128)(2,1)S(1)}, u32[]{:S(2)}, u32[]{:S(2)}) %all-to-all-start.15) | async-done | bytes 204832 | tf_op jit(solution)/shard_map/all_to_all | solution.py:21
  315.9 14.8 %conv_grad.1 = (f32[256,2304]{1,0:T(8,128)S(1)}, f32[256,1024]{1,0:T(8,128)S(1)}) custom-call(bf16[4096,256]{1,0:T(8,128)(2,1)S(1)} %copy-done.10, bf16[4096,512]{1,0:T(8,128)(2,1)} %copy-done.8, bf16[4096,1024]{1,0:T(8,128)(2,1)} %bitcast.124, f32[4096,256]{1,0:T(8,128)} %get-tuple-element.79.dfirst_ref), custom_call_target="tpu_custom_call" | custom-call | tf_op jit(solution)/shard_map/conv_grad/pallas_call | solution.py:989
  349.8 5.0 %all-to-all-start.11 = ((bf16[32,64,128]{2,1,0:T(8,128)(2,1)}), bf16[32,64,128]{2,1,0:T(8,128)(2,1)S(1)}, u32[]{:S(2)}, u32[]{:S(2)}) async-start(bf16[32,64,128]{2,1,0:T(8,128)(2,1)} %bitcast.132), calls=%async_computation.11 | async-start | bytes 1048576 | tf_op jit(solution)/shard_map/all_to_all | solution.py:21
  356.0 14.4 %all-to-all-done.11 = bf16[32,64,128]{2,1,0:T(8,128)(2,1)S(1)} async-done(((bf16[32,64,128]{2,1,0:T(8,128)(2,1)}), bf16[32,64,128]{2,1,0:T(8,128)(2,1)S(1)}, u32[]{:S(2)}, u32[]{:S(2)}) %all-to-all-start.11) | async-done | bytes 524320 | tf_op jit(solution)/shard_map/all_to_all | solution.py:21
  380.9 3.8 fusion.29
  390.0 15.5 %last.1 = f32[4096,1024]{1,0:T(8,128)} custom-call(s32[16]{0:T(128)S(1)} %copy-done.25, f32[4096,256]{1,0:T(8,128)S(1)} %copy-done.4, f32[4096,256]{1,0:T(8,128)} %copy-done.2, f32[8,256]{1,0:T(8,128)S(1)} %fusion.19.ab_ref, bf16[1024,256]{1,0:T(8,128)(2,1)S(1)} %bitcast.116, bf16[4096,1024]{1,0:T(8,128)(2,1)} %get-tuple-element.81.slope_ref, ...), custom_call_target="tpu_custom_call" | custom-call | tf_op jit(solution)/shard_map/last/pallas_call | solution.py:998
  416.7 3.3 all-to-all-start.14
  420.8 4.0 all-to-all-done.14
  (314 shorter events, 120.9 us)
Async XLA Ops:
  2.2 16.2 %all-to-all-start = ((bf16[8,64,256]{2,1,0:T(8,128)(2,1)}), bf16[8,64,256]{2,1,0:T(8,128)(2,1)S(1)}, u32[]{:S(2)}, u32[]{:S(2)}) async-start(bf16[8,64,256]{2,1,0:T(8,128)(2,1)} %broadcast_in_dim.46), calls=%async_computation | async-start | bytes 524288 | tf_op jit(solution)/shard_map/all_to_all | solution.py:21
  18.4 8.0 %collective-permute-start = (bf16[8,64,256]{2,1,0:T(8,128)(2,1)S(1)}, bf16[8,64,256]{2,1,0:T(8,128)(2,1)S(1)}, u32[]{:S(2)}, u32[]{:S(2)}) collective-permute-start(bf16[8,64,256]{2,1,0:T(8,128)(2,1)S(1)} %all-to-all-done), channel_id=1, source_target_pairs={{0,1},{1,0},{2,3},{3,2},{4,5},{5,4},{6,7},{7,6},{8,9},{9,8},{10,11... | collective-permute-start | bytes 786440 | tf_op jit(solution)/shard_map/ppermute | solution.py:42
  19.3 18.8 %all-to-all-start.1 = ((bf16[8,180,128]{2,1,0:T(8,128)(2,1)}), bf16[8,180,128]{2,1,0:T(8,128)(2,1)S(1)}, u32[]{:S(2)}, u32[]{:S(2)}) async-start(bf16[8,180,128]{2,1,0:T(8,128)(2,1)} %broadcast_in_dim.47), calls=%async_computation.1 | async-start | bytes 753664 | tf_op jit(solution)/shard_map/all_to_all | solution.py:21
  38.8 14.5 %all-to-all-start.2 = ((f32[32,3,256]{2,1,0:T(4,128)}), f32[32,3,256]{2,1,0:T(4,128)S(1)}, u32[]{:S(2)}, u32[]{:S(2)}) async-start(f32[32,3,256]{2,1,0:T(4,128)} %broadcast_in_dim.48), calls=%async_computation.2 | async-start | bytes 262144 | tf_op jit(solution)/shard_map/all_to_all | solution.py:21
  54.2 20.0 %all-to-all-start.3 = ((bf16[8,16,2304]{2,1,0:T(8,128)(2,1)}), bf16[8,16,2304]{2,1,0:T(8,128)(2,1)S(1)}, u32[]{:S(2)}, u32[]{:S(2)}) async-start(bf16[8,16,2304]{2,1,0:T(8,128)(2,1)} %broadcast_in_dim.49), calls=%async_computation.3 | async-start | bytes 1179648 | tf_op jit(solution)/shard_map/all_to_all | solution.py:21
  57.8 15.8 %collective-permute-start.1 = (bf16[8,180,128]{2,0,1:T(8,128)(2,1)S(1)}, bf16[8,180,128]{2,0,1:T(8,128)(2,1)S(1)}, u32[]{:S(2)}, u32[]{:S(2)}) collective-permute-start(bf16[8,180,128]{2,0,1:T(8,128)(2,1)S(1)} %copy.100), channel_id=1, source_target_pairs={{0,1},{1,0},{2,3},{3,2},{4,5},{5,4},{6,7},{7,6},{8,9},{9,8},{10,11... | collective-permute-start | bytes 1105928 | tf_op jit(solution)/shard_map/ppermute | solution.py:42
  71.8 74.0 %copy-start.39 = (f32[1024]{0:T(1024)}, f32[1024]{0:T(1024)S(1)}, u32[]{:S(2)}) copy-start(f32[1024]{0:T(1024)S(1)} %reduce_sum.193) | copy-start | bytes 12292
  74.2 2.1 collective-permute-start.2
  74.3 75.8 %copy-start.35 = (bf16[8,1024]{1,0:T(8,128)(2,1)}, bf16[8,1024]{1,0:T(8,128)(2,1)S(1)}, u32[]{:S(2)}) copy-start(bf16[8,1024]{1,0:T(8,128)(2,1)S(1)} %slice_bitcast_fusion.1) | copy-start | bytes 49156
  96.4 12.8 %all-to-all-start.4 = ((f32[32,2,512]{2,1,0:T(2,128)}), f32[32,2,512]{2,1,0:T(2,128)S(1)}, u32[]{:S(2)}, u32[]{:S(2)}) async-start(f32[32,2,512]{2,1,0:T(2,128)} %broadcast_in_dim.50), calls=%async_computation.4 | async-start | bytes 262144 | tf_op jit(solution)/shard_map/all_to_all | solution.py:21
  118.9 9.8 %all-to-all-start.5 = ((f32[32,2,128]{2,1,0:T(2,128)}), f32[32,2,128]{2,1,0:T(2,128)S(1)}, u32[]{:S(2)}, u32[]{:S(2)}) async-start(f32[32,2,128]{2,1,0:T(2,128)} %broadcast_in_dim.51), calls=%async_computation.5 | async-start | bytes 65536 | tf_op jit(solution)/shard_map/all_to_all | solution.py:21
  146.7 18.9 %all-to-all-start.6 = ((f32[32,4,1024]{2,1,0:T(4,128)}), f32[32,4,1024]{2,1,0:T(4,128)}, u32[]{:S(2)}, u32[]{:S(2)}) async-start(f32[32,4,1024]{2,1,0:T(4,128)} %broadcast_in_dim.56), calls=%async_computation.6 | async-start | bytes 1048576 | tf_op jit(solution)/shard_map/all_to_all | solution.py:21
  168.0 53.0 %copy-start.36 = (f32[1,1024]{1,0:T(1,128)}, f32[1,1024]{1,0:T(1,128)S(1)}, u32[]{:S(2)}) copy-start(f32[1,1024]{1,0:T(1,128)S(1)} %get-tuple-element.168) | copy-start | bytes 12292
  168.0 53.0 %copy-start.48 = (f32[1,1024]{1,0:T(1,128)}, f32[1,1024]{1,0:T(1,128)S(1)}, u32[]{:S(2)}) copy-start(f32[1,1024]{1,0:T(1,128)S(1)} %get-tuple-element.166) | copy-start | bytes 12292
  201.0 18.9 %all-to-all-start.7 = ((f32[32,3,1024]{2,1,0:T(4,128)}), f32[32,3,1024]{2,1,0:T(4,128)}, u32[]{:S(2)}, u32[]{:S(2)}) async-start(f32[32,3,1024]{2,1,0:T(4,128)} %broadcast_in_dim.57), calls=%async_computation.7 | async-start | bytes 1048576 | tf_op jit(solution)/shard_map/all_to_all | solution.py:21
  225.6 35.4 %copy-start.51 = (f32[1,512]{1,0:T(1,128)S(1)}, f32[1,512]{1,0:T(1,128)}, u32[]{:S(2)}) copy-start(f32[1,512]{1,0:T(1,128)} %copy-done.50) | copy-start | bytes 6148
  225.7 35.4 %copy-start.53 = (f32[1,512]{1,0:T(1,128)S(1)}, f32[1,512]{1,0:T(1,128)}, u32[]{:S(2)}) copy-start(f32[1,512]{1,0:T(1,128)} %copy-done.52) | copy-start | bytes 6148
  225.7 35.4 %copy-start.55 = (f32[1,512]{1,0:T(1,128)S(1)}, f32[1,512]{1,0:T(1,128)}, u32[]{:S(2)}) copy-start(f32[1,512]{1,0:T(1,128)} %copy-done.54) | copy-start | bytes 6148
  225.7 36.6 %copy-start.57 = (f32[1,512]{1,0:T(1,128)S(1)}, f32[1,512]{1,0:T(1,128)}, u32[]{:S(2)}) copy-start(f32[1,512]{1,0:T(1,128)} %copy-done.56) | copy-start | bytes 6148
  225.7 36.6 %copy-start.25 = (s32[16]{0:T(128)S(1)}, s32[16]{0:T(128)}, u32[]{:S(2)}) copy-start(s32[16]{0:T(128)} %sides.17) | copy-start | bytes 196
  225.7 36.6 %copy-start.26 = (f32[8,256]{1,0:T(8,128)S(1)}, f32[8,256]{1,0:T(8,128)}, u32[]{:S(2)}) copy-start(f32[8,256]{1,0:T(8,128)} %get-tuple-element.213.ab_in_ref) | copy-start | bytes 24580
  288.4 10.0 %all-to-all-start.10 = ((f32[32,2,256]{2,1,0:T(2,128)}), f32[32,2,256]{2,1,0:T(2,128)S(1)}, u32[]{:S(2)}, u32[]{:S(2)}) async-start(f32[32,2,256]{2,1,0:T(2,128)} %broadcast_in_dim.61), calls=%async_computation.10 | async-start | bytes 131072 | tf_op jit(solution)/shard_map/all_to_all | solution.py:21
  298.4 13.2 %all-to-all-start.15 = ((bf16[32,25,128]{2,1,0:T(8,128)(2,1)}), bf16[32,25,128]{2,1,0:T(8,128)(2,1)S(1)}, u32[]{:S(2)}, u32[]{:S(2)}) async-start(bf16[32,25,128]{2,1,0:T(8,128)(2,1)} %convert_element_type.276), calls=%async_computation.15 | async-start | bytes 524288 | tf_op jit(solution)/shard_map/all_to_all | solution.py:21
  311.6 22.4 %all-to-all-start.17 = ((bf16[32,64,128]{2,1,0:T(8,128)(2,1)}), bf16[32,64,128]{2,1,0:T(8,128)(2,1)S(1)}, u32[]{:S(2)}, u32[]{:S(2)}) async-start(bf16[32,64,128]{2,1,0:T(8,128)(2,1)} %bitcast.53), calls=%async_computation.17 | async-start | bytes 1048576 | tf_op jit(solution)/shard_map/all_to_all | solution.py:21
  334.6 7.2 %all-to-all-start.16 = ((bf16[4,25,128]{2,1,0:T(8,128)(2,1)}), bf16[4,25,128]{2,1,0:T(8,128)(2,1)S(1)}, u32[]{:S(2)}, u32[]{:S(2)}) async-start(bf16[4,25,128]{2,1,0:T(8,128)(2,1)} %broadcast_in_dim.64), calls=%async_computation.16 | async-start | bytes 65536 | tf_op jit(solution)/shard_map/all_to_all | solution.py:21
  342.5 7.4 %all-to-all-start.18 = ((bf16[4,64,128]{2,1,0:T(8,128)(2,1)}), bf16[4,64,128]{2,1,0:T(8,128)(2,1)S(1)}, u32[]{:S(2)}, u32[]{:S(2)}) async-start(bf16[4,64,128]{2,1,0:T(8,128)(2,1)} %broadcast_in_dim.65), calls=%async_computation.18 | async-start | bytes 131072 | tf_op jit(solution)/shard_map/all_to_all | solution.py:21
  348.5 37.5 %copy-start.68 = (f32[1,512]{1,0:T(1,128)S(1)}, f32[1,512]{1,0:T(1,128)}, u32[]{:S(2)}) copy-start(f32[1,512]{1,0:T(1,128)} %get-tuple-element.208) | copy-start | bytes 6148
  349.8 20.6 %all-to-all-start.11 = ((bf16[32,64,128]{2,1,0:T(8,128)(2,1)}), bf16[32,64,128]{2,1,0:T(8,128)(2,1)S(1)}, u32[]{:S(2)}, u32[]{:S(2)}) async-start(bf16[32,64,128]{2,1,0:T(8,128)(2,1)} %bitcast.132), calls=%async_computation.11 | async-start | bytes 1048576 | tf_op jit(solution)/shard_map/all_to_all | solution.py:21
  370.4 37.6 %all-to-all-start.13 = ((bf16[32,8,2304]{2,1,0:T(8,128)(2,1)}), bf16[32,8,2304]{2,1,0:T(8,128)(2,1)S(1)}, u32[]{:S(2)}, u32[]{:S(2)}) async-start(bf16[32,8,2304]{2,1,0:T(8,128)(2,1)} %convert_bitcast_fusion), calls=%async_computation.13 | async-start | bytes 2359296 | tf_op jit(solution)/shard_map/all_to_all | solution.py:21
  390.0 35.8 %copy-start.1 = (bf16[128,256]{1,0:T(8,128)(2,1)S(1)}, bf16[128,256]{1,0:T(8,128)(2,1)}, u32[]{:S(2)}) copy-start(bf16[128,256]{1,0:T(8,128)(2,1)} %param.21) | copy-start | bytes 196612
  408.7 7.4 %all-to-all-start.12 = ((bf16[4,64,128]{2,1,0:T(8,128)(2,1)}), bf16[4,64,128]{2,1,0:T(8,128)(2,1)S(1)}, u32[]{:S(2)}, u32[]{:S(2)}) async-start(bf16[4,64,128]{2,1,0:T(8,128)(2,1)} %broadcast_in_dim.62), calls=%async_computation.12 | async-start | bytes 131072 | tf_op jit(solution)/shard_map/all_to_all | solution.py:21
  416.7 8.1 %all-to-all-start.14 = ((bf16[4,8,2304]{2,1,0:T(8,128)(2,1)}), bf16[4,8,2304]{2,1,0:T(8,128)(2,1)S(1)}, u32[]{:S(2)}, u32[]{:S(2)}) async-start(bf16[4,8,2304]{2,1,0:T(8,128)(2,1)} %broadcast_in_dim.63), calls=%async_computation.14 | async-start | bytes 294912 | tf_op jit(solution)/shard_map/all_to_all | solution.py:21
  (64 other events, 778.6 us)

commit v2 on v1

v2 whole, which is shorter than its diff:
```python
import functools

import jax
import jax.numpy as jnp
from jax import lax
from jax.experimental import pallas as pl
from jax.experimental.pallas import tpu as pltpu
from jax.sharding import PartitionSpec as P

RADIX = 2
SIDE = 16
TAPS = 9
STEP = 2

epsilon = 1e-05
AXES = ("fsdp", "dp")
f32 = jnp.float32
bf16 = jnp.bfloat16
HIGH = lax.Precision.HIGHEST


def swap_all(values, axes):
    return lax.all_to_all(values, axes, 0, 0)


def gather_all(shard):
    pieces = lax.axis_size("fsdp")
    return swap_all(jnp.broadcast_to(shard[None], (pieces,) + shard.shape), "fsdp")


def neighbour(values):
    return lax.ppermute(values, "dp", [(i, i ^ 1) for i in range(lax.axis_size("dp"))])


def half_of(shard, axis):
    odd = lax.rem(lax.axis_index("dp"), 2)
    return lax.dynamic_slice_in_dim(shard, odd * (shard.shape[axis] // 2), shard.shape[axis] // 2, axis)


def sigmoid(values):
    return 0.5 * jnp.tanh(0.5 * values) + 0.5


def fold(values):
    return values[:8] + values[8:]


def wide(mask, lanes):
    return jnp.concatenate([mask] * (lanes // mask.shape[1]), axis=1)


def places():
    return lax.broadcasted_iota(jnp.int32, (SIDE, 128), 0)


def row_mask(place, row, limit):
    return jnp.where((place < limit) & (row < limit), 1.0, 0.0).astype(f32)


def chunk(image, row):
    return pl.ds(pl.multiple_of(image * 256 + row * SIDE, SIDE), SIDE)


def rows_of(carry, body, unroll=8):
    return lax.fori_loop(0, SIDE, body, carry, unroll=unroll)


def contract_lead(left, right):
    return lax.dot_general(left, right, (((0,), (0,)), ((), ())), preferred_element_type=f32)


def contract_last(left, right):
    return lax.dot_general(left, right, (((1,), (1,)), ((), ())), preferred_element_type=f32)


def zeros_at_start(*refs):
    @pl.when(pl.program_id(0) == 0)
    def _():
        for ref in refs:
            ref[...] = jnp.zeros(ref.shape, ref.dtype)


def last_step():
    return pl.program_id(0) == pl.num_programs(0) - 1


def column_total(values):
    return jnp.sum(values, axis=0, keepdims=True)


def take(recv_ref, tile_ref):
    tile_ref[...] = lax.fori_loop(
        1,
        recv_ref.shape[0],
        lambda j, total: total + recv_ref[j].astype(f32),
        recv_ref[0].astype(f32),
        unroll=True if recv_ref.shape[0] <= 32 else 1,
    )


def row_at(tile_ref, start, lanes):
    return jnp.concatenate(
        [tile_ref[start + q : start + q + 1, :] for q in range(lanes // 128)], axis=1
    )


def put(tile_ref, start, row):
    for q in range(row.shape[1] // 128):
        tile_ref[start + q : start + q + 1, :] = row[:, q * 128 : (q + 1) * 128]


def send(send_ref, tile_ref):
    tile = tile_ref[...].astype(send_ref.dtype)

    def body(j, carry):
        send_ref[j] = tile
        return carry

    lax.fori_loop(0, send_ref.shape[0], body, 0, unroll=True if send_ref.shape[0] <= 32 else 1)


def norm_rows(sums, squares, counted, gain, shift):
    center = sums / counted
    spread = squares / counted - center * center
    inv = lax.rsqrt(spread + epsilon)
    scale = gain * inv
    return center, spread, inv, scale, shift - center * scale


def fill_half(whole_ref, mine_ref, other_ref, odd_ref):
    half = whole_ref.shape[1] // 2

    @pl.when(odd_ref[0] == 0)
    def _():
        whole_ref[:, :half] = mine_ref[...]
        whole_ref[:, half:] = other_ref[...]

    @pl.when(odd_ref[0] != 0)
    def _():
        whole_ref[:, :half] = other_ref[...]
        whole_ref[:, half:] = mine_ref[...]


def at_start(body):
    pl.when(pl.program_id(0) == 0)(body)


def at_end(body):
    pl.when(pl.program_id(0) == pl.num_programs(0) - 1)(body)


def lane_parts(values):
    total = values[:, :128]
    for at in range(128, values.shape[1], 128):
        total = total + values[:, at : at + 128]
    return total


def lane_sum(row):
    return jnp.broadcast_to(jnp.sum(row, axis=1, keepdims=True), (1, 128))


def first_kernel(
    sides, odd, x_ref, mine_ref, other_ref, first_ref, w_ref, send_ref, acc_ref, tile_ref
):
    step = pl.program_id(0)
    zeros_at_start(acc_ref)
    at_start(lambda: fill_half(w_ref, mine_ref, other_ref, odd))
    first_ref[...] = jnp.dot(x_ref[...], w_ref[...], preferred_element_type=f32)
    place = places()
    lanes = first_ref.shape[1]
    for image in range(STEP):
        limit = 2 * sides[step * STEP + image]

        def body(row, carry):
            total, square = carry
            here = chunk(image, row)
            values = first_ref[here, :] * wide(row_mask(place, row, limit), lanes)
            first_ref[here, :] = values
            return (total + fold(values), square + fold(values * values))

        total, square = rows_of((acc_ref[0], acc_ref[1]), body)
        acc_ref[0] = total
        acc_ref[1] = square

    @at_end
    def _():
        count = jnp.int32(0)
        for image in range(sides.shape[0]):
            count = count + 4 * sides[image] * sides[image]
        tile_ref[...] = jnp.zeros(tile_ref.shape, f32)
        put(tile_ref, 0, column_total(acc_ref[0]))
        put(tile_ref, lanes // 128, column_total(acc_ref[1]))
        put(tile_ref, 2 * lanes // 128, jnp.full((1, 128), count, jnp.int32).astype(f32))
        send(send_ref, tile_ref)


def cross_kernel(
    sides, x_ref, first_ref, part_ref, cross_ref, ones_ref, power_ref, copies_ref, square_ref
):
    step = pl.program_id(0)
    zeros_at_start(cross_ref, square_ref, ones_ref)
    cross_ref[...] += contract_lead(first_ref[...].astype(bf16), x_ref[...])
    place = places()
    lanes = x_ref.shape[1]
    for image in range(STEP):
        limit = 2 * sides[step * STEP + image]

        def body(row, carry):
            square, total = carry
            values = x_ref[chunk(image, row), :].astype(f32) * wide(
                row_mask(place, row, limit), lanes
            )
            return (square + fold(values * values), total + fold(values))

        square, total = rows_of((square_ref[...], ones_ref[...]), body)
        square_ref[...] = square
        ones_ref[...] = total

    @at_end
    def _():
        power_ref[...] = lane_parts(square_ref[...])
        for j in range(copies_ref.shape[0]):
            copies_ref[j] = part_ref[...]


def write_patches(patch_ref, image, row, low, place):
    values = low.astype(f32)
    lanes = values.shape[1]
    inner = wide(place, lanes)
    left = jnp.where(inner == 0, 0.0, pltpu.roll(values, 1, 0)).astype(bf16)
    right = jnp.where(inner == SIDE - 1, 0.0, pltpu.roll(values, SIDE - 1, 0)).astype(bf16)
    for tap in range(TAPS):
        up, side = tap // 3, tap % 3
        source = (left, low, right)[side]
        here = pl.ds(pl.multiple_of((row + 2 - up) * SIDE, SIDE), SIDE)
        for group in range(lanes // 128):
            at = (group * TAPS + tap) * 128
            patch_ref[image, here, at : at + 128] = source[:, group * 128 : (group + 1) * 128]


def second_kernel(
    sides,
    odd,
    first_ref,
    recv_ref,
    param_ref,
    mine_ref,
    other_ref,
    _,
    act_ref,
    second_ref,
    terms_ref,
    count_ref,
    w_ref,
    send_ref,
    patch_ref,
    acc_ref,
    tile_ref,
):
    step = pl.program_id(0)
    zeros_at_start(acc_ref, patch_ref)
    place = places()
    lanes = first_ref.shape[1]
    columns = TAPS * lanes // RADIX

    @at_start
    def _():
        fill_half(w_ref, mine_ref, other_ref, odd)
        take(recv_ref, tile_ref)
        count = tile_ref[2 * lanes // 128 : 2 * lanes // 128 + 1, :]
        count_ref[...] = jnp.broadcast_to(count, count_ref.shape)
        center, _, inv, scale, offset = norm_rows(
            row_at(tile_ref, 0, lanes),
            row_at(tile_ref, lanes // 128, lanes),
            wide(count, lanes),
            param_ref[0:1, :],
            param_ref[1:2, :],
        )
        terms_ref[0:1, :] = scale
        terms_ref[1:2, :] = offset
        terms_ref[2:3, :] = inv
        terms_ref[3:4, :] = -center * inv
        terms_ref[4:5, :] = center

    for image in range(STEP):
        limit = 2 * sides[step * STEP + image]

        def body(row, carry):
            here = chunk(image, row)
            pre = first_ref[here, :] * terms_ref[0:1, :] + terms_ref[1:2, :]
            act = pre * (sigmoid(pre) * wide(row_mask(place, row, limit), lanes))
            low = act.astype(bf16)
            act_ref[here, :] = low
            write_patches(patch_ref, image, row, low, place)
            return carry

        rows_of(0, body)
    for image in range(STEP):
        for group in range(RADIX):
            second_ref[image * 256 : image * 256 + 256, group * lanes : (group + 1) * lanes] = (
                contract_last(
                    patch_ref[image, SIDE : SIDE + 256, group * columns : (group + 1) * columns],
                    w_ref[:, group * columns : (group + 1) * columns],
                )
            )
    for image in range(STEP):
        limit = 2 * sides[step * STEP + image]

        def body(row, carry):
            total, square = carry
            values = second_ref[chunk(image, row), :]
            values = values * wide(row_mask(place, row, limit), values.shape[1])
            return (total + fold(values), square + fold(values * values))

        total, square = rows_of((acc_ref[0], acc_ref[1]), body)
        acc_ref[0] = total
        acc_ref[1] = square

    @at_end
    def _():
        tile_ref[...] = jnp.zeros(tile_ref.shape, f32)
        put(tile_ref, 0, column_total(acc_ref[0]))
        put(tile_ref, RADIX * lanes // 128, column_total(acc_ref[1]))
        send(send_ref, tile_ref)


def pool_kernel(
    sides,
    second_ref,
    recv_ref,
    param_ref,
    count_ref,
    down_ref,
    power_ref,
    _,
    pooled_ref,
    squeeze_ref,
    terms_ref,
    send_ref,
    pool_ref,
    tile_ref,
):
    step = pl.program_id(0)
    place = places()
    lanes = second_ref.shape[1]

    @at_start
    def _():
        take(recv_ref, tile_ref)
        _, _, _, scale, offset = norm_rows(
            row_at(tile_ref, 0, lanes),
            row_at(tile_ref, lanes // 128, lanes),
            wide(count_ref[0:1, :], lanes),
            param_ref[0:1, :],
            param_ref[1:2, :],
        )
        terms_ref[0:1, :] = scale
        terms_ref[1:2, :] = offset

    for image in range(STEP):
        limit = 2 * sides[step * STEP + image]

        def body(row, total):
            pre = second_ref[chunk(image, row), :] * terms_ref[0:1, :] + terms_ref[1:2, :]
            act = pre * (sigmoid(pre) * wide(row_mask(place, row, limit), lanes))
            return total + fold(act)

        total = column_total(rows_of(jnp.zeros((8, lanes), f32), body))
        both = total[:, : lanes // 2] + total[:, lanes // 2 :]
        area = jnp.full(both.shape, limit * limit, jnp.int32).astype(f32)
        pool_ref[pl.ds(step * STEP + image, 1), :] = both / area

    @at_end
    def _():
        low = pool_ref[...].astype(bf16)
        pooled_ref[...] = low
        squeeze = jnp.dot(low, down_ref[...], preferred_element_type=f32)
        squeeze_ref[...] = squeeze
        tile_ref[...] = jnp.zeros(tile_ref.shape, f32)
        tile_ref[0:1, :] = column_total(squeeze)
        tile_ref[1:2, :] = column_total(squeeze * squeeze)
        tile_ref[2:3, :] = column_total(power_ref[...])
        send(send_ref, tile_ref)


def mix_kernel(
    images_all,
    sides,
    second_ref,
    ab_ref,
    squeeze_ref,
    recv_ref,
    param_ref,
    up_ref,
    bias_ref,
    out_ref,
    mixed_ref,
    weights_ref,
    excite_ref,
    gate_ref,
    gw_ref,
    colsum_ref,
    power_ref,
    send_ref,
    gram_ref,
    acc_ref,
    tile_ref,
):
    step = pl.program_id(0)
    zeros_at_start(acc_ref, gram_ref)
    place = places()
    lanes = second_ref.shape[1]
    half = lanes // 2

    @at_start
    def _():
        tile_ref[0:8, :] = recv_ref[0]
        for j in range(1, recv_ref.shape[0]):
            tile_ref[0:8, :] += recv_ref[j]
        center, _, inv, scale, offset = norm_rows(
            tile_ref[0:1, :],
            tile_ref[1:2, :],
            jnp.float32(images_all),
            param_ref[0:1, :],
            param_ref[1:2, :],
        )
        gate_ref[0:1, :] = scale
        gate_ref[1:2, :] = offset
        gate_ref[2:3, :] = inv
        gate_ref[3:4, :] = -center * inv
        gate_ref[4:5, :] = tile_ref[2:3, :]
        pre = squeeze_ref[...] * scale + offset
        excite = (pre * sigmoid(pre)).astype(bf16)
        excite_ref[...] = excite
        logits = contract_last(excite, up_ref[...]) + bias_ref[0:1, :]
        one, two = logits[:, :half], logits[:, half:]
        top = jnp.maximum(one, two)
        one, two = jnp.exp(one - top), jnp.exp(two - top)
        weights_ref[:, :half] = one / (one + two)
        weights_ref[:, half:] = two / (one + two)

    for image in range(STEP):
        limit = 2 * sides[step * STEP + image]
        weights = weights_ref[pl.ds(step * STEP + image, 1), :]

        def body(row, carry):
            total, square = carry
            here = chunk(image, row)
            pre = second_ref[here, :] * ab_ref[0:1, :] + ab_ref[1:2, :]
            act = pre * (sigmoid(pre) * wide(row_mask(place, row, limit), lanes))
            act = act * weights
            mixed = act[:, :half] + act[:, half:]
            low = mixed.astype(bf16)
            mixed_ref[here, :] = low
            return (total + fold(low.astype(f32)), square + fold(mixed * mixed))

        total, square = rows_of((acc_ref[0], acc_ref[1]), body)
        acc_ref[0] = total
        acc_ref[1] = square
    gram_ref[...] += contract_lead(mixed_ref[...], mixed_ref[...])

    @at_end
    def _():
        whole = out_ref[...].astype(f32)
        total = column_total(acc_ref[0])
        colsum_ref[...] = jnp.broadcast_to(total, colsum_ref.shape)
        power_ref[...] = lane_parts(acc_ref[1])
        gw = jnp.dot(gram_ref[...], whole, precision=HIGH, preferred_element_type=f32)
        gw_ref[...] = gw
        sums = jnp.dot(
            jnp.broadcast_to(total, (8, half)), whole, precision=HIGH, preferred_element_type=f32
        )
        put(tile_ref, 0, sums[0:1, :])
        put(tile_ref, whole.shape[1] // 128, column_total(gw * whole))
        send(send_ref, tile_ref)


def out_kernel(
    sides,
    mixed_ref,
    x_ref,
    cot_ref,
    recv_ref,
    param_ref,
    count_ref,
    w_ref,
    wt_ref,
    block_ref,
    slope_ref,
    back_ref,
    grad_ref,
    terms_ref,
    power_ref,
    send_ref,
    third_ref,
    acc_ref,
    square_ref,
    tile_ref,
):
    step = pl.program_id(0)
    zeros_at_start(acc_ref, square_ref, grad_ref)
    place = places()
    lanes = x_ref.shape[1]
    part = 512 if lanes % 512 == 0 else lanes

    @at_start
    def _():
        take(recv_ref, tile_ref)
        count = count_ref[0:1, :]
        gain, shift = param_ref[0:1, :], param_ref[1:2, :]
        center, spread, inv, scale, offset = norm_rows(
            row_at(tile_ref, 0, lanes),
            row_at(tile_ref, lanes // 128, lanes),
            wide(count, lanes),
            gain,
            shift,
        )
        branch = gain * gain * spread * inv * inv + shift * shift
        terms_ref[0:1, :] = scale
        terms_ref[1:2, :] = offset
        terms_ref[2:3, :] = center
        terms_ref[3:4, :] = inv
        terms_ref[4:5, :] = 1.0 / scale
        terms_ref[5:6, :] = wide(lane_sum(branch), lanes)

    third_ref[...] = jnp.dot(mixed_ref[...], w_ref[...], preferred_element_type=f32)
    for image in range(STEP):
        limit = 2 * sides[step * STEP + image]

        def body(row, square):
            here = chunk(image, row)
            mask = wide(row_mask(place, row, limit), part)
            for at in range(0, lanes, part):
                cut = slice(at, at + part)
                total = (
                    x_ref[here, cut].astype(f32)
                    + third_ref[here, cut] * terms_ref[0:1, cut]
                    + terms_ref[1:2, cut]
                )
                plain = sigmoid(total)
                gate = plain * mask
                output = total * gate
                block_ref[here, cut] = output.astype(bf16)
                slope = gate + output * (1.0 - plain)
                grad = cot_ref[here, cut].astype(f32) * (slope * terms_ref[0:1, cut])
                slope_ref[here, cut] = grad.astype(bf16)
                acc_ref[:, cut] += fold(grad)
                square = square + lane_parts(fold(output * output))
            return square

        square_ref[...] = rows_of(square_ref[...], body, 4)
    back_ref[...] = jnp.dot(slope_ref[...], wt_ref[...], preferred_element_type=f32)
    grad_ref[...] += contract_lead(mixed_ref[...], slope_ref[...])

    @at_end
    def _():
        power_ref[...] = square_ref[...]
        total = column_total(acc_ref[...])
        put(tile_ref, 0, total)
        turned = column_total(grad_ref[...] * w_ref[...].astype(f32))
        put(tile_ref, lanes // 128, turned - terms_ref[2:3, :] * total)
        send(send_ref, tile_ref)


def mid_terms(second_ref, ab_ref, here, mask):
    pre = second_ref[here, :] * ab_ref[0:1, :] + ab_ref[1:2, :]
    plain = sigmoid(pre)
    gate = plain * mask
    act = pre * gate
    return pre, act, gate + act * (1.0 - plain)


def gate_kernel(
    sides,
    second_ref,
    ab_ref,
    back_ref,
    mixed_ref,
    recv_ref,
    terms_ref,
    param_ref,
    count_ref,
    w_ref,
    wt_ref,
    weights_ref,
    excite_ref,
    squeeze_ref,
    gate_ref,
    up_ref,
    power_out_ref,
    power_mix_ref,
    dmixed_ref,
    sums_ref,
    dup_ref,
    dbias_ref,
    dq_ref,
    grads_ref,
    send_ref,
    turn_ref,
    row_ref,
    tile_ref,
):
    step = pl.program_id(0)
    place = places()
    lanes = second_ref.shape[1]
    half = lanes // 2
    width = w_ref.shape[1]

    @at_start
    def _():
        take(recv_ref, tile_ref)
        count = wide(count_ref[0:1, :], width)
        total = row_at(tile_ref, 0, width)
        scale, center, inv = terms_ref[0:1, :], terms_ref[2:3, :], terms_ref[3:4, :]
        gain_grad = row_at(tile_ref, width // 128, width) / param_ref[0:1, :]
        slant = scale * inv * gain_grad / count
        level = total / count - center * slant
        grads_ref[0:1, :] = total * terms_ref[4:5, :]
        grads_ref[1:2, :] = gain_grad
        grads_ref[2:3, :] = slant
        grads_ref[3:4, :] = level
        whole = w_ref[...].astype(f32)
        turn_ref[...] = jnp.dot(
            (whole * slant).astype(bf16), wt_ref[...], preferred_element_type=f32
        ).astype(bf16)
        row_ref[...] = jnp.dot(
            jnp.broadcast_to(level, (8, width)),
            wt_ref[...].astype(f32),
            precision=HIGH,
            preferred_element_type=f32,
        )

    dmixed_ref[...] = back_ref[...] - jnp.dot(
        mixed_ref[...], turn_ref[...], preferred_element_type=f32
    )
    for image in range(STEP):
        limit = 2 * sides[step * STEP + image]

        def body(row, carry):
            here = chunk(image, row)
            mask = row_mask(place, row, limit)
            dmixed = (dmixed_ref[here, :] - row_ref[0:1, :]) * wide(mask, half)
            dmixed_ref[here, :] = dmixed
            both = jnp.concatenate([dmixed, dmixed], axis=1)
            pre, act, slope = mid_terms(second_ref, ab_ref, here, wide(mask, lanes))
            along = slope * both
            terms = (act * both, along, along * pre, slope, slope * pre)
            return tuple(old + fold(new) for old, new in zip(carry, terms))

        start = tuple(jnp.zeros((8, lanes), f32) for _ in range(5))
        totals = rows_of(start, body, 4)
        for index in range(5):
            sums_ref[index, pl.ds(step * STEP + image, 1), :] = column_total(totals[index])

    @at_end
    def _():
        weights = weights_ref[...]
        grads = sums_ref[0]
        mean = weights * grads
        mean = mean[:, :half] + mean[:, half:]
        dlogits = weights * (grads - jnp.concatenate([mean, mean], axis=1))
        dbias_ref[...] = jnp.broadcast_to(column_total(dlogits), dbias_ref.shape)
        low = dlogits.astype(bf16)
        dup_ref[...] = contract_lead(low, excite_ref[...])
        dexcite = jnp.dot(low, up_ref[...], preferred_element_type=f32)
        squeeze = squeeze_ref[...]
        pre = squeeze * gate_ref[0:1, :] + gate_ref[1:2, :]
        normed = squeeze * gate_ref[2:3, :] + gate_ref[3:4, :]
        plain = sigmoid(pre)
        dq = dexcite * (plain * (1.0 + pre * (1.0 - plain)))
        dq_ref[...] = dq
        tile_ref[0:1, :] = column_total(dq)
        tile_ref[1:2, :] = column_total(dq * normed)
        tile_ref[2:3, :] = column_total(power_out_ref[...])
        tile_ref[3:4, :] = column_total(power_mix_ref[...])
        tile_ref[4:8, :] = jnp.zeros((4, 128), f32)
        tile = tile_ref[0:8, :]
        for j in range(send_ref.shape[0]):
            send_ref[j] = tile


def squeeze_kernel(
    images_all,
    width,
    sides,
    dq_ref,
    squeeze_ref,
    gate_ref,
    recv_ref,
    pooled_ref,
    down_ref,
    weights_ref,
    sums_ref,
    param_ref,
    count_ref,
    terms_ref,
    ddown_ref,
    dpool_ref,
    grads_ref,
    send_ref,
    tile_ref,
    area_ref,
):
    take(recv_ref, tile_ref)
    shift, gain = tile_ref[0:1, :], tile_ref[1:2, :]
    grads_ref[0:1, :] = shift
    grads_ref[1:2, :] = gain
    bottleneck = pooled_ref.shape[1]
    count = count_ref[0:1, :]
    powers = (
        lane_sum(gate_ref[4:5, :]) / (count * width),
        lane_sum(tile_ref[3:4, :]) / (count * bottleneck),
        terms_ref[5:6, :128] / width,
        lane_sum(tile_ref[2:3, :]) / (count * width),
    )
    place = lax.broadcasted_iota(jnp.int32, (1, 128), 1)
    norms = powers[3]
    for index in range(3):
        norms = jnp.where(place == index, powers[index], norms)
    grads_ref[2:3, :] = jnp.sqrt(norms)
    normed = squeeze_ref[...] * gate_ref[2:3, :] + gate_ref[3:4, :]
    dsqueeze = gate_ref[0:1, :] * (
        dq_ref[...] - (shift + normed * gain) / jnp.float32(images_all)
    )
    low = dsqueeze.astype(bf16)
    ddown_ref[...] = contract_lead(pooled_ref[...], low)
    for image in range(area_ref.shape[0]):
        area = 4 * sides[image] * sides[image]
        area_ref[image : image + 1, :] = jnp.full((1, bottleneck), area, jnp.int32).astype(f32)
    dpool = contract_last(low, down_ref[...]) / area_ref[...]
    dpool_ref[...] = dpool
    both = jnp.concatenate([dpool, dpool], axis=1)
    weights = weights_ref[...]
    total = column_total(weights * sums_ref[1] + both * sums_ref[3])
    product = column_total(weights * sums_ref[2] + both * sums_ref[4])
    lanes = weights.shape[1]
    put(tile_ref, 0, total)
    put(tile_ref, lanes // 128, (product - param_ref[1:2, :] * total) / param_ref[0:1, :])
    send(send_ref, tile_ref)


def conv_back_kernel(
    sides,
    second_ref,
    ab_ref,
    recv_ref,
    param_ref,
    count_ref,
    dmixed_ref,
    weights_ref,
    dpool_ref,
    first_ref,
    ab_in_ref,
    w_ref,
    dsecond_ref,
    dfirst_ref,
    grads_ref,
    stat_ref,
    column_ref,
    acc_ref,
    tile_ref,
):
    step = pl.program_id(0)
    zeros_at_start(acc_ref, column_ref)
    place = places()
    lanes = second_ref.shape[1]
    half = lanes // 2
    quarter = half // RADIX
    columns = TAPS * quarter

    @at_start
    def _():
        take(recv_ref, tile_ref)
        total = row_at(tile_ref, 0, lanes)
        product = row_at(tile_ref, lanes // 128, lanes)
        count = wide(count_ref[0:1, :], lanes)
        slant = ab_ref[0:1, :] * product / (count * param_ref[0:1, :])
        grads_ref[0:1, :] = total
        grads_ref[1:2, :] = product
        grads_ref[2:3, :] = slant
        grads_ref[3:4, :] = ab_ref[0:1, :] * total / count - param_ref[1:2, :] * slant

    for image in range(STEP):
        limit = 2 * sides[step * STEP + image]
        weights = weights_ref[pl.ds(step * STEP + image, 1), :] * ab_ref[0:1, :]
        dpool = dpool_ref[pl.ds(step * STEP + image, 1), :]
        dpool = jnp.concatenate([dpool, dpool], axis=1) * ab_ref[0:1, :]

        def body(row, carry):
            here = chunk(image, row)
            mask = wide(row_mask(place, row, limit), lanes)
            dmixed = dmixed_ref[here, :]
            both = jnp.concatenate([dmixed, dmixed], axis=1)
            pre = second_ref[here, :] * ab_ref[0:1, :] + ab_ref[1:2, :]
            plain = sigmoid(pre)
            slope = plain + pre * plain * (1.0 - plain)
            grad = slope * (weights * both + dpool)
            grad = mask * (grad - (pre * grads_ref[2:3, :] + grads_ref[3:4, :]))
            dsecond_ref[here, :] = grad.astype(bf16)
            return carry

        rows_of(0, body)
    for image in range(STEP):
        for group in range(RADIX):
            column_ref[image, SIDE : SIDE + 256, group * columns : (group + 1) * columns] = jnp.dot(
                dsecond_ref[image * 256 : image * 256 + 256, group * half : (group + 1) * half],
                w_ref[:, group * columns : (group + 1) * columns],
                preferred_element_type=f32,
            )
    for image in range(STEP):
        limit = 2 * sides[step * STEP + image]

        def body(row, carry):
            total, product = carry
            here = chunk(image, row)
            mask = row_mask(place, row, limit)
            parts = []
            for group in range(RADIX):
                sides_sum = []
                for side in range(3):
                    summed = None
                    for up in range(3):
                        at = group * columns + (up * 3 + side) * quarter
                        rows = pl.ds(pl.multiple_of((row + 2 - up) * SIDE, SIDE), SIDE)
                        piece = column_ref[image, rows, at : at + quarter]
                        summed = piece if summed is None else summed + piece
                    sides_sum.append(summed)
                inner = wide(place, quarter)
                low = jnp.where(inner == SIDE - 1, 0.0, pltpu.roll(sides_sum[0], SIDE - 1, 0))
                high = jnp.where(inner == 0, 0.0, pltpu.roll(sides_sum[2], 1, 0))
                parts.append(sides_sum[1] + low + high)
            dact = jnp.concatenate(parts, axis=1)
            first = first_ref[here, :]
            pre = first * ab_in_ref[0:1, :] + ab_in_ref[1:2, :]
            normed = first * ab_in_ref[2:3, :] + ab_in_ref[3:4, :]
            plain = sigmoid(pre)
            grad = dact * (plain * (1.0 + pre * (1.0 - plain)) * wide(mask, half))
            dfirst_ref[here, :] = grad
            return (total + fold(grad), product + fold(grad * normed))

        total, product = rows_of((acc_ref[0], acc_ref[1]), body, 4)
        acc_ref[0] = total
        acc_ref[1] = product

    @at_end
    def _():
        stat_ref[...] = jnp.zeros(stat_ref.shape, f32)
        put(stat_ref, 0, column_total(acc_ref[0]))
        put(stat_ref, half // 128, column_total(acc_ref[1]))


def conv_grad_kernel(act_ref, dsecond_ref, x_ref, dfirst_ref, part_ref, in_ref, conv_ref, patch_ref):
    zeros_at_start(conv_ref, in_ref, patch_ref)
    place = places()
    lanes = act_ref.shape[1]
    columns = TAPS * lanes // RADIX
    for image in range(STEP):

        def body(row, carry):
            write_patches(patch_ref, image, row, act_ref[chunk(image, row), :], place)
            return carry

        rows_of(0, body)
    for image in range(STEP):
        for group in range(RADIX):
            conv_ref[:, group * columns : (group + 1) * columns] += contract_lead(
                dsecond_ref[image * 256 : image * 256 + 256, group * lanes : (group + 1) * lanes],
                patch_ref[image, SIDE : SIDE + 256, group * columns : (group + 1) * columns],
            )
    in_ref[...] += contract_lead(dfirst_ref[...].astype(bf16), x_ref[...])

    @at_end
    def _():
        rows = conv_ref.shape[0] // part_ref.shape[0]
        if rows % 8:
            for tap in range(RADIX * TAPS):
                tile = conv_ref[:, tap * 128 : (tap + 1) * 128]
                part_ref[:, tap * rows : (tap + 1) * rows, :] = tile.reshape(-1, rows, 128)
            return
        for piece in range(part_ref.shape[0]):
            for tap in range(RADIX * TAPS):
                part_ref[piece, tap * rows : (tap + 1) * rows, :] = conv_ref[
                    piece * rows : (piece + 1) * rows, tap * 128 : (tap + 1) * 128
                ]


def in_kernel(recv_ref, terms_ref, count_ref, grads_ref, tile_ref):
    take(recv_ref, tile_ref)
    lanes = terms_ref.shape[1]
    total = row_at(tile_ref, 0, lanes)
    product = row_at(tile_ref, lanes // 128, lanes)
    count = wide(count_ref[0:1, :], lanes)
    slant = terms_ref[0:1, :] * terms_ref[2:3, :] * product / count
    grads_ref[0:1, :] = total
    grads_ref[1:2, :] = product
    grads_ref[2:3, :] = slant
    grads_ref[3:4, :] = terms_ref[0:1, :] * total / count - terms_ref[4:5, :] * slant
    grads_ref[4:5, :] = terms_ref[0:1, :]


def last_kernel(
    sides, dfirst_ref, first_ref, grads_ref, w_ref, slope_ref, terms_ref, out_ref, done_ref, low_ref
):
    step = pl.program_id(0)
    place = places()
    lanes = first_ref.shape[1]
    width = out_ref.shape[1]
    part = 512 if width % 512 == 0 else width
    for image in range(STEP):
        limit = 2 * sides[step * STEP + image]

        def body(row, carry):
            here = chunk(image, row)
            mask = wide(row_mask(place, row, limit), lanes)
            grad = dfirst_ref[here, :] * grads_ref[4:5, :]
            grad = grad - mask * (first_ref[here, :] * grads_ref[2:3, :] + grads_ref[3:4, :])
            low_ref[here, :] = grad.astype(bf16)
            return carry

        rows_of(0, body)
    out_ref[...] = contract_last(low_ref[...], w_ref[...])
    for image in range(STEP):

        def body(row, carry):
            here = chunk(image, row)
            for at in range(0, width, part):
                cut = slice(at, at + part)
                out_ref[here, cut] += slope_ref[here, cut].astype(f32) * terms_ref[4:5, cut]
            return carry

        rows_of(0, body)

    @at_end
    def _():
        done_ref[...] = jnp.zeros(done_ref.shape, f32)


def total_of(ref):
    total = ref[0].astype(f32)
    for j in range(1, ref.shape[0]):
        total = total + ref[j].astype(f32)
    return total.astype(bf16)


def total_kernel(part_ref, tile_ref, sum_ref, send_ref):
    sum_ref[...] = total_of(part_ref)
    send(send_ref, tile_ref)


def spread_kernel(one_ref, part_ref, _, send_ref):
    cut = one_ref.shape[0]
    one = one_ref[...]
    total = total_of(part_ref)
    for j in range(send_ref.shape[0]):
        send_ref[j, :cut, :] = one
        send_ref[j, cut:, :] = total


def tiles(lanes, block=0):
    return pl.BlockSpec((STEP * 256, lanes), lambda i: (i, block))


def held(*shape):
    return pl.BlockSpec(shape, lambda i: (0,) * len(shape))


def token():
    return pl.BlockSpec(memory_space=pl.ANY)


def scalars():
    return pl.BlockSpec(memory_space=pltpu.SMEM)


def shaped(shape, dtype=f32):
    return jax.ShapeDtypeStruct(shape, dtype)


def call(kernel, steps, ins, outs, scratch=(), cost=5, limit=56, name=None):
    return pl.pallas_call(
        kernel,
        grid=(steps,),
        in_specs=ins,
        out_specs=[spec for spec, _ in outs],
        out_shape=[shape for _, shape in outs],
        scratch_shapes=[pltpu.VMEM(shape, dtype) for shape, dtype in scratch],
        compiler_params=pltpu.CompilerParams(
            dimension_semantics=("arbitrary",), vmem_limit_bytes=limit * 1024 * 1024
        ),
        cost_estimate=pl.CostEstimate(
            flops=int(cost * 1e9), bytes_accessed=int(cost * 3e6), transcendentals=0
        ),
        name=name,
    )


def whole_out(shape, dtype=f32):
    return held(*shape), shaped(shape, dtype)


def rows8(*vectors):
    stacked = jnp.stack(vectors, axis=0)
    return jnp.pad(stacked, ((0, 8 - len(vectors)), (0, 0)))


def local(
    features,
    half_sides,
    cotangent,
    conv_in,
    conv_mid,
    attn_down,
    attn_up,
    attn_bias,
    conv_out,
    gain_in,
    shift_in,
    gain_mid,
    shift_mid,
    gain_attn,
    shift_attn,
    gain_out,
    shift_out,
):
    images, pixels, width = features.shape
    rows = images * pixels
    steps = images // STEP
    pieces = lax.axis_size("fsdp")
    groups = lax.axis_size("dp")
    devices = pieces * groups
    images_all = images * devices
    bottleneck = conv_in.shape[1]
    att = attn_down.shape[1]
    mid = RADIX * bottleneck
    columns = TAPS * conv_mid.shape[2]
    odd = lax.rem(lax.axis_index("dp"), 2).reshape(1)

    in_mine = gather_all(half_of(conv_in, 1)).reshape(width, bottleneck // 2)
    in_other = neighbour(in_mine)
    down_rows, up_rows = attn_down.shape[0], attn_up.shape[1]
    own_columns = conv_mid.shape[3]
    small = [gain_in, shift_in, gain_mid, shift_mid, gain_attn, shift_attn, gain_out, shift_out, attn_bias]
    lengths = [item.shape[0] for item in small]
    vectors = jnp.stack([jnp.pad(item, (0, 128 - item.shape[0])) for item in small])
    vectors = jnp.pad(vectors, ((0, 16 - len(small)), (0, 0)))
    mid_cut = half_of(conv_mid, 0)[0].transpose(0, 2, 1).reshape(TAPS * own_columns, 128)
    packed = gather_all(jnp.concatenate([mid_cut, attn_down, attn_up.T, vectors], axis=0))
    at = TAPS * own_columns
    mid_mine = packed[:, :at].reshape(pieces, TAPS, own_columns, 128).transpose(0, 2, 1, 3)
    mid_mine = mid_mine.reshape(bottleneck, columns)
    mid_other = neighbour(mid_mine)
    whole_down = packed[:, at : at + down_rows].reshape(bottleneck, att)
    at += down_rows
    whole_up = packed[:, at : at + up_rows].reshape(mid, att)
    at += up_rows
    found = [
        packed[:, at + k, :length].reshape(-1).astype(f32) for k, length in enumerate(lengths)
    ]
    p_in, p_mid, p_attn, p_out = [rows8(found[2 * k], found[2 * k + 1]) for k in range(4)]
    p_bias = rows8(found[8])

    x = features.reshape(rows, width)
    cot = cotangent.reshape(rows, width)

    def tiled(lanes, dtype=f32):
        return tiles(lanes), shaped((rows, lanes), dtype)

    def sending(count, dtype=f32):
        return whole_out((devices, count, 128), dtype)

    def received(count):
        return held(devices, count, 128)

    first, whole_in, out = call(
        first_kernel,
        steps,
        [scalars(), scalars(), tiles(width), held(width, bottleneck // 2), held(width, bottleneck // 2)],
        [tiled(bottleneck), whole_out((width, bottleneck), bf16), sending(8)],
        [((2, 8, bottleneck), f32), ((8, 128), f32)],
        8,
        name="first",
    )(half_sides, odd, x, in_mine, in_other)
    got = swap_all(out, AXES)
    out_half = half_of(conv_out, 0).T
    cross, x_sum, power_x, out_copies = call(
        cross_kernel,
        steps,
        [scalars(), tiles(width), tiles(bottleneck), held(*out_half.shape)],
        [
            whole_out((bottleneck, width)),
            whole_out((8, width)),
            whole_out((8, 128)),
            whole_out((pieces,) + out_half.shape, bf16),
        ],
        [((8, width), f32)],
        10,
        name="cross",
    )(half_sides, x, first, out_half)
    out_mine = swap_all(out_copies, "fsdp").reshape(width, bottleneck // 2)
    out_other = neighbour(out_mine)
    whole_out_t = jnp.where(
        odd[0] == 0,
        jnp.concatenate([out_mine, out_other], axis=1),
        jnp.concatenate([out_other, out_mine], axis=1),
    )
    whole_w_out = whole_out_t.T

    act_low, second, terms_in, count, whole_mid, out = call(
        second_kernel,
        steps,
        [
            scalars(),
            scalars(),
            tiles(bottleneck),
            received(8),
            held(8, bottleneck),
            held(bottleneck, columns),
            held(bottleneck, columns),
            token(),
        ],
        [
            tiled(bottleneck, bf16),
            tiled(mid),
            whole_out((8, bottleneck)),
            whole_out((8, 128)),
            whole_out((bottleneck, RADIX * columns), bf16),
            sending(8),
        ],
        [
            ((STEP, 256 + 2 * SIDE, RADIX * columns), bf16),
            ((2, 8, mid), f32),
            ((8, 128), f32),
        ],
        15,
        name="second",
    )(half_sides, odd, first, got, p_in, mid_mine, mid_other, power_x)
    got = swap_all(out, AXES)

    pooled, squeeze, terms_mid, out = call(
        pool_kernel,
        steps,
        [
            scalars(),
            tiles(mid),
            received(8),
            held(8, mid),
            held(8, 128),
            held(bottleneck, att),
            held(8, 128),
            token(),
        ],
        [
            whole_out((images, bottleneck), bf16),
            whole_out((images, att)),
            whole_out((8, mid)),
            sending(8),
        ],
        [((images, bottleneck), f32), ((8, 128), f32)],
        7,
        name="pool",
    )(half_sides, second, got, p_mid, count, whole_down, power_x, out_other)
    got = swap_all(out, AXES)

    wide_rows = 2 * width // 128
    mixed, weights, excite, gate, gram_out, colsum, power_mix, out = call(
        functools.partial(mix_kernel, images_all),
        steps,
        [
            scalars(),
            tiles(mid),
            held(8, mid),
            held(images, att),
            received(8),
            held(8, att),
            held(mid, att),
            held(8, mid),
            held(bottleneck, width),
        ],
        [
            tiled(bottleneck, bf16),
            whole_out((images, mid)),
            whole_out((images, att), bf16),
            whole_out((8, att)),
            whole_out((bottleneck, width)),
            whole_out((8, bottleneck)),
            whole_out((8, 128)),
            sending(wide_rows),
        ],
        [((bottleneck, bottleneck), f32), ((2, 8, bottleneck), f32), ((wide_rows, 128), f32)],
        11,
        name="mix",
    )(half_sides, second, terms_mid, squeeze, got, p_attn, whole_up, p_bias, whole_w_out)
    got = swap_all(out, AXES)

    block, slope, back, grad_out, terms_out, power_out, out = call(
        out_kernel,
        steps,
        [
            scalars(),
            tiles(bottleneck),
            tiles(width),
            tiles(width),
            received(wide_rows),
            held(8, width),
            held(8, 128),
            held(bottleneck, width),
            held(width, bottleneck),
        ],
        [
            tiled(width, bf16),
            tiled(width, bf16),
            tiled(bottleneck),
            whole_out((bottleneck, width)),
            whole_out((8, width)),
            whole_out((8, 128)),
            sending(wide_rows, bf16),
        ],
        [
            ((STEP * 256, width), f32),
            ((8, width), f32),
            ((8, 128), f32),
            ((wide_rows, 128), f32),
        ],
        25,
        name="output",
    )(half_sides, mixed, x, cot, got, p_out, count, whole_w_out, whole_out_t)
    got = swap_all(out, AXES)

    dmixed, sums, dup, dbias, dq, grads_out, out = call(
        gate_kernel,
        steps,
        [
            scalars(),
            tiles(mid),
            held(8, mid),
            tiles(bottleneck),
            tiles(bottleneck),
            received(wide_rows),
            held(8, width),
            held(8, width),
            held(8, 128),
            held(bottleneck, width),
            held(width, bottleneck),
            held(images, mid),
            held(images, att),
            held(images, att),
            held(8, att),
            held(mid, att),
            held(8, 128),
            held(8, 128),
        ],
        [
            tiled(bottleneck),
            whole_out((5, images, mid)),
            whole_out((mid, att)),
            whole_out((8, mid)),
            whole_out((images, att)),
            whole_out((8, width)),
            sending(8),
        ],
        [
            ((bottleneck, bottleneck), bf16),
            ((8, bottleneck), f32),
            ((wide_rows, 128), f32),
        ],
        13,
        name="gate",
    )(
        half_sides,
        second,
        terms_mid,
        back,
        mixed,
        got,
        terms_out,
        p_out,
        count,
        whole_w_out,
        whole_out_t,
        weights,
        excite,
        squeeze,
        gate,
        whole_up,
        power_out,
        power_mix,
    )
    got = swap_all(out, AXES)
    grad_conv_out = grad_out - colsum[0][:, None] * grads_out[3] - gram_out * grads_out[2]

    ddown, dpool, grads_attn, out = call(
        functools.partial(squeeze_kernel, images_all, width),
        1,
        [
            scalars(),
            held(images, att),
            held(images, att),
            held(8, att),
            received(8),
            held(images, bottleneck),
            held(bottleneck, att),
            held(images, mid),
            held(5, images, mid),
            held(8, mid),
            held(8, 128),
            held(8, width),
        ],
        [
            whole_out((bottleneck, att)),
            whole_out((images, bottleneck)),
            whole_out((8, att)),
            sending(8),
        ],
        [((8, 128), f32), ((images, bottleneck), f32)],
        1,
        name="squeeze",
    )(
        half_sides,
        dq,
        squeeze,
        gate,
        got,
        pooled,
        whole_down,
        weights,
        sums,
        p_mid,
        count,
        terms_out,
    )
    got = swap_all(out, AXES)

    out_cut = grad_conv_out.astype(bf16).reshape(bottleneck, pieces, -1).transpose(1, 0, 2)
    out_cut = out_cut.reshape(devices, -1, 128)
    bias_rows = jnp.pad(dbias[0].reshape(pieces, 1, up_rows), ((0, 0), (0, 0), (0, att - up_rows)))
    gates = jnp.concatenate(
        [
            dup.reshape(devices, -1, att),
            ddown.reshape(devices, -1, att),
            jnp.repeat(bias_rows, groups, axis=0),
        ],
        axis=1,
    ).astype(bf16)
    marks = [out_cut.shape[1], up_rows // groups, down_rows // groups]
    gates = jnp.concatenate([out_cut, gates], axis=1)
    gates = jnp.pad(gates, ((0, 0), (0, -gates.shape[1] % 16), (0, 0)))

    gates = swap_all(gates, AXES)
    dsecond, dfirst, grads_mid, stat = call(
        conv_back_kernel,
        steps,
        [
            scalars(),
            tiles(mid),
            held(8, mid),
            received(8),
            held(8, mid),
            held(8, 128),
            tiles(bottleneck),
            held(images, mid),
            held(images, bottleneck),
            tiles(bottleneck),
            held(8, bottleneck),
            held(bottleneck, RADIX * columns),
        ],
        [tiled(mid, bf16), tiled(bottleneck), whole_out((8, mid)), whole_out((8, 128))],
        [
            ((STEP, 256 + 2 * SIDE, RADIX * columns), f32),
            ((2, 8, bottleneck), f32),
            ((8, 128), f32),
        ],
        20,
        name="conv_back",
    )(
        half_sides,
        second,
        terms_mid,
        got,
        p_mid,
        count,
        dmixed,
        weights,
        dpool,
        first,
        terms_in,
        whole_mid,
    )
    gates, out = call(
        total_kernel,
        1,
        [held(*gates.shape), held(8, 128)],
        [whole_out(gates.shape[1:], bf16), sending(8)],
        (),
        2,
        name="last_gates",
    )(gates, stat)
    got = swap_all(out, AXES)

    conv_parts, in_grad = call(
        conv_grad_kernel,
        steps,
        [tiles(bottleneck), tiles(mid), tiles(width), tiles(bottleneck)],
        [
            whole_out((devices, bottleneck // devices * RADIX * TAPS, 128)),
            whole_out((bottleneck, width)),
        ],
        [
            ((bottleneck, RADIX * columns), f32),
            ((STEP, 256 + 2 * SIDE, RADIX * columns), bf16),
        ],
        15,
        name="conv_grad",
    )(act_low, dsecond, x, dfirst)
    (grads_in,) = call(
        in_kernel,
        1,
        [received(8), held(8, bottleneck), held(8, 128)],
        [whole_out((8, bottleneck))],
        [((8, 128), f32)],
        1,
        name="last_terms",
    )(got, terms_in, count)
    grad_features, done = call(
        last_kernel,
        steps,
        [
            scalars(),
            tiles(bottleneck),
            tiles(bottleneck),
            held(8, bottleneck),
            held(width, bottleneck),
            tiles(width),
            held(8, width),
        ],
        [tiled(width), whole_out((8, 128))],
        [((STEP * 256, bottleneck), bf16)],
        15,
        name="last",
    )(half_sides, dfirst, first, grads_in, whole_in, slope, terms_out)

    grad_conv_in = (
        in_grad * grads_in[4][:, None]
        - cross * grads_in[2][:, None]
        - column_total(x_sum) * grads_in[3][:, None]
    )
    in_cut = grad_conv_in.astype(bf16).reshape(bottleneck, pieces, -1).transpose(1, 0, 2)
    in_cut = in_cut.reshape(devices, -1, 128)
    mid_rows = bottleneck // devices
    marks += [in_cut.shape[1], conv_parts.shape[1]]
    late = jnp.concatenate([in_cut, conv_parts.astype(bf16)], axis=1)
    late = jnp.pad(late, ((0, 0), (0, -late.shape[1] % 16), (0, 0)))
    late = late.reshape(devices // 2, 2, -1, 128)
    mine = lax.dynamic_index_in_dim(late, odd[0], 1, False)
    other = lax.dynamic_index_in_dim(late, 1 - odd[0], 1, False)
    late = (mine.astype(f32) + neighbour(other).astype(f32)).astype(bf16)
    sides_of = [[2 * i + side for i in range(devices // 2)] for side in range(2)]
    late = lax.all_to_all(late, AXES, 0, 0, axis_index_groups=sides_of)
    (summed,) = call(
        spread_kernel,
        1,
        [held(*gates.shape), held(*late.shape), token()],
        [whole_out((groups, gates.shape[0] + late.shape[1], 128), bf16)],
        (),
        2,
        name="last_total",
    )(gates, late, done)
    summed = swap_all(summed, "dp").astype(f32)
    shard_out = summed[:, : marks[0]].reshape(bottleneck, -1)
    at = marks[0]
    shard_up = summed[:, at : at + marks[1]].reshape(up_rows, att).T
    at += marks[1]
    shard_down = summed[:, at : at + marks[2]].reshape(down_rows, att)
    at += marks[2]
    shard_bias = summed[0, at, :up_rows]
    at = gates.shape[0]
    shard_in = summed[:, at : at + marks[3]].reshape(bottleneck, -1).T
    at += marks[3]
    shard_mid = summed[:, at : at + marks[4]].reshape(groups, RADIX, TAPS, mid_rows, 128)
    shard_mid = shard_mid.transpose(1, 2, 4, 0, 3).reshape(RADIX, TAPS, 128, own_columns)

    def own_part(row):
        length = row.shape[0] // pieces
        return lax.dynamic_slice_in_dim(row, lax.axis_index("fsdp") * length, length, 0)

    return (
        block.reshape(images, pixels, width),
        grad_features.reshape(images, pixels, width),
        grads_attn[2, :4],
        shard_in,
        shard_mid,
        shard_down,
        shard_up,
        shard_bias,
        shard_out,
        own_part(grads_in[1]),
        own_part(grads_in[0]),
        own_part(grads_mid[1]),
        own_part(grads_mid[0]),
        own_part(grads_attn[1]),
        own_part(grads_attn[0]),
        own_part(grads_out[1]),
        own_part(grads_out[0]),
    )


def solution(mesh):
    return jax.shard_map(
        local,
        mesh=mesh,
        in_specs=(
            P(("fsdp", "dp"), None, None),
            P(("fsdp", "dp")),
            P(("fsdp", "dp"), None, None),
            P("fsdp", None),
            P(None, None, None, "fsdp"),
            P("fsdp", None),
            P(None, "fsdp"),
            P("fsdp"),
            P(None, "fsdp"),
            P("fsdp"),
            P("fsdp"),
            P("fsdp"),
            P("fsdp"),
            P("fsdp"),
            P("fsdp"),
            P("fsdp"),
            P("fsdp"),
        ),
        out_specs=(
            P(("fsdp", "dp"), None, None),
            P(("fsdp", "dp"), None, None),
            P(),
            P("fsdp", None),
            P(None, None, None, "fsdp"),
            P("fsdp", None),
            P(None, "fsdp"),
            P("fsdp"),
            P(None, "fsdp"),
            P("fsdp"),
            P("fsdp"),
            P("fsdp"),
            P("fsdp"),
            P("fsdp"),
            P("fsdp"),
            P("fsdp"),
            P("fsdp"),
        ),
        check_vma=False,
    )
```

time: 429 us -> 338 us (0.79)
  local copies, waits for them, and re-layouts: 60.3 us -> 32.1 us
  other arithmetic: 35.5 us -> 11.4 us
  waiting for transfers between devices: 91.6 us -> 70.8 us
  blocking collectives: 20 us -> 0 us
  Pallas kernels: 150 us -> 164 us
  starting transfers between devices: 64.5 us -> 55.7 us
    all_to_all x17 -> x13, waiting for transfers between devices: 90.4 us -> 67.7 us  [swap_all(): return lax.all_to_all(values, axes, 0, 0)]
    all_to_all x2 -> x0, blocking collectives: 20 us -> none  [swap_all(): return lax.all_to_all(values, axes, 0, 0)]
    all_to_all x17 -> x13, starting transfers between devices: 64.2 us -> 48.2 us  [swap_all(): return lax.all_to_all(values, axes, 0, 0)]
    unnamed x154 -> x50, local copies, waits for them, and re-layouts: 23.4 us -> 8.28 us
    pallas_call x7 -> x10, Pallas kernels: 78.2 us -> 88.6 us  [the longest x1 22.5 us: local(): call(conv_back_kernel, steps, [scalars(), tiles(mid), held(8, mid), recei...]
    broadcast_in_dim x16 -> x4, local copies, waits for them, and re-layouts: 9.55 us -> 1.76 us  [the longest x2 1.73 us: gather_all(): jnp.broadcast_to(shard[None], (pieces,) + shard.shape)]
    reduce_sum x16 -> x0, other arithmetic: 7.17 us -> none  [the longest x8 2.57 us: all_sum(): return jnp.sum(swap_all(copies, AXES), axis=0)]
    all_to_all x0 -> x1, starting transfers between devices: none -> 6.76 us  [local(): late = lax.all_to_all(late, AXES, 0, 0, axis_index_groups=sides_of)]
  transfers between devices with their start and end apart: 20 -> 18, of which waited for: 15 -> 11; matrix products, arithmetic and copies ran while one was open for 12% -> 8% of each run, Pallas kernels for 11% -> 28%
where the time goes in v2:
time: 338 us; the launch traced here: 336 us
  Pallas kernels  164 us (49%)
  waiting for transfers between devices  70.8 us (21%)
  starting transfers between devices  55.7 us (16%)
  local copies, waits for them, and re-layouts  32.1 us (9%)
  other arithmetic  11.4 us (3%)
    all_to_all x13, waiting for transfers between devices, swap_all(): return lax.all_to_all(values, axes, 0, 0)  67.7 us
    all_to_all x13, starting transfers between devices, swap_all(): return lax.all_to_all(values, axes, 0, 0)  48.2 us
    pallas_call x1, Pallas kernels, local(): call(out_kernel, steps, [scalars(), tiles(bottleneck), tiles(width), tile...  27.3 us
    pallas_call x1, Pallas kernels, local(): call(conv_back_kernel, steps, [scalars(), tiles(mid), held(8, mid), recei...  22.5 us
    pallas_call x1, Pallas kernels, local(): call(last_kernel, steps, [scalars(), tiles(bottleneck), tiles(bottleneck)...  16.8 us
    pallas_call x1, Pallas kernels, local(): call(conv_grad_kernel, steps, [tiles(bottleneck), tiles(mid), tiles(width...  16.6 us
    pallas_call x1, Pallas kernels, local(): call(second_kernel, steps, [scalars(), scalars(), tiles(bottleneck), rece...  16.5 us
    pallas_call x1, Pallas kernels, local(): call(gate_kernel, steps, [scalars(), tiles(mid), held(8, mid), tiles(bott...  15.1 us
  transfers between devices with their start and end apart: 18, of which 11 were waited for; matrix products, arithmetic and copies ran while one was open for 8% of the time, Pallas kernels for 28%

profile of v2, /device:TPU:0, one launch (start us, length us, event | category | flops | bytes accessed | tf_op | source)
XLA Modules:
  0.0 335.5 jit_solution(2079681658332173014)
XLA Ops:
  2.2 7.4 %all-to-all-start = ((bf16[8,128,128]{2,1,0:T(8,128)(2,1)}), bf16[8,128,128]{2,1,0:T(8,128)(2,1)S(1)}, u32[]{:S(2)}, u32[]{:S(2)}) async-start(bf16[8,128,128]{2,1,0:T(8,128)(2,1)} %broadcast_in_dim.8), calls=%async_computation | async-start | bytes 524288 | tf_op jit(solution)/shard_map/all_to_all | solution.py:23
  11.7 6.9 %all-to-all-done = bf16[8,128,128]{2,1,0:T(8,128)(2,1)S(1)} async-done(((bf16[8,128,128]{2,1,0:T(8,128)(2,1)}), bf16[8,128,128]{2,1,0:T(8,128)(2,1)S(1)}, u32[]{:S(2)}, u32[]{:S(2)}) %all-to-all-start) | async-done | bytes 262176 | tf_op jit(solution)/shard_map/all_to_all | solution.py:23
  21.7 3.6 %all-to-all-start.2 = ((bf16[8,400,128]{2,1,0:T(8,128)(2,1)}), bf16[8,400,128]{2,1,0:T(8,128)(2,1)S(1)}, u32[]{:S(2)}, u32[]{:S(2)}) async-start(bf16[8,400,128]{2,1,0:T(8,128)(2,1)} %broadcast_in_dim.9), calls=%async_computation.2 | async-start | bytes 1638400 | tf_op jit(solution)/shard_map/all_to_all | solution.py:23
  26.7 10.2 %first.1 = (f32[4096,256]{1,0:T(8,128)}, bf16[1024,256]{1,0:T(8,128)(2,1)}, f32[32,8,128]{2,1,0:T(8,128)}) custom-call(s32[16]{0:T(128)} %sides.19, s32[1]{0:T(128)} %bitcast.odd, bf16[4096,1024]{1,0:T(8,128)(2,1)} %bitcast.156, bf16[1024,128]{1,0:T(8,128)(2,1)} %bitcast.136, bf16[1024,128]{1,0:T(8,128)(2,1)} %copy-done.23), custom_call_target="tpu_custom_call" | custom-call | flops 8000000000 | bytes 24000000 | tf_op jit(solution)/shard_map/first/pallas_call | solution.py:1075
  36.9 11.4 %cross.1 = (f32[256,1024]{1,0:T(8,128)}, f32[8,1024]{1,0:T(8,128)}, f32[8,128]{1,0:T(8,128)}, bf16[8,128,128]{2,1,0:T(8,128)(2,1)}) custom-call(s32[16]{0:T(128)} %sides.19, bf16[4096,1024]{1,0:T(8,128)(2,1)} %bitcast.157, f32[4096,256]{1,0:T(8,128)} %get-tuple-element.70.first_ref, bf16[128,128]{1,0:T(8,128)(2,1)} %bitcast.145), custom_call_target="tpu_custom_call" | custom-call | flops 10000000000 | bytes 30000000 | tf_op jit(solution)/shard_map/cross/pallas_call | solution.py:1086
  48.3 6.0 %all-to-all-start.4 = ((bf16[8,128,128]{2,1,0:T(8,128)(2,1)}), bf16[8,128,128]{2,1,0:T(8,128)(2,1)S(1)}, u32[]{:S(2)}, u32[]{:S(2)}) async-start(bf16[8,128,128]{2,1,0:T(8,128)(2,1)} %get-tuple-element.76), calls=%async_computation.4 | async-start | bytes 524288 | tf_op jit(solution)/shard_map/all_to_all | solution.py:23
  55.0 8.6 %all-to-all-done.4 = bf16[8,128,128]{2,1,0:T(8,128)(2,1)S(1)} async-done(((bf16[8,128,128]{2,1,0:T(8,128)(2,1)}), bf16[8,128,128]{2,1,0:T(8,128)(2,1)S(1)}, u32[]{:S(2)}, u32[]{:S(2)}) %all-to-all-start.4) | async-done | bytes 262176 | tf_op jit(solution)/shard_map/all_to_all | solution.py:23
  63.6 3.6 %all-to-all-start.1 = ((f32[32,8,128]{2,1,0:T(8,128)}), f32[32,8,128]{2,1,0:T(8,128)S(1)}, u32[]{:S(2)}, u32[]{:S(2)}) async-start(f32[32,8,128]{2,1,0:T(8,128)} %get-tuple-element.71), calls=%async_computation.1 | async-start | bytes 262144 | tf_op jit(solution)/shard_map/all_to_all | solution.py:23
  68.3 7.1 %all-to-all-done.1.recv_ref = f32[32,8,128]{2,1,0:T(8,128)S(1)} async-done(((f32[32,8,128]{2,1,0:T(8,128)}), f32[32,8,128]{2,1,0:T(8,128)S(1)}, u32[]{:S(2)}, u32[]{:S(2)}) %all-to-all-start.1) | async-done | bytes 131104 | tf_op jit(solution)/shard_map/all_to_all | solution.py:23
  76.3 16.5 %second.1 = (bf16[4096,256]{1,0:T(8,128)(2,1)}, f32[4096,512]{1,0:T(8,128)}, f32[8,256]{1,0:T(8,128)}, f32[8,128]{1,0:T(8,128)}, bf16[256,2304]{1,0:T(8,128)(2,1)}, /*index=5*/f32[32,8,128]{2,1,0:T(8,128)}) custom-call(s32[16]{0:T(128)} %sides.19, s32[1]{0:T(128)} %bitcast.odd, f32[4096,256]{1,0:T(8,128)} %get-tuple-element.70.first_ref, ...), custom_call_target="tpu_custom_call" | custom-call | flops 15000000512 | bytes 45000000 | tf_op jit(solution)/shard_map/second/pallas_call | solution.py:1109
  92.8 2.6 all-to-all-start.3
  97.1 6.5 %all-to-all-done.3.recv_ref = f32[32,8,128]{2,1,0:T(8,128)S(1)} async-done(((f32[32,8,128]{2,1,0:T(8,128)}), f32[32,8,128]{2,1,0:T(8,128)S(1)}, u32[]{:S(2)}, u32[]{:S(2)}) %all-to-all-start.3) | async-done | bytes 131104 | tf_op jit(solution)/shard_map/all_to_all | solution.py:23
  104.3 8.1 %pool.1 = (bf16[16,256]{1,0:T(8,128)(2,1)}, f32[16,128]{1,0:T(8,128)}, f32[8,512]{1,0:T(8,128)}, f32[32,8,128]{2,1,0:T(8,128)}) custom-call(s32[16]{0:T(128)} %sides.19, f32[4096,512]{1,0:T(8,128)} %get-tuple-element.73.second_ref, f32[32,8,128]{2,1,0:T(8,128)} %copy-done.14, f32[8,512]{1,0:T(8,128)} %fusion.23.param_ref, ...), custom_call_target="tpu_custom_call" | custom-call | flops 7000000000 | bytes 21000000 | tf_op jit(solution)/shard_map/pool/pallas_call | solution.py:1140
  119.1 4.1 %all-to-all-done.5.recv_ref = f32[32,8,128]{2,1,0:T(8,128)S(1)} async-done(((f32[32,8,128]{2,1,0:T(8,128)}), f32[32,8,128]{2,1,0:T(8,128)S(1)}, u32[]{:S(2)}, u32[]{:S(2)}) %all-to-all-start.5) | async-done | bytes 131104 | tf_op jit(solution)/shard_map/all_to_all | solution.py:23
  123.9 12.5 %mix.1 = (bf16[4096,256]{1,0:T(8,128)(2,1)}, f32[16,512]{1,0:T(8,128)}, bf16[16,128]{1,0:T(8,128)(2,1)}, f32[8,128]{1,0:T(8,128)}, f32[256,1024]{1,0:T(8,128)}, ...) custom-call(s32[16]{0:T(128)} %sides.19, f32[4096,512]{1,0:T(8,128)} %get-tuple-element.73.second_ref, ...), custom_call_target="tpu_custom_call" | custom-call | flops 11000000512 | bytes 33000000 | tf_op jit(solution)/shard_map/mix/pallas_call | solution.py:1166
  136.4 2.6 all-to-all-start.6
  139.6 10.0 %all-to-all-done.6.recv_ref = f32[32,16,128]{2,1,0:T(8,128)S(1)} async-done(((f32[32,16,128]{2,1,0:T(8,128)}), f32[32,16,128]{2,1,0:T(8,128)S(1)}, u32[]{:S(2)}, u32[]{:S(2)}) %all-to-all-start.6) | async-done | bytes 262176 | tf_op jit(solution)/shard_map/all_to_all | solution.py:23
  150.3 27.3 %output.1 = (bf16[4096,1024]{1,0:T(8,128)(2,1)}, bf16[4096,1024]{1,0:T(8,128)(2,1)}, f32[4096,256]{1,0:T(8,128)}, f32[256,1024]{1,0:T(8,128)}, f32[8,1024]{1,0:T...) custom-call(s32[16]{0:T(128)} %sides.19, bf16[4096,256]{1,0:T(8,128)(2,1)} %get-tuple-element.80.mixed_ref, ...), custom_call_target="tpu_custom_call" | custom-call | flops 24999999488 | bytes 75000000 | tf_op jit(solution)/shard_map/output/pallas_call | solution.py:1196
  180.9 7.5 %all-to-all-done.7.recv_ref = bf16[32,16,128]{2,1,0:T(8,128)(2,1)S(1)} async-done(((bf16[32,16,128]{2,1,0:T(8,128)(2,1)}), bf16[32,16,128]{2,1,0:T(8,128)(2,1)S(1)}, u32[]{:S(2)}, u32[]{:S(2)}) %all-to-all-start.7) | async-done | bytes 131104 | tf_op jit(solution)/shard_map/all_to_all | solution.py:23
  189.1 15.1 %gate.1 = (f32[4096,256]{1,0:T(8,128)}, f32[5,16,512]{2,1,0:T(8,128)}, f32[512,128]{1,0:T(8,128)}, f32[8,512]{1,0:T(8,128)}, f32[16,128]{1,0:T(8,128)}, /*index=5*/f32[8,1024]{1,0:T(8,128)}, f32[32,8,128]{2,1,0:T(8,128)}) custom-call(s32[16]{0:T(128)} %sides.19, f32[4096,512]{1,0:T(8,128)} %get-tuple-element.73.second_ref, ...), custom_call_target="tpu_custom_call" | custom-call | flops 12999999488 | bytes 39000000 | tf_op jit(solution)/shard_map/gate/pallas_call | solution.py:1230
  205.0 2.8 all-to-all-start.8
  210.0 5.9 %all-to-all-done.8.recv_ref = f32[32,8,128]{2,1,0:T(8,128)S(1)} async-done(((f32[32,8,128]{2,1,0:T(8,128)}), f32[32,8,128]{2,1,0:T(8,128)S(1)}, u32[]{:S(2)}, u32[]{:S(2)}) %all-to-all-start.8) | async-done | bytes 131104 | tf_op jit(solution)/shard_map/all_to_all | solution.py:23
  222.9 6.3 %all-to-all-done.9.recv_ref = f32[32,8,128]{2,1,0:T(8,128)S(1)} async-done(((f32[32,8,128]{2,1,0:T(8,128)}), f32[32,8,128]{2,1,0:T(8,128)S(1)}, u32[]{:S(2)}, u32[]{:S(2)}) %all-to-all-start.9) | async-done | bytes 131104 | tf_op jit(solution)/shard_map/all_to_all | solution.py:23
  229.3 2.6 all-to-all-start.10
  231.9 22.5 %conv_back.1 = (bf16[4096,512]{1,0:T(8,128)(2,1)}, f32[4096,256]{1,0:T(8,128)}, f32[8,512]{1,0:T(8,128)}, f32[8,128]{1,0:T(8,128)}) custom-call(s32[16]{0:T(128)} %sides.19, f32[4096,512]{1,0:T(8,128)} %get-tuple-element.73.second_ref, f32[8,512]{1,0:T(8,128)} %get-tuple-element.77.ab_ref, f32[32,8,128]{2,1,0:T(8,128)} %copy-done.17, ...), custom_call_target="tpu_custom_call" | custom-call | flops 20000000000 | bytes 60000000 | tf_op jit(solution)/shard_map/conv_back/pallas_call | solution.py:1350
  257.1 5.8 %all-to-all-start.11 = ((f32[32,8,128]{2,1,0:T(8,128)}), f32[32,8,128]{2,1,0:T(8,128)S(1)}, u32[]{:S(2)}, u32[]{:S(2)}) async-start(f32[32,8,128]{2,1,0:T(8,128)} %get-tuple-element.109), calls=%async_computation.11 | async-start | bytes 262144 | tf_op jit(solution)/shard_map/all_to_all | solution.py:23
  263.0 16.6 %conv_grad.1 = (f32[32,144,128]{2,1,0:T(8,128)}, f32[256,1024]{1,0:T(8,128)}) custom-call(bf16[4096,256]{1,0:T(8,128)(2,1)} %get-tuple-element.115.act_ref, bf16[4096,512]{1,0:T(8,128)(2,1)} %get-tuple-element.116.dsecond_ref, bf16[4096,1024]{1,0:T(8,128)(2,1)} %bitcast.159, f32[4096,256]{1,0:T(8,128)} %get-tuple-element.100.dfirst_ref), custom_call_target="tpu_custom_call" | custom-call | flops 15000000512 | bytes 45000000 | tf_op jit(solution)/shard_map/conv_grad/pallas_call | solution.py:1400
  290.6 6.8 %all-to-all-start.12 = ((bf16[16,208,128]{2,1,0:T(8,128)(2,1)}), bf16[16,208,128]{2,1,0:T(8,128)(2,1)S(1)}, u32[]{:S(2)}, u32[]{:S(2)}) async-start(bf16[16,208,128]{2,1,0:T(8,128)(2,1)} %fusion), calls=%async_computation.12 | async-start | bytes 1703936 | tf_op jit(solution)/shard_map/all_to_all | solution.py:1458
  298.7 16.8 %last.1 = (f32[4096,1024]{1,0:T(8,128)}, f32[8,128]{1,0:T(8,128)}) custom-call(s32[16]{0:T(128)} %sides.19, f32[4096,256]{1,0:T(8,128)} %get-tuple-element.100.dfirst_ref, f32[4096,256]{1,0:T(8,128)} %get-tuple-element.70.first_ref, f32[8,256]{1,0:T(8,128)} %last_terms.1.grads_ref, bf16[1024,256]{1,0:T(8,128)(2,1)} %get-tuple-element.110.w_ref, ...), custom_call_target="tpu_custom_call" | custom-call | flops 15000000512 | bytes 45000000 | tf_op jit(solution)/shard_map/last/pallas_call | solution.py:1424
  315.5 3.1 all-to-all-done.12.part_ref
  321.6 3.5 %all-to-all-start.13 = ((bf16[4,304,128]{2,1,0:T(8,128)(2,1)}), bf16[4,304,128]{2,1,0:T(8,128)(2,1)S(1)}, u32[]{:S(2)}, u32[]{:S(2)}) async-start(bf16[4,304,128]{2,1,0:T(8,128)(2,1)} %last_total.1), calls=%async_computation.13 | async-start | bytes 622592 | tf_op jit(solution)/shard_map/all_to_all | solution.py:23
  326.8 4.8 %all-to-all-done.13 = bf16[4,304,128]{2,1,0:T(8,128)(2,1)S(1)} async-done(((bf16[4,304,128]{2,1,0:T(8,128)(2,1)}), bf16[4,304,128]{2,1,0:T(8,128)(2,1)S(1)}, u32[]{:S(2)}, u32[]{:S(2)}) %all-to-all-start.13) | async-done | bytes 311328 | tf_op jit(solution)/shard_map/all_to_all | solution.py:23
  (137 shorter events, 59.5 us)
Async XLA Ops:
  0.7 11.0 %copy-start = (bf16[2,9,128,32]{2,3,1,0:T(8,128)(2,1)S(1)}, bf16[2,9,128,32]{2,3,1,0:T(8,128)(2,1)}, u32[]{:S(2)}) copy-start(bf16[2,9,128,32]{2,3,1,0:T(8,128)(2,1)} %param.21) | copy-start | bytes 442372
  2.2 23.0 %copy-start.21 = (bf16[256,128]{1,0:T(8,128)(2,1)S(1)}, bf16[256,128]{1,0:T(8,128)(2,1)}, u32[]{:S(2)}) copy-start(bf16[256,128]{1,0:T(8,128)(2,1)} %param.25) | copy-start | bytes 196612
  2.2 16.3 %all-to-all-start = ((bf16[8,128,128]{2,1,0:T(8,128)(2,1)}), bf16[8,128,128]{2,1,0:T(8,128)(2,1)S(1)}, u32[]{:S(2)}, u32[]{:S(2)}) async-start(bf16[8,128,128]{2,1,0:T(8,128)(2,1)} %broadcast_in_dim.8), calls=%async_computation | async-start | bytes 524288 | tf_op jit(solution)/shard_map/all_to_all | solution.py:23
  18.5 7.5 %copy-start.10 = (bf16[8,128,128]{2,1,0:T(8,128)(2,1)}, bf16[8,128,128]{2,1,0:T(8,128)(2,1)S(1)}, u32[]{:S(2)}) copy-start(bf16[8,128,128]{2,1,0:T(8,128)(2,1)S(1)} %all-to-all-done) | copy-start | bytes 786436
  18.5 7.5 %collective-permute-start = (bf16[1024,128]{1,0:T(8,128)(2,1)S(1)}, bf16[1024,128]{1,0:T(8,128)(2,1)S(1)}, u32[]{:S(2)}, u32[]{:S(2)}) collective-permute-start(bf16[1024,128]{1,0:T(8,128)(2,1)S(1)} %bitcast.135), channel_id=1, source_target_pairs={{0,1},{1,0},{2,3},{3,2},{4,5},{5,4},{6,7},{7,6},{8,9},{9,8},{10,11... | collective-permute-start | bytes 786440 | tf_op jit(solution)/shard_map/ppermute | solution.py:32
  21.7 26.7 %all-to-all-start.2 = ((bf16[8,400,128]{2,1,0:T(8,128)(2,1)}), bf16[8,400,128]{2,1,0:T(8,128)(2,1)S(1)}, u32[]{:S(2)}, u32[]{:S(2)}) async-start(bf16[8,400,128]{2,1,0:T(8,128)(2,1)} %broadcast_in_dim.9), calls=%async_computation.2 | async-start | bytes 1638400 | tf_op jit(solution)/shard_map/all_to_all | solution.py:23
  48.3 15.2 %all-to-all-start.4 = ((bf16[8,128,128]{2,1,0:T(8,128)(2,1)}), bf16[8,128,128]{2,1,0:T(8,128)(2,1)S(1)}, u32[]{:S(2)}, u32[]{:S(2)}) async-start(bf16[8,128,128]{2,1,0:T(8,128)(2,1)} %get-tuple-element.76), calls=%async_computation.4 | async-start | bytes 524288 | tf_op jit(solution)/shard_map/all_to_all | solution.py:23
  54.9 20.6 %copy-start.9 = (bf16[32,8,9,128]{3,1,2,0:T(8,128)(2,1)}, bf16[32,8,9,128]{3,1,2,0:T(8,128)(2,1)S(1)}, u32[]{:S(2)}) copy-start(bf16[32,8,9,128]{3,1,2,0:T(8,128)(2,1)S(1)} %copy.93) | copy-start | bytes 1769476
  54.9 20.6 %collective-permute-start.1 = (bf16[256,1152]{1,0:T(8,128)(2,1)S(1)}, bf16[256,1152]{1,0:T(8,128)(2,1)S(1)}, u32[]{:S(2)}, u32[]{:S(2)}) collective-permute-start(bf16[256,1152]{1,0:T(8,128)(2,1)S(1)} %bitcast.129), channel_id=1, source_target_pairs={{0,1},{1,0},{2,3},{3,2},{4,5},{5,4},{6,7},{7,6},{8,9},{9,8},{10,11... | collective-permute-start | bytes 1769480 | tf_op jit(solution)/shard_map/ppermute | solution.py:32
  63.6 11.9 %all-to-all-start.1 = ((f32[32,8,128]{2,1,0:T(8,128)}), f32[32,8,128]{2,1,0:T(8,128)S(1)}, u32[]{:S(2)}, u32[]{:S(2)}) async-start(f32[32,8,128]{2,1,0:T(8,128)} %get-tuple-element.71), calls=%async_computation.1 | async-start | bytes 262144 | tf_op jit(solution)/shard_map/all_to_all | solution.py:23
  67.2 29.9 %collective-permute-start.2 = (bf16[1024,128]{1,0:T(8,128)(2,1)S(1)}, bf16[1024,128]{1,0:T(8,128)(2,1)S(1)}, u32[]{:S(2)}, u32[]{:S(2)}) collective-permute-start(bf16[1024,128]{1,0:T(8,128)(2,1)S(1)} %bitcast.127), channel_id=1, source_target_pairs={{0,1},{1,0},{2,3},{3,2},{4,5},{5,4},{6,7},{7,6},{8,9},{9,8},{10,11... | collective-permute-start | bytes 786440 | tf_op jit(solution)/shard_map/ppermute | solution.py:32
  92.8 10.8 %all-to-all-start.3 = ((f32[32,8,128]{2,1,0:T(8,128)}), f32[32,8,128]{2,1,0:T(8,128)S(1)}, u32[]{:S(2)}, u32[]{:S(2)}) async-start(f32[32,8,128]{2,1,0:T(8,128)} %get-tuple-element.74), calls=%async_computation.3 | async-start | bytes 262144 | tf_op jit(solution)/shard_map/all_to_all | solution.py:23
  97.1 6.6 %copy-start.12 = (bf16[1024,128]{1,0:T(8,128)(2,1)}, bf16[1024,128]{1,0:T(8,128)(2,1)S(1)}, u32[]{:S(2)}) copy-start(bf16[1024,128]{1,0:T(8,128)(2,1)S(1)} %collective-permute-done.2._) | copy-start | bytes 786436
  112.4 10.8 %all-to-all-start.5 = ((f32[32,8,128]{2,1,0:T(8,128)}), f32[32,8,128]{2,1,0:T(8,128)S(1)}, u32[]{:S(2)}, u32[]{:S(2)}) async-start(f32[32,8,128]{2,1,0:T(8,128)} %get-tuple-element.79), calls=%async_computation.5 | async-start | bytes 262144 | tf_op jit(solution)/shard_map/all_to_all | solution.py:23
  118.1 18.3 %copy-start.2 = (bf16[1024,256]{1,0:T(8,128)(2,1)}, bf16[1024,256]{1,0:T(8,128)(2,1)S(1)}, u32[]{:S(2)}) copy-start(bf16[1024,256]{1,0:T(8,128)(2,1)S(1)} %maximum_select_fusion.wt_ref) | copy-start | bytes 1572868
  136.4 13.2 %all-to-all-start.6 = ((f32[32,16,128]{2,1,0:T(8,128)}), f32[32,16,128]{2,1,0:T(8,128)S(1)}, u32[]{:S(2)}, u32[]{:S(2)}) async-start(f32[32,16,128]{2,1,0:T(8,128)} %get-tuple-element.81), calls=%async_computation.6 | async-start | bytes 524288 | tf_op jit(solution)/shard_map/all_to_all | solution.py:23
  150.3 29.9 %copy-start.20 = (f32[8,1024]{1,0:T(8,128)S(1)}, f32[8,1024]{1,0:T(8,128)}, u32[]{:S(2)}) copy-start(f32[8,1024]{1,0:T(8,128)} %get-tuple-element.119) | copy-start | bytes 98308
  177.6 10.8 %all-to-all-start.7 = ((bf16[32,16,128]{2,1,0:T(8,128)(2,1)}), bf16[32,16,128]{2,1,0:T(8,128)(2,1)S(1)}, u32[]{:S(2)}, u32[]{:S(2)}) async-start(bf16[32,16,128]{2,1,0:T(8,128)(2,1)} %get-tuple-element.84), calls=%async_computation.7 | async-start | bytes 262144 | tf_op jit(solution)/shard_map/all_to_all | solution.py:23
  189.1 20.6 %copy-start.3 = (f32[256,1024]{1,0:T(8,128)S(1)}, f32[256,1024]{1,0:T(8,128)}, u32[]{:S(2)}) copy-start(f32[256,1024]{1,0:T(8,128)} %get-tuple-element.104) | copy-start | bytes 3145732
  189.1 20.6 %copy-start.4 = (f32[256,1024]{1,0:T(8,128)S(1)}, f32[256,1024]{1,0:T(8,128)}, u32[]{:S(2)}) copy-start(f32[256,1024]{1,0:T(8,128)} %get-tuple-element.101) | copy-start | bytes 3145732
  205.0 10.8 %all-to-all-start.8 = ((f32[32,8,128]{2,1,0:T(8,128)}), f32[32,8,128]{2,1,0:T(8,128)S(1)}, u32[]{:S(2)}, u32[]{:S(2)}) async-start(f32[32,8,128]{2,1,0:T(8,128)} %get-tuple-element.92), calls=%async_computation.8 | async-start | bytes 262144 | tf_op jit(solution)/shard_map/all_to_all | solution.py:23
  218.4 10.8 %all-to-all-start.9 = ((f32[32,8,128]{2,1,0:T(8,128)}), f32[32,8,128]{2,1,0:T(8,128)S(1)}, u32[]{:S(2)}, u32[]{:S(2)}) async-start(f32[32,8,128]{2,1,0:T(8,128)} %get-tuple-element.95), calls=%async_computation.9 | async-start | bytes 262144 | tf_op jit(solution)/shard_map/all_to_all | solution.py:23
  229.3 2.6 copy-start.17
  229.3 25.1 %all-to-all-start.10 = ((bf16[32,96,128]{2,1,0:T(8,128)(2,1)}), bf16[32,96,128]{2,1,0:T(8,128)(2,1)S(1)}, u32[]{:S(2)}, u32[]{:S(2)}) async-start(bf16[32,96,128]{2,1,0:T(8,128)(2,1)} %fusion.11), calls=%async_computation.10 | async-start | bytes 1572864 | tf_op jit(solution)/shard_map/all_to_all | solution.py:23
  257.1 24.3 %all-to-all-start.11 = ((f32[32,8,128]{2,1,0:T(8,128)}), f32[32,8,128]{2,1,0:T(8,128)S(1)}, u32[]{:S(2)}, u32[]{:S(2)}) async-start(f32[32,8,128]{2,1,0:T(8,128)} %get-tuple-element.109), calls=%async_computation.11 | async-start | bytes 262144 | tf_op jit(solution)/shard_map/all_to_all | solution.py:23
  281.4 3.1 copy-start.5
  281.4 3.1 copy-start.6
  285.0 4.4 %collective-permute-start.3 = (bf16[16,208,128]{2,1,0:T(8,128)(2,1)S(1)}, bf16[16,208,128]{2,1,0:T(8,128)(2,1)S(1)}, u32[]{:S(2)}, u32[]{:S(2)}) collective-permute-start(bf16[16,208,128]{2,1,0:T(8,128)(2,1)S(1)} %fusion.6), channel_id=1, source_target_pairs={{0,1},{1,0},{2,3},{3,2},{4,5},{5,4},{6,7},{7,6},{8,9},{9,8},{10,11... | collective-permute-start | bytes 2555912 | tf_op jit(solution)/shard_map/ppermute | solution.py:32
  290.6 28.0 %all-to-all-start.12 = ((bf16[16,208,128]{2,1,0:T(8,128)(2,1)}), bf16[16,208,128]{2,1,0:T(8,128)(2,1)S(1)}, u32[]{:S(2)}, u32[]{:S(2)}) async-start(bf16[16,208,128]{2,1,0:T(8,128)(2,1)} %fusion), calls=%async_computation.12 | async-start | bytes 1703936 | tf_op jit(solution)/shard_map/all_to_all | solution.py:1458
  318.6 0.9 copy-start.7
  319.5 16.0 %copy-start.1 = (bf16[2,9,128,32]{2,3,1,0:T(8,128)(2,1)S(1)}, bf16[2,9,128,32]{2,3,1,0:T(8,128)(2,1)}, u32[]{:S(2)}) copy-start(bf16[2,9,128,32]{2,3,1,0:T(8,128)(2,1)} %param.21) | copy-start | bytes 442372
  321.6 10.0 %all-to-all-start.13 = ((bf16[4,304,128]{2,1,0:T(8,128)(2,1)}), bf16[4,304,128]{2,1,0:T(8,128)(2,1)S(1)}, u32[]{:S(2)}, u32[]{:S(2)}) async-start(bf16[4,304,128]{2,1,0:T(8,128)(2,1)} %last_total.1), calls=%async_computation.13 | async-start | bytes 622592 | tf_op jit(solution)/shard_map/all_to_all | solution.py:23
  (10 other events, 7.1 us)

commit v3 on v2

--- a/solution.py
+++ b/solution.py
@@ -10,7 +10,7 @@
 RADIX = 2
 SIDE = 16
 TAPS = 9
-STEP = 2
+STEP = 4
 
 epsilon = 1e-05
 AXES = ("fsdp", "dp")
@@ -30,6 +30,14 @@
 
 def neighbour(values):
     return lax.ppermute(values, "dp", [(i, i ^ 1) for i in range(lax.axis_size("dp"))])
+
+
+ORDER = (0, 4, 2, 6, 1, 5, 3, 7)
+
+
+def partner(values, k):
+    pieces = lax.axis_size("fsdp")
+    return lax.ppermute(values, "fsdp", [(i, i ^ k) for i in range(pieces)])
 
 
 def half_of(shard, axis):
@@ -158,6 +166,27 @@
 
 def lane_sum(row):
     return jnp.broadcast_to(jnp.sum(row, axis=1, keepdims=True), (1, 128))
+
+
+def prepare_kernel(odd, in_ref, mid_ref, down_ref, up_ref, out_ref, *refs):
+    *vector_refs, in_send, most_send, rows_ref = refs
+    rows_ref[...] = jnp.zeros(rows_ref.shape, f32)
+    for k, ref in enumerate(vector_refs):
+        rows_ref[k : k + 1, : ref.shape[1]] = ref[...].astype(f32)
+    at = mid_ref.shape[1] + 128
+    for ref in (down_ref, up_ref):
+        most_send[at : at + ref.shape[0], :] = ref[...]
+        at += ref.shape[0]
+    most_send[at : at + 16, :] = rows_ref[...].astype(bf16)
+    for side in range(2):
+
+        @pl.when(odd[0] == side)
+        def _():
+            for j in range(in_send.shape[0]):
+                in_send[j] = in_ref[:, side * 128 : side * 128 + 128]
+            at = mid_ref.shape[1]
+            most_send[:at, :] = mid_ref[side]
+            most_send[at : at + 128, :] = jnp.transpose(out_ref[side * 128 : side * 128 + 128, :])
 
 
 def first_kernel(
@@ -196,7 +225,7 @@
 
 
 def cross_kernel(
-    sides, x_ref, first_ref, part_ref, cross_ref, ones_ref, power_ref, copies_ref, square_ref
+    sides, x_ref, first_ref, cross_ref, ones_ref, power_ref, square_ref
 ):
     step = pl.program_id(0)
     zeros_at_start(cross_ref, square_ref, ones_ref)
@@ -220,8 +249,6 @@
     @at_end
     def _():
         power_ref[...] = lane_parts(square_ref[...])
-        for j in range(copies_ref.shape[0]):
-            copies_ref[j] = part_ref[...]
 
 
 def write_patches(patch_ref, image, row, low, place):
@@ -239,25 +266,15 @@
             patch_ref[image, here, at : at + 128] = source[:, group * 128 : (group + 1) * 128]
 
 
-def second_kernel(
-    sides,
-    odd,
-    first_ref,
-    recv_ref,
-    param_ref,
-    mine_ref,
-    other_ref,
-    _,
-    act_ref,
-    second_ref,
-    terms_ref,
-    count_ref,
-    w_ref,
-    send_ref,
-    patch_ref,
-    acc_ref,
-    tile_ref,
-):
+def second_kernel(lengths, sides, first_ref, recv_ref, _, *refs):
+    if lengths:
+        member, odd, *refs = refs
+        shard_refs, refs = refs[:4], refs[4:]
+        act_ref, second_ref, terms_ref, count_ref, send_ref, w_ref, down_ref, up_ref, *refs = refs
+        *param_refs, patch_ref, acc_ref, tile_ref, param_ref = refs
+    else:
+        w_ref, param_ref, act_ref, second_ref, terms_ref, count_ref, send_ref, *refs = refs
+        patch_ref, acc_ref, tile_ref = refs
     step = pl.program_id(0)
     zeros_at_start(acc_ref, patch_ref)
     place = places()
@@ -266,7 +283,49 @@
 
     @at_start
     def _():
-        fill_half(w_ref, mine_ref, other_ref, odd)
+        if lengths:
+            own = w_ref.shape[0] // len(ORDER)
+            downs, ups = down_ref.shape[0] // len(ORDER), up_ref.shape[0] // len(ORDER)
+            wholes = [jnp.zeros((16, length * len(ORDER)), f32) for length in lengths]
+            lane = lax.broadcasted_iota(jnp.int32, (16, 128), 1)
+            for index, k in enumerate(ORDER):
+                piece = member[0] ^ k
+                ref = shard_refs[index // 4]
+                index = index % 4
+                at = TAPS * own + 128
+                down_ref[pl.ds(pl.multiple_of(piece * downs, downs), downs), :] = ref[
+                    index, at : at + downs, :
+                ]
+                at += downs
+                up_ref[pl.ds(pl.multiple_of(piece * ups, ups), ups), :] = ref[
+                    index, at : at + ups, :
+                ]
+                at += ups
+                rows = ref[index, at : at + 16, :].astype(f32)
+                for length in sorted(set(lengths)):
+                    part = jnp.where(lane < length, rows, 0.0)
+                    spare = (length * len(ORDER) - 128) // 128
+                    part = jnp.concatenate([part] + [jnp.zeros((16, 128), f32)] * spare, axis=1)
+                    part = pltpu.roll(part, piece * length, 1)
+                    wholes = [
+                        whole + part if whole.shape == part.shape else whole for whole in wholes
+                    ]
+            for side in range(2):
+
+                @pl.when(odd[0] == side)
+                def _():
+                    for index, k in enumerate(ORDER):
+                        here = pl.ds(pl.multiple_of((member[0] ^ k) * own, own), own)
+                        for refs, group in ((shard_refs[:2], side), (shard_refs[2:], 1 - side)):
+                            for tap in range(TAPS):
+                                at = (group * TAPS + tap) * 128
+                                w_ref[here, at : at + 128] = refs[index // 4][
+                                    index % 4, tap * own : (tap + 1) * own, :
+                                ]
+
+            for k, whole in enumerate(wholes):
+                ref = ([param_ref] + param_refs)[k // 2]
+                ref[k % 2 : k % 2 + 1, :] = whole[k : k + 1, :]
         take(recv_ref, tile_ref)
         count = tile_ref[2 * lanes // 128 : 2 * lanes // 128 + 1, :]
         count_ref[...] = jnp.broadcast_to(count, count_ref.shape)
@@ -333,7 +392,6 @@
     count_ref,
     down_ref,
     power_ref,
-    _,
     pooled_ref,
     squeeze_ref,
     terms_ref,
@@ -382,6 +440,22 @@
         tile_ref[1:2, :] = column_total(squeeze * squeeze)
         tile_ref[2:3, :] = column_total(power_ref[...])
         send(send_ref, tile_ref)
+
+
+def out_weights_kernel(start, place, odd, _, *refs):
+    *shard_refs, w_ref, wt_ref = refs
+    for side in range(2):
+
+        @pl.when(odd[0] == side)
+        def _():
+            for index, k in enumerate(ORDER):
+                here = pl.ds(pl.multiple_of((place[0] ^ k) * 128, 128), 128)
+                for refs, half in ((shard_refs[:2], side), (shard_refs[2:], 1 - side)):
+                    wt_ref[here, half * 128 : half * 128 + 128] = refs[index // 4][
+                        index % 4, start : start + 128, :
+                    ]
+
+    w_ref[...] = jnp.transpose(wt_ref[...])
 
 
 def mix_kernel(
@@ -850,7 +924,11 @@
         put(stat_ref, half // 128, column_total(acc_ref[1]))
 
 
-def conv_grad_kernel(act_ref, dsecond_ref, x_ref, dfirst_ref, part_ref, in_ref, conv_ref, patch_ref):
+def conv_grad_kernel(aligned, odd, act_ref, dsecond_ref, x_ref, dfirst_ref, _, in_ref, *refs):
+    if aligned:
+        mine_ref, other_ref, conv_ref, patch_ref = refs
+    else:
+        conv_ref, patch_ref = refs
     zeros_at_start(conv_ref, in_ref, patch_ref)
     place = places()
     lanes = act_ref.shape[1]
@@ -870,33 +948,68 @@
             )
     in_ref[...] += contract_lead(dfirst_ref[...].astype(bf16), x_ref[...])
 
-    @at_end
-    def _():
-        rows = conv_ref.shape[0] // part_ref.shape[0]
-        if rows % 8:
-            for tap in range(RADIX * TAPS):
-                tile = conv_ref[:, tap * 128 : (tap + 1) * 128]
-                part_ref[:, tap * rows : (tap + 1) * rows, :] = tile.reshape(-1, rows, 128)
-            return
-        for piece in range(part_ref.shape[0]):
-            for tap in range(RADIX * TAPS):
-                part_ref[piece, tap * rows : (tap + 1) * rows, :] = conv_ref[
-                    piece * rows : (piece + 1) * rows, tap * 128 : (tap + 1) * 128
-                ]
-
-
-def in_kernel(recv_ref, terms_ref, count_ref, grads_ref, tile_ref):
+    if aligned:
+
+        @at_end
+        def _():
+            for piece in range(mine_ref.shape[0]):
+                for ref, side in ((mine_ref, odd[0]), (other_ref, 1 - odd[0])):
+                    here = pl.ds(pl.multiple_of((2 * piece + side) * 8, 8), 8)
+                    for pair in range(RADIX * TAPS // 2):
+                        two = [
+                            conv_ref[here, (2 * pair + k) * 128 : (2 * pair + k + 1) * 128]
+                            for k in range(2)
+                        ]
+                        ref[piece, pair * 16 : pair * 16 + 16, :] = jnp.concatenate(
+                            two, axis=0
+                        ).astype(bf16)
+
+
+def late_kernel(
+    aligned, odd, recv_ref, terms_ref, count_ref, in_ref, cross_ref, ones_ref, grads_ref, *refs
+):
+    tile_ref = refs[-1]
     take(recv_ref, tile_ref)
     lanes = terms_ref.shape[1]
     total = row_at(tile_ref, 0, lanes)
     product = row_at(tile_ref, lanes // 128, lanes)
     count = wide(count_ref[0:1, :], lanes)
     slant = terms_ref[0:1, :] * terms_ref[2:3, :] * product / count
+    level = terms_ref[0:1, :] * total / count - terms_ref[4:5, :] * slant
     grads_ref[0:1, :] = total
     grads_ref[1:2, :] = product
     grads_ref[2:3, :] = slant
-    grads_ref[3:4, :] = terms_ref[0:1, :] * total / count - terms_ref[4:5, :] * slant
+    grads_ref[3:4, :] = level
     grads_ref[4:5, :] = terms_ref[0:1, :]
+    grads_ref[5:8, :] = jnp.zeros((3, lanes), f32)
+    if not aligned:
+        return
+    mine_ref, other_ref, full_ref, _ = refs
+    columns = jnp.transpose(grads_ref[...])
+    ones = column_total(ones_ref[...])
+    full_ref[...] = (
+        in_ref[...] * columns[:, 4:5]
+        - cross_ref[...] * columns[:, 2:3]
+        - ones * columns[:, 3:4]
+    )
+    rows = mine_ref.shape[1]
+    groups = lanes // rows
+    for piece in range(mine_ref.shape[0]):
+        owner, pair = 2 * piece // groups, piece % (groups // 2)
+        for ref, side in ((mine_ref, odd[0]), (other_ref, 1 - odd[0])):
+            here = pl.ds(pl.multiple_of((2 * pair + side) * rows, rows), rows)
+            ref[piece] = full_ref[here, owner * 128 : (owner + 1) * 128].astype(bf16)
+
+
+def merge_kernel(mid_ref, mid_got_ref, in_ref, in_got_ref, out_ref):
+    cut = in_ref.shape[1]
+    for piece in range(out_ref.shape[0]):
+        out_ref[piece, :cut, :] = (
+            in_ref[piece].astype(f32) + in_got_ref[piece].astype(f32)
+        ).astype(bf16)
+        out_ref[piece, cut:, :] = (
+            mid_ref[piece].astype(f32) + mid_got_ref[piece].astype(f32)
+        ).astype(bf16)
 
 
 def last_kernel(
@@ -948,13 +1061,36 @@
     send(send_ref, tile_ref)
 
 
-def spread_kernel(one_ref, part_ref, _, send_ref):
+def total_last_kernel(one_ref, part_ref, _, sum_ref):
     cut = one_ref.shape[0]
-    one = one_ref[...]
-    total = total_of(part_ref)
-    for j in range(send_ref.shape[0]):
-        send_ref[j, :cut, :] = one
-        send_ref[j, cut:, :] = total
+    sum_ref[:cut, :] = one_ref[...]
+    sum_ref[cut:, :] = total_of(part_ref)
+
+
+def shards_kernel(
+    marks, place, *refs
+):
+    groups = len(refs) - 7
+    out_ref, up_ref, down_ref, bias_ref, in_ref, mid_ref, all_ref = refs[groups:]
+    for k in range(groups):
+        all_ref[place[0] ^ k] = refs[k][...].astype(f32)
+
+    def rows_from(start, count):
+        return jnp.concatenate([all_ref[k, start : start + count, :] for k in range(groups)], axis=0)
+
+    at = 0
+    out_ref[...] = rows_from(at, marks[0])
+    at += marks[0]
+    up_ref[...] = rows_from(at, marks[1])
+    at += marks[1]
+    down_ref[...] = rows_from(at, marks[2])
+    at += marks[2]
+    bias_ref[...] = all_ref[0, at : at + 8, :]
+    at = marks[3]
+    in_ref[...] = jnp.transpose(rows_from(at, marks[4]))
+    at += marks[4]
+    for tap in range(RADIX * TAPS):
+        mid_ref[tap] = rows_from(at + tap * 8, 8)
 
 
 def tiles(lanes, block=0):
@@ -1036,29 +1172,68 @@
     columns = TAPS * conv_mid.shape[2]
     odd = lax.rem(lax.axis_index("dp"), 2).reshape(1)
 
-    in_mine = gather_all(half_of(conv_in, 1)).reshape(width, bottleneck // 2)
-    in_other = neighbour(in_mine)
     down_rows, up_rows = attn_down.shape[0], attn_up.shape[1]
     own_columns = conv_mid.shape[3]
     small = [gain_in, shift_in, gain_mid, shift_mid, gain_attn, shift_attn, gain_out, shift_out, attn_bias]
     lengths = [item.shape[0] for item in small]
-    vectors = jnp.stack([jnp.pad(item, (0, 128 - item.shape[0])) for item in small])
-    vectors = jnp.pad(vectors, ((0, 16 - len(small)), (0, 0)))
-    mid_cut = half_of(conv_mid, 0)[0].transpose(0, 2, 1).reshape(TAPS * own_columns, 128)
-    packed = gather_all(jnp.concatenate([mid_cut, attn_down, attn_up.T, vectors], axis=0))
-    at = TAPS * own_columns
-    mid_mine = packed[:, :at].reshape(pieces, TAPS, own_columns, 128).transpose(0, 2, 1, 3)
-    mid_mine = mid_mine.reshape(bottleneck, columns)
-    mid_other = neighbour(mid_mine)
-    whole_down = packed[:, at : at + down_rows].reshape(bottleneck, att)
-    at += down_rows
-    whole_up = packed[:, at : at + up_rows].reshape(mid, att)
-    at += up_rows
-    found = [
-        packed[:, at + k, :length].reshape(-1).astype(f32) for k, length in enumerate(lengths)
-    ]
-    p_in, p_mid, p_attn, p_out = [rows8(found[2 * k], found[2 * k + 1]) for k in range(4)]
-    p_bias = rows8(found[8])
+    aligned = (
+        own_columns % 16 == 0
+        and width == 128 * pieces
+        and bottleneck == 8 * devices
+        and groups == 4
+        and pieces == len(ORDER)
+    )
+    mid_cut = conv_mid.transpose(0, 1, 3, 2)
+    if aligned:
+        place = lax.axis_index("fsdp").reshape(1)
+        at = TAPS * own_columns
+        cut = (at + 128 + down_rows + up_rows + 16, 128)
+        in_send, most = call(
+            prepare_kernel,
+            1,
+            [
+                scalars(),
+                held(*conv_in.shape),
+                held(RADIX, at, 128),
+                held(*attn_down.shape),
+                held(up_rows, att),
+                held(*conv_out.shape),
+            ]
+            + [held(1, length) for length in lengths],
+            [
+                whole_out((pieces, conv_in.shape[0], 128), bf16),
+                whole_out(cut, bf16),
+            ],
+            [((16, 128), f32)],
+            2,
+            name="last_prepare",
+        )(
+            odd,
+            conv_in,
+            mid_cut.reshape(RADIX, at, 128),
+            attn_down,
+            attn_up.T,
+            conv_out,
+            *[item.reshape(1, -1) for item in small],
+        )
+        in_mine = swap_all(in_send, "fsdp").reshape(width, bottleneck // 2)
+        in_other = neighbour(in_mine)
+
+        most = most[None]
+        most = jnp.concatenate([most, partner(most, 4)], axis=0)
+        most = jnp.concatenate([most, partner(most, 2)], axis=0)
+        shards = [most, partner(most, 1)]
+        shards += [neighbour(item) for item in shards]
+    else:
+        in_send = jnp.broadcast_to(half_of(conv_in, 1)[None], (pieces, conv_in.shape[0], 128))
+        vectors = jnp.stack([jnp.pad(item, (0, 128 - item.shape[0])) for item in small])
+        most = jnp.concatenate([mid_cut.reshape(-1, 128), attn_down, attn_up.T, vectors], axis=0)
+        most = lax.all_gather(most, "fsdp")
+        at = RADIX * TAPS * own_columns
+        in_mine = swap_all(in_send, "fsdp").reshape(width, bottleneck // 2)
+        in_other = neighbour(in_mine)
+        whole_down = most[:, at : at + down_rows].reshape(bottleneck, att)
+        whole_up = most[:, at + down_rows : at + down_rows + up_rows].reshape(mid, att)
 
     x = features.reshape(rows, width)
     cot = cotangent.reshape(rows, width)
@@ -1082,59 +1257,63 @@
         name="first",
     )(half_sides, odd, x, in_mine, in_other)
     got = swap_all(out, AXES)
-    out_half = half_of(conv_out, 0).T
-    cross, x_sum, power_x, out_copies = call(
+    cross, x_sum, power_x = call(
         cross_kernel,
         steps,
-        [scalars(), tiles(width), tiles(bottleneck), held(*out_half.shape)],
+        [scalars(), tiles(width), tiles(bottleneck)],
         [
             whole_out((bottleneck, width)),
             whole_out((8, width)),
             whole_out((8, 128)),
-            whole_out((pieces,) + out_half.shape, bf16),
         ],
         [((8, width), f32)],
         10,
         name="cross",
-    )(half_sides, x, first, out_half)
-    out_mine = swap_all(out_copies, "fsdp").reshape(width, bottleneck // 2)
-    out_other = neighbour(out_mine)
-    whole_out_t = jnp.where(
-        odd[0] == 0,
-        jnp.concatenate([out_mine, out_other], axis=1),
-        jnp.concatenate([out_other, out_mine], axis=1),
-    )
-    whole_w_out = whole_out_t.T
-
-    act_low, second, terms_in, count, whole_mid, out = call(
-        second_kernel,
+    )(half_sides, x, first)
+
+    ins = [scalars(), tiles(bottleneck), received(8), token()]
+    args = (half_sides, first, got, power_x)
+    outs = [
+        tiled(bottleneck, bf16),
+        tiled(mid),
+        whole_out((8, bottleneck)),
+        whole_out((8, 128)),
+        sending(8),
+    ]
+    scratch = [
+        ((STEP, 256 + 2 * SIDE, RADIX * columns), bf16),
+        ((2, 8, mid), f32),
+        ((8, 128), f32),
+    ]
+    if aligned:
+        ins += [scalars(), scalars()] + [held(*item.shape) for item in shards]
+        args += (place, odd) + tuple(shards)
+        outs += [whole_out((bottleneck, RADIX * columns), bf16)]
+        outs += [whole_out((bottleneck, att), bf16), whole_out((mid, att), bf16)]
+        outs += [whole_out((8, lanes)) for lanes in (mid, att, width, mid)]
+        scratch += [((8, bottleneck), f32)]
+    else:
+        whole_mid = most[:, :at].reshape(pieces, RADIX * TAPS, own_columns, 128)
+        whole_mid = whole_mid.transpose(0, 2, 1, 3).reshape(bottleneck, RADIX * columns)
+        at += down_rows + up_rows
+        found = [
+            most[:, at + k, :length].reshape(-1).astype(f32) for k, length in enumerate(lengths)
+        ]
+        p_in, p_mid, p_attn, p_out = [rows8(found[2 * k], found[2 * k + 1]) for k in range(4)]
+        p_bias = rows8(found[8])
+        ins += [held(bottleneck, RADIX * columns), held(8, bottleneck)]
+        args += (whole_mid, p_in)
+    act_low, second, terms_in, count, out, *rest = call(
+        functools.partial(second_kernel, lengths if aligned else None),
         steps,
-        [
-            scalars(),
-            scalars(),
-            tiles(bottleneck),
-            received(8),
-            held(8, bottleneck),
-            held(bottleneck, columns),
-            held(bottleneck, columns),
-            token(),
-        ],
-        [
-            tiled(bottleneck, bf16),
-            tiled(mid),
-            whole_out((8, bottleneck)),
-            whole_out((8, 128)),
-            whole_out((bottleneck, RADIX * columns), bf16),
-            sending(8),
-        ],
-        [
-            ((STEP, 256 + 2 * SIDE, RADIX * columns), bf16),
-            ((2, 8, mid), f32),
-            ((8, 128), f32),
-        ],
+        ins,
+        outs,
+        scratch,
         15,
         name="second",
-    )(half_sides, odd, first, got, p_in, mid_mine, mid_other, power_x)
+    )(*args)
+    if aligned:
+        whole_mid, whole_down, whole_up, p_mid, p_attn, p_out, p_bias = rest
     got = swap_all(out, AXES)
 
     pooled, squeeze, terms_mid, out = call(
@@ -1148,7 +1327,6 @@
             held(8, 128),
             held(bottleneck, att),
             held(8, 128),
-            token(),
         ],
         [
             whole_out((images, bottleneck), bf16),
@@ -1159,9 +1337,22 @@
         [((images, bottleneck), f32), ((8, 128), f32)],
         7,
         name="pool",
-    )(half_sides, second, got, p_mid, count, whole_down, power_x, out_other)
+    )(half_sides, second, got, p_mid, count, whole_down, power_x)
     got = swap_all(out, AXES)
 
+    if aligned:
+        whole_w_out, whole_out_t = call(
+            functools.partial(out_weights_kernel, TAPS * own_columns),
+            1,
+            [scalars(), scalars(), token()] + [held(*item.shape) for item in shards],
+            [whole_out((bottleneck, width), bf16), whole_out((width, bottleneck), bf16)],
+            (),
+            1,
+            name="last_weights",
+        )(place, odd, pooled, *shards)
+    else:
+        whole_w_out = lax.all_gather(conv_out, "fsdp", axis=1, tiled=True)
+        whole_out_t = whole_w_out.T
     wide_rows = 2 * width // 128
     mixed, weights, excite, gate, gram_out, colsum, power_mix, out = call(
         functools.partial(mix_kernel, images_all),
@@ -1397,30 +1588,46 @@
     )(gates, stat)
     got = swap_all(out, AXES)
 
-    conv_parts, in_grad = call(
-        conv_grad_kernel,
+    outs = [whole_out((bottleneck, width))]
+    scratch = [((STEP, 256 + 2 * SIDE, RADIX * columns), bf16)]
+    mid_rows = bottleneck // devices * RADIX * TAPS
+    if aligned:
+        outs += [whole_out((devices // 2, mid_rows, 128), bf16)] * 2
+        scratch = [((bottleneck, RADIX * columns), f32)] + scratch
+    else:
+        outs += [whole_out((bottleneck, RADIX * columns))]
+    in_grad, *conv_parts = call(
+        functools.partial(conv_grad_kernel, aligned),
         steps,
-        [tiles(bottleneck), tiles(mid), tiles(width), tiles(bottleneck)],
-        [
-            whole_out((devices, bottleneck // devices * RADIX * TAPS, 128)),
-            whole_out((bottleneck, width)),
-        ],
-        [
-            ((bottleneck, RADIX * columns), f32),
-            ((STEP, 256 + 2 * SIDE, RADIX * columns), bf16),
-        ],
+        [scalars(), tiles(bottleneck), tiles(mid), tiles(width), tiles(bottleneck), token()],
+        outs,
+        scratch,
         15,
         name="conv_grad",
-    )(act_low, dsecond, x, dfirst)
-    (grads_in,) = call(
-        in_kernel,
+    )(odd, act_low, dsecond, x, dfirst, gates)
+    outs = [whole_out((8, bottleneck))]
+    scratch = [((8, 128), f32)]
+    in_rows = bottleneck // groups * (width // pieces) // 128
+    if aligned:
+        outs += [whole_out((devices // 2, in_rows, 128), bf16)] * 2
+        scratch = [((bottleneck, width), f32)] + scratch
+    grads_in, *in_parts = call(
+        functools.partial(late_kernel, aligned),
         1,
-        [received(8), held(8, bottleneck), held(8, 128)],
-        [whole_out((8, bottleneck))],
-        [((8, 128), f32)],
-        1,
+        [
+            scalars(),
+            received(8),
+            held(8, bottleneck),
+            held(8, 128),
+            held(bottleneck, width),
+            held(bottleneck, width),
+            held(8, width),
+        ],
+        outs,
+        scratch,
+        2,
         name="last_terms",
-    )(got, terms_in, count)
+    )(odd, got, terms_in, count, in_grad, cross, x_sum)
     grad_features, done = call(
         last_kernel,
         steps,
@@ -1439,45 +1646,84 @@
         name="last",
     )(half_sides, dfirst, first, grads_in, whole_in, slope, terms_out)
 
-    grad_conv_in = (
-        in_grad * grads_in[4][:, None]
-        - cross * grads_in[2][:, None]
-        - column_total(x_sum) * grads_in[3][:, None]
-    )
-    in_cut = grad_conv_in.astype(bf16).reshape(bottleneck, pieces, -1).transpose(1, 0, 2)
-    in_cut = in_cut.reshape(devices, -1, 128)
-    mid_rows = bottleneck // devices
-    marks += [in_cut.shape[1], conv_parts.shape[1]]
-    late = jnp.concatenate([in_cut, conv_parts.astype(bf16)], axis=1)
-    late = jnp.pad(late, ((0, 0), (0, -late.shape[1] % 16), (0, 0)))
-    late = late.reshape(devices // 2, 2, -1, 128)
-    mine = lax.dynamic_index_in_dim(late, odd[0], 1, False)
-    other = lax.dynamic_index_in_dim(late, 1 - odd[0], 1, False)
-    late = (mine.astype(f32) + neighbour(other).astype(f32)).astype(bf16)
+    if aligned:
+        mid_got, in_got = neighbour(conv_parts[1]), neighbour(in_parts[1])
+        (late,) = call(
+            merge_kernel,
+            1,
+            [held(*mid_got.shape)] * 2 + [held(*in_got.shape)] * 2,
+            [whole_out((devices // 2, in_rows + mid_rows, 128), bf16)],
+            (),
+            2,
+            name="last_merge",
+        )(conv_parts[0], mid_got, in_parts[0], in_got)
+    else:
+        grad_conv_in = (
+            in_grad * grads_in[4][:, None]
+            - cross * grads_in[2][:, None]
+            - column_total(x_sum) * grads_in[3][:, None]
+        )
+        in_cut = grad_conv_in.astype(bf16).reshape(bottleneck, pieces, -1).transpose(1, 0, 2)
+        mid_cut = conv_parts[0].astype(bf16).reshape(devices, -1, RADIX * TAPS, 128)
+        mid_cut = mid_cut.transpose(0, 2, 1, 3).reshape(devices, -1, 128)
+        late = jnp.concatenate([in_cut.reshape(devices, -1, 128), mid_cut], axis=1)
+        late = jnp.pad(late, ((0, 0), (0, -late.shape[1] % 16), (0, 0)))
+        late = late.reshape(devices // 2, 2, -1, 128)
+        mine = lax.dynamic_index_in_dim(late, odd[0], 1, False)
+        other = lax.dynamic_index_in_dim(late, 1 - odd[0], 1, False)
+        late = (mine.astype(f32) + neighbour(other).astype(f32)).astype(bf16)
     sides_of = [[2 * i + side for i in range(devices // 2)] for side in range(2)]
     late = lax.all_to_all(late, AXES, 0, 0, axis_index_groups=sides_of)
     (summed,) = call(
-        spread_kernel,
+        total_last_kernel,
         1,
         [held(*gates.shape), held(*late.shape), token()],
-        [whole_out((groups, gates.shape[0] + late.shape[1], 128), bf16)],
+        [whole_out((gates.shape[0] + late.shape[1], 128), bf16)],
         (),
         2,
         name="last_total",
     )(gates, late, done)
-    summed = swap_all(summed, "dp").astype(f32)
-    shard_out = summed[:, : marks[0]].reshape(bottleneck, -1)
-    at = marks[0]
-    shard_up = summed[:, at : at + marks[1]].reshape(up_rows, att).T
-    at += marks[1]
-    shard_down = summed[:, at : at + marks[2]].reshape(down_rows, att)
-    at += marks[2]
-    shard_bias = summed[0, at, :up_rows]
-    at = gates.shape[0]
-    shard_in = summed[:, at : at + marks[3]].reshape(bottleneck, -1).T
-    at += marks[3]
-    shard_mid = summed[:, at : at + marks[4]].reshape(groups, RADIX, TAPS, mid_rows, 128)
-    shard_mid = shard_mid.transpose(1, 2, 4, 0, 3).reshape(RADIX, TAPS, 128, own_columns)
+    marks += [gates.shape[0], in_rows]
+    own_width = width // pieces
+    if aligned:
+        members = [summed] + [
+            lax.ppermute(summed, "dp", [(i, i ^ k) for i in range(groups)])
+            for k in range(1, groups)
+        ]
+        shard_out, shard_up, shard_down, shard_bias, shard_in, shard_mid = call(
+            functools.partial(shards_kernel, marks),
+            1,
+            [scalars()] + [held(*summed.shape)] * groups,
+            [
+                whole_out((bottleneck, own_width)),
+                whole_out((up_rows, att)),
+                whole_out((down_rows, att)),
+                whole_out((8, 128)),
+                whole_out((own_width, bottleneck)),
+                whole_out((RADIX * TAPS, own_columns, 128)),
+            ],
+            [((groups,) + summed.shape, f32)],
+            2,
+            name="last_shards",
+        )(lax.axis_index("dp").reshape(1), *members)
+        shard_bias = shard_bias[0, :up_rows]
+        shard_up = shard_up.T
+        shard_mid = shard_mid.reshape(RADIX, TAPS, own_columns, 128).transpose(0, 1, 3, 2)
+    else:
+        summed = swap_all(jnp.broadcast_to(summed[None], (groups,) + summed.shape), "dp")
+        summed = summed.astype(f32)
+        shard_out = summed[:, : marks[0]].reshape(bottleneck, -1)
+        at = marks[0]
+        shard_up = summed[:, at : at + marks[1]].reshape(up_rows, att).T
+        at += marks[1]
+        shard_down = summed[:, at : at + marks[2]].reshape(down_rows, att)
+        at += marks[2]
+        shard_bias = summed[0, at, :up_rows]
+        at = marks[3]
+        shard_in = summed[:, at : at + in_rows].reshape(bottleneck, -1).T
+        at += in_rows
+        shard_mid = summed[:, at : at + mid_rows].reshape(groups, RADIX, TAPS, -1, 128)
+        shard_mid = shard_mid.transpose(1, 2, 4, 0, 3).reshape(RADIX, TAPS, 128, own_columns)
 
     def own_part(row):
         length = row.shape[0] // pieces

time: 338 us -> 313 us (0.926)
  blocking collectives: 0 us -> 28 us
  waiting for transfers between devices: 70.8 us -> 50.8 us
  local copies, waits for them, and re-layouts: 32.1 us -> 17.2 us
  starting transfers between devices: 55.7 us -> 44.3 us
  other arithmetic: 11.4 us -> 4.95 us
    all_to_all x13 -> x8, waiting for transfers between devices: 67.7 us -> 23.2 us  [swap_all(): return lax.all_to_all(values, axes, 0, 0)]
    all_to_all x0 -> x2, blocking collectives: none -> 28 us  [swap_all(): return lax.all_to_all(values, axes, 0, 0)]
    ppermute x0 -> x6, waiting for transfers between devices: none -> 21.7 us  [the longest x3 18.8 us: partner(): return lax.ppermute(values, 'fsdp', [(i, i ^ k) for i in range(pieces)])]
    all_to_all x13 -> x8, starting transfers between devices: 48.2 us -> 29.8 us  [swap_all(): return lax.all_to_all(values, axes, 0, 0)]
    pallas_call x5 -> x9, Pallas kernels: 48.2 us -> 56.4 us  [the longest x1 16.9 us: local(): call(functools.partial(second_kernel, lengths if aligned else None), step...]
    ppermute x0 -> x6, starting transfers between devices: none -> 6.91 us  [the longest x3 4.77 us: partner(): return lax.ppermute(values, 'fsdp', [(i, i ^ k) for i in range(pieces)])]
    another operation x6 -> x1, local copies, waits for them, and re-layouts: 3.42 us -> 0.01 us  [the longest x5 3.41 us: local(): jnp.stack([jnp.pad(item, (0, 128 - item.shape[0])) for item in small])]
    unnamed x50 -> x42, local copies, waits for them, and re-layouts: 8.28 us -> 7.69 us
  transfers between devices with their start and end apart: 18 -> 20, of which waited for: 11 -> 9; matrix products, arithmetic and copies ran while one was open for 8% -> 4% of each run, Pallas kernels for 28% -> 25%
where the time goes in v3:
time: 313 us; the launch traced here: 311 us
  Pallas kernels  165 us (53%)
  waiting for transfers between devices  50.8 us (16%)
  starting transfers between devices  44.3 us (14%)
  blocking collectives  28 us (9%)
  local copies, waits for them, and re-layouts  17.2 us (5%)
  other arithmetic  4.95 us (2%)
    all_to_all x8, starting transfers between devices, swap_all(): return lax.all_to_all(values, axes, 0, 0)  29.8 us
    all_to_all x2, blocking collectives, swap_all(): return lax.all_to_all(values, axes, 0, 0)  28 us
    pallas_call x1, Pallas kernels, local(): call(out_kernel, steps, [scalars(), tiles(bottleneck), tiles(width), tile...  27.3 us
    all_to_all x8, waiting for transfers between devices, swap_all(): return lax.all_to_all(values, axes, 0, 0)  23.2 us
    pallas_call x1, Pallas kernels, local(): call(conv_back_kernel, steps, [scalars(), tiles(mid), held(8, mid), recei...  22.9 us
    ppermute x3, waiting for transfers between devices, partner(): return lax.ppermute(values, 'fsdp', [(i, i ^ k) for i in range(pieces)])  18.8 us
    pallas_call x1, Pallas kernels, local(): call(functools.partial(second_kernel, lengths if aligned else None), step...  16.9 us
    pallas_call x1, Pallas kernels, local(): call(functools.partial(conv_grad_kernel, aligned), steps, [scalars(), til...  16.2 us
  transfers between devices with their start and end apart: 20, of which 9 were waited for; matrix products, arithmetic and copies ran while one was open for 4% of the time, Pallas kernels for 25%

profile of v3, /device:TPU:0, one launch (start us, length us, event | category | flops | bytes accessed | tf_op | source)
XLA Modules:
  0.0 310.8 jit_solution(6754610798767181155)
XLA Ops:
  2.6 7.3 %all-to-all-start = ((bf16[8,128,128]{2,1,0:T(8,128)(2,1)}), bf16[8,128,128]{2,1,0:T(8,128)(2,1)S(1)}, u32[]{:S(2)}, u32[]{:S(2)}) async-start(bf16[8,128,128]{2,1,0:T(8,128)(2,1)} %get-tuple-element.89), calls=%async_computation | async-start | bytes 524288 | tf_op jit(solution)/shard_map/all_to_all | solution.py:23
  9.8 2.9 collective-permute-start.1
  12.7 11.8 %collective-permute-done.1 = bf16[1,528,128]{2,1,0:T(8,128)(2,1)S(1)} collective-permute-done((bf16[1,528,128]{2,1,0:T(8,128)(2,1)}, bf16[1,528,128]{2,1,0:T(8,128)(2,1)S(1)}, u32[]{:S(2)}, u32[]{:S(2)}) %collective-permute-start.1) | collective-permute-done | bytes 135200 | tf_op jit(solution)/shard_map/ppermute | solution.py:40
  25.6 7.0 %collective-permute-done.2 = bf16[2,528,128]{2,1,0:T(8,128)(2,1)S(1)} collective-permute-done((bf16[2,528,128]{2,1,0:T(8,128)(2,1)S(1)}, bf16[2,528,128]{2,1,0:T(8,128)(2,1)S(1)}, u32[]{:S(2)}, u32[]{:S(2)}) %collective-permute-start.2) | collective-permute-done | bytes 270368 | tf_op jit(solution)/shard_map/ppermute | solution.py:40
  36.1 8.4 %first.1 = (f32[4096,256]{1,0:T(8,128)}, bf16[1024,256]{1,0:T(8,128)(2,1)}, f32[32,8,128]{2,1,0:T(8,128)}) custom-call(s32[16]{0:T(128)} %sides.19, s32[1]{0:T(128)} %bitcast.odd.refs_1_, bf16[4096,1024]{1,0:T(8,128)(2,1)} %bitcast.75, bf16[1024,128]{1,0:T(8,128)(2,1)} %bitcast.69, bf16[1024,128]{1,0:T(8,128)(2,1)} %copy-done.16), custom_call_target="tpu_custom_call" | custom-call | flops 8000000000 | bytes 24000000 | tf_op jit(solution)/shard_map/first/pallas_call | solution.py:1250
  44.5 3.6 %all-to-all-start.1 = ((f32[32,8,128]{2,1,0:T(8,128)}), f32[32,8,128]{2,1,0:T(8,128)S(1)}, u32[]{:S(2)}, u32[]{:S(2)}) async-start(f32[32,8,128]{2,1,0:T(8,128)} %get-tuple-element.91), calls=%async_computation.1 | async-start | bytes 262144 | tf_op jit(solution)/shard_map/all_to_all | solution.py:23
  48.4 9.6 %cross.1 = (f32[256,1024]{1,0:T(8,128)}, f32[8,1024]{1,0:T(8,128)}, f32[8,128]{1,0:T(8,128)}) custom-call(s32[16]{0:T(128)} %sides.19, bf16[4096,1024]{1,0:T(8,128)(2,1)} %bitcast.76, f32[4096,256]{1,0:T(8,128)} %get-tuple-element.90.first_ref), custom_call_target="tpu_custom_call" | custom-call | flops 10000000000 | bytes 30000000 | tf_op jit(solution)/shard_map/cross/pallas_call | solution.py:1260
  59.1 16.9 %second.1 = (bf16[4096,256]{1,0:T(8,128)(2,1)}, f32[4096,512]{1,0:T(8,128)}, f32[8,256]{1,0:T(8,128)}, f32[8,128]{1,0:T(8,128)}, f32[32,8,128]{2,1,0:T(8,128)}, ...) custom-call(s32[16]{0:T(128)} %sides.19, ...), custom_call_target="tpu_custom_call" | custom-call | flops 15000000512 | bytes 45000000 | tf_op jit(solution)/shard_map/second/pallas_call | solution.py:1306
  76.0 14.1 %all_to_all.55.recv_ref = f32[32,8,128]{2,1,0:T(8,128)} all-to-all(f32[32,8,128]{2,1,0:T(8,128)} %get-tuple-element.95), channel_id=1, replica_groups=mesh['fsdp'=8,'dp'=4] {'fsdp','dp'}, dimensions={0} | all-to-all | bytes 262144 | tf_op jit(solution)/shard_map/all_to_all | solution.py:23
  90.1 6.6 %pool.1 = (bf16[16,256]{1,0:T(8,128)(2,1)}, f32[16,128]{1,0:T(8,128)}, f32[8,512]{1,0:T(8,128)}, f32[32,8,128]{2,1,0:T(8,128)}) custom-call(s32[16]{0:T(128)} %sides.19, f32[4096,512]{1,0:T(8,128)} %get-tuple-element.94.second_ref, f32[32,8,128]{2,1,0:T(8,128)} %all_to_all.55.recv_ref, f32[8,512]{1,0:T(8,128)} %get-tuple-element.96.param_ref, ...), custom_call_target="tpu_custom_call" | custom-call | flops 7000000000 | bytes 21000000 | tf_op jit(solution)/shard_map/pool/pallas_call | solution.py:1319
  96.7 2.6 all-to-all-start.3
  99.3 2.6 last_weights.1
  101.9 5.6 %all-to-all-done.3.recv_ref = f32[32,8,128]{2,1,0:T(8,128)S(1)} async-done(((f32[32,8,128]{2,1,0:T(8,128)}), f32[32,8,128]{2,1,0:T(8,128)S(1)}, u32[]{:S(2)}, u32[]{:S(2)}) %all-to-all-start.3) | async-done | bytes 131104 | tf_op jit(solution)/shard_map/all_to_all | solution.py:23
  108.2 10.7 %mix.1 = (bf16[4096,256]{1,0:T(8,128)(2,1)}, f32[16,512]{1,0:T(8,128)}, bf16[16,128]{1,0:T(8,128)(2,1)}, f32[8,128]{1,0:T(8,128)}, f32[256,1024]{1,0:T(8,128)}, ...) custom-call(s32[16]{0:T(128)} %sides.19, f32[4096,512]{1,0:T(8,128)} %get-tuple-element.94.second_ref, ...), custom_call_target="tpu_custom_call" | custom-call | flops 11000000512 | bytes 33000000 | tf_op jit(solution)/shard_map/mix/pallas_call | solution.py:1357
  118.8 13.9 %all_to_all.56.recv_ref = f32[32,16,128]{2,1,0:T(8,128)} all-to-all(f32[32,16,128]{2,1,0:T(8,128)} %get-tuple-element.108), channel_id=1, replica_groups=mesh['fsdp'=8,'dp'=4] {'fsdp','dp'}, dimensions={0} | all-to-all | bytes 524288 | tf_op jit(solution)/shard_map/all_to_all | solution.py:23
  132.7 27.3 %output.1 = (bf16[4096,1024]{1,0:T(8,128)(2,1)}, bf16[4096,1024]{1,0:T(8,128)(2,1)}, f32[4096,256]{1,0:T(8,128)}, f32[256,1024]{1,0:T(8,128)}, f32[8,1024]{1,0:T...) custom-call(s32[16]{0:T(128)} %sides.19, bf16[4096,256]{1,0:T(8,128)(2,1)} %get-tuple-element.107.mixed_ref, ...), custom_call_target="tpu_custom_call" | custom-call | flops 24999999488 | bytes 75000000 | tf_op jit(solution)/shard_map/output/pallas_call | solution.py:1387
  160.1 2.6 all-to-all-start.5
  163.4 7.5 %all-to-all-done.5.recv_ref = bf16[32,16,128]{2,1,0:T(8,128)(2,1)S(1)} async-done(((bf16[32,16,128]{2,1,0:T(8,128)(2,1)}), bf16[32,16,128]{2,1,0:T(8,128)(2,1)S(1)}, u32[]{:S(2)}, u32[]{:S(2)}) %all-to-all-start.5) | async-done | bytes 131104 | tf_op jit(solution)/shard_map/all_to_all | solution.py:23
  171.6 13.9 %gate.1 = (f32[4096,256]{1,0:T(8,128)}, f32[5,16,512]{2,1,0:T(8,128)}, f32[512,128]{1,0:T(8,128)}, f32[8,512]{1,0:T(8,128)}, f32[16,128]{1,0:T(8,128)}, /*index=5*/f32[8,1024]{1,0:T(8,128)}, f32[32,8,128]{2,1,0:T(8,128)}) custom-call(s32[16]{0:T(128)} %sides.19, f32[4096,512]{1,0:T(8,128)} %get-tuple-element.94.second_ref, ...), custom_call_target="tpu_custom_call" | custom-call | flops 12999999488 | bytes 39000000 | tf_op jit(solution)/shard_map/gate/pallas_call | solution.py:1421
  186.4 2.6 all-to-all-start.6
  191.6 5.6 %all-to-all-done.6.recv_ref = f32[32,8,128]{2,1,0:T(8,128)S(1)} async-done(((f32[32,8,128]{2,1,0:T(8,128)}), f32[32,8,128]{2,1,0:T(8,128)S(1)}, u32[]{:S(2)}, u32[]{:S(2)}) %all-to-all-start.6) | async-done | bytes 131104 | tf_op jit(solution)/shard_map/all_to_all | solution.py:23
  199.8 2.6 all-to-all-start.7
  206.2 4.4 %all-to-all-done.7.recv_ref = f32[32,8,128]{2,1,0:T(8,128)S(1)} async-done(((f32[32,8,128]{2,1,0:T(8,128)}), f32[32,8,128]{2,1,0:T(8,128)S(1)}, u32[]{:S(2)}, u32[]{:S(2)}) %all-to-all-start.7) | async-done | bytes 131104 | tf_op jit(solution)/shard_map/all_to_all | solution.py:23
  210.6 2.6 all-to-all-start.8
  213.3 22.9 %conv_back.1 = (bf16[4096,512]{1,0:T(8,128)(2,1)}, f32[4096,256]{1,0:T(8,128)}, f32[8,512]{1,0:T(8,128)}, f32[8,128]{1,0:T(8,128)}) custom-call(s32[16]{0:T(128)} %sides.19, f32[4096,512]{1,0:T(8,128)} %get-tuple-element.94.second_ref, f32[8,512]{1,0:T(8,128)} %get-tuple-element.99.ab_ref, f32[32,8,128]{2,1,0:T(8,128)} %copy-done.8, ...), custom_call_target="tpu_custom_call" | custom-call | flops 20000000000 | bytes 60000000 | tf_op jit(solution)/shard_map/conv_back/pallas_call | solution.py:1541
  239.0 6.1 %all-to-all-start.9 = ((f32[32,8,128]{2,1,0:T(8,128)}), f32[32,8,128]{2,1,0:T(8,128)S(1)}, u32[]{:S(2)}, u32[]{:S(2)}) async-start(f32[32,8,128]{2,1,0:T(8,128)} %get-tuple-element.137), calls=%async_computation.9 | async-start | bytes 262144 | tf_op jit(solution)/shard_map/all_to_all | solution.py:23
  245.0 16.2 %conv_grad.1 = (f32[256,1024]{1,0:T(8,128)}, bf16[16,144,128]{2,1,0:T(8,128)(2,1)}, bf16[16,144,128]{2,1,0:T(8,128)(2,1)}) custom-call(s32[1]{0:T(128)} %bitcast.odd.refs_1_, bf16[4096,256]{1,0:T(8,128)(2,1)} %get-tuple-element.138.act_ref, bf16[4096,512]{1,0:T(8,128)(2,1)} %get-tuple-element.139.dsecond_ref, bf16[4096,1024]{1,0:T(8,128)(2,1)} %bitcast.78, ...), custom_call_target="tpu_custom_call" | custom-call | flops 15000000512 | bytes 45000000 | tf_op jit(solution)/shard_map/conv_grad/pallas_call | solution.py:1599
  262.5 2.9 last_terms.1
  268.2 2.5 last_merge.1
  270.7 6.6 %all-to-all-start.10 = ((bf16[16,208,128]{2,1,0:T(8,128)(2,1)}), bf16[16,208,128]{2,1,0:T(8,128)(2,1)S(1)}, u32[]{:S(2)}, u32[]{:S(2)}) async-start(bf16[16,208,128]{2,1,0:T(8,128)(2,1)} %last_merge.1), calls=%async_computation.10 | async-start | bytes 1703936 | tf_op jit(solution)/shard_map/all_to_all | solution.py:1676
  278.1 14.5 %last.1 = (f32[4096,1024]{1,0:T(8,128)}, f32[8,128]{1,0:T(8,128)}) custom-call(s32[16]{0:T(128)} %sides.19, f32[4096,256]{1,0:T(8,128)} %get-tuple-element.128.dfirst_ref, f32[4096,256]{1,0:T(8,128)} %get-tuple-element.90.first_ref, f32[8,256]{1,0:T(8,128)} %get-tuple-element.144.grads_ref, bf16[1024,256]{1,0:T(8,128)(2,1)} %get-tuple-element.145.w_ref, ...), custom_call_target="tpu_custom_call" | custom-call | flops 15000000512 | bytes 45000000 | tf_op jit(solution)/shard_map/last/pallas_call | solution.py:1631
  292.6 5.9 %all-to-all-done.10.part_ref = bf16[16,208,128]{2,1,0:T(8,128)(2,1)S(1)} async-done(((bf16[16,208,128]{2,1,0:T(8,128)(2,1)}), bf16[16,208,128]{2,1,0:T(8,128)(2,1)S(1)}, u32[]{:S(2)}, u32[]{:S(2)}) %all-to-all-start.10) | async-done | bytes 852000 | tf_op jit(solution)/shard_map/all_to_all | solution.py:1676
  (92 shorter events, 39.5 us)
Async XLA Ops:
  2.6 23.0 %all-to-all-start = ((bf16[8,128,128]{2,1,0:T(8,128)(2,1)}), bf16[8,128,128]{2,1,0:T(8,128)(2,1)S(1)}, u32[]{:S(2)}, u32[]{:S(2)}) async-start(bf16[8,128,128]{2,1,0:T(8,128)(2,1)} %get-tuple-element.89), calls=%async_computation | async-start | bytes 524288 | tf_op jit(solution)/shard_map/all_to_all | solution.py:23
  9.8 14.7 %collective-permute-start.1 = (bf16[1,528,128]{2,1,0:T(8,128)(2,1)}, bf16[1,528,128]{2,1,0:T(8,128)(2,1)S(1)}, u32[]{:S(2)}, u32[]{:S(2)}) collective-permute-start(bf16[1,528,128]{2,1,0:T(8,128)(2,1)} %bitcast.64), channel_id=1, source_target_pairs={{0,16},{4,20},{8,24},{12,28},{16,0},{20,4},{24,8},{28,12},{1,17},{... | collective-permute-start | bytes 405512 | tf_op jit(solution)/shard_map/ppermute | solution.py:40
  25.5 7.2 %collective-permute-start.2 = (bf16[2,528,128]{2,1,0:T(8,128)(2,1)S(1)}, bf16[2,528,128]{2,1,0:T(8,128)(2,1)S(1)}, u32[]{:S(2)}, u32[]{:S(2)}) collective-permute-start(bf16[2,528,128]{2,1,0:T(8,128)(2,1)S(1)} %pad_maximum_fusion.1), channel_id=1, source_target_pairs={{0,8},{4,12},{8,0},{12,4},{16,24},{20,28},{24,16},{28,20},{1,9},{5... | collective-permute-start | bytes 811016 | tf_op jit(solution)/shard_map/ppermute | solution.py:40
  25.5 9.8 %copy-start.5 = (bf16[8,128,128]{2,1,0:T(8,128)(2,1)}, bf16[8,128,128]{2,1,0:T(8,128)(2,1)S(1)}, u32[]{:S(2)}) copy-start(bf16[8,128,128]{2,1,0:T(8,128)(2,1)S(1)} %all-to-all-done) | copy-start | bytes 786436
  25.6 9.8 %collective-permute-start = (bf16[1024,128]{1,0:T(8,128)(2,1)S(1)}, bf16[1024,128]{1,0:T(8,128)(2,1)S(1)}, u32[]{:S(2)}, u32[]{:S(2)}) collective-permute-start(bf16[1024,128]{1,0:T(8,128)(2,1)S(1)} %bitcast.68), channel_id=1, source_target_pairs={{0,1},{1,0},{2,3},{3,2},{4,5},{5,4},{6,7},{7,6},{8,9},{9,8},{10,11... | collective-permute-start | bytes 786440 | tf_op jit(solution)/shard_map/ppermute | solution.py:32
  33.6 10.9 %copy-start.4 = (bf16[4,528,128]{2,1,0:T(8,128)(2,1)}, bf16[4,528,128]{2,1,0:T(8,128)(2,1)S(1)}, u32[]{:S(2)}) copy-start(bf16[4,528,128]{2,1,0:T(8,128)(2,1)S(1)} %pad_maximum_fusion.refs_2_.refs_0_) | copy-start | bytes 1622020
  33.6 14.5 %collective-permute-start.3 = (bf16[4,528,128]{2,1,0:T(8,128)(2,1)S(1)}, bf16[4,528,128]{2,1,0:T(8,128)(2,1)S(1)}, u32[]{:S(2)}, u32[]{:S(2)}) collective-permute-start(bf16[4,528,128]{2,1,0:T(8,128)(2,1)S(1)} %pad_maximum_fusion.refs_2_.refs_0_), channel_id=1, source_target_pairs={{0,4},{4,0},{8,12},{12,8},{16,20},{20,16},{24,28},{28,24},{1,5},{5... | collective-permute-start | bytes 1622024 | tf_op jit(solution)/shard_map/ppermute | solution.py:40
  35.4 22.7 %collective-permute-start.4 = (bf16[4,528,128]{2,1,0:T(8,128)(2,1)S(1)}, bf16[4,528,128]{2,1,0:T(8,128)(2,1)S(1)}, u32[]{:S(2)}, u32[]{:S(2)}) collective-permute-start(bf16[4,528,128]{2,1,0:T(8,128)(2,1)S(1)} %pad_maximum_fusion.refs_2_.refs_0_), channel_id=1, source_target_pairs={{0,1},{1,0},{2,3},{3,2},{4,5},{5,4},{6,7},{7,6},{8,9},{9,8},{10,11... | collective-permute-start | bytes 1622024 | tf_op jit(solution)/shard_map/ppermute | solution.py:32
  44.5 13.6 %all-to-all-start.1 = ((f32[32,8,128]{2,1,0:T(8,128)}), f32[32,8,128]{2,1,0:T(8,128)S(1)}, u32[]{:S(2)}, u32[]{:S(2)}) async-start(f32[32,8,128]{2,1,0:T(8,128)} %get-tuple-element.91), calls=%async_computation.1 | async-start | bytes 262144 | tf_op jit(solution)/shard_map/all_to_all | solution.py:23
  48.1 10.0 %copy-start.13 = (bf16[4,528,128]{2,1,0:T(8,128)(2,1)}, bf16[4,528,128]{2,1,0:T(8,128)(2,1)S(1)}, u32[]{:S(2)}) copy-start(bf16[4,528,128]{2,1,0:T(8,128)(2,1)S(1)} %collective-permute-done.3.refs_3_.refs_1_) | copy-start | bytes 1622020
  48.1 10.0 %collective-permute-start.5 = (bf16[4,528,128]{2,1,0:T(8,128)(2,1)S(1)}, bf16[4,528,128]{2,1,0:T(8,128)(2,1)S(1)}, u32[]{:S(2)}, u32[]{:S(2)}) collective-permute-start(bf16[4,528,128]{2,1,0:T(8,128)(2,1)S(1)} %collective-permute-done.3.refs_3_.refs_1_), channel_id=1, source_target_pairs={{0,1},{1,0},{2,3},{3,2},{4,5},{5,4},{6,7},{7,6},{8,9},{9,8},{10,11... | collective-permute-start | bytes 1622024 | tf_op jit(solution)/shard_map/ppermute | solution.py:32
  58.1 1.0 copy-start.15
  96.7 10.8 %all-to-all-start.3 = ((f32[32,8,128]{2,1,0:T(8,128)}), f32[32,8,128]{2,1,0:T(8,128)S(1)}, u32[]{:S(2)}, u32[]{:S(2)}) async-start(f32[32,8,128]{2,1,0:T(8,128)} %get-tuple-element.101), calls=%async_computation.3 | async-start | bytes 262144 | tf_op jit(solution)/shard_map/all_to_all | solution.py:23
  160.1 10.8 %all-to-all-start.5 = ((bf16[32,16,128]{2,1,0:T(8,128)(2,1)}), bf16[32,16,128]{2,1,0:T(8,128)(2,1)S(1)}, u32[]{:S(2)}, u32[]{:S(2)}) async-start(bf16[32,16,128]{2,1,0:T(8,128)(2,1)} %get-tuple-element.113), calls=%async_computation.5 | async-start | bytes 262144 | tf_op jit(solution)/shard_map/all_to_all | solution.py:23
  171.6 19.8 %copy-start = (f32[256,1024]{1,0:T(8,128)S(1)}, f32[256,1024]{1,0:T(8,128)}, u32[]{:S(2)}) copy-start(f32[256,1024]{1,0:T(8,128)} %get-tuple-element.132) | copy-start | bytes 3145732
  171.6 19.8 %copy-start.1 = (f32[256,1024]{1,0:T(8,128)S(1)}, f32[256,1024]{1,0:T(8,128)}, u32[]{:S(2)}) copy-start(f32[256,1024]{1,0:T(8,128)} %get-tuple-element.129) | copy-start | bytes 3145732
  186.4 10.8 %all-to-all-start.6 = ((f32[32,8,128]{2,1,0:T(8,128)}), f32[32,8,128]{2,1,0:T(8,128)S(1)}, u32[]{:S(2)}, u32[]{:S(2)}) async-start(f32[32,8,128]{2,1,0:T(8,128)} %get-tuple-element.121), calls=%async_computation.6 | async-start | bytes 262144 | tf_op jit(solution)/shard_map/all_to_all | solution.py:23
  199.8 10.8 %all-to-all-start.7 = ((f32[32,8,128]{2,1,0:T(8,128)}), f32[32,8,128]{2,1,0:T(8,128)S(1)}, u32[]{:S(2)}, u32[]{:S(2)}) async-start(f32[32,8,128]{2,1,0:T(8,128)} %get-tuple-element.123), calls=%async_computation.7 | async-start | bytes 262144 | tf_op jit(solution)/shard_map/all_to_all | solution.py:23
  210.6 2.6 copy-start.8
  210.6 25.6 %all-to-all-start.8 = ((bf16[32,96,128]{2,1,0:T(8,128)(2,1)}), bf16[32,96,128]{2,1,0:T(8,128)(2,1)S(1)}, u32[]{:S(2)}, u32[]{:S(2)}) async-start(bf16[32,96,128]{2,1,0:T(8,128)(2,1)} %fusion.6), calls=%async_computation.8 | async-start | bytes 1572864 | tf_op jit(solution)/shard_map/all_to_all | solution.py:23
  236.2 0.9 copy-start.3
  239.0 22.9 %all-to-all-start.9 = ((f32[32,8,128]{2,1,0:T(8,128)}), f32[32,8,128]{2,1,0:T(8,128)S(1)}, u32[]{:S(2)}, u32[]{:S(2)}) async-start(f32[32,8,128]{2,1,0:T(8,128)} %get-tuple-element.137), calls=%async_computation.9 | async-start | bytes 262144 | tf_op jit(solution)/shard_map/all_to_all | solution.py:23
  261.2 6.0 %collective-permute-start.6 = (bf16[16,144,128]{2,1,0:T(8,128)(2,1)}, bf16[16,144,128]{2,1,0:T(8,128)(2,1)S(1)}, u32[]{:S(2)}, u32[]{:S(2)}) collective-permute-start(bf16[16,144,128]{2,1,0:T(8,128)(2,1)} %get-tuple-element.150), channel_id=1, source_target_pairs={{0,1},{1,0},{2,3},{3,2},{4,5},{5,4},{6,7},{7,6},{8,9},{9,8},{10,11... | collective-permute-start | bytes 1769480 | tf_op jit(solution)/shard_map/ppermute | solution.py:32
  265.4 1.9 collective-permute-start.7
  267.3 0.9 copy-start.12
  270.7 27.9 %all-to-all-start.10 = ((bf16[16,208,128]{2,1,0:T(8,128)(2,1)}), bf16[16,208,128]{2,1,0:T(8,128)(2,1)S(1)}, u32[]{:S(2)}, u32[]{:S(2)}) async-start(bf16[16,208,128]{2,1,0:T(8,128)(2,1)} %last_merge.1), calls=%async_computation.10 | async-start | bytes 1703936 | tf_op jit(solution)/shard_map/all_to_all | solution.py:1676
  298.5 1.0 copy-start.2
  301.4 4.0 %collective-permute-start.10 = (bf16[304,128]{1,0:T(8,128)(2,1)}, bf16[304,128]{1,0:T(8,128)(2,1)S(1)}, u32[]{:S(2)}, u32[]{:S(2)}) collective-permute-start(bf16[304,128]{1,0:T(8,128)(2,1)} %last_total.1.refs_0_), channel_id=1, source_target_pairs={{0,3},{1,2},{2,1},{3,0},{4,7},{5,6},{6,5},{7,4},{8,11},{9,10},{10,... | collective-permute-start | bytes 233480 | tf_op jit(solution)/shard_map/ppermute | solution.py:1690
  301.4 4.0 %collective-permute-start.8 = (bf16[304,128]{1,0:T(8,128)(2,1)}, bf16[304,128]{1,0:T(8,128)(2,1)S(1)}, u32[]{:S(2)}, u32[]{:S(2)}) collective-permute-start(bf16[304,128]{1,0:T(8,128)(2,1)} %last_total.1.refs_0_), channel_id=1, source_target_pairs={{0,1},{1,0},{2,3},{3,2},{4,5},{5,4},{6,7},{7,6},{8,9},{9,8},{10,11... | collective-permute-start | bytes 233480 | tf_op jit(solution)/shard_map/ppermute | solution.py:1690
  302.1 5.0 %collective-permute-start.9 = (bf16[304,128]{1,0:T(8,128)(2,1)}, bf16[304,128]{1,0:T(8,128)(2,1)S(1)}, u32[]{:S(2)}, u32[]{:S(2)}) collective-permute-start(bf16[304,128]{1,0:T(8,128)(2,1)} %last_total.1.refs_0_), channel_id=1, source_target_pairs={{0,2},{1,3},{2,0},{3,1},{4,6},{5,7},{6,4},{7,5},{8,10},{9,11},{10,... | collective-permute-start | bytes 233480 | tf_op jit(solution)/shard_map/ppermute | solution.py:1690
  305.5 1.7 copy-start.18
  305.5 1.7 copy-start.19
  (9 other events, 6.3 us)

commit v4 on v3

--- a/solution.py
+++ b/solution.py
@@ -67,6 +67,21 @@
 
 def chunk(image, row):
     return pl.ds(pl.multiple_of(image * 256 + row * SIDE, SIDE), SIDE)
+
+
+def of_image(image):
+    return slice(image * 256, image * 256 + 256)
+
+
+def of_row(image, row):
+    return slice(image * 256 + row * SIDE, image * 256 + row * SIDE + SIDE)
+
+
+def stages(*parts):
+    for stage in range(STEP + len(parts) - 1):
+        for late, part in reversed(list(enumerate(parts))):
+            if 0 <= stage - late < STEP:
+                part(stage - late)
 
 
 def rows_of(carry, body, unroll=8):
@@ -195,22 +210,26 @@
     step = pl.program_id(0)
     zeros_at_start(acc_ref)
     at_start(lambda: fill_half(w_ref, mine_ref, other_ref, odd))
-    first_ref[...] = jnp.dot(x_ref[...], w_ref[...], preferred_element_type=f32)
     place = places()
     lanes = first_ref.shape[1]
-    for image in range(STEP):
+    sums = [acc_ref[0], acc_ref[1]]
+
+    def multiply(image):
+        first_ref[of_image(image), :] = jnp.dot(
+            x_ref[of_image(image), :], w_ref[...], preferred_element_type=f32
+        )
+
+    def finish(image):
         limit = 2 * sides[step * STEP + image]
-
-        def body(row, carry):
-            total, square = carry
-            here = chunk(image, row)
+        for row in range(SIDE):
+            here = of_row(image, row)
             values = first_ref[here, :] * wide(row_mask(place, row, limit), lanes)
             first_ref[here, :] = values
-            return (total + fold(values), square + fold(values * values))
-
-        total, square = rows_of((acc_ref[0], acc_ref[1]), body)
-        acc_ref[0] = total
-        acc_ref[1] = square
+            sums[0] = sums[0] + fold(values)
+            sums[1] = sums[1] + fold(values * values)
+
+    stages(multiply, finish)
+    acc_ref[0], acc_ref[1] = sums
 
     @at_end
     def _():
@@ -260,7 +279,11 @@
     for tap in range(TAPS):
         up, side = tap // 3, tap % 3
         source = (left, low, right)[side]
-        here = pl.ds(pl.multiple_of((row + 2 - up) * SIDE, SIDE), SIDE)
+        here = (row + 2 - up) * SIDE
+        if isinstance(row, int):
+            here = slice(here, here + SIDE)
+        else:
+            here = pl.ds(pl.multiple_of(here, SIDE), SIDE)
         for group in range(lanes // 128):
             at = (group * TAPS + tap) * 128
             patch_ref[image, here, at : at + 128] = source[:, group * 128 : (group + 1) * 128]
@@ -342,20 +365,17 @@
         terms_ref[3:4, :] = -center * inv
         terms_ref[4:5, :] = center
 
-    for image in range(STEP):
+    def start_image(image):
         limit = 2 * sides[step * STEP + image]
-
-        def body(row, carry):
-            here = chunk(image, row)
+        for row in range(SIDE):
+            here = slice(image * 256 + row * SIDE, image * 256 + row * SIDE + SIDE)
             pre = first_ref[here, :] * terms_ref[0:1, :] + terms_ref[1:2, :]
             act = pre * (sigmoid(pre) * wide(row_mask(place, row, limit), lanes))
             low = act.astype(bf16)
             act_ref[here, :] = low
             write_patches(patch_ref, image, row, low, place)
-            return carry
-
-        rows_of(0, body)
-    for image in range(STEP):
+
+    def multiply_image(image):
         for group in range(RADIX):
             second_ref[image * 256 : image * 256 + 256, group * lanes : (group + 1) * lanes] = (
                 contract_last(
@@ -363,18 +383,25 @@
                     w_ref[:, group * columns : (group + 1) * columns],
                 )
             )
-    for image in range(STEP):
+
+    def sum_image(image, carry):
         limit = 2 * sides[step * STEP + image]
-
-        def body(row, carry):
-            total, square = carry
-            values = second_ref[chunk(image, row), :]
+        total, square = carry
+        for row in range(SIDE):
+            values = second_ref[image * 256 + row * SIDE : image * 256 + row * SIDE + SIDE, :]
             values = values * wide(row_mask(place, row, limit), values.shape[1])
-            return (total + fold(values), square + fold(values * values))
-
-        total, square = rows_of((acc_ref[0], acc_ref[1]), body)
-        acc_ref[0] = total
-        acc_ref[1] = square
+            total, square = total + fold(values), square + fold(values * values)
+        return total, square
+
+    carry = (acc_ref[0], acc_ref[1])
+    for stage in range(STEP + 2):
+        if 0 <= stage - 1 < STEP:
+            multiply_image(stage - 1)
+        if stage < STEP:
+            start_image(stage)
+        if stage >= 2:
+            carry = sum_image(stage - 2, carry)
+    acc_ref[0], acc_ref[1] = carry
 
     @at_end
     def _():
@@ -514,25 +541,28 @@
         weights_ref[:, :half] = one / (one + two)
         weights_ref[:, half:] = two / (one + two)
 
-    for image in range(STEP):
+    sums = [acc_ref[0], acc_ref[1]]
+
+    def mix(image):
         limit = 2 * sides[step * STEP + image]
         weights = weights_ref[pl.ds(step * STEP + image, 1), :]
-
-        def body(row, carry):
-            total, square = carry
-            here = chunk(image, row)
+        for row in range(SIDE):
+            here = of_row(image, row)
             pre = second_ref[here, :] * ab_ref[0:1, :] + ab_ref[1:2, :]
             act = pre * (sigmoid(pre) * wide(row_mask(place, row, limit), lanes))
             act = act * weights
             mixed = act[:, :half] + act[:, half:]
             low = mixed.astype(bf16)
             mixed_ref[here, :] = low
-            return (total + fold(low.astype(f32)), square + fold(mixed * mixed))
-
-        total, square = rows_of((acc_ref[0], acc_ref[1]), body)
-        acc_ref[0] = total
-        acc_ref[1] = square
-    gram_ref[...] += contract_lead(mixed_ref[...], mixed_ref[...])
+            sums[0] = sums[0] + fold(low.astype(f32))
+            sums[1] = sums[1] + fold(mixed * mixed)
+
+    def square(image):
+        values = mixed_ref[of_image(image), :]
+        gram_ref[...] += contract_lead(values, values)
+
+    stages(mix, square)
+    acc_ref[0], acc_ref[1] = sums
 
     @at_end
     def _():
@@ -571,6 +601,7 @@
     acc_ref,
     square_ref,
     tile_ref,
+    half_ref,
 ):
     step = pl.program_id(0)
     zeros_at_start(acc_ref, square_ref, grad_ref)
@@ -597,35 +628,45 @@
         terms_ref[3:4, :] = inv
         terms_ref[4:5, :] = 1.0 / scale
         terms_ref[5:6, :] = wide(lane_sum(branch), lanes)
-
-    third_ref[...] = jnp.dot(mixed_ref[...], w_ref[...], preferred_element_type=f32)
-    for image in range(STEP):
+        half_ref[0:1, :] = 0.5 * scale
+        half_ref[1:2, :] = 0.5 * offset
+
+    squares = [square_ref[...]]
+
+    def expand(image):
+        third_ref[of_image(image), :] = jnp.dot(
+            mixed_ref[of_image(image), :], w_ref[...], preferred_element_type=f32
+        )
+
+    def finish(image):
         limit = 2 * sides[step * STEP + image]
-
-        def body(row, square):
-            here = chunk(image, row)
+        for row in range(SIDE):
+            here = of_row(image, row)
             mask = wide(row_mask(place, row, limit), part)
             for at in range(0, lanes, part):
                 cut = slice(at, at + part)
-                total = (
-                    x_ref[here, cut].astype(f32)
-                    + third_ref[here, cut] * terms_ref[0:1, cut]
-                    + terms_ref[1:2, cut]
+                half = (
+                    (x_ref[here, cut] * bf16(0.5)).astype(f32)
+                    + third_ref[here, cut] * half_ref[0:1, cut]
+                    + half_ref[1:2, cut]
                 )
-                plain = sigmoid(total)
-                gate = plain * mask
-                output = total * gate
+                turned = jnp.tanh(half)
+                gate = (1.0 + turned) * mask
+                output = half * gate
                 block_ref[here, cut] = output.astype(bf16)
-                slope = gate + output * (1.0 - plain)
-                grad = cot_ref[here, cut].astype(f32) * (slope * terms_ref[0:1, cut])
+                slope = gate + output * (1.0 - turned)
+                grad = cot_ref[here, cut].astype(f32) * (slope * half_ref[0:1, cut])
                 slope_ref[here, cut] = grad.astype(bf16)
                 acc_ref[:, cut] += fold(grad)
-                square = square + lane_parts(fold(output * output))
-            return square
-
-        square_ref[...] = rows_of(square_ref[...], body, 4)
-    back_ref[...] = jnp.dot(slope_ref[...], wt_ref[...], preferred_element_type=f32)
-    grad_ref[...] += contract_lead(mixed_ref[...], slope_ref[...])
+                squares[0] = squares[0] + lane_parts(fold(output * output))
+
+    def contract(image):
+        here = of_image(image)
+        back_ref[here, :] = jnp.dot(slope_ref[here, :], wt_ref[...], preferred_element_type=f32)
+        grad_ref[...] += contract_lead(mixed_ref[here, :], slope_ref[here, :])
+
+    stages(expand, finish, contract)
+    square_ref[...] = squares[0]
 
     @at_end
     def _():
@@ -705,14 +746,17 @@
             preferred_element_type=f32,
         )
 
-    dmixed_ref[...] = back_ref[...] - jnp.dot(
-        mixed_ref[...], turn_ref[...], preferred_element_type=f32
-    )
-    for image in range(STEP):
+    def turn(image):
+        here = of_image(image)
+        dmixed_ref[here, :] = back_ref[here, :] - jnp.dot(
+            mixed_ref[here, :], turn_ref[...], preferred_element_type=f32
+        )
+
+    def add_up(image):
         limit = 2 * sides[step * STEP + image]
-
-        def body(row, carry):
-            here = chunk(image, row)
+        totals = [jnp.zeros((8, lanes), f32) for _ in range(5)]
+        for row in range(SIDE):
+            here = of_row(image, row)
             mask = row_mask(place, row, limit)
             dmixed = (dmixed_ref[here, :] - row_ref[0:1, :]) * wide(mask, half)
             dmixed_ref[here, :] = dmixed
@@ -720,12 +764,11 @@
             pre, act, slope = mid_terms(second_ref, ab_ref, here, wide(mask, lanes))
             along = slope * both
             terms = (act * both, along, along * pre, slope, slope * pre)
-            return tuple(old + fold(new) for old, new in zip(carry, terms))
-
-        start = tuple(jnp.zeros((8, lanes), f32) for _ in range(5))
-        totals = rows_of(start, body, 4)
+            totals = [old + fold(new) for old, new in zip(totals, terms)]
         for index in range(5):
             sums_ref[index, pl.ds(step * STEP + image, 1), :] = column_total(totals[index])
+
+    stages(turn, add_up)
 
     @at_end
     def _():
@@ -855,14 +898,13 @@
         grads_ref[2:3, :] = slant
         grads_ref[3:4, :] = ab_ref[0:1, :] * total / count - param_ref[1:2, :] * slant
 
-    for image in range(STEP):
+    def start(image):
         limit = 2 * sides[step * STEP + image]
         weights = weights_ref[pl.ds(step * STEP + image, 1), :] * ab_ref[0:1, :]
         dpool = dpool_ref[pl.ds(step * STEP + image, 1), :]
         dpool = jnp.concatenate([dpool, dpool], axis=1) * ab_ref[0:1, :]
-
-        def body(row, carry):
-            here = chunk(image, row)
+        for row in range(SIDE):
+            here = of_row(image, row)
             mask = wide(row_mask(place, row, limit), lanes)
             dmixed = dmixed_ref[here, :]
             both = jnp.concatenate([dmixed, dmixed], axis=1)
@@ -872,38 +914,38 @@
             grad = slope * (weights * both + dpool)
             grad = mask * (grad - (pre * grads_ref[2:3, :] + grads_ref[3:4, :]))
             dsecond_ref[here, :] = grad.astype(bf16)
-            return carry
-
-        rows_of(0, body)
-    for image in range(STEP):
+
+    def multiply(image):
         for group in range(RADIX):
             column_ref[image, SIDE : SIDE + 256, group * columns : (group + 1) * columns] = jnp.dot(
-                dsecond_ref[image * 256 : image * 256 + 256, group * half : (group + 1) * half],
+                dsecond_ref[of_image(image), group * half : (group + 1) * half],
                 w_ref[:, group * columns : (group + 1) * columns],
                 preferred_element_type=f32,
             )
-    for image in range(STEP):
+
+    sums = [acc_ref[0], acc_ref[1]]
+    inner = wide(place, quarter)
+
+    def finish(image):
         limit = 2 * sides[step * STEP + image]
-
-        def body(row, carry):
-            total, product = carry
-            here = chunk(image, row)
+        for row in range(SIDE):
+            here = of_row(image, row)
             mask = row_mask(place, row, limit)
             parts = []
             for group in range(RADIX):
-                sides_sum = []
+                summed = []
                 for side in range(3):
-                    summed = None
+                    pieces = []
                     for up in range(3):
                         at = group * columns + (up * 3 + side) * quarter
-                        rows = pl.ds(pl.multiple_of((row + 2 - up) * SIDE, SIDE), SIDE)
-                        piece = column_ref[image, rows, at : at + quarter]
-                        summed = piece if summed is None else summed + piece
-                    sides_sum.append(summed)
-                inner = wide(place, quarter)
-                low = jnp.where(inner == SIDE - 1, 0.0, pltpu.roll(sides_sum[0], SIDE - 1, 0))
-                high = jnp.where(inner == 0, 0.0, pltpu.roll(sides_sum[2], 1, 0))
-                parts.append(sides_sum[1] + low + high)
+                        start_row = (row + 2 - up) * SIDE
+                        pieces.append(
+                            column_ref[image, start_row : start_row + SIDE, at : at + quarter]
+                        )
+                    summed.append(pieces[0] + pieces[1] + pieces[2])
+                low = jnp.where(inner == SIDE - 1, 0.0, pltpu.roll(summed[0], SIDE - 1, 0))
+                high = jnp.where(inner == 0, 0.0, pltpu.roll(summed[2], 1, 0))
+                parts.append(summed[1] + low + high)
             dact = jnp.concatenate(parts, axis=1)
             first = first_ref[here, :]
             pre = first * ab_in_ref[0:1, :] + ab_in_ref[1:2, :]
@@ -911,11 +953,11 @@
             plain = sigmoid(pre)
             grad = dact * (plain * (1.0 + pre * (1.0 - plain)) * wide(mask, half))
             dfirst_ref[here, :] = grad
-            return (total + fold(grad), product + fold(grad * normed))
-
-        total, product = rows_of((acc_ref[0], acc_ref[1]), body, 4)
-        acc_ref[0] = total
-        acc_ref[1] = product
+            sums[0] = sums[0] + fold(grad)
+            sums[1] = sums[1] + fold(grad * normed)
+
+    stages(start, multiply, finish)
+    acc_ref[0], acc_ref[1] = sums
 
     @at_end
     def _():
@@ -933,19 +975,19 @@
     place = places()
     lanes = act_ref.shape[1]
     columns = TAPS * lanes // RADIX
-    for image in range(STEP):
-
-        def body(row, carry):
-            write_patches(patch_ref, image, row, act_ref[chunk(image, row), :], place)
-            return carry
-
-        rows_of(0, body)
-    for image in range(STEP):
+    def start(image):
+        for row in range(SIDE):
+            write_patches(patch_ref, image, row, act_ref[of_row(image, row), :], place)
+
+    def multiply(image):
+        here = of_image(image)
         for group in range(RADIX):
             conv_ref[:, group * columns : (group + 1) * columns] += contract_lead(
-                dsecond_ref[image * 256 : image * 256 + 256, group * lanes : (group + 1) * lanes],
+                dsecond_ref[here, group * lanes : (group + 1) * lanes],
                 patch_ref[image, SIDE : SIDE + 256, group * columns : (group + 1) * columns],
             )
+
+    stages(start, multiply)
     in_ref[...] += contract_lead(dfirst_ref[...].astype(bf16), x_ref[...])
 
     if aligned:
@@ -1020,29 +1062,27 @@
     lanes = first_ref.shape[1]
     width = out_ref.shape[1]
     part = 512 if width % 512 == 0 else width
-    for image in range(STEP):
+    def start(image):
         limit = 2 * sides[step * STEP + image]
-
-        def body(row, carry):
-            here = chunk(image, row)
+        for row in range(SIDE):
+            here = of_row(image, row)
             mask = wide(row_mask(place, row, limit), lanes)
             grad = dfirst_ref[here, :] * grads_ref[4:5, :]
             grad = grad - mask * (first_ref[here, :] * grads_ref[2:3, :] + grads_ref[3:4, :])
             low_ref[here, :] = grad.astype(bf16)
-            return carry
-
-        rows_of(0, body)
-    out_ref[...] = contract_last(low_ref[...], w_ref[...])
-    for image in range(STEP):
-
-        def body(row, carry):
-            here = chunk(image, row)
+
+    def multiply(image):
+        here = of_image(image)
+        out_ref[here, :] = contract_last(low_ref[here, :], w_ref[...])
+
+    def finish(image):
+        for row in range(SIDE):
+            here = of_row(image, row)
             for at in range(0, width, part):
                 cut = slice(at, at + part)
                 out_ref[here, cut] += slope_ref[here, cut].astype(f32) * terms_ref[4:5, cut]
-            return carry
-
-        rows_of(0, body)
+
+    stages(start, multiply, finish)
 
     @at_end
     def _():
@@ -1412,6 +1452,7 @@
             ((8, width), f32),
             ((8, 128), f32),
             ((wide_rows, 128), f32),
+            ((8, width), f32),
         ],
         25,
         name="output",

time: 313 us -> 293 us (0.936)
  Pallas kernels: 165 us -> 141 us
  waiting for transfers between devices: 50.8 us -> 57.2 us
    pallas_call x1, Pallas kernels: 22.9 us -> 15.8 us  [local(): call(conv_back_kernel, steps, [scalars(), tiles(mid), held(8, mid), recei...]
    pallas_call x1, Pallas kernels: 27.3 us -> 22.5 us  [local(): call(out_kernel, steps, [scalars(), tiles(bottleneck), tiles(width), tile...]
    all_to_all x8, waiting for transfers between devices: 23.2 us -> 28 us  [swap_all(): return lax.all_to_all(values, axes, 0, 0)]
    pallas_call x1, Pallas kernels: 16.9 us -> 12.6 us  [local(): call(functools.partial(second_kernel, lengths if aligned else None), step...]
  transfers between devices with their start and end apart: 20 -> 20, of which waited for: 9 -> 10; matrix products, arithmetic and copies ran while one was open for 4% -> 4% of each run, Pallas kernels for 25% -> 22%
where the time goes in v4:
time: 293 us; the launch traced here: 292 us
  Pallas kernels  141 us (48%)
  waiting for transfers between devices  57.2 us (20%)
  starting transfers between devices  42 us (14%)
  blocking collectives  28 us (10%)
  local copies, waits for them, and re-layouts  17.2 us (6%)
  other arithmetic  4.95 us (2%)
    all_to_all x2, blocking collectives, swap_all(): return lax.all_to_all(values, axes, 0, 0)  28 us
    all_to_all x8, waiting for transfers between devices, swap_all(): return lax.all_to_all(values, axes, 0, 0)  28 us
    all_to_all x8, starting transfers between devices, swap_all(): return lax.all_to_all(values, axes, 0, 0)  27.5 us
    pallas_call x1, Pallas kernels, local(): call(out_kernel, steps, [scalars(), tiles(bottleneck), tiles(width), tile...  22.5 us
    ppermute x3, waiting for transfers between devices, partner(): return lax.ppermute(values, 'fsdp', [(i, i ^ k) for i in range(pieces)])  18.8 us
    pallas_call x1, Pallas kernels, local(): call(conv_back_kernel, steps, [scalars(), tiles(mid), held(8, mid), recei...  15.8 us
    pallas_call x1, Pallas kernels, local(): call(functools.partial(conv_grad_kernel, aligned), steps, [scalars(), til...  13.3 us
    pallas_call x1, Pallas kernels, local(): call(last_kernel, steps, [scalars(), tiles(bottleneck), tiles(bottleneck)...  13 us
  transfers between devices with their start and end apart: 20, of which 10 were waited for; matrix products, arithmetic and copies ran while one was open for 4% of the time, Pallas kernels for 22%

profile of v4, /device:TPU:0, one launch (start us, length us, event | category | flops | bytes accessed | tf_op | source)
XLA Modules:
  0.0 291.7 jit_solution(17578777476341161481)
XLA Ops:
  2.6 7.3 %all-to-all-start = ((bf16[8,128,128]{2,1,0:T(8,128)(2,1)}), bf16[8,128,128]{2,1,0:T(8,128)(2,1)S(1)}, u32[]{:S(2)}, u32[]{:S(2)}) async-start(bf16[8,128,128]{2,1,0:T(8,128)(2,1)} %get-tuple-element.89), calls=%async_computation | async-start | bytes 524288 | tf_op jit(solution)/shard_map/all_to_all | solution.py:23
  9.8 2.9 %collective-permute-start.1 = (bf16[1,528,128]{2,1,0:T(8,128)(2,1)}, bf16[1,528,128]{2,1,0:T(8,128)(2,1)S(1)}, u32[]{:S(2)}, u32[]{:S(2)}) collective-permute-start(bf16[1,528,128]{2,1,0:T(8,128)(2,1)} %bitcast.64), channel_id=1, source_target_pairs={{0,16},{4,20},{8,24},{12,28},{16,0},{20,4},{24,8},{28,12},{1,17},{... | collective-permute-start | bytes 405512 | tf_op jit(solution)/shard_map/ppermute | solution.py:40
  12.7 11.8 %collective-permute-done.1 = bf16[1,528,128]{2,1,0:T(8,128)(2,1)S(1)} collective-permute-done((bf16[1,528,128]{2,1,0:T(8,128)(2,1)}, bf16[1,528,128]{2,1,0:T(8,128)(2,1)S(1)}, u32[]{:S(2)}, u32[]{:S(2)}) %collective-permute-start.1) | collective-permute-done | bytes 135200 | tf_op jit(solution)/shard_map/ppermute | solution.py:40
  25.6 7.0 %collective-permute-done.2 = bf16[2,528,128]{2,1,0:T(8,128)(2,1)S(1)} collective-permute-done((bf16[2,528,128]{2,1,0:T(8,128)(2,1)S(1)}, bf16[2,528,128]{2,1,0:T(8,128)(2,1)S(1)}, u32[]{:S(2)}, u32[]{:S(2)}) %collective-permute-start.2) | collective-permute-done | bytes 270368 | tf_op jit(solution)/shard_map/ppermute | solution.py:40
  36.1 7.7 %first.1 = (f32[4096,256]{1,0:T(8,128)}, bf16[1024,256]{1,0:T(8,128)(2,1)}, f32[32,8,128]{2,1,0:T(8,128)}) custom-call(s32[16]{0:T(128)} %sides.19, s32[1]{0:T(128)} %bitcast.odd.refs_1_, bf16[4096,1024]{1,0:T(8,128)(2,1)} %bitcast.75, bf16[1024,128]{1,0:T(8,128)(2,1)} %bitcast.69, bf16[1024,128]{1,0:T(8,128)(2,1)} %copy-done.16), custom_call_target="tpu_custom_call" | custom-call | flops 8000000000 | bytes 24000000 | tf_op jit(solution)/shard_map/first/pallas_call | solution.py:1290
  43.7 3.6 %all-to-all-start.1 = ((f32[32,8,128]{2,1,0:T(8,128)}), f32[32,8,128]{2,1,0:T(8,128)S(1)}, u32[]{:S(2)}, u32[]{:S(2)}) async-start(f32[32,8,128]{2,1,0:T(8,128)} %get-tuple-element.91), calls=%async_computation.1 | async-start | bytes 262144 | tf_op jit(solution)/shard_map/all_to_all | solution.py:23
  47.6 9.6 %cross.1 = (f32[256,1024]{1,0:T(8,128)}, f32[8,1024]{1,0:T(8,128)}, f32[8,128]{1,0:T(8,128)}) custom-call(s32[16]{0:T(128)} %sides.19, bf16[4096,1024]{1,0:T(8,128)(2,1)} %bitcast.76, f32[4096,256]{1,0:T(8,128)} %get-tuple-element.90.first_ref), custom_call_target="tpu_custom_call" | custom-call | flops 10000000000 | bytes 30000000 | tf_op jit(solution)/shard_map/cross/pallas_call | solution.py:1300
  58.3 12.6 %second.1 = (bf16[4096,256]{1,0:T(8,128)(2,1)}, f32[4096,512]{1,0:T(8,128)}, f32[8,256]{1,0:T(8,128)}, f32[8,128]{1,0:T(8,128)}, f32[32,8,128]{2,1,0:T(8,128)}, ...) custom-call(s32[16]{0:T(128)} %sides.19, ...), custom_call_target="tpu_custom_call" | custom-call | flops 15000000512 | bytes 45000000 | tf_op jit(solution)/shard_map/second/pallas_call | solution.py:1346
  71.0 14.1 %all_to_all.55.recv_ref = f32[32,8,128]{2,1,0:T(8,128)} all-to-all(f32[32,8,128]{2,1,0:T(8,128)} %get-tuple-element.95), channel_id=1, replica_groups=mesh['fsdp'=8,'dp'=4] {'fsdp','dp'}, dimensions={0} | all-to-all | bytes 262144 | tf_op jit(solution)/shard_map/all_to_all | solution.py:23
  85.1 6.6 %pool.1 = (bf16[16,256]{1,0:T(8,128)(2,1)}, f32[16,128]{1,0:T(8,128)}, f32[8,512]{1,0:T(8,128)}, f32[32,8,128]{2,1,0:T(8,128)}) custom-call(s32[16]{0:T(128)} %sides.19, f32[4096,512]{1,0:T(8,128)} %get-tuple-element.94.second_ref, f32[32,8,128]{2,1,0:T(8,128)} %all_to_all.55.recv_ref, f32[8,512]{1,0:T(8,128)} %get-tuple-element.96.param_ref, ...), custom_call_target="tpu_custom_call" | custom-call | flops 7000000000 | bytes 21000000 | tf_op jit(solution)/shard_map/pool/pallas_call | solution.py:1359
  91.7 2.6 all-to-all-start.3
  94.3 2.6 last_weights.1
  96.9 5.6 %all-to-all-done.3.recv_ref = f32[32,8,128]{2,1,0:T(8,128)S(1)} async-done(((f32[32,8,128]{2,1,0:T(8,128)}), f32[32,8,128]{2,1,0:T(8,128)S(1)}, u32[]{:S(2)}, u32[]{:S(2)}) %all-to-all-start.3) | async-done | bytes 131104 | tf_op jit(solution)/shard_map/all_to_all | solution.py:23
  103.2 10.0 %mix.1 = (bf16[4096,256]{1,0:T(8,128)(2,1)}, f32[16,512]{1,0:T(8,128)}, bf16[16,128]{1,0:T(8,128)(2,1)}, f32[8,128]{1,0:T(8,128)}, f32[256,1024]{1,0:T(8,128)}, ...) custom-call(s32[16]{0:T(128)} %sides.19, f32[4096,512]{1,0:T(8,128)} %get-tuple-element.94.second_ref, ...), custom_call_target="tpu_custom_call" | custom-call | flops 11000000512 | bytes 33000000 | tf_op jit(solution)/shard_map/mix/pallas_call | solution.py:1397
  113.2 13.9 %all_to_all.56.recv_ref = f32[32,16,128]{2,1,0:T(8,128)} all-to-all(f32[32,16,128]{2,1,0:T(8,128)} %get-tuple-element.108), channel_id=1, replica_groups=mesh['fsdp'=8,'dp'=4] {'fsdp','dp'}, dimensions={0} | all-to-all | bytes 524288 | tf_op jit(solution)/shard_map/all_to_all | solution.py:23
  127.1 22.5 %output.1 = (bf16[4096,1024]{1,0:T(8,128)(2,1)}, bf16[4096,1024]{1,0:T(8,128)(2,1)}, f32[4096,256]{1,0:T(8,128)}, f32[256,1024]{1,0:T(8,128)}, f32[8,1024]{1,0:T...) custom-call(s32[16]{0:T(128)} %sides.19, bf16[4096,256]{1,0:T(8,128)(2,1)} %get-tuple-element.107.mixed_ref, ...), custom_call_target="tpu_custom_call" | custom-call | flops 24999999488 | bytes 75000000 | tf_op jit(solution)/shard_map/output/pallas_call | solution.py:1427
  149.6 2.6 all-to-all-start.5
  152.9 7.5 %all-to-all-done.5.recv_ref = bf16[32,16,128]{2,1,0:T(8,128)(2,1)S(1)} async-done(((bf16[32,16,128]{2,1,0:T(8,128)(2,1)}), bf16[32,16,128]{2,1,0:T(8,128)(2,1)S(1)}, u32[]{:S(2)}, u32[]{:S(2)}) %all-to-all-start.5) | async-done | bytes 131104 | tf_op jit(solution)/shard_map/all_to_all | solution.py:23
  161.1 12.9 %gate.1 = (f32[4096,256]{1,0:T(8,128)}, f32[5,16,512]{2,1,0:T(8,128)}, f32[512,128]{1,0:T(8,128)}, f32[8,512]{1,0:T(8,128)}, f32[16,128]{1,0:T(8,128)}, /*index=5*/f32[8,1024]{1,0:T(8,128)}, f32[32,8,128]{2,1,0:T(8,128)}) custom-call(s32[16]{0:T(128)} %sides.19, f32[4096,512]{1,0:T(8,128)} %get-tuple-element.94.second_ref, ...), custom_call_target="tpu_custom_call" | custom-call | flops 12999999488 | bytes 39000000 | tf_op jit(solution)/shard_map/gate/pallas_call | solution.py:1462
  174.9 2.6 all-to-all-start.6
  180.1 5.6 %all-to-all-done.6.recv_ref = f32[32,8,128]{2,1,0:T(8,128)S(1)} async-done(((f32[32,8,128]{2,1,0:T(8,128)}), f32[32,8,128]{2,1,0:T(8,128)S(1)}, u32[]{:S(2)}, u32[]{:S(2)}) %all-to-all-start.6) | async-done | bytes 131104 | tf_op jit(solution)/shard_map/all_to_all | solution.py:23
  188.3 2.6 all-to-all-start.7
  194.7 4.4 %all-to-all-done.7.recv_ref = f32[32,8,128]{2,1,0:T(8,128)S(1)} async-done(((f32[32,8,128]{2,1,0:T(8,128)}), f32[32,8,128]{2,1,0:T(8,128)S(1)}, u32[]{:S(2)}, u32[]{:S(2)}) %all-to-all-start.7) | async-done | bytes 131104 | tf_op jit(solution)/shard_map/all_to_all | solution.py:23
  199.1 2.6 all-to-all-start.8
  201.7 15.8 %conv_back.1 = (bf16[4096,512]{1,0:T(8,128)(2,1)}, f32[4096,256]{1,0:T(8,128)}, f32[8,512]{1,0:T(8,128)}, f32[8,128]{1,0:T(8,128)}) custom-call(s32[16]{0:T(128)} %sides.19, f32[4096,512]{1,0:T(8,128)} %get-tuple-element.94.second_ref, f32[8,512]{1,0:T(8,128)} %get-tuple-element.99.ab_ref, f32[32,8,128]{2,1,0:T(8,128)} %copy-done.8, ...), custom_call_target="tpu_custom_call" | custom-call | flops 20000000000 | bytes 60000000 | tf_op jit(solution)/shard_map/conv_back/pallas_call | solution.py:1582
  217.5 4.8 %all-to-all-done.8.part_ref = bf16[32,96,128]{2,1,0:T(8,128)(2,1)S(1)} async-done(((bf16[32,96,128]{2,1,0:T(8,128)(2,1)}), bf16[32,96,128]{2,1,0:T(8,128)(2,1)S(1)}, u32[]{:S(2)}, u32[]{:S(2)}) %all-to-all-start.8) | async-done | bytes 786464 | tf_op jit(solution)/shard_map/all_to_all | solution.py:23
  225.1 3.8 %all-to-all-start.9 = ((f32[32,8,128]{2,1,0:T(8,128)}), f32[32,8,128]{2,1,0:T(8,128)S(1)}, u32[]{:S(2)}, u32[]{:S(2)}) async-start(f32[32,8,128]{2,1,0:T(8,128)} %get-tuple-element.137), calls=%async_computation.9 | async-start | bytes 262144 | tf_op jit(solution)/shard_map/all_to_all | solution.py:23
  228.8 13.3 %conv_grad.1 = (f32[256,1024]{1,0:T(8,128)}, bf16[16,144,128]{2,1,0:T(8,128)(2,1)}, bf16[16,144,128]{2,1,0:T(8,128)(2,1)}) custom-call(s32[1]{0:T(128)} %bitcast.odd.refs_1_, bf16[4096,256]{1,0:T(8,128)(2,1)} %get-tuple-element.138.act_ref, bf16[4096,512]{1,0:T(8,128)(2,1)} %get-tuple-element.139.dsecond_ref, bf16[4096,1024]{1,0:T(8,128)(2,1)} %bitcast.78, ...), custom_call_target="tpu_custom_call" | custom-call | flops 15000000512 | bytes 45000000 | tf_op jit(solution)/shard_map/conv_grad/pallas_call | solution.py:1640
  243.5 2.9 last_terms.1
  251.6 6.7 %all-to-all-start.10 = ((bf16[16,208,128]{2,1,0:T(8,128)(2,1)}), bf16[16,208,128]{2,1,0:T(8,128)(2,1)S(1)}, u32[]{:S(2)}, u32[]{:S(2)}) async-start(bf16[16,208,128]{2,1,0:T(8,128)(2,1)} %last_merge.1), calls=%async_computation.10 | async-start | bytes 1703936 | tf_op jit(solution)/shard_map/all_to_all | solution.py:1717
  259.0 13.0 %last.1 = (f32[4096,1024]{1,0:T(8,128)}, f32[8,128]{1,0:T(8,128)}) custom-call(s32[16]{0:T(128)} %sides.19, f32[4096,256]{1,0:T(8,128)} %get-tuple-element.128.dfirst_ref, f32[4096,256]{1,0:T(8,128)} %get-tuple-element.90.first_ref, f32[8,256]{1,0:T(8,128)} %get-tuple-element.144.grads_ref, bf16[1024,256]{1,0:T(8,128)(2,1)} %get-tuple-element.145.w_ref, ...), custom_call_target="tpu_custom_call" | custom-call | flops 15000000512 | bytes 45000000 | tf_op jit(solution)/shard_map/last/pallas_call | solution.py:1672
  272.0 7.4 %all-to-all-done.10.part_ref = bf16[16,208,128]{2,1,0:T(8,128)(2,1)S(1)} async-done(((bf16[16,208,128]{2,1,0:T(8,128)(2,1)}), bf16[16,208,128]{2,1,0:T(8,128)(2,1)S(1)}, u32[]{:S(2)}, u32[]{:S(2)}) %all-to-all-start.10) | async-done | bytes 852000 | tf_op jit(solution)/shard_map/all_to_all | solution.py:1717
  (92 shorter events, 42.0 us)
Async XLA Ops:
  2.6 23.0 %all-to-all-start = ((bf16[8,128,128]{2,1,0:T(8,128)(2,1)}), bf16[8,128,128]{2,1,0:T(8,128)(2,1)S(1)}, u32[]{:S(2)}, u32[]{:S(2)}) async-start(bf16[8,128,128]{2,1,0:T(8,128)(2,1)} %get-tuple-element.89), calls=%async_computation | async-start | bytes 524288 | tf_op jit(solution)/shard_map/all_to_all | solution.py:23
  9.8 14.7 %collective-permute-start.1 = (bf16[1,528,128]{2,1,0:T(8,128)(2,1)}, bf16[1,528,128]{2,1,0:T(8,128)(2,1)S(1)}, u32[]{:S(2)}, u32[]{:S(2)}) collective-permute-start(bf16[1,528,128]{2,1,0:T(8,128)(2,1)} %bitcast.64), channel_id=1, source_target_pairs={{0,16},{4,20},{8,24},{12,28},{16,0},{20,4},{24,8},{28,12},{1,17},{... | collective-permute-start | bytes 405512 | tf_op jit(solution)/shard_map/ppermute | solution.py:40
  25.5 7.2 %collective-permute-start.2 = (bf16[2,528,128]{2,1,0:T(8,128)(2,1)S(1)}, bf16[2,528,128]{2,1,0:T(8,128)(2,1)S(1)}, u32[]{:S(2)}, u32[]{:S(2)}) collective-permute-start(bf16[2,528,128]{2,1,0:T(8,128)(2,1)S(1)} %pad_maximum_fusion.1), channel_id=1, source_target_pairs={{0,8},{4,12},{8,0},{12,4},{16,24},{20,28},{24,16},{28,20},{1,9},{5... | collective-permute-start | bytes 811016 | tf_op jit(solution)/shard_map/ppermute | solution.py:40
  25.5 9.8 %copy-start.5 = (bf16[8,128,128]{2,1,0:T(8,128)(2,1)}, bf16[8,128,128]{2,1,0:T(8,128)(2,1)S(1)}, u32[]{:S(2)}) copy-start(bf16[8,128,128]{2,1,0:T(8,128)(2,1)S(1)} %all-to-all-done) | copy-start | bytes 786436
  25.6 9.8 %collective-permute-start = (bf16[1024,128]{1,0:T(8,128)(2,1)S(1)}, bf16[1024,128]{1,0:T(8,128)(2,1)S(1)}, u32[]{:S(2)}, u32[]{:S(2)}) collective-permute-start(bf16[1024,128]{1,0:T(8,128)(2,1)S(1)} %bitcast.68), channel_id=1, source_target_pairs={{0,1},{1,0},{2,3},{3,2},{4,5},{5,4},{6,7},{7,6},{8,9},{9,8},{10,11... | collective-permute-start | bytes 786440 | tf_op jit(solution)/shard_map/ppermute | solution.py:32
  33.6 10.2 %copy-start.4 = (bf16[4,528,128]{2,1,0:T(8,128)(2,1)}, bf16[4,528,128]{2,1,0:T(8,128)(2,1)S(1)}, u32[]{:S(2)}) copy-start(bf16[4,528,128]{2,1,0:T(8,128)(2,1)S(1)} %pad_maximum_fusion.refs_2_.refs_0_) | copy-start | bytes 1622020
  33.6 13.7 %collective-permute-start.3 = (bf16[4,528,128]{2,1,0:T(8,128)(2,1)S(1)}, bf16[4,528,128]{2,1,0:T(8,128)(2,1)S(1)}, u32[]{:S(2)}, u32[]{:S(2)}) collective-permute-start(bf16[4,528,128]{2,1,0:T(8,128)(2,1)S(1)} %pad_maximum_fusion.refs_2_.refs_0_), channel_id=1, source_target_pairs={{0,4},{4,0},{8,12},{12,8},{16,20},{20,16},{24,28},{28,24},{1,5},{5... | collective-permute-start | bytes 1622024 | tf_op jit(solution)/shard_map/ppermute | solution.py:40
  35.4 21.9 %collective-permute-start.4 = (bf16[4,528,128]{2,1,0:T(8,128)(2,1)S(1)}, bf16[4,528,128]{2,1,0:T(8,128)(2,1)S(1)}, u32[]{:S(2)}, u32[]{:S(2)}) collective-permute-start(bf16[4,528,128]{2,1,0:T(8,128)(2,1)S(1)} %pad_maximum_fusion.refs_2_.refs_0_), channel_id=1, source_target_pairs={{0,1},{1,0},{2,3},{3,2},{4,5},{5,4},{6,7},{7,6},{8,9},{9,8},{10,11... | collective-permute-start | bytes 1622024 | tf_op jit(solution)/shard_map/ppermute | solution.py:32
  43.7 13.6 %all-to-all-start.1 = ((f32[32,8,128]{2,1,0:T(8,128)}), f32[32,8,128]{2,1,0:T(8,128)S(1)}, u32[]{:S(2)}, u32[]{:S(2)}) async-start(f32[32,8,128]{2,1,0:T(8,128)} %get-tuple-element.91), calls=%async_computation.1 | async-start | bytes 262144 | tf_op jit(solution)/shard_map/all_to_all | solution.py:23
  47.3 10.0 %copy-start.13 = (bf16[4,528,128]{2,1,0:T(8,128)(2,1)}, bf16[4,528,128]{2,1,0:T(8,128)(2,1)S(1)}, u32[]{:S(2)}) copy-start(bf16[4,528,128]{2,1,0:T(8,128)(2,1)S(1)} %collective-permute-done.3.refs_3_.refs_1_) | copy-start | bytes 1622020
  47.3 10.0 %collective-permute-start.5 = (bf16[4,528,128]{2,1,0:T(8,128)(2,1)S(1)}, bf16[4,528,128]{2,1,0:T(8,128)(2,1)S(1)}, u32[]{:S(2)}, u32[]{:S(2)}) collective-permute-start(bf16[4,528,128]{2,1,0:T(8,128)(2,1)S(1)} %collective-permute-done.3.refs_3_.refs_1_), channel_id=1, source_target_pairs={{0,1},{1,0},{2,3},{3,2},{4,5},{5,4},{6,7},{7,6},{8,9},{9,8},{10,11... | collective-permute-start | bytes 1622024 | tf_op jit(solution)/shard_map/ppermute | solution.py:32
  57.3 1.0 copy-start.15
  91.7 10.8 %all-to-all-start.3 = ((f32[32,8,128]{2,1,0:T(8,128)}), f32[32,8,128]{2,1,0:T(8,128)S(1)}, u32[]{:S(2)}, u32[]{:S(2)}) async-start(f32[32,8,128]{2,1,0:T(8,128)} %get-tuple-element.101), calls=%async_computation.3 | async-start | bytes 262144 | tf_op jit(solution)/shard_map/all_to_all | solution.py:23
  149.6 10.8 %all-to-all-start.5 = ((bf16[32,16,128]{2,1,0:T(8,128)(2,1)}), bf16[32,16,128]{2,1,0:T(8,128)(2,1)S(1)}, u32[]{:S(2)}, u32[]{:S(2)}) async-start(bf16[32,16,128]{2,1,0:T(8,128)(2,1)} %get-tuple-element.113), calls=%async_computation.5 | async-start | bytes 262144 | tf_op jit(solution)/shard_map/all_to_all | solution.py:23
  161.1 18.8 %copy-start = (f32[256,1024]{1,0:T(8,128)S(1)}, f32[256,1024]{1,0:T(8,128)}, u32[]{:S(2)}) copy-start(f32[256,1024]{1,0:T(8,128)} %get-tuple-element.132) | copy-start | bytes 3145732
  161.1 18.8 %copy-start.1 = (f32[256,1024]{1,0:T(8,128)S(1)}, f32[256,1024]{1,0:T(8,128)}, u32[]{:S(2)}) copy-start(f32[256,1024]{1,0:T(8,128)} %get-tuple-element.129) | copy-start | bytes 3145732
  174.9 10.8 %all-to-all-start.6 = ((f32[32,8,128]{2,1,0:T(8,128)}), f32[32,8,128]{2,1,0:T(8,128)S(1)}, u32[]{:S(2)}, u32[]{:S(2)}) async-start(f32[32,8,128]{2,1,0:T(8,128)} %get-tuple-element.121), calls=%async_computation.6 | async-start | bytes 262144 | tf_op jit(solution)/shard_map/all_to_all | solution.py:23
  188.3 10.8 %all-to-all-start.7 = ((f32[32,8,128]{2,1,0:T(8,128)}), f32[32,8,128]{2,1,0:T(8,128)S(1)}, u32[]{:S(2)}, u32[]{:S(2)}) async-start(f32[32,8,128]{2,1,0:T(8,128)} %get-tuple-element.123), calls=%async_computation.7 | async-start | bytes 262144 | tf_op jit(solution)/shard_map/all_to_all | solution.py:23
  199.1 2.6 copy-start.8
  199.1 23.2 %all-to-all-start.8 = ((bf16[32,96,128]{2,1,0:T(8,128)(2,1)}), bf16[32,96,128]{2,1,0:T(8,128)(2,1)S(1)}, u32[]{:S(2)}, u32[]{:S(2)}) async-start(bf16[32,96,128]{2,1,0:T(8,128)(2,1)} %fusion.6), calls=%async_computation.8 | async-start | bytes 1572864 | tf_op jit(solution)/shard_map/all_to_all | solution.py:23
  222.3 0.9 copy-start.3
  225.1 17.7 %all-to-all-start.9 = ((f32[32,8,128]{2,1,0:T(8,128)}), f32[32,8,128]{2,1,0:T(8,128)S(1)}, u32[]{:S(2)}, u32[]{:S(2)}) async-start(f32[32,8,128]{2,1,0:T(8,128)} %get-tuple-element.137), calls=%async_computation.9 | async-start | bytes 262144 | tf_op jit(solution)/shard_map/all_to_all | solution.py:23
  242.2 6.0 %collective-permute-start.6 = (bf16[16,144,128]{2,1,0:T(8,128)(2,1)}, bf16[16,144,128]{2,1,0:T(8,128)(2,1)S(1)}, u32[]{:S(2)}, u32[]{:S(2)}) collective-permute-start(bf16[16,144,128]{2,1,0:T(8,128)(2,1)} %get-tuple-element.150), channel_id=1, source_target_pairs={{0,1},{1,0},{2,3},{3,2},{4,5},{5,4},{6,7},{7,6},{8,9},{9,8},{10,11... | collective-permute-start | bytes 1769480 | tf_op jit(solution)/shard_map/ppermute | solution.py:32
  246.3 1.9 collective-permute-start.7
  248.2 0.9 copy-start.12
  251.6 27.9 %all-to-all-start.10 = ((bf16[16,208,128]{2,1,0:T(8,128)(2,1)}), bf16[16,208,128]{2,1,0:T(8,128)(2,1)S(1)}, u32[]{:S(2)}, u32[]{:S(2)}) async-start(bf16[16,208,128]{2,1,0:T(8,128)(2,1)} %last_merge.1), calls=%async_computation.10 | async-start | bytes 1703936 | tf_op jit(solution)/shard_map/all_to_all | solution.py:1717
  279.5 1.0 copy-start.2
  282.4 4.0 %collective-permute-start.10 = (bf16[304,128]{1,0:T(8,128)(2,1)}, bf16[304,128]{1,0:T(8,128)(2,1)S(1)}, u32[]{:S(2)}, u32[]{:S(2)}) collective-permute-start(bf16[304,128]{1,0:T(8,128)(2,1)} %last_total.1.refs_0_), channel_id=1, source_target_pairs={{0,3},{1,2},{2,1},{3,0},{4,7},{5,6},{6,5},{7,4},{8,11},{9,10},{10,... | collective-permute-start | bytes 233480 | tf_op jit(solution)/shard_map/ppermute | solution.py:1731
  282.4 4.0 %collective-permute-start.8 = (bf16[304,128]{1,0:T(8,128)(2,1)}, bf16[304,128]{1,0:T(8,128)(2,1)S(1)}, u32[]{:S(2)}, u32[]{:S(2)}) collective-permute-start(bf16[304,128]{1,0:T(8,128)(2,1)} %last_total.1.refs_0_), channel_id=1, source_target_pairs={{0,1},{1,0},{2,3},{3,2},{4,5},{5,4},{6,7},{7,6},{8,9},{9,8},{10,11... | collective-permute-start | bytes 233480 | tf_op jit(solution)/shard_map/ppermute | solution.py:1731
  283.0 5.0 %collective-permute-start.9 = (bf16[304,128]{1,0:T(8,128)(2,1)}, bf16[304,128]{1,0:T(8,128)(2,1)S(1)}, u32[]{:S(2)}, u32[]{:S(2)}) collective-permute-start(bf16[304,128]{1,0:T(8,128)(2,1)} %last_total.1.refs_0_), channel_id=1, source_target_pairs={{0,2},{1,3},{2,0},{3,1},{4,6},{5,7},{6,4},{7,5},{8,10},{9,11},{10,... | collective-permute-start | bytes 233480 | tf_op jit(solution)/shard_map/ppermute | solution.py:1731
  286.4 1.7 copy-start.18
  286.4 1.7 copy-start.19
  (9 other events, 6.3 us)

commit v5 on v4

--- a/solution.py
+++ b/solution.py
@@ -40,6 +40,24 @@
     return lax.ppermute(values, "fsdp", [(i, i ^ k) for i in range(pieces)])
 
 
+def on_own_side(parts):
+    odd = lax.rem(lax.axis_index("dp"), 2)
+    parts = parts.reshape((parts.shape[0] // 2, 2) + parts.shape[1:])
+    mine = lax.dynamic_index_in_dim(parts, odd, 1, False)
+    other = lax.dynamic_index_in_dim(parts, 1 - odd, 1, False)
+    return (mine.astype(f32) + neighbour(other).astype(f32)).astype(bf16)
+
+
+def across_sides(parts):
+    count = parts.shape[0]
+    sides = [[2 * i + side for i in range(count)] for side in range(2)]
+    return lax.all_to_all(parts, AXES, 0, 0, axis_index_groups=sides)
+
+
+def to_owners(parts):
+    return across_sides(on_own_side(parts))
+
+
 def half_of(shard, axis):
     odd = lax.rem(lax.axis_index("dp"), 2)
     return lax.dynamic_slice_in_dim(shard, odd * (shard.shape[axis] // 2), shard.shape[axis] // 2, axis)
@@ -94,6 +112,20 @@
 
 def contract_last(left, right):
     return lax.dot_general(left, right, (((1,), (1,)), ((), ())), preferred_element_type=f32)
+
+
+def three_parts(values):
+    high = values.astype(bf16)
+    rest = values - high.astype(f32)
+    middle = rest.astype(bf16)
+    low = (rest - middle.astype(f32)).astype(bf16)
+    return jnp.concatenate([high, middle, low], axis=0)
+
+
+def exact_dot(values, right):
+    rows = values.shape[0]
+    parts = jnp.dot(three_parts(values), right, preferred_element_type=f32)
+    return parts[:rows] + (parts[rows : 2 * rows] + parts[2 * rows :])
 
 
 def zeros_at_start(*refs):
@@ -570,11 +602,11 @@
         total = column_total(acc_ref[0])
         colsum_ref[...] = jnp.broadcast_to(total, colsum_ref.shape)
         power_ref[...] = lane_parts(acc_ref[1])
-        gw = jnp.dot(gram_ref[...], whole, precision=HIGH, preferred_element_type=f32)
+        both = jnp.concatenate([gram_ref[...], jnp.broadcast_to(total, (16, half))], axis=0)
+        both = exact_dot(both, out_ref[...])
+        gw = both[:half]
         gw_ref[...] = gw
-        sums = jnp.dot(
-            jnp.broadcast_to(total, (8, half)), whole, precision=HIGH, preferred_element_type=f32
-        )
+        sums = both[half:]
         put(tile_ref, 0, sums[0:1, :])
         put(tile_ref, whole.shape[1] // 128, column_total(gw * whole))
         send(send_ref, tile_ref)
@@ -632,6 +664,7 @@
         half_ref[1:2, :] = 0.5 * offset
 
     squares = [square_ref[...]]
+    sums = {at: acc_ref[:, at : at + part] for at in range(0, lanes, part)}
 
     def expand(image):
         third_ref[of_image(image), :] = jnp.dot(
@@ -657,7 +690,7 @@
                 slope = gate + output * (1.0 - turned)
                 grad = cot_ref[here, cut].astype(f32) * (slope * half_ref[0:1, cut])
                 slope_ref[here, cut] = grad.astype(bf16)
-                acc_ref[:, cut] += fold(grad)
+                sums[at] = sums[at] + fold(grad)
                 squares[0] = squares[0] + lane_parts(fold(output * output))
 
     def contract(image):
@@ -667,6 +700,8 @@
 
     stages(expand, finish, contract)
     square_ref[...] = squares[0]
+    for at, total in sums.items():
+        acc_ref[:, at : at + part] = total
 
     @at_end
     def _():
@@ -739,12 +774,7 @@
         turn_ref[...] = jnp.dot(
             (whole * slant).astype(bf16), wt_ref[...], preferred_element_type=f32
         ).astype(bf16)
-        row_ref[...] = jnp.dot(
-            jnp.broadcast_to(level, (8, width)),
-            wt_ref[...].astype(f32),
-            precision=HIGH,
-            preferred_element_type=f32,
-        )
+        row_ref[...] = exact_dot(jnp.broadcast_to(level, (16, width)), wt_ref[...])[:8]
 
     def turn(image):
         here = of_image(image)
@@ -870,8 +900,10 @@
     first_ref,
     ab_in_ref,
     w_ref,
+    x_ref,
     dsecond_ref,
     dfirst_ref,
+    in_ref,
     grads_ref,
     stat_ref,
     column_ref,
@@ -879,7 +911,7 @@
     tile_ref,
 ):
     step = pl.program_id(0)
-    zeros_at_start(acc_ref, column_ref)
+    zeros_at_start(acc_ref, column_ref, in_ref)
     place = places()
     lanes = second_ref.shape[1]
     half = lanes // 2
@@ -956,7 +988,11 @@
             sums[0] = sums[0] + fold(grad)
             sums[1] = sums[1] + fold(grad * normed)
 
-    stages(start, multiply, finish)
+    def cross(image):
+        here = of_image(image)
+        in_ref[...] += contract_lead(dfirst_ref[here, :].astype(bf16), x_ref[here, :])
+
+    stages(start, multiply, finish, cross)
     acc_ref[0], acc_ref[1] = sums
 
     @at_end
@@ -966,12 +1002,12 @@
         put(stat_ref, half // 128, column_total(acc_ref[1]))
 
 
-def conv_grad_kernel(aligned, odd, act_ref, dsecond_ref, x_ref, dfirst_ref, _, in_ref, *refs):
+def conv_grad_kernel(aligned, odd, act_ref, dsecond_ref, _, *refs):
     if aligned:
         mine_ref, other_ref, conv_ref, patch_ref = refs
     else:
         conv_ref, patch_ref = refs
-    zeros_at_start(conv_ref, in_ref, patch_ref)
+    zeros_at_start(conv_ref, patch_ref)
     place = places()
     lanes = act_ref.shape[1]
     columns = TAPS * lanes // RADIX
@@ -988,7 +1024,6 @@
             )
 
     stages(start, multiply)
-    in_ref[...] += contract_lead(dfirst_ref[...].astype(bf16), x_ref[...])
 
     if aligned:
 
@@ -1125,7 +1160,7 @@
     at += marks[1]
     down_ref[...] = rows_from(at, marks[2])
     at += marks[2]
-    bias_ref[...] = all_ref[0, at : at + 8, :]
+    bias_ref[...] = all_ref[0, at : at + 1, : bias_ref.shape[1]]
     at = marks[3]
     in_ref[...] = jnp.transpose(rows_from(at, marks[4]))
     at += marks[4]
@@ -1153,7 +1188,9 @@
     return jax.ShapeDtypeStruct(shape, dtype)
 
 
-def call(kernel, steps, ins, outs, scratch=(), cost=5, limit=56, name=None):
+def call(kernel, steps, ins, outs, scratch=(), cost=5, limit=None, name=None):
+    if limit is None:
+        limit = 56 if steps > 1 else 24
     return pl.pallas_call(
         kernel,
         grid=(steps,),
@@ -1246,6 +1283,7 @@
             ],
             [((16, 128), f32)],
             2,
+            56,
             name="last_prepare",
         )(
             odd,
@@ -1578,8 +1616,8 @@
     gates = jnp.concatenate([out_cut, gates], axis=1)
     gates = jnp.pad(gates, ((0, 0), (0, -gates.shape[1] % 16), (0, 0)))
 
-    gates = swap_all(gates, AXES)
-    dsecond, dfirst, grads_mid, stat = call(
+    gates = to_owners(gates)
+    dsecond, dfirst, in_grad, grads_mid, stat = call(
         conv_back_kernel,
         steps,
         [
@@ -1595,8 +1633,15 @@
             tiles(bottleneck),
             held(8, bottleneck),
             held(bottleneck, RADIX * columns),
+            tiles(width),
         ],
-        [tiled(mid, bf16), tiled(bottleneck), whole_out((8, mid)), whole_out((8, 128))],
+        [
+            tiled(mid, bf16),
+            tiled(bottleneck),
+            whole_out((bottleneck, width)),
+            whole_out((8, mid)),
+            whole_out((8, 128)),
+        ],
         [
             ((STEP, 256 + 2 * SIDE, RADIX * columns), f32),
             ((2, 8, bottleneck), f32),
@@ -1617,6 +1662,7 @@
         first,
         terms_in,
         whole_mid,
+        x,
     )
     gates, out = call(
         total_kernel,
@@ -1629,7 +1675,7 @@
     )(gates, stat)
     got = swap_all(out, AXES)
 
-    outs = [whole_out((bottleneck, width))]
+    outs = []
     scratch = [((STEP, 256 + 2 * SIDE, RADIX * columns), bf16)]
     mid_rows = bottleneck // devices * RADIX * TAPS
     if aligned:
@@ -1637,15 +1683,15 @@
         scratch = [((bottleneck, RADIX * columns), f32)] + scratch
     else:
         outs += [whole_out((bottleneck, RADIX * columns))]
-    in_grad, *conv_parts = call(
+    conv_parts = call(
         functools.partial(conv_grad_kernel, aligned),
         steps,
-        [scalars(), tiles(bottleneck), tiles(mid), tiles(width), tiles(bottleneck), token()],
+        [scalars(), tiles(bottleneck), tiles(mid), token()],
         outs,
         scratch,
         15,
         name="conv_grad",
-    )(odd, act_low, dsecond, x, dfirst, gates)
+    )(odd, act_low, dsecond, gates)
     outs = [whole_out((8, bottleneck))]
     scratch = [((8, 128), f32)]
     in_rows = bottleneck // groups * (width // pieces) // 128
@@ -1709,12 +1755,8 @@
         mid_cut = mid_cut.transpose(0, 2, 1, 3).reshape(devices, -1, 128)
         late = jnp.concatenate([in_cut.reshape(devices, -1, 128), mid_cut], axis=1)
         late = jnp.pad(late, ((0, 0), (0, -late.shape[1] % 16), (0, 0)))
-        late = late.reshape(devices // 2, 2, -1, 128)
-        mine = lax.dynamic_index_in_dim(late, odd[0], 1, False)
-        other = lax.dynamic_index_in_dim(late, 1 - odd[0], 1, False)
-        late = (mine.astype(f32) + neighbour(other).astype(f32)).astype(bf16)
-    sides_of = [[2 * i + side for i in range(devices // 2)] for side in range(2)]
-    late = lax.all_to_all(late, AXES, 0, 0, axis_index_groups=sides_of)
+        late = on_own_side(late)
+    late = across_sides(late)
     (summed,) = call(
         total_last_kernel,
         1,
@@ -1739,7 +1781,7 @@
                 whole_out((bottleneck, own_width)),
                 whole_out((up_rows, att)),
                 whole_out((down_rows, att)),
-                whole_out((8, 128)),
+                whole_out((1, up_rows)),
                 whole_out((own_width, bottleneck)),
                 whole_out((RADIX * TAPS, own_columns, 128)),
             ],
@@ -1747,7 +1789,7 @@
             2,
             name="last_shards",
         )(lax.axis_index("dp").reshape(1), *members)
-        shard_bias = shard_bias[0, :up_rows]
+        shard_bias = shard_bias.reshape(-1)
         shard_up = shard_up.T
         shard_mid = shard_mid.reshape(RADIX, TAPS, own_columns, 128).transpose(0, 1, 3, 2)
     else:

time: 293 us -> 279 us (0.952)
  Pallas kernels: 141 us -> 129 us
  starting transfers between devices: 42 us -> 45.5 us
  local copies, waits for them, and re-layouts: 17.2 us -> 14.1 us
    all_to_all x1 -> x2, starting transfers between devices: 6.65 us -> 10.6 us  [across_sides(): return lax.all_to_all(parts, AXES, 0, 0, axis_index_groups=sides)]
    all_to_all x8 -> x7, waiting for transfers between devices: 28 us -> 24.2 us  [swap_all(): return lax.all_to_all(values, axes, 0, 0)]
    pallas_call x1, Pallas kernels: 13.3 us -> 9.8 us  [local(): call(functools.partial(conv_grad_kernel, aligned), steps, [scalars(), til...]
    all_to_all x8 -> x7, starting transfers between devices: 27.5 us -> 26.8 us  [swap_all(): return lax.all_to_all(values, axes, 0, 0)]
    all_to_all x1 -> x2, waiting for transfers between devices: 7.44 us -> 8.03 us  [across_sides(): return lax.all_to_all(parts, AXES, 0, 0, axis_index_groups=sides)]
    unnamed x42 -> x84, local copies, waits for them, and re-layouts: 7.7 us -> 7.98 us
  transfers between devices with their start and end apart: 20 -> 21, of which waited for: 10 -> 9; matrix products, arithmetic and copies ran while one was open for 4% -> 3% of each run, Pallas kernels for 22% -> 21%
where the time goes in v5:
time: 279 us; the launch traced here: 277 us
  Pallas kernels  129 us (46%)
  waiting for transfers between devices  54.6 us (20%)
  starting transfers between devices  45.5 us (16%)
  blocking collectives  28 us (10%)
  local copies, waits for them, and re-layouts  14.1 us (5%)
  other arithmetic  4.03 us (1%)
    all_to_all x2, blocking collectives, swap_all(): return lax.all_to_all(values, axes, 0, 0)  28 us
    all_to_all x7, starting transfers between devices, swap_all(): return lax.all_to_all(values, axes, 0, 0)  26.8 us
    all_to_all x7, waiting for transfers between devices, swap_all(): return lax.all_to_all(values, axes, 0, 0)  24.2 us
    pallas_call x1, Pallas kernels, local(): call(out_kernel, steps, [scalars(), tiles(bottleneck), tiles(width), tile...  22.6 us
    ppermute x3, waiting for transfers between devices, partner(): return lax.ppermute(values, 'fsdp', [(i, i ^ k) for i in range(pieces)])  18.8 us
    pallas_call x1, Pallas kernels, local(): call(conv_back_kernel, steps, [scalars(), tiles(mid), held(8, mid), recei...  18.5 us
    pallas_call x1, Pallas kernels, local(): call(last_kernel, steps, [scalars(), tiles(bottleneck), tiles(bottleneck)...  13.1 us
    pallas_call x1, Pallas kernels, local(): call(functools.partial(second_kernel, lengths if aligned else None), step...  12.6 us
  transfers between devices with their start and end apart: 21, of which 9 were waited for; matrix products, arithmetic and copies ran while one was open for 3% of the time, Pallas kernels for 21%

profile of v5, /device:TPU:0, one launch (start us, length us, event | category | flops | bytes accessed | tf_op | source)
XLA Modules:
  0.0 276.8 jit_solution(13977358499726207866)
XLA Ops:
  0.7 1.9 last_prepare.1
  2.6 7.3 %all-to-all-start = ((bf16[8,128,128]{2,1,0:T(8,128)(2,1)}), bf16[8,128,128]{2,1,0:T(8,128)(2,1)S(1)}, u32[]{:S(2)}, u32[]{:S(2)}) async-start(bf16[8,128,128]{2,1,0:T(8,128)(2,1)} %get-tuple-element.89), calls=%async_computation | async-start | bytes 524288 | tf_op jit(solution)/shard_map/all_to_all | solution.py:23
  9.8 2.9 %collective-permute-start.1 = (bf16[1,528,128]{2,1,0:T(8,128)(2,1)}, bf16[1,528,128]{2,1,0:T(8,128)(2,1)S(1)}, u32[]{:S(2)}, u32[]{:S(2)}) collective-permute-start(bf16[1,528,128]{2,1,0:T(8,128)(2,1)} %bitcast.73), channel_id=1, source_target_pairs={{0,16},{4,20},{8,24},{12,28},{16,0},{20,4},{24,8},{28,12},{1,17},{... | collective-permute-start | bytes 405512 | tf_op jit(solution)/shard_map/ppermute | solution.py:40
  12.7 11.8 %collective-permute-done.1 = bf16[1,528,128]{2,1,0:T(8,128)(2,1)S(1)} collective-permute-done((bf16[1,528,128]{2,1,0:T(8,128)(2,1)}, bf16[1,528,128]{2,1,0:T(8,128)(2,1)S(1)}, u32[]{:S(2)}, u32[]{:S(2)}) %collective-permute-start.1) | collective-permute-done | bytes 135200 | tf_op jit(solution)/shard_map/ppermute | solution.py:40
  25.6 7.0 %collective-permute-done.2 = bf16[2,528,128]{2,1,0:T(8,128)(2,1)S(1)} collective-permute-done((bf16[2,528,128]{2,1,0:T(8,128)(2,1)S(1)}, bf16[2,528,128]{2,1,0:T(8,128)(2,1)S(1)}, u32[]{:S(2)}, u32[]{:S(2)}) %collective-permute-start.2) | collective-permute-done | bytes 270368 | tf_op jit(solution)/shard_map/ppermute | solution.py:40
  33.6 1.8 collective-permute-start.3
  36.1 7.7 %first.1 = (f32[4096,256]{1,0:T(8,128)}, bf16[1024,256]{1,0:T(8,128)(2,1)}, f32[32,8,128]{2,1,0:T(8,128)}) custom-call(s32[16]{0:T(128)} %sides.19, s32[1]{0:T(128)} %bitcast.odd.refs_1_, bf16[4096,1024]{1,0:T(8,128)(2,1)} %bitcast.84, bf16[1024,128]{1,0:T(8,128)(2,1)} %bitcast.78, bf16[1024,128]{1,0:T(8,128)(2,1)} %copy-done.41), custom_call_target="tpu_custom_call" | custom-call | flops 8000000000 | bytes 24000000 | tf_op jit(solution)/shard_map/first/pallas_call | solution.py:1328
  43.7 3.6 %all-to-all-start.1 = ((f32[32,8,128]{2,1,0:T(8,128)}), f32[32,8,128]{2,1,0:T(8,128)S(1)}, u32[]{:S(2)}, u32[]{:S(2)}) async-start(f32[32,8,128]{2,1,0:T(8,128)} %get-tuple-element.91), calls=%async_computation.1 | async-start | bytes 262144 | tf_op jit(solution)/shard_map/all_to_all | solution.py:23
  47.6 9.6 %cross.1 = (f32[256,1024]{1,0:T(8,128)}, f32[8,1024]{1,0:T(8,128)}, f32[8,128]{1,0:T(8,128)}) custom-call(s32[16]{0:T(128)} %sides.19, bf16[4096,1024]{1,0:T(8,128)(2,1)} %bitcast.85, f32[4096,256]{1,0:T(8,128)} %get-tuple-element.90.first_ref), custom_call_target="tpu_custom_call" | custom-call | flops 10000000000 | bytes 30000000 | tf_op jit(solution)/shard_map/cross/pallas_call | solution.py:1338
  58.3 12.6 %second.1 = (bf16[4096,256]{1,0:T(8,128)(2,1)}, f32[4096,512]{1,0:T(8,128)}, f32[8,256]{1,0:T(8,128)}, f32[8,128]{1,0:T(8,128)}, f32[32,8,128]{2,1,0:T(8,128)}, ...) custom-call(s32[16]{0:T(128)} %sides.19, ...), custom_call_target="tpu_custom_call" | custom-call | flops 15000000512 | bytes 45000000 | tf_op jit(solution)/shard_map/second/pallas_call | solution.py:1384
  70.9 14.1 %all_to_all.55.recv_ref = f32[32,8,128]{2,1,0:T(8,128)} all-to-all(f32[32,8,128]{2,1,0:T(8,128)} %get-tuple-element.95), channel_id=1, replica_groups=mesh['fsdp'=8,'dp'=4] {'fsdp','dp'}, dimensions={0} | all-to-all | bytes 262144 | tf_op jit(solution)/shard_map/all_to_all | solution.py:23
  85.0 6.8 %pool.1 = (bf16[16,256]{1,0:T(8,128)(2,1)}, f32[16,128]{1,0:T(8,128)}, f32[8,512]{1,0:T(8,128)}, f32[32,8,128]{2,1,0:T(8,128)}) custom-call(s32[16]{0:T(128)} %sides.19, f32[4096,512]{1,0:T(8,128)} %get-tuple-element.94.second_ref, f32[32,8,128]{2,1,0:T(8,128)} %all_to_all.55.recv_ref, f32[8,512]{1,0:T(8,128)} %get-tuple-element.96.param_ref, ...), custom_call_target="tpu_custom_call" | custom-call | flops 7000000000 | bytes 21000000 | tf_op jit(solution)/shard_map/pool/pallas_call | solution.py:1397
  91.8 2.6 all-to-all-start.3
  97.0 5.6 %all-to-all-done.3.recv_ref = f32[32,8,128]{2,1,0:T(8,128)S(1)} async-done(((f32[32,8,128]{2,1,0:T(8,128)}), f32[32,8,128]{2,1,0:T(8,128)S(1)}, u32[]{:S(2)}, u32[]{:S(2)}) %all-to-all-start.3) | async-done | bytes 131104 | tf_op jit(solution)/shard_map/all_to_all | solution.py:23
  103.3 9.2 %mix.1 = (bf16[4096,256]{1,0:T(8,128)(2,1)}, f32[16,512]{1,0:T(8,128)}, bf16[16,128]{1,0:T(8,128)(2,1)}, f32[8,128]{1,0:T(8,128)}, f32[256,1024]{1,0:T(8,128)}, ...) custom-call(s32[16]{0:T(128)} %sides.19, f32[4096,512]{1,0:T(8,128)} %get-tuple-element.94.second_ref, ...), custom_call_target="tpu_custom_call" | custom-call | flops 11000000512 | bytes 33000000 | tf_op jit(solution)/shard_map/mix/pallas_call | solution.py:1435
  112.5 13.9 %all_to_all.56.recv_ref = f32[32,16,128]{2,1,0:T(8,128)} all-to-all(f32[32,16,128]{2,1,0:T(8,128)} %get-tuple-element.108), channel_id=1, replica_groups=mesh['fsdp'=8,'dp'=4] {'fsdp','dp'}, dimensions={0} | all-to-all | bytes 524288 | tf_op jit(solution)/shard_map/all_to_all | solution.py:23
  126.4 22.6 %output.1 = (bf16[4096,1024]{1,0:T(8,128)(2,1)}, bf16[4096,1024]{1,0:T(8,128)(2,1)}, f32[4096,256]{1,0:T(8,128)}, f32[256,1024]{1,0:T(8,128)}, f32[8,1024]{1,0:T...) custom-call(s32[16]{0:T(128)} %sides.19, bf16[4096,256]{1,0:T(8,128)(2,1)} %get-tuple-element.107.mixed_ref, ...), custom_call_target="tpu_custom_call" | custom-call | flops 24999999488 | bytes 75000000 | tf_op jit(solution)/shard_map/output/pallas_call | solution.py:1465
  149.0 2.6 all-to-all-start.5
  152.3 7.5 %all-to-all-done.5.recv_ref = bf16[32,16,128]{2,1,0:T(8,128)(2,1)S(1)} async-done(((bf16[32,16,128]{2,1,0:T(8,128)(2,1)}), bf16[32,16,128]{2,1,0:T(8,128)(2,1)S(1)}, u32[]{:S(2)}, u32[]{:S(2)}) %all-to-all-start.5) | async-done | bytes 131104 | tf_op jit(solution)/shard_map/all_to_all | solution.py:23
  160.4 12.6 %gate.1 = (f32[4096,256]{1,0:T(8,128)}, f32[5,16,512]{2,1,0:T(8,128)}, f32[512,128]{1,0:T(8,128)}, f32[8,512]{1,0:T(8,128)}, f32[16,128]{1,0:T(8,128)}, /*index=5*/f32[8,1024]{1,0:T(8,128)}, f32[32,8,128]{2,1,0:T(8,128)}) custom-call(s32[16]{0:T(128)} %sides.19, f32[4096,512]{1,0:T(8,128)} %get-tuple-element.94.second_ref, ...), custom_call_target="tpu_custom_call" | custom-call | flops 12999999488 | bytes 39000000 | tf_op jit(solution)/shard_map/gate/pallas_call | solution.py:1500
  174.1 2.6 all-to-all-start.6
  179.3 5.6 %all-to-all-done.6.recv_ref = f32[32,8,128]{2,1,0:T(8,128)S(1)} async-done(((f32[32,8,128]{2,1,0:T(8,128)}), f32[32,8,128]{2,1,0:T(8,128)S(1)}, u32[]{:S(2)}, u32[]{:S(2)}) %all-to-all-start.6) | async-done | bytes 131104 | tf_op jit(solution)/shard_map/all_to_all | solution.py:23
  187.0 2.6 all-to-all-start.7
  192.4 5.5 %all-to-all-done.7.recv_ref = f32[32,8,128]{2,1,0:T(8,128)S(1)} async-done(((f32[32,8,128]{2,1,0:T(8,128)}), f32[32,8,128]{2,1,0:T(8,128)S(1)}, u32[]{:S(2)}, u32[]{:S(2)}) %all-to-all-start.7) | async-done | bytes 131104 | tf_op jit(solution)/shard_map/all_to_all | solution.py:23
  197.8 3.8 %all-to-all-start.8 = ((bf16[16,96,128]{2,1,0:T(8,128)(2,1)}), bf16[16,96,128]{2,1,0:T(8,128)(2,1)S(1)}, u32[]{:S(2)}, u32[]{:S(2)}) async-start(bf16[16,96,128]{2,1,0:T(8,128)(2,1)} %fusion.7), calls=%async_computation.8 | async-start | bytes 786432 | tf_op jit(solution)/shard_map/all_to_all | solution.py:54
  201.6 18.5 %conv_back.1 = (bf16[4096,512]{1,0:T(8,128)(2,1)}, f32[4096,256]{1,0:T(8,128)}, f32[256,1024]{1,0:T(8,128)}, f32[8,512]{1,0:T(8,128)}, f32[8,128]{1,0:T(8,128)}) custom-call(s32[16]{0:T(128)} %sides.19, f32[4096,512]{1,0:T(8,128)} %get-tuple-element.94.second_ref, f32[8,512]{1,0:T(8,128)} %get-tuple-element.99.ab_ref, f32[32,8,128]{2,1,0:T(8,128)} %copy-done.38, ...), custom_call_target="tpu_custom_call" | custom-call | flops 20000000000 | bytes 60000000 | tf_op jit(solution)/shard_map/conv_back/pallas_call | solution.py:1620
  222.1 5.6 %all-to-all-start.9 = ((f32[32,8,128]{2,1,0:T(8,128)}), f32[32,8,128]{2,1,0:T(8,128)S(1)}, u32[]{:S(2)}, u32[]{:S(2)}) async-start(f32[32,8,128]{2,1,0:T(8,128)} %get-tuple-element.137), calls=%async_computation.9 | async-start | bytes 262144 | tf_op jit(solution)/shard_map/all_to_all | solution.py:23
  227.8 9.8 %conv_grad.1 = (bf16[16,144,128]{2,1,0:T(8,128)(2,1)}, bf16[16,144,128]{2,1,0:T(8,128)(2,1)}) custom-call(s32[1]{0:T(128)} %bitcast.odd.refs_1_, bf16[4096,256]{1,0:T(8,128)(2,1)} %get-tuple-element.147.act_ref, bf16[4096,512]{1,0:T(8,128)(2,1)} %get-tuple-element.148.dsecond_ref, bf16[96,128]{1,0:T(8,128)(2,1)} %copy-done.26), custom_call_target="tpu_custom_call" | custom-call | flops 15000000512 | bytes 45000000 | tf_op jit(solution)/shard_map/conv_grad/pallas_call | solution.py:1686
  241.8 6.8 %all-to-all-start.10 = ((bf16[16,208,128]{2,1,0:T(8,128)(2,1)}), bf16[16,208,128]{2,1,0:T(8,128)(2,1)S(1)}, u32[]{:S(2)}, u32[]{:S(2)}) async-start(bf16[16,208,128]{2,1,0:T(8,128)(2,1)} %last_merge.1), calls=%async_computation.10 | async-start | bytes 1703936 | tf_op jit(solution)/shard_map/all_to_all | solution.py:54
  248.7 13.1 %last.1 = (f32[4096,1024]{1,0:T(8,128)}, f32[8,128]{1,0:T(8,128)}) custom-call(s32[16]{0:T(128)} %sides.19, f32[4096,256]{1,0:T(8,128)} %get-tuple-element.128.dfirst_ref, f32[4096,256]{1,0:T(8,128)} %get-tuple-element.90.first_ref, f32[8,256]{1,0:T(8,128)} %copy-done.2, bf16[1024,256]{1,0:T(8,128)(2,1)} %get-tuple-element.142.w_ref, ...), custom_call_target="tpu_custom_call" | custom-call | flops 15000000512 | bytes 45000000 | tf_op jit(solution)/shard_map/last/pallas_call | solution.py:1718
  261.8 8.0 %all-to-all-done.10.part_ref = bf16[16,208,128]{2,1,0:T(8,128)(2,1)S(1)} async-done(((bf16[16,208,128]{2,1,0:T(8,128)(2,1)}), bf16[16,208,128]{2,1,0:T(8,128)(2,1)S(1)}, u32[]{:S(2)}, u32[]{:S(2)}) %all-to-all-start.10) | async-done | bytes 852000 | tf_op jit(solution)/shard_map/all_to_all | solution.py:54
  273.5 2.5 collective-permute-done.10.refs_2_
  (137 shorter events, 27.6 us)
Async XLA Ops:
  2.6 23.0 %all-to-all-start = ((bf16[8,128,128]{2,1,0:T(8,128)(2,1)}), bf16[8,128,128]{2,1,0:T(8,128)(2,1)S(1)}, u32[]{:S(2)}, u32[]{:S(2)}) async-start(bf16[8,128,128]{2,1,0:T(8,128)(2,1)} %get-tuple-element.89), calls=%async_computation | async-start | bytes 524288 | tf_op jit(solution)/shard_map/all_to_all | solution.py:23
  9.8 14.7 %collective-permute-start.1 = (bf16[1,528,128]{2,1,0:T(8,128)(2,1)}, bf16[1,528,128]{2,1,0:T(8,128)(2,1)S(1)}, u32[]{:S(2)}, u32[]{:S(2)}) collective-permute-start(bf16[1,528,128]{2,1,0:T(8,128)(2,1)} %bitcast.73), channel_id=1, source_target_pairs={{0,16},{4,20},{8,24},{12,28},{16,0},{20,4},{24,8},{28,12},{1,17},{... | collective-permute-start | bytes 405512 | tf_op jit(solution)/shard_map/ppermute | solution.py:40
  25.5 7.2 %collective-permute-start.2 = (bf16[2,528,128]{2,1,0:T(8,128)(2,1)S(1)}, bf16[2,528,128]{2,1,0:T(8,128)(2,1)S(1)}, u32[]{:S(2)}, u32[]{:S(2)}) collective-permute-start(bf16[2,528,128]{2,1,0:T(8,128)(2,1)S(1)} %pad_maximum_fusion.1), channel_id=1, source_target_pairs={{0,8},{4,12},{8,0},{12,4},{16,24},{20,28},{24,16},{28,20},{1,9},{5... | collective-permute-start | bytes 811016 | tf_op jit(solution)/shard_map/ppermute | solution.py:40
  25.6 9.8 %collective-permute-start = (bf16[1024,128]{1,0:T(8,128)(2,1)S(1)}, bf16[1024,128]{1,0:T(8,128)(2,1)S(1)}, u32[]{:S(2)}, u32[]{:S(2)}) collective-permute-start(bf16[1024,128]{1,0:T(8,128)(2,1)S(1)} %bitcast.77), channel_id=1, source_target_pairs={{0,1},{1,0},{2,3},{3,2},{4,5},{5,4},{6,7},{7,6},{8,9},{9,8},{10,11... | collective-permute-start | bytes 786440 | tf_op jit(solution)/shard_map/ppermute | solution.py:32
  33.6 13.7 %collective-permute-start.3 = (bf16[4,528,128]{2,1,0:T(8,128)(2,1)S(1)}, bf16[4,528,128]{2,1,0:T(8,128)(2,1)S(1)}, u32[]{:S(2)}, u32[]{:S(2)}) collective-permute-start(bf16[4,528,128]{2,1,0:T(8,128)(2,1)S(1)} %pad_maximum_fusion.refs_2_.refs_0_), channel_id=1, source_target_pairs={{0,4},{4,0},{8,12},{12,8},{16,20},{20,16},{24,28},{28,24},{1,5},{5... | collective-permute-start | bytes 1622024 | tf_op jit(solution)/shard_map/ppermute | solution.py:40
  35.4 21.9 %collective-permute-start.4 = (bf16[4,528,128]{2,1,0:T(8,128)(2,1)S(1)}, bf16[4,528,128]{2,1,0:T(8,128)(2,1)S(1)}, u32[]{:S(2)}, u32[]{:S(2)}) collective-permute-start(bf16[4,528,128]{2,1,0:T(8,128)(2,1)S(1)} %pad_maximum_fusion.refs_2_.refs_0_), channel_id=1, source_target_pairs={{0,1},{1,0},{2,3},{3,2},{4,5},{5,4},{6,7},{7,6},{8,9},{9,8},{10,11... | collective-permute-start | bytes 1622024 | tf_op jit(solution)/shard_map/ppermute | solution.py:32
  43.7 13.5 %all-to-all-start.1 = ((f32[32,8,128]{2,1,0:T(8,128)}), f32[32,8,128]{2,1,0:T(8,128)S(1)}, u32[]{:S(2)}, u32[]{:S(2)}) async-start(f32[32,8,128]{2,1,0:T(8,128)} %get-tuple-element.91), calls=%async_computation.1 | async-start | bytes 262144 | tf_op jit(solution)/shard_map/all_to_all | solution.py:23
  47.3 10.0 %collective-permute-start.5 = (bf16[4,528,128]{2,1,0:T(8,128)(2,1)S(1)}, bf16[4,528,128]{2,1,0:T(8,128)(2,1)S(1)}, u32[]{:S(2)}, u32[]{:S(2)}) collective-permute-start(bf16[4,528,128]{2,1,0:T(8,128)(2,1)S(1)} %collective-permute-done.3.refs_3_.refs_1_), channel_id=1, source_target_pairs={{0,1},{1,0},{2,3},{3,2},{4,5},{5,4},{6,7},{7,6},{8,9},{9,8},{10,11... | collective-permute-start | bytes 1622024 | tf_op jit(solution)/shard_map/ppermute | solution.py:32
  91.8 10.8 %all-to-all-start.3 = ((f32[32,8,128]{2,1,0:T(8,128)}), f32[32,8,128]{2,1,0:T(8,128)S(1)}, u32[]{:S(2)}, u32[]{:S(2)}) async-start(f32[32,8,128]{2,1,0:T(8,128)} %get-tuple-element.101), calls=%async_computation.3 | async-start | bytes 262144 | tf_op jit(solution)/shard_map/all_to_all | solution.py:23
  149.0 10.8 %all-to-all-start.5 = ((bf16[32,16,128]{2,1,0:T(8,128)(2,1)}), bf16[32,16,128]{2,1,0:T(8,128)(2,1)S(1)}, u32[]{:S(2)}, u32[]{:S(2)}) async-start(bf16[32,16,128]{2,1,0:T(8,128)(2,1)} %get-tuple-element.113), calls=%async_computation.5 | async-start | bytes 262144 | tf_op jit(solution)/shard_map/all_to_all | solution.py:23
  160.4 18.6 %copy-start.34 = (f32[256,1024]{1,0:T(8,128)S(1)}, f32[256,1024]{1,0:T(8,128)}, u32[]{:S(2)}) copy-start(f32[256,1024]{1,0:T(8,128)} %get-tuple-element.132) | copy-start | bytes 3145732
  160.4 18.6 %copy-start.35 = (f32[256,1024]{1,0:T(8,128)S(1)}, f32[256,1024]{1,0:T(8,128)}, u32[]{:S(2)}) copy-start(f32[256,1024]{1,0:T(8,128)} %get-tuple-element.129) | copy-start | bytes 3145732
  173.0 11.9 %copy-start.9 = (s32[16]{0:T(128)S(1)}, s32[16]{0:T(128)}, u32[]{:S(2)}) copy-start(s32[16]{0:T(128)} %sides.19) | copy-start | bytes 196
  173.0 11.9 %copy-start.15 = (f32[5,16,512]{2,1,0:T(8,128)S(1)}, f32[5,16,512]{2,1,0:T(8,128)}, u32[]{:S(2)}) copy-start(f32[5,16,512]{2,1,0:T(8,128)} %get-tuple-element.122.sums_ref) | copy-start | bytes 491524
  173.1 11.9 %copy-start.16 = (bf16[256,128]{1,0:T(8,128)(2,1)S(1)}, bf16[256,128]{1,0:T(8,128)(2,1)}, u32[]{:S(2)}) copy-start(bf16[256,128]{1,0:T(8,128)(2,1)} %get-tuple-element.98.down_ref) | copy-start | bytes 196612
  173.1 11.9 %copy-start.18 = (bf16[16,256]{1,0:T(8,128)(2,1)S(1)}, bf16[16,256]{1,0:T(8,128)(2,1)}, u32[]{:S(2)}) copy-start(bf16[16,256]{1,0:T(8,128)(2,1)} %get-tuple-element.105._.pooled_ref) | copy-start | bytes 24580
  173.1 11.9 %copy-start.19 = (f32[8,1024]{1,0:T(8,128)S(1)}, f32[8,1024]{1,0:T(8,128)}, u32[]{:S(2)}) copy-start(f32[8,1024]{1,0:T(8,128)} %get-tuple-element.114.terms_ref) | copy-start | bytes 98308
  173.1 11.9 %copy-start.20 = (f32[16,512]{1,0:T(8,128)S(1)}, f32[16,512]{1,0:T(8,128)}, u32[]{:S(2)}) copy-start(f32[16,512]{1,0:T(8,128)} %get-tuple-element.115.weights_ref) | copy-start | bytes 98308
  173.1 11.9 %copy-start.21 = (f32[8,512]{1,0:T(8,128)S(1)}, f32[8,512]{1,0:T(8,128)}, u32[]{:S(2)}) copy-start(f32[8,512]{1,0:T(8,128)} %get-tuple-element.96.param_ref) | copy-start | bytes 49156
  173.1 11.9 %copy-start.24 = (f32[16,128]{1,0:T(8,128)S(1)}, f32[16,128]{1,0:T(8,128)}, u32[]{:S(2)}) copy-start(f32[16,128]{1,0:T(8,128)} %get-tuple-element.100.squeeze_ref) | copy-start | bytes 24580
  174.1 10.8 %all-to-all-start.6 = ((f32[32,8,128]{2,1,0:T(8,128)}), f32[32,8,128]{2,1,0:T(8,128)S(1)}, u32[]{:S(2)}, u32[]{:S(2)}) async-start(f32[32,8,128]{2,1,0:T(8,128)} %get-tuple-element.121), calls=%async_computation.6 | async-start | bytes 262144 | tf_op jit(solution)/shard_map/all_to_all | solution.py:23
  187.0 10.8 %all-to-all-start.7 = ((f32[32,8,128]{2,1,0:T(8,128)}), f32[32,8,128]{2,1,0:T(8,128)S(1)}, u32[]{:S(2)}, u32[]{:S(2)}) async-start(f32[32,8,128]{2,1,0:T(8,128)} %get-tuple-element.123), calls=%async_computation.7 | async-start | bytes 262144 | tf_op jit(solution)/shard_map/all_to_all | solution.py:23
  189.7 1.8 collective-permute-start.6
  197.8 22.3 %all-to-all-start.8 = ((bf16[16,96,128]{2,1,0:T(8,128)(2,1)}), bf16[16,96,128]{2,1,0:T(8,128)(2,1)S(1)}, u32[]{:S(2)}, u32[]{:S(2)}) async-start(bf16[16,96,128]{2,1,0:T(8,128)(2,1)} %fusion.7), calls=%async_computation.8 | async-start | bytes 786432 | tf_op jit(solution)/shard_map/all_to_all | solution.py:54
  222.1 16.3 %all-to-all-start.9 = ((f32[32,8,128]{2,1,0:T(8,128)}), f32[32,8,128]{2,1,0:T(8,128)S(1)}, u32[]{:S(2)}, u32[]{:S(2)}) async-start(f32[32,8,128]{2,1,0:T(8,128)} %get-tuple-element.137), calls=%async_computation.9 | async-start | bytes 262144 | tf_op jit(solution)/shard_map/all_to_all | solution.py:23
  237.6 3.2 %collective-permute-start.7 = (bf16[16,144,128]{2,1,0:T(8,128)(2,1)}, bf16[16,144,128]{2,1,0:T(8,128)(2,1)S(1)}, u32[]{:S(2)}, u32[]{:S(2)}) collective-permute-start(bf16[16,144,128]{2,1,0:T(8,128)(2,1)} %get-tuple-element.150), channel_id=1, source_target_pairs={{0,1},{1,0},{2,3},{3,2},{4,5},{5,4},{6,7},{7,6},{8,9},{9,8},{10,11... | collective-permute-start | bytes 1769480 | tf_op jit(solution)/shard_map/ppermute | solution.py:32
  239.0 1.7 collective-permute-start.8
  241.8 28.0 %all-to-all-start.10 = ((bf16[16,208,128]{2,1,0:T(8,128)(2,1)}), bf16[16,208,128]{2,1,0:T(8,128)(2,1)S(1)}, u32[]{:S(2)}, u32[]{:S(2)}) async-start(bf16[16,208,128]{2,1,0:T(8,128)(2,1)} %last_merge.1), calls=%async_computation.10 | async-start | bytes 1703936 | tf_op jit(solution)/shard_map/all_to_all | solution.py:54
  248.7 21.1 %copy-start.27 = (bf16[96,128]{1,0:T(8,128)(2,1)S(1)}, bf16[96,128]{1,0:T(8,128)(2,1)}, u32[]{:S(2)}) copy-start(bf16[96,128]{1,0:T(8,128)(2,1)} %copy-done.26) | copy-start | bytes 73732
  270.7 5.3 %collective-permute-start.10 = (bf16[304,128]{1,0:T(8,128)(2,1)S(1)}, bf16[304,128]{1,0:T(8,128)(2,1)S(1)}, u32[]{:S(2)}, u32[]{:S(2)}) collective-permute-start(bf16[304,128]{1,0:T(8,128)(2,1)S(1)} %last_total.1.refs_0_), channel_id=1, source_target_pairs={{0,2},{1,3},{2,0},{3,1},{4,6},{5,7},{6,4},{7,5},{8,10},{9,11},{10,... | collective-permute-start | bytes 233480 | tf_op jit(solution)/shard_map/ppermute | solution.py:1773
  271.3 4.7 %collective-permute-start.11 = (bf16[304,128]{1,0:T(8,128)(2,1)S(1)}, bf16[304,128]{1,0:T(8,128)(2,1)S(1)}, u32[]{:S(2)}, u32[]{:S(2)}) collective-permute-start(bf16[304,128]{1,0:T(8,128)(2,1)S(1)} %last_total.1.refs_0_), channel_id=1, source_target_pairs={{0,3},{1,2},{2,1},{3,0},{4,7},{5,6},{6,5},{7,4},{8,11},{9,10},{10,... | collective-permute-start | bytes 233480 | tf_op jit(solution)/shard_map/ppermute | solution.py:1773
  271.3 4.7 %collective-permute-start.9 = (bf16[304,128]{1,0:T(8,128)(2,1)S(1)}, bf16[304,128]{1,0:T(8,128)(2,1)S(1)}, u32[]{:S(2)}, u32[]{:S(2)}) collective-permute-start(bf16[304,128]{1,0:T(8,128)(2,1)S(1)} %last_total.1.refs_0_), channel_id=1, source_target_pairs={{0,1},{1,0},{2,3},{3,2},{4,5},{5,4},{6,7},{7,6},{8,9},{9,8},{10,11... | collective-permute-start | bytes 233480 | tf_op jit(solution)/shard_map/ppermute | solution.py:1773
  (31 other events, 181.7 us)

commit v6 on v5

--- a/solution.py
+++ b/solution.py
@@ -73,6 +73,15 @@
 
 def wide(mask, lanes):
     return jnp.concatenate([mask] * (lanes // mask.shape[1]), axis=1)
+
+
+def half_silu(half, mask):
+    return half * ((1.0 + jnp.tanh(half)) * mask)
+
+
+def twice_slope(half):
+    turned = jnp.tanh(half)
+    return (1.0 + turned) * (1.0 + half * (1.0 - turned))
 
 
 def places():
@@ -215,8 +224,8 @@
     return jnp.broadcast_to(jnp.sum(row, axis=1, keepdims=True), (1, 128))
 
 
-def prepare_kernel(odd, in_ref, mid_ref, down_ref, up_ref, out_ref, *refs):
-    *vector_refs, in_send, most_send, rows_ref = refs
+def prepare_kernel(odd, mid_ref, down_ref, up_ref, out_ref, *refs):
+    *vector_refs, most_send, rows_ref = refs
     rows_ref[...] = jnp.zeros(rows_ref.shape, f32)
     for k, ref in enumerate(vector_refs):
         rows_ref[k : k + 1, : ref.shape[1]] = ref[...].astype(f32)
@@ -229,8 +238,6 @@
 
         @pl.when(odd[0] == side)
         def _():
-            for j in range(in_send.shape[0]):
-                in_send[j] = in_ref[:, side * 128 : side * 128 + 128]
             at = mid_ref.shape[1]
             most_send[:at, :] = mid_ref[side]
             most_send[at : at + 128, :] = jnp.transpose(out_ref[side * 128 : side * 128 + 128, :])
@@ -280,22 +287,25 @@
 ):
     step = pl.program_id(0)
     zeros_at_start(cross_ref, square_ref, ones_ref)
-    cross_ref[...] += contract_lead(first_ref[...].astype(bf16), x_ref[...])
     place = places()
     lanes = x_ref.shape[1]
-    for image in range(STEP):
+    sums = [square_ref[...], ones_ref[...]]
+
+    def multiply(image):
+        here = of_image(image)
+        cross_ref[...] += contract_lead(first_ref[here, :].astype(bf16), x_ref[here, :])
+
+    def add_up(image):
         limit = 2 * sides[step * STEP + image]
-
-        def body(row, carry):
-            square, total = carry
-            values = x_ref[chunk(image, row), :].astype(f32) * wide(
+        for row in range(SIDE):
+            values = x_ref[of_row(image, row), :].astype(f32) * wide(
                 row_mask(place, row, limit), lanes
             )
-            return (square + fold(values * values), total + fold(values))
-
-        square, total = rows_of((square_ref[...], ones_ref[...]), body)
-        square_ref[...] = square
-        ones_ref[...] = total
+            sums[0] = sums[0] + fold(values * values)
+            sums[1] = sums[1] + fold(values)
+
+    stages(multiply, add_up)
+    square_ref[...], ones_ref[...] = sums
 
     @at_end
     def _():
@@ -396,13 +406,17 @@
         terms_ref[2:3, :] = inv
         terms_ref[3:4, :] = -center * inv
         terms_ref[4:5, :] = center
+        terms_ref[5:6, :] = 0.5 * scale
+        terms_ref[6:7, :] = 0.5 * offset
 
     def start_image(image):
         limit = 2 * sides[step * STEP + image]
         for row in range(SIDE):
             here = slice(image * 256 + row * SIDE, image * 256 + row * SIDE + SIDE)
-            pre = first_ref[here, :] * terms_ref[0:1, :] + terms_ref[1:2, :]
-            act = pre * (sigmoid(pre) * wide(row_mask(place, row, limit), lanes))
+            act = half_silu(
+                first_ref[here, :] * terms_ref[5:6, :] + terms_ref[6:7, :],
+                wide(row_mask(place, row, limit), lanes),
+            )
             low = act.astype(bf16)
             act_ref[here, :] = low
             write_patches(patch_ref, image, row, low, place)
@@ -474,16 +488,20 @@
         )
         terms_ref[0:1, :] = scale
         terms_ref[1:2, :] = offset
+        terms_ref[2:3, :] = 0.5 * scale
+        terms_ref[3:4, :] = 0.5 * offset
 
     for image in range(STEP):
         limit = 2 * sides[step * STEP + image]
 
-        def body(row, total):
-            pre = second_ref[chunk(image, row), :] * terms_ref[0:1, :] + terms_ref[1:2, :]
-            act = pre * (sigmoid(pre) * wide(row_mask(place, row, limit), lanes))
-            return total + fold(act)
-
-        total = column_total(rows_of(jnp.zeros((8, lanes), f32), body))
+        total = jnp.zeros((8, lanes), f32)
+        for row in range(SIDE):
+            act = half_silu(
+                second_ref[of_row(image, row), :] * terms_ref[2:3, :] + terms_ref[3:4, :],
+                wide(row_mask(place, row, limit), lanes),
+            )
+            total = total + fold(act)
+        total = column_total(total)
         both = total[:, : lanes // 2] + total[:, lanes // 2 :]
         area = jnp.full(both.shape, limit * limit, jnp.int32).astype(f32)
         pool_ref[pl.ds(step * STEP + image, 1), :] = both / area
@@ -580,8 +598,10 @@
         weights = weights_ref[pl.ds(step * STEP + image, 1), :]
         for row in range(SIDE):
             here = of_row(image, row)
-            pre = second_ref[here, :] * ab_ref[0:1, :] + ab_ref[1:2, :]
-            act = pre * (sigmoid(pre) * wide(row_mask(place, row, limit), lanes))
+            act = half_silu(
+                second_ref[here, :] * ab_ref[2:3, :] + ab_ref[3:4, :],
+                wide(row_mask(place, row, limit), lanes),
+            )
             act = act * weights
             mixed = act[:, :half] + act[:, half:]
             low = mixed.astype(bf16)
@@ -714,11 +734,11 @@
 
 
 def mid_terms(second_ref, ab_ref, here, mask):
-    pre = second_ref[here, :] * ab_ref[0:1, :] + ab_ref[1:2, :]
-    plain = sigmoid(pre)
-    gate = plain * mask
-    act = pre * gate
-    return pre, act, gate + act * (1.0 - plain)
+    half = second_ref[here, :] * ab_ref[2:3, :] + ab_ref[3:4, :]
+    turned = jnp.tanh(half)
+    gate = (1.0 + turned) * mask
+    act = half * gate
+    return half, act, gate + act * (1.0 - turned)
 
 
 def gate_kernel(
@@ -796,7 +816,8 @@
             terms = (act * both, along, along * pre, slope, slope * pre)
             totals = [old + fold(new) for old, new in zip(totals, terms)]
         for index in range(5):
-            sums_ref[index, pl.ds(step * STEP + image, 1), :] = column_total(totals[index])
+            part = column_total(totals[index]) * (0.5 if index in (1, 3) else 1.0)
+            sums_ref[index, pl.ds(step * STEP + image, 1), :] = part
 
     stages(turn, add_up)
 
@@ -932,19 +953,18 @@
 
     def start(image):
         limit = 2 * sides[step * STEP + image]
-        weights = weights_ref[pl.ds(step * STEP + image, 1), :] * ab_ref[0:1, :]
+        weights = weights_ref[pl.ds(step * STEP + image, 1), :] * ab_ref[2:3, :]
         dpool = dpool_ref[pl.ds(step * STEP + image, 1), :]
-        dpool = jnp.concatenate([dpool, dpool], axis=1) * ab_ref[0:1, :]
+        dpool = jnp.concatenate([dpool, dpool], axis=1) * ab_ref[2:3, :]
+        slant, level = 2.0 * grads_ref[2:3, :], grads_ref[3:4, :]
         for row in range(SIDE):
             here = of_row(image, row)
             mask = wide(row_mask(place, row, limit), lanes)
             dmixed = dmixed_ref[here, :]
             both = jnp.concatenate([dmixed, dmixed], axis=1)
-            pre = second_ref[here, :] * ab_ref[0:1, :] + ab_ref[1:2, :]
-            plain = sigmoid(pre)
-            slope = plain + pre * plain * (1.0 - plain)
-            grad = slope * (weights * both + dpool)
-            grad = mask * (grad - (pre * grads_ref[2:3, :] + grads_ref[3:4, :]))
+            pre = second_ref[here, :] * ab_ref[2:3, :] + ab_ref[3:4, :]
+            grad = twice_slope(pre) * (weights * both + dpool)
+            grad = mask * (grad - (pre * slant + level))
             dsecond_ref[here, :] = grad.astype(bf16)
 
     def multiply(image):
@@ -980,10 +1000,9 @@
                 parts.append(summed[1] + low + high)
             dact = jnp.concatenate(parts, axis=1)
             first = first_ref[here, :]
-            pre = first * ab_in_ref[0:1, :] + ab_in_ref[1:2, :]
+            pre = first * ab_in_ref[5:6, :] + ab_in_ref[6:7, :]
             normed = first * ab_in_ref[2:3, :] + ab_in_ref[3:4, :]
-            plain = sigmoid(pre)
-            grad = dact * (plain * (1.0 + pre * (1.0 - plain)) * wide(mask, half))
+            grad = dact * (twice_slope(pre) * wide(0.5 * mask, half))
             dfirst_ref[here, :] = grad
             sums[0] = sums[0] + fold(grad)
             sums[1] = sums[1] + fold(grad * normed)
@@ -1265,12 +1284,11 @@
         place = lax.axis_index("fsdp").reshape(1)
         at = TAPS * own_columns
         cut = (at + 128 + down_rows + up_rows + 16, 128)
-        in_send, most = call(
+        (most,) = call(
             prepare_kernel,
             1,
             [
                 scalars(),
-                held(*conv_in.shape),
                 held(RADIX, at, 128),
                 held(*attn_down.shape),
                 held(up_rows, att),
@@ -1278,7 +1296,6 @@
             ]
             + [held(1, length) for length in lengths],
             [
-                whole_out((pieces, conv_in.shape[0], 128), bf16),
                 whole_out(cut, bf16),
             ],
             [((16, 128), f32)],
@@ -1287,18 +1304,18 @@
             name="last_prepare",
         )(
             odd,
-            conv_in,
             mid_cut.reshape(RADIX, at, 128),
             attn_down,
             attn_up.T,
             conv_out,
             *[item.reshape(1, -1) for item in small],
         )
-        in_mine = swap_all(in_send, "fsdp").reshape(width, bottleneck // 2)
+        most = most[None]
+        got = partner(most, 4)
+        half, _ = lax.optimization_barrier((half_of(conv_in, 1), got))
+        in_mine = gather_all(half).reshape(width, bottleneck // 2)
         in_other = neighbour(in_mine)
-
-        most = most[None]
-        most = jnp.concatenate([most, partner(most, 4)], axis=0)
+        most = jnp.concatenate([most, got], axis=0)
         most = jnp.concatenate([most, partner(most, 2)], axis=0)
         shards = [most, partner(most, 1)]
         shards += [neighbour(item) for item in shards]

time: 279 us -> 275 us (0.986)
  Pallas kernels: 129 us -> 126 us
    ppermute x3, waiting for transfers between devices: 18.8 us -> 9.31 us  [partner(): return lax.ppermute(values, 'fsdp', [(i, i ^ k) for i in range(pieces)])]
    all_to_all x7, waiting for transfers between devices: 24.2 us -> 31.2 us  [swap_all(): return lax.all_to_all(values, axes, 0, 0)]
    ppermute x3, starting transfers between devices: 4.77 us -> 7.75 us  [partner(): return lax.ppermute(values, 'fsdp', [(i, i ^ k) for i in range(pieces)])]
    unnamed x84 -> x88, local copies, waits for them, and re-layouts: 7.98 us -> 7.98 us
  transfers between devices with their start and end apart: 21 -> 21, of which waited for: 9 -> 10; matrix products, arithmetic and copies ran while one was open for 3% -> 3% of each run, Pallas kernels for 21% -> 21%
where the time goes in v6:
time: 275 us; the launch traced here: 273 us
  Pallas kernels  126 us (46%)
  waiting for transfers between devices  52.1 us (19%)
  starting transfers between devices  47 us (17%)
  blocking collectives  28 us (10%)
  local copies, waits for them, and re-layouts  14.8 us (5%)
  other arithmetic  4.04 us (1%)
    all_to_all x7, waiting for transfers between devices, swap_all(): return lax.all_to_all(values, axes, 0, 0)  31.2 us
    all_to_all x2, blocking collectives, swap_all(): return lax.all_to_all(values, axes, 0, 0)  28 us
    all_to_all x7, starting transfers between devices, swap_all(): return lax.all_to_all(values, axes, 0, 0)  25.8 us
    pallas_call x1, Pallas kernels, local(): call(out_kernel, steps, [scalars(), tiles(bottleneck), tiles(width), tile...  22.6 us
    pallas_call x1, Pallas kernels, local(): call(conv_back_kernel, steps, [scalars(), tiles(mid), held(8, mid), recei...  17.8 us
    pallas_call x1, Pallas kernels, local(): call(last_kernel, steps, [scalars(), tiles(bottleneck), tiles(bottleneck)...  13.1 us
    pallas_call x1, Pallas kernels, local(): call(functools.partial(second_kernel, lengths if aligned else None), step...  12.3 us
    pallas_call x1, Pallas kernels, local(): call(gate_kernel, steps, [scalars(), tiles(mid), held(8, mid), tiles(bott...  12.2 us
  transfers between devices with their start and end apart: 21, of which 10 were waited for; matrix products, arithmetic and copies ran while one was open for 3% of the time, Pallas kernels for 21%

profile of v6, /device:TPU:0, one launch (start us, length us, event | category | flops | bytes accessed | tf_op | source)
XLA Modules:
  0.0 273.1 jit_solution(15472149664165988010)
XLA Ops:
  2.5 4.0 %collective-permute-start = (bf16[1,528,128]{2,1,0:T(8,128)(2,1)}, bf16[1,528,128]{2,1,0:T(8,128)(2,1)S(1)}, u32[]{:S(2)}, u32[]{:S(2)}) collective-permute-start(bf16[1,528,128]{2,1,0:T(8,128)(2,1)} %bitcast.73), channel_id=1, source_target_pairs={{0,16},{4,20},{8,24},{12,28},{16,0},{20,4},{24,8},{28,12},{1,17},{... | collective-permute-start | bytes 405512 | tf_op jit(solution)/shard_map/ppermute | solution.py:40
  6.5 6.7 %collective-permute-done = bf16[1,528,128]{2,1,0:T(8,128)(2,1)S(1)} collective-permute-done((bf16[1,528,128]{2,1,0:T(8,128)(2,1)}, bf16[1,528,128]{2,1,0:T(8,128)(2,1)S(1)}, u32[]{:S(2)}, u32[]{:S(2)}) %collective-permute-start) | collective-permute-done | bytes 135200 | tf_op jit(solution)/shard_map/ppermute | solution.py:40
  14.0 5.7 %all-to-all-start = ((bf16[8,128,128]{2,1,0:T(8,128)(2,1)}), bf16[8,128,128]{2,1,0:T(8,128)(2,1)S(1)}, u32[]{:S(2)}, u32[]{:S(2)}) async-start(bf16[8,128,128]{2,1,0:T(8,128)(2,1)} %broadcast_in_dim.15), calls=%async_computation | async-start | bytes 524288 | tf_op jit(solution)/shard_map/all_to_all | solution.py:23
  20.6 2.1 collective-permute-start.2
  22.7 7.0 %all-to-all-done = bf16[8,128,128]{2,1,0:T(8,128)(2,1)S(1)} async-done(((bf16[8,128,128]{2,1,0:T(8,128)(2,1)}), bf16[8,128,128]{2,1,0:T(8,128)(2,1)S(1)}, u32[]{:S(2)}, u32[]{:S(2)}) %all-to-all-start) | async-done | bytes 262176 | tf_op jit(solution)/shard_map/all_to_all | solution.py:23
  29.7 2.6 collective-permute-done.2
  35.7 7.7 %first.1 = (f32[4096,256]{1,0:T(8,128)}, bf16[1024,256]{1,0:T(8,128)(2,1)}, f32[32,8,128]{2,1,0:T(8,128)}) custom-call(s32[16]{0:T(128)} %sides.19, s32[1]{0:T(128)} %bitcast.odd.refs_1_, bf16[4096,1024]{1,0:T(8,128)(2,1)} %bitcast.84, bf16[1024,128]{1,0:T(8,128)(2,1)} %bitcast.78, bf16[1024,128]{1,0:T(8,128)(2,1)} %copy-done.43), custom_call_target="tpu_custom_call" | custom-call | flops 8000000000 | bytes 24000000 | tf_op jit(solution)/shard_map/first/pallas_call | solution.py:1345
  43.3 3.6 %all-to-all-start.1 = ((f32[32,8,128]{2,1,0:T(8,128)}), f32[32,8,128]{2,1,0:T(8,128)S(1)}, u32[]{:S(2)}, u32[]{:S(2)}) async-start(f32[32,8,128]{2,1,0:T(8,128)} %get-tuple-element.90), calls=%async_computation.1 | async-start | bytes 262144 | tf_op jit(solution)/shard_map/all_to_all | solution.py:23
  47.3 8.7 %cross.1 = (f32[256,1024]{1,0:T(8,128)}, f32[8,1024]{1,0:T(8,128)}, f32[8,128]{1,0:T(8,128)}) custom-call(s32[16]{0:T(128)} %sides.19, bf16[4096,1024]{1,0:T(8,128)(2,1)} %bitcast.85, f32[4096,256]{1,0:T(8,128)} %get-tuple-element.89.first_ref), custom_call_target="tpu_custom_call" | custom-call | flops 10000000000 | bytes 30000000 | tf_op jit(solution)/shard_map/cross/pallas_call | solution.py:1355
  57.0 12.3 %second.1 = (bf16[4096,256]{1,0:T(8,128)(2,1)}, f32[4096,512]{1,0:T(8,128)}, f32[8,256]{1,0:T(8,128)}, f32[8,128]{1,0:T(8,128)}, f32[32,8,128]{2,1,0:T(8,128)}, ...) custom-call(s32[16]{0:T(128)} %sides.19, ...), custom_call_target="tpu_custom_call" | custom-call | flops 15000000512 | bytes 45000000 | tf_op jit(solution)/shard_map/second/pallas_call | solution.py:1401
  69.2 14.1 %all_to_all.55.recv_ref = f32[32,8,128]{2,1,0:T(8,128)} all-to-all(f32[32,8,128]{2,1,0:T(8,128)} %get-tuple-element.93), channel_id=1, replica_groups=mesh['fsdp'=8,'dp'=4] {'fsdp','dp'}, dimensions={0} | all-to-all | bytes 262144 | tf_op jit(solution)/shard_map/all_to_all | solution.py:23
  83.3 6.2 %pool.1 = (bf16[16,256]{1,0:T(8,128)(2,1)}, f32[16,128]{1,0:T(8,128)}, f32[8,512]{1,0:T(8,128)}, f32[32,8,128]{2,1,0:T(8,128)}) custom-call(s32[16]{0:T(128)} %sides.19, f32[4096,512]{1,0:T(8,128)} %get-tuple-element.92.second_ref, f32[32,8,128]{2,1,0:T(8,128)} %all_to_all.55.recv_ref, f32[8,512]{1,0:T(8,128)} %get-tuple-element.94.param_ref, ...), custom_call_target="tpu_custom_call" | custom-call | flops 7000000000 | bytes 21000000 | tf_op jit(solution)/shard_map/pool/pallas_call | solution.py:1414
  89.5 2.6 all-to-all-start.3
  94.7 5.6 %all-to-all-done.3.recv_ref = f32[32,8,128]{2,1,0:T(8,128)S(1)} async-done(((f32[32,8,128]{2,1,0:T(8,128)}), f32[32,8,128]{2,1,0:T(8,128)S(1)}, u32[]{:S(2)}, u32[]{:S(2)}) %all-to-all-start.3) | async-done | bytes 131104 | tf_op jit(solution)/shard_map/all_to_all | solution.py:23
  101.0 8.8 %mix.1 = (bf16[4096,256]{1,0:T(8,128)(2,1)}, f32[16,512]{1,0:T(8,128)}, bf16[16,128]{1,0:T(8,128)(2,1)}, f32[8,128]{1,0:T(8,128)}, f32[256,1024]{1,0:T(8,128)}, ...) custom-call(s32[16]{0:T(128)} %sides.19, f32[4096,512]{1,0:T(8,128)} %get-tuple-element.92.second_ref, ...), custom_call_target="tpu_custom_call" | custom-call | flops 11000000512 | bytes 33000000 | tf_op jit(solution)/shard_map/mix/pallas_call | solution.py:1452
  109.8 13.9 %all_to_all.56.recv_ref = f32[32,16,128]{2,1,0:T(8,128)} all-to-all(f32[32,16,128]{2,1,0:T(8,128)} %get-tuple-element.106), channel_id=1, replica_groups=mesh['fsdp'=8,'dp'=4] {'fsdp','dp'}, dimensions={0} | all-to-all | bytes 524288 | tf_op jit(solution)/shard_map/all_to_all | solution.py:23
  123.7 22.6 %output.1 = (bf16[4096,1024]{1,0:T(8,128)(2,1)}, bf16[4096,1024]{1,0:T(8,128)(2,1)}, f32[4096,256]{1,0:T(8,128)}, f32[256,1024]{1,0:T(8,128)}, f32[8,1024]{1,0:T...) custom-call(s32[16]{0:T(128)} %sides.19, bf16[4096,256]{1,0:T(8,128)(2,1)} %get-tuple-element.105.mixed_ref, ...), custom_call_target="tpu_custom_call" | custom-call | flops 24999999488 | bytes 75000000 | tf_op jit(solution)/shard_map/output/pallas_call | solution.py:1482
  146.3 2.6 all-to-all-start.5
  149.6 7.5 %all-to-all-done.5.recv_ref = bf16[32,16,128]{2,1,0:T(8,128)(2,1)S(1)} async-done(((bf16[32,16,128]{2,1,0:T(8,128)(2,1)}), bf16[32,16,128]{2,1,0:T(8,128)(2,1)S(1)}, u32[]{:S(2)}, u32[]{:S(2)}) %all-to-all-start.5) | async-done | bytes 131104 | tf_op jit(solution)/shard_map/all_to_all | solution.py:23
  157.8 12.2 %gate.1 = (f32[4096,256]{1,0:T(8,128)}, f32[5,16,512]{2,1,0:T(8,128)}, f32[512,128]{1,0:T(8,128)}, f32[8,512]{1,0:T(8,128)}, f32[16,128]{1,0:T(8,128)}, /*index=5*/f32[8,1024]{1,0:T(8,128)}, f32[32,8,128]{2,1,0:T(8,128)}) custom-call(s32[16]{0:T(128)} %sides.19, f32[4096,512]{1,0:T(8,128)} %get-tuple-element.92.second_ref, ...), custom_call_target="tpu_custom_call" | custom-call | flops 12999999488 | bytes 39000000 | tf_op jit(solution)/shard_map/gate/pallas_call | solution.py:1517
  171.0 2.6 all-to-all-start.6
  176.2 5.6 %all-to-all-done.6.recv_ref = f32[32,8,128]{2,1,0:T(8,128)S(1)} async-done(((f32[32,8,128]{2,1,0:T(8,128)}), f32[32,8,128]{2,1,0:T(8,128)S(1)}, u32[]{:S(2)}, u32[]{:S(2)}) %all-to-all-start.6) | async-done | bytes 131104 | tf_op jit(solution)/shard_map/all_to_all | solution.py:23
  184.0 2.6 all-to-all-start.7
  189.3 5.4 %all-to-all-done.7.recv_ref = f32[32,8,128]{2,1,0:T(8,128)S(1)} async-done(((f32[32,8,128]{2,1,0:T(8,128)}), f32[32,8,128]{2,1,0:T(8,128)S(1)}, u32[]{:S(2)}, u32[]{:S(2)}) %all-to-all-start.7) | async-done | bytes 131104 | tf_op jit(solution)/shard_map/all_to_all | solution.py:23
  194.8 3.6 %all-to-all-start.8 = ((bf16[16,96,128]{2,1,0:T(8,128)(2,1)}), bf16[16,96,128]{2,1,0:T(8,128)(2,1)S(1)}, u32[]{:S(2)}, u32[]{:S(2)}) async-start(bf16[16,96,128]{2,1,0:T(8,128)(2,1)} %fusion.7), calls=%async_computation.8 | async-start | bytes 786432 | tf_op jit(solution)/shard_map/all_to_all | solution.py:54
  198.3 17.8 %conv_back.1 = (bf16[4096,512]{1,0:T(8,128)(2,1)}, f32[4096,256]{1,0:T(8,128)}, f32[256,1024]{1,0:T(8,128)}, f32[8,512]{1,0:T(8,128)}, f32[8,128]{1,0:T(8,128)}) custom-call(s32[16]{0:T(128)} %sides.19, f32[4096,512]{1,0:T(8,128)} %get-tuple-element.92.second_ref, f32[8,512]{1,0:T(8,128)} %get-tuple-element.97.ab_ref, f32[32,8,128]{2,1,0:T(8,128)} %copy-done.40, ...), custom_call_target="tpu_custom_call" | custom-call | flops 20000000000 | bytes 60000000 | tf_op jit(solution)/shard_map/conv_back/pallas_call | solution.py:1637
  218.2 6.1 %all-to-all-start.9 = ((f32[32,8,128]{2,1,0:T(8,128)}), f32[32,8,128]{2,1,0:T(8,128)S(1)}, u32[]{:S(2)}, u32[]{:S(2)}) async-start(f32[32,8,128]{2,1,0:T(8,128)} %get-tuple-element.135), calls=%async_computation.9 | async-start | bytes 262144 | tf_op jit(solution)/shard_map/all_to_all | solution.py:23
  224.3 9.8 %conv_grad.1 = (bf16[16,144,128]{2,1,0:T(8,128)(2,1)}, bf16[16,144,128]{2,1,0:T(8,128)(2,1)}) custom-call(s32[1]{0:T(128)} %bitcast.odd.refs_1_, bf16[4096,256]{1,0:T(8,128)(2,1)} %get-tuple-element.145.act_ref, bf16[4096,512]{1,0:T(8,128)(2,1)} %get-tuple-element.146.dsecond_ref, bf16[96,128]{1,0:T(8,128)(2,1)} %copy-done.28), custom_call_target="tpu_custom_call" | custom-call | flops 15000000512 | bytes 45000000 | tf_op jit(solution)/shard_map/conv_grad/pallas_call | solution.py:1703
  238.3 6.6 %all-to-all-start.10 = ((bf16[16,208,128]{2,1,0:T(8,128)(2,1)}), bf16[16,208,128]{2,1,0:T(8,128)(2,1)S(1)}, u32[]{:S(2)}, u32[]{:S(2)}) async-start(bf16[16,208,128]{2,1,0:T(8,128)(2,1)} %last_merge.1), calls=%async_computation.10 | async-start | bytes 1703936 | tf_op jit(solution)/shard_map/all_to_all | solution.py:54
  245.0 13.1 %last.1 = (f32[4096,1024]{1,0:T(8,128)}, f32[8,128]{1,0:T(8,128)}) custom-call(s32[16]{0:T(128)} %sides.19, f32[4096,256]{1,0:T(8,128)} %get-tuple-element.126.dfirst_ref, f32[4096,256]{1,0:T(8,128)} %get-tuple-element.89.first_ref, f32[8,256]{1,0:T(8,128)} %copy-done.4, bf16[1024,256]{1,0:T(8,128)(2,1)} %get-tuple-element.140.w_ref, ...), custom_call_target="tpu_custom_call" | custom-call | flops 15000000512 | bytes 45000000 | tf_op jit(solution)/shard_map/last/pallas_call | solution.py:1735
  258.1 8.1 %all-to-all-done.10.part_ref = bf16[16,208,128]{2,1,0:T(8,128)(2,1)S(1)} async-done(((bf16[16,208,128]{2,1,0:T(8,128)(2,1)}), bf16[16,208,128]{2,1,0:T(8,128)(2,1)S(1)}, u32[]{:S(2)}, u32[]{:S(2)}) %all-to-all-start.10) | async-done | bytes 852000 | tf_op jit(solution)/shard_map/all_to_all | solution.py:54
  269.7 2.5 collective-permute-done.10.refs_2_
  (143 shorter events, 31.7 us)
Async XLA Ops:
  2.5 10.7 %collective-permute-start = (bf16[1,528,128]{2,1,0:T(8,128)(2,1)}, bf16[1,528,128]{2,1,0:T(8,128)(2,1)S(1)}, u32[]{:S(2)}, u32[]{:S(2)}) collective-permute-start(bf16[1,528,128]{2,1,0:T(8,128)(2,1)} %bitcast.73), channel_id=1, source_target_pairs={{0,16},{4,20},{8,24},{12,28},{16,0},{20,4},{24,8},{28,12},{1,17},{... | collective-permute-start | bytes 405512 | tf_op jit(solution)/shard_map/ppermute | solution.py:40
  14.0 15.8 %all-to-all-start = ((bf16[8,128,128]{2,1,0:T(8,128)(2,1)}), bf16[8,128,128]{2,1,0:T(8,128)(2,1)S(1)}, u32[]{:S(2)}, u32[]{:S(2)}) async-start(bf16[8,128,128]{2,1,0:T(8,128)(2,1)} %broadcast_in_dim.15), calls=%async_computation | async-start | bytes 524288 | tf_op jit(solution)/shard_map/all_to_all | solution.py:23
  20.6 11.7 %collective-permute-start.2 = (bf16[2,528,128]{2,1,0:T(8,128)(2,1)S(1)}, bf16[2,528,128]{2,1,0:T(8,128)(2,1)S(1)}, u32[]{:S(2)}, u32[]{:S(2)}) collective-permute-start(bf16[2,528,128]{2,1,0:T(8,128)(2,1)S(1)} %pad_maximum_fusion.1), channel_id=1, source_target_pairs={{0,8},{4,12},{8,0},{12,4},{16,24},{20,28},{24,16},{28,20},{1,9},{5... | collective-permute-start | bytes 811016 | tf_op jit(solution)/shard_map/ppermute | solution.py:40
  29.7 5.2 %collective-permute-start.1 = (bf16[1024,128]{1,0:T(8,128)(2,1)S(1)}, bf16[1024,128]{1,0:T(8,128)(2,1)S(1)}, u32[]{:S(2)}, u32[]{:S(2)}) collective-permute-start(bf16[1024,128]{1,0:T(8,128)(2,1)S(1)} %bitcast.77), channel_id=1, source_target_pairs={{0,1},{1,0},{2,3},{3,2},{4,5},{5,4},{6,7},{7,6},{8,9},{9,8},{10,11... | collective-permute-start | bytes 786440 | tf_op jit(solution)/shard_map/ppermute | solution.py:32
  33.3 13.6 %collective-permute-start.3 = (bf16[4,528,128]{2,1,0:T(8,128)(2,1)S(1)}, bf16[4,528,128]{2,1,0:T(8,128)(2,1)S(1)}, u32[]{:S(2)}, u32[]{:S(2)}) collective-permute-start(bf16[4,528,128]{2,1,0:T(8,128)(2,1)S(1)} %pad_maximum_fusion.refs_2_.refs_0_), channel_id=1, source_target_pairs={{0,4},{4,0},{8,12},{12,8},{16,20},{20,16},{24,28},{28,24},{1,5},{5... | collective-permute-start | bytes 1622024 | tf_op jit(solution)/shard_map/ppermute | solution.py:40
  34.9 21.0 %collective-permute-start.4 = (bf16[4,528,128]{2,1,0:T(8,128)(2,1)S(1)}, bf16[4,528,128]{2,1,0:T(8,128)(2,1)S(1)}, u32[]{:S(2)}, u32[]{:S(2)}) collective-permute-start(bf16[4,528,128]{2,1,0:T(8,128)(2,1)S(1)} %pad_maximum_fusion.refs_2_.refs_0_), channel_id=1, source_target_pairs={{0,1},{1,0},{2,3},{3,2},{4,5},{5,4},{6,7},{7,6},{8,9},{9,8},{10,11... | collective-permute-start | bytes 1622024 | tf_op jit(solution)/shard_map/ppermute | solution.py:32
  43.3 12.6 %all-to-all-start.1 = ((f32[32,8,128]{2,1,0:T(8,128)}), f32[32,8,128]{2,1,0:T(8,128)S(1)}, u32[]{:S(2)}, u32[]{:S(2)}) async-start(f32[32,8,128]{2,1,0:T(8,128)} %get-tuple-element.90), calls=%async_computation.1 | async-start | bytes 262144 | tf_op jit(solution)/shard_map/all_to_all | solution.py:23
  47.0 9.0 %collective-permute-start.5 = (bf16[4,528,128]{2,1,0:T(8,128)(2,1)S(1)}, bf16[4,528,128]{2,1,0:T(8,128)(2,1)S(1)}, u32[]{:S(2)}, u32[]{:S(2)}) collective-permute-start(bf16[4,528,128]{2,1,0:T(8,128)(2,1)S(1)} %collective-permute-done.3.refs_3_.refs_1_), channel_id=1, source_target_pairs={{0,1},{1,0},{2,3},{3,2},{4,5},{5,4},{6,7},{7,6},{8,9},{9,8},{10,11... | collective-permute-start | bytes 1622024 | tf_op jit(solution)/shard_map/ppermute | solution.py:32
  89.5 10.8 %all-to-all-start.3 = ((f32[32,8,128]{2,1,0:T(8,128)}), f32[32,8,128]{2,1,0:T(8,128)S(1)}, u32[]{:S(2)}, u32[]{:S(2)}) async-start(f32[32,8,128]{2,1,0:T(8,128)} %get-tuple-element.99), calls=%async_computation.3 | async-start | bytes 262144 | tf_op jit(solution)/shard_map/all_to_all | solution.py:23
  146.3 10.8 %all-to-all-start.5 = ((bf16[32,16,128]{2,1,0:T(8,128)(2,1)}), bf16[32,16,128]{2,1,0:T(8,128)(2,1)S(1)}, u32[]{:S(2)}, u32[]{:S(2)}) async-start(bf16[32,16,128]{2,1,0:T(8,128)(2,1)} %get-tuple-element.111), calls=%async_computation.5 | async-start | bytes 262144 | tf_op jit(solution)/shard_map/all_to_all | solution.py:23
  157.8 18.2 %copy-start.36 = (f32[256,1024]{1,0:T(8,128)S(1)}, f32[256,1024]{1,0:T(8,128)}, u32[]{:S(2)}) copy-start(f32[256,1024]{1,0:T(8,128)} %get-tuple-element.130) | copy-start | bytes 3145732
  157.8 18.2 %copy-start.37 = (f32[256,1024]{1,0:T(8,128)S(1)}, f32[256,1024]{1,0:T(8,128)}, u32[]{:S(2)}) copy-start(f32[256,1024]{1,0:T(8,128)} %get-tuple-element.127) | copy-start | bytes 3145732
  170.0 11.9 %copy-start.11 = (s32[16]{0:T(128)S(1)}, s32[16]{0:T(128)}, u32[]{:S(2)}) copy-start(s32[16]{0:T(128)} %sides.19) | copy-start | bytes 196
  170.0 11.9 %copy-start.17 = (f32[5,16,512]{2,1,0:T(8,128)S(1)}, f32[5,16,512]{2,1,0:T(8,128)}, u32[]{:S(2)}) copy-start(f32[5,16,512]{2,1,0:T(8,128)} %get-tuple-element.120.sums_ref) | copy-start | bytes 491524
  170.0 11.9 %copy-start.18 = (bf16[256,128]{1,0:T(8,128)(2,1)S(1)}, bf16[256,128]{1,0:T(8,128)(2,1)}, u32[]{:S(2)}) copy-start(bf16[256,128]{1,0:T(8,128)(2,1)} %get-tuple-element.96.down_ref) | copy-start | bytes 196612
  170.0 11.9 %copy-start.20 = (bf16[16,256]{1,0:T(8,128)(2,1)S(1)}, bf16[16,256]{1,0:T(8,128)(2,1)}, u32[]{:S(2)}) copy-start(bf16[16,256]{1,0:T(8,128)(2,1)} %get-tuple-element.103._.pooled_ref) | copy-start | bytes 24580
  170.0 11.9 %copy-start.21 = (f32[8,1024]{1,0:T(8,128)S(1)}, f32[8,1024]{1,0:T(8,128)}, u32[]{:S(2)}) copy-start(f32[8,1024]{1,0:T(8,128)} %get-tuple-element.112.terms_ref) | copy-start | bytes 98308
  170.0 11.9 %copy-start.22 = (f32[16,512]{1,0:T(8,128)S(1)}, f32[16,512]{1,0:T(8,128)}, u32[]{:S(2)}) copy-start(f32[16,512]{1,0:T(8,128)} %get-tuple-element.113.weights_ref) | copy-start | bytes 98308
  170.0 11.9 %copy-start.23 = (f32[8,512]{1,0:T(8,128)S(1)}, f32[8,512]{1,0:T(8,128)}, u32[]{:S(2)}) copy-start(f32[8,512]{1,0:T(8,128)} %get-tuple-element.94.param_ref) | copy-start | bytes 49156
  170.1 11.9 %copy-start.26 = (f32[16,128]{1,0:T(8,128)S(1)}, f32[16,128]{1,0:T(8,128)}, u32[]{:S(2)}) copy-start(f32[16,128]{1,0:T(8,128)} %get-tuple-element.98.squeeze_ref) | copy-start | bytes 24580
  171.0 10.8 %all-to-all-start.6 = ((f32[32,8,128]{2,1,0:T(8,128)}), f32[32,8,128]{2,1,0:T(8,128)S(1)}, u32[]{:S(2)}, u32[]{:S(2)}) async-start(f32[32,8,128]{2,1,0:T(8,128)} %get-tuple-element.119), calls=%async_computation.6 | async-start | bytes 262144 | tf_op jit(solution)/shard_map/all_to_all | solution.py:23
  184.0 10.8 %all-to-all-start.7 = ((f32[32,8,128]{2,1,0:T(8,128)}), f32[32,8,128]{2,1,0:T(8,128)S(1)}, u32[]{:S(2)}, u32[]{:S(2)}) async-start(f32[32,8,128]{2,1,0:T(8,128)} %get-tuple-element.121), calls=%async_computation.7 | async-start | bytes 262144 | tf_op jit(solution)/shard_map/all_to_all | solution.py:23
  186.7 1.8 collective-permute-start.6
  194.8 21.4 %all-to-all-start.8 = ((bf16[16,96,128]{2,1,0:T(8,128)(2,1)}), bf16[16,96,128]{2,1,0:T(8,128)(2,1)S(1)}, u32[]{:S(2)}, u32[]{:S(2)}) async-start(bf16[16,96,128]{2,1,0:T(8,128)(2,1)} %fusion.7), calls=%async_computation.8 | async-start | bytes 786432 | tf_op jit(solution)/shard_map/all_to_all | solution.py:54
  218.2 16.6 %all-to-all-start.9 = ((f32[32,8,128]{2,1,0:T(8,128)}), f32[32,8,128]{2,1,0:T(8,128)S(1)}, u32[]{:S(2)}, u32[]{:S(2)}) async-start(f32[32,8,128]{2,1,0:T(8,128)} %get-tuple-element.135), calls=%async_computation.9 | async-start | bytes 262144 | tf_op jit(solution)/shard_map/all_to_all | solution.py:23
  234.1 3.1 %collective-permute-start.7 = (bf16[16,144,128]{2,1,0:T(8,128)(2,1)}, bf16[16,144,128]{2,1,0:T(8,128)(2,1)S(1)}, u32[]{:S(2)}, u32[]{:S(2)}) collective-permute-start(bf16[16,144,128]{2,1,0:T(8,128)(2,1)} %get-tuple-element.148), channel_id=1, source_target_pairs={{0,1},{1,0},{2,3},{3,2},{4,5},{5,4},{6,7},{7,6},{8,9},{9,8},{10,11... | collective-permute-start | bytes 1769480 | tf_op jit(solution)/shard_map/ppermute | solution.py:32
  235.3 1.9 collective-permute-start.8
  238.3 27.8 %all-to-all-start.10 = ((bf16[16,208,128]{2,1,0:T(8,128)(2,1)}), bf16[16,208,128]{2,1,0:T(8,128)(2,1)S(1)}, u32[]{:S(2)}, u32[]{:S(2)}) async-start(bf16[16,208,128]{2,1,0:T(8,128)(2,1)} %last_merge.1), calls=%async_computation.10 | async-start | bytes 1703936 | tf_op jit(solution)/shard_map/all_to_all | solution.py:54
  245.0 21.1 %copy-start.29 = (bf16[96,128]{1,0:T(8,128)(2,1)S(1)}, bf16[96,128]{1,0:T(8,128)(2,1)}, u32[]{:S(2)}) copy-start(bf16[96,128]{1,0:T(8,128)(2,1)} %copy-done.28) | copy-start | bytes 73732
  266.9 5.3 %collective-permute-start.10 = (bf16[304,128]{1,0:T(8,128)(2,1)S(1)}, bf16[304,128]{1,0:T(8,128)(2,1)S(1)}, u32[]{:S(2)}, u32[]{:S(2)}) collective-permute-start(bf16[304,128]{1,0:T(8,128)(2,1)S(1)} %last_total.1.refs_0_), channel_id=1, source_target_pairs={{0,2},{1,3},{2,0},{3,1},{4,6},{5,7},{6,4},{7,5},{8,10},{9,11},{10,... | collective-permute-start | bytes 233480 | tf_op jit(solution)/shard_map/ppermute | solution.py:1790
  267.6 4.7 %collective-permute-start.11 = (bf16[304,128]{1,0:T(8,128)(2,1)S(1)}, bf16[304,128]{1,0:T(8,128)(2,1)S(1)}, u32[]{:S(2)}, u32[]{:S(2)}) collective-permute-start(bf16[304,128]{1,0:T(8,128)(2,1)S(1)} %last_total.1.refs_0_), channel_id=1, source_target_pairs={{0,3},{1,2},{2,1},{3,0},{4,7},{5,6},{6,5},{7,4},{8,11},{9,10},{10,... | collective-permute-start | bytes 233480 | tf_op jit(solution)/shard_map/ppermute | solution.py:1790
  267.6 4.7 %collective-permute-start.9 = (bf16[304,128]{1,0:T(8,128)(2,1)S(1)}, bf16[304,128]{1,0:T(8,128)(2,1)S(1)}, u32[]{:S(2)}, u32[]{:S(2)}) collective-permute-start(bf16[304,128]{1,0:T(8,128)(2,1)S(1)} %last_total.1.refs_0_), channel_id=1, source_target_pairs={{0,1},{1,0},{2,3},{3,2},{4,5},{5,4},{6,7},{7,6},{8,9},{9,8},{10,11... | collective-permute-start | bytes 233480 | tf_op jit(solution)/shard_map/ppermute | solution.py:1790
  (33 other events, 179.3 us)

commit v7 on v6

--- a/solution.py
+++ b/solution.py
@@ -142,6 +142,14 @@
     def _():
         for ref in refs:
             ref[...] = jnp.zeros(ref.shape, ref.dtype)
+
+
+def edge_zeros_at_start(ref, first, last):
+    @pl.when(pl.program_id(0) == 0)
+    def _():
+        for row in (first, last):
+            here = slice(row * SIDE, row * SIDE + SIDE)
+            ref[:, here, :] = jnp.zeros((ref.shape[0], SIDE, ref.shape[2]), ref.dtype)
 
 
 def last_step():
@@ -341,7 +349,8 @@
         w_ref, param_ref, act_ref, second_ref, terms_ref, count_ref, send_ref, *refs = refs
         patch_ref, acc_ref, tile_ref = refs
     step = pl.program_id(0)
-    zeros_at_start(acc_ref, patch_ref)
+    zeros_at_start(acc_ref)
+    edge_zeros_at_start(patch_ref, 1, SIDE)
     place = places()
     lanes = first_ref.shape[1]
     columns = TAPS * lanes // RADIX
@@ -627,8 +636,20 @@
         gw = both[:half]
         gw_ref[...] = gw
         sums = both[half:]
-        put(tile_ref, 0, sums[0:1, :])
-        put(tile_ref, whole.shape[1] // 128, column_total(gw * whole))
+        count = jnp.int32(0)
+        for image in range(sides.shape[0]):
+            count = count + 4 * sides[image] * sides[image]
+        count = jnp.full((1, 128), count, jnp.int32).astype(f32)
+        sums = sums[0:1, :]
+        wide_count = wide(count, sums.shape[1])
+        put(tile_ref, 0, column_total(gw * whole) - sums * sums / wide_count)
+        at = sums.shape[1] // 128
+        parts = three_parts(jnp.broadcast_to(total, (16, half))).astype(f32)
+        for index in range(3):
+            put(tile_ref, at + index * half // 128, parts[16 * index : 16 * index + 1, :])
+        high = count.astype(bf16).astype(f32)
+        tile_ref[at + 6 : at + 7, :] = high
+        tile_ref[at + 7 : at + 8, :] = count - high
         send(send_ref, tile_ref)
 
 
@@ -654,24 +675,38 @@
     square_ref,
     tile_ref,
     half_ref,
+    flat_ref,
 ):
     step = pl.program_id(0)
     zeros_at_start(acc_ref, square_ref, grad_ref)
     place = places()
     lanes = x_ref.shape[1]
-    part = 512 if lanes % 512 == 0 else lanes
+    part = 256 if lanes % 256 == 0 else lanes
 
     @at_start
     def _():
+        devices, rows = recv_ref.shape[:2]
+        for device in range(devices):
+            flat_ref[device * rows : (device + 1) * rows, :] = recv_ref[device].astype(f32)
         take(recv_ref, tile_ref)
+
+        def of_all(row):
+            return flat_ref[pl.ds(row, devices, stride=rows), :]
+
+        at = lanes // 128
+        parts = [
+            jnp.concatenate([of_all(at + 2 * index), of_all(at + 2 * index + 1)], axis=1)
+            for index in range(3)
+        ]
+        parts = jnp.concatenate(parts, axis=0).astype(bf16)
+        parts = jnp.dot(parts, w_ref[...], preferred_element_type=f32)
+        sums = parts[:devices] + (parts[devices : 2 * devices] + parts[2 * devices :])
+        counts = wide(of_all(at + 6) + of_all(at + 7), lanes)
+        squares = column_total(sums * sums / counts) + row_at(tile_ref, 0, lanes)
         count = count_ref[0:1, :]
         gain, shift = param_ref[0:1, :], param_ref[1:2, :]
         center, spread, inv, scale, offset = norm_rows(
-            row_at(tile_ref, 0, lanes),
-            row_at(tile_ref, lanes // 128, lanes),
-            wide(count, lanes),
-            gain,
-            shift,
+            column_total(sums), squares, wide(count, lanes), gain, shift
         )
         branch = gain * gain * spread * inv * inv + shift * shift
         terms_ref[0:1, :] = scale
@@ -932,7 +967,8 @@
     tile_ref,
 ):
     step = pl.program_id(0)
-    zeros_at_start(acc_ref, column_ref, in_ref)
+    zeros_at_start(acc_ref, in_ref)
+    edge_zeros_at_start(column_ref, 0, SIDE + 1)
     place = places()
     lanes = second_ref.shape[1]
     half = lanes // 2
@@ -1026,7 +1062,8 @@
         mine_ref, other_ref, conv_ref, patch_ref = refs
     else:
         conv_ref, patch_ref = refs
-    zeros_at_start(conv_ref, patch_ref)
+    zeros_at_start(conv_ref)
+    edge_zeros_at_start(patch_ref, 1, SIDE)
     place = places()
     lanes = act_ref.shape[1]
     columns = TAPS * lanes // RADIX
@@ -1471,7 +1508,7 @@
             whole_out((bottleneck, width)),
             whole_out((8, bottleneck)),
             whole_out((8, 128)),
-            sending(wide_rows),
+            sending(wide_rows, bf16),
         ],
         [((bottleneck, bottleneck), f32), ((2, 8, bottleneck), f32), ((wide_rows, 128), f32)],
         11,
@@ -1508,6 +1545,7 @@
             ((8, 128), f32),
             ((wide_rows, 128), f32),
             ((8, width), f32),
+            ((devices * wide_rows, 128), f32),
         ],
         25,
         name="output",

time: 275 us -> 272 us (0.989)
  no operation moved by 1% of the time
where the time goes in v7:
time: 272 us; the launch traced here: 270 us
  Pallas kernels  125 us (46%)
  waiting for transfers between devices  52.2 us (19%)
  starting transfers between devices  47 us (17%)
  blocking collectives  25.6 us (9%)
  local copies, waits for them, and re-layouts  14.8 us (5%)
  other arithmetic  4.04 us (1%)
    all_to_all x7, waiting for transfers between devices, swap_all(): return lax.all_to_all(values, axes, 0, 0)  31.2 us
    all_to_all x7, starting transfers between devices, swap_all(): return lax.all_to_all(values, axes, 0, 0)  25.8 us
    all_to_all x2, blocking collectives, swap_all(): return lax.all_to_all(values, axes, 0, 0)  25.6 us
    pallas_call x1, Pallas kernels, local(): call(out_kernel, steps, [scalars(), tiles(bottleneck), tiles(width), tile...  22.8 us
    pallas_call x1, Pallas kernels, local(): call(conv_back_kernel, steps, [scalars(), tiles(mid), held(8, mid), recei...  17.6 us
    pallas_call x1, Pallas kernels, local(): call(last_kernel, steps, [scalars(), tiles(bottleneck), tiles(bottleneck)...  13.1 us
    pallas_call x1, Pallas kernels, local(): call(gate_kernel, steps, [scalars(), tiles(mid), held(8, mid), tiles(bott...  12.2 us
    pallas_call x1, Pallas kernels, local(): call(functools.partial(second_kernel, lengths if aligned else None), step...  12 us
  transfers between devices with their start and end apart: 21, of which 10 were waited for; matrix products, arithmetic and copies ran while one was open for 3% of the time, Pallas kernels for 21%

profile of v7, /device:TPU:0, one launch (start us, length us, event | category | flops | bytes accessed | tf_op | source)
XLA Modules:
  0.0 270.2 jit_solution(7447713441452677064)
XLA Ops:
  2.5 4.0 %collective-permute-start = (bf16[1,528,128]{2,1,0:T(8,128)(2,1)}, bf16[1,528,128]{2,1,0:T(8,128)(2,1)S(1)}, u32[]{:S(2)}, u32[]{:S(2)}) collective-permute-start(bf16[1,528,128]{2,1,0:T(8,128)(2,1)} %bitcast.73), channel_id=1, source_target_pairs={{0,16},{4,20},{8,24},{12,28},{16,0},{20,4},{24,8},{28,12},{1,17},{... | collective-permute-start | bytes 405512 | tf_op jit(solution)/shard_map/ppermute | solution.py:40
  6.5 6.7 %collective-permute-done = bf16[1,528,128]{2,1,0:T(8,128)(2,1)S(1)} collective-permute-done((bf16[1,528,128]{2,1,0:T(8,128)(2,1)}, bf16[1,528,128]{2,1,0:T(8,128)(2,1)S(1)}, u32[]{:S(2)}, u32[]{:S(2)}) %collective-permute-start) | collective-permute-done | bytes 135200 | tf_op jit(solution)/shard_map/ppermute | solution.py:40
  14.0 5.7 %all-to-all-start = ((bf16[8,128,128]{2,1,0:T(8,128)(2,1)}), bf16[8,128,128]{2,1,0:T(8,128)(2,1)S(1)}, u32[]{:S(2)}, u32[]{:S(2)}) async-start(bf16[8,128,128]{2,1,0:T(8,128)(2,1)} %broadcast_in_dim.15), calls=%async_computation | async-start | bytes 524288 | tf_op jit(solution)/shard_map/all_to_all | solution.py:23
  20.6 2.1 collective-permute-start.2
  22.7 7.0 %all-to-all-done = bf16[8,128,128]{2,1,0:T(8,128)(2,1)S(1)} async-done(((bf16[8,128,128]{2,1,0:T(8,128)(2,1)}), bf16[8,128,128]{2,1,0:T(8,128)(2,1)S(1)}, u32[]{:S(2)}, u32[]{:S(2)}) %all-to-all-start) | async-done | bytes 262176 | tf_op jit(solution)/shard_map/all_to_all | solution.py:23
  29.7 2.6 collective-permute-done.2
  35.7 7.7 %first.1 = (f32[4096,256]{1,0:T(8,128)}, bf16[1024,256]{1,0:T(8,128)(2,1)}, f32[32,8,128]{2,1,0:T(8,128)}) custom-call(s32[16]{0:T(128)} %sides.19, s32[1]{0:T(128)} %bitcast.odd.refs_1_, bf16[4096,1024]{1,0:T(8,128)(2,1)} %bitcast.84, bf16[1024,128]{1,0:T(8,128)(2,1)} %bitcast.78, bf16[1024,128]{1,0:T(8,128)(2,1)} %copy-done.43), custom_call_target="tpu_custom_call" | custom-call | flops 8000000000 | bytes 24000000 | tf_op jit(solution)/shard_map/first/pallas_call | solution.py:1382
  43.3 3.6 %all-to-all-start.1 = ((f32[32,8,128]{2,1,0:T(8,128)}), f32[32,8,128]{2,1,0:T(8,128)S(1)}, u32[]{:S(2)}, u32[]{:S(2)}) async-start(f32[32,8,128]{2,1,0:T(8,128)} %get-tuple-element.90), calls=%async_computation.1 | async-start | bytes 262144 | tf_op jit(solution)/shard_map/all_to_all | solution.py:23
  47.3 8.7 %cross.1 = (f32[256,1024]{1,0:T(8,128)}, f32[8,1024]{1,0:T(8,128)}, f32[8,128]{1,0:T(8,128)}) custom-call(s32[16]{0:T(128)} %sides.19, bf16[4096,1024]{1,0:T(8,128)(2,1)} %bitcast.85, f32[4096,256]{1,0:T(8,128)} %get-tuple-element.89.first_ref), custom_call_target="tpu_custom_call" | custom-call | flops 10000000000 | bytes 30000000 | tf_op jit(solution)/shard_map/cross/pallas_call | solution.py:1392
  57.0 12.0 %second.1 = (bf16[4096,256]{1,0:T(8,128)(2,1)}, f32[4096,512]{1,0:T(8,128)}, f32[8,256]{1,0:T(8,128)}, f32[8,128]{1,0:T(8,128)}, f32[32,8,128]{2,1,0:T(8,128)}, ...) custom-call(s32[16]{0:T(128)} %sides.19, ...), custom_call_target="tpu_custom_call" | custom-call | flops 15000000512 | bytes 45000000 | tf_op jit(solution)/shard_map/second/pallas_call | solution.py:1438
  69.0 14.1 %all_to_all.55.recv_ref = f32[32,8,128]{2,1,0:T(8,128)} all-to-all(f32[32,8,128]{2,1,0:T(8,128)} %get-tuple-element.93), channel_id=1, replica_groups=mesh['fsdp'=8,'dp'=4] {'fsdp','dp'}, dimensions={0} | all-to-all | bytes 262144 | tf_op jit(solution)/shard_map/all_to_all | solution.py:23
  83.1 6.2 %pool.1 = (bf16[16,256]{1,0:T(8,128)(2,1)}, f32[16,128]{1,0:T(8,128)}, f32[8,512]{1,0:T(8,128)}, f32[32,8,128]{2,1,0:T(8,128)}) custom-call(s32[16]{0:T(128)} %sides.19, f32[4096,512]{1,0:T(8,128)} %get-tuple-element.92.second_ref, f32[32,8,128]{2,1,0:T(8,128)} %all_to_all.55.recv_ref, f32[8,512]{1,0:T(8,128)} %get-tuple-element.94.param_ref, ...), custom_call_target="tpu_custom_call" | custom-call | flops 7000000000 | bytes 21000000 | tf_op jit(solution)/shard_map/pool/pallas_call | solution.py:1451
  89.3 2.6 all-to-all-start.3
  94.5 5.6 %all-to-all-done.3.recv_ref = f32[32,8,128]{2,1,0:T(8,128)S(1)} async-done(((f32[32,8,128]{2,1,0:T(8,128)}), f32[32,8,128]{2,1,0:T(8,128)S(1)}, u32[]{:S(2)}, u32[]{:S(2)}) %all-to-all-start.3) | async-done | bytes 131104 | tf_op jit(solution)/shard_map/all_to_all | solution.py:23
  100.8 8.8 %mix.1 = (bf16[4096,256]{1,0:T(8,128)(2,1)}, f32[16,512]{1,0:T(8,128)}, bf16[16,128]{1,0:T(8,128)(2,1)}, f32[8,128]{1,0:T(8,128)}, f32[256,1024]{1,0:T(8,128)}, ...) custom-call(s32[16]{0:T(128)} %sides.19, f32[4096,512]{1,0:T(8,128)} %get-tuple-element.92.second_ref, ...), custom_call_target="tpu_custom_call" | custom-call | flops 11000000512 | bytes 33000000 | tf_op jit(solution)/shard_map/mix/pallas_call | solution.py:1489
  109.6 11.5 %all_to_all.56.recv_ref = bf16[32,16,128]{2,1,0:T(8,128)(2,1)} all-to-all(bf16[32,16,128]{2,1,0:T(8,128)(2,1)} %get-tuple-element.106), channel_id=1, replica_groups=mesh['fsdp'=8,'dp'=4] {'fsdp','dp'}, dimensions={0} | all-to-all | bytes 262144 | tf_op jit(solution)/shard_map/all_to_all | solution.py:23
  121.1 22.8 %output.1 = (bf16[4096,1024]{1,0:T(8,128)(2,1)}, bf16[4096,1024]{1,0:T(8,128)(2,1)}, f32[4096,256]{1,0:T(8,128)}, f32[256,1024]{1,0:T(8,128)}, f32[8,1024]{1,0:T...) custom-call(s32[16]{0:T(128)} %sides.19, bf16[4096,256]{1,0:T(8,128)(2,1)} %get-tuple-element.105.mixed_ref, ...), custom_call_target="tpu_custom_call" | custom-call | flops 24999999488 | bytes 75000000 | tf_op jit(solution)/shard_map/output/pallas_call | solution.py:1519
  143.8 2.6 all-to-all-start.5
  147.2 7.5 %all-to-all-done.5.recv_ref = bf16[32,16,128]{2,1,0:T(8,128)(2,1)S(1)} async-done(((bf16[32,16,128]{2,1,0:T(8,128)(2,1)}), bf16[32,16,128]{2,1,0:T(8,128)(2,1)S(1)}, u32[]{:S(2)}, u32[]{:S(2)}) %all-to-all-start.5) | async-done | bytes 131104 | tf_op jit(solution)/shard_map/all_to_all | solution.py:23
  155.3 12.2 %gate.1 = (f32[4096,256]{1,0:T(8,128)}, f32[5,16,512]{2,1,0:T(8,128)}, f32[512,128]{1,0:T(8,128)}, f32[8,512]{1,0:T(8,128)}, f32[16,128]{1,0:T(8,128)}, /*index=5*/f32[8,1024]{1,0:T(8,128)}, f32[32,8,128]{2,1,0:T(8,128)}) custom-call(s32[16]{0:T(128)} %sides.19, f32[4096,512]{1,0:T(8,128)} %get-tuple-element.92.second_ref, ...), custom_call_target="tpu_custom_call" | custom-call | flops 12999999488 | bytes 39000000 | tf_op jit(solution)/shard_map/gate/pallas_call | solution.py:1555
  168.6 2.6 all-to-all-start.6
  173.8 5.6 %all-to-all-done.6.recv_ref = f32[32,8,128]{2,1,0:T(8,128)S(1)} async-done(((f32[32,8,128]{2,1,0:T(8,128)}), f32[32,8,128]{2,1,0:T(8,128)S(1)}, u32[]{:S(2)}, u32[]{:S(2)}) %all-to-all-start.6) | async-done | bytes 131104 | tf_op jit(solution)/shard_map/all_to_all | solution.py:23
  181.5 2.6 all-to-all-start.7
  186.9 5.4 %all-to-all-done.7.recv_ref = f32[32,8,128]{2,1,0:T(8,128)S(1)} async-done(((f32[32,8,128]{2,1,0:T(8,128)}), f32[32,8,128]{2,1,0:T(8,128)S(1)}, u32[]{:S(2)}, u32[]{:S(2)}) %all-to-all-start.7) | async-done | bytes 131104 | tf_op jit(solution)/shard_map/all_to_all | solution.py:23
  192.3 3.6 %all-to-all-start.8 = ((bf16[16,96,128]{2,1,0:T(8,128)(2,1)}), bf16[16,96,128]{2,1,0:T(8,128)(2,1)S(1)}, u32[]{:S(2)}, u32[]{:S(2)}) async-start(bf16[16,96,128]{2,1,0:T(8,128)(2,1)} %fusion.7), calls=%async_computation.8 | async-start | bytes 786432 | tf_op jit(solution)/shard_map/all_to_all | solution.py:54
  195.9 17.6 %conv_back.1 = (bf16[4096,512]{1,0:T(8,128)(2,1)}, f32[4096,256]{1,0:T(8,128)}, f32[256,1024]{1,0:T(8,128)}, f32[8,512]{1,0:T(8,128)}, f32[8,128]{1,0:T(8,128)}) custom-call(s32[16]{0:T(128)} %sides.19, f32[4096,512]{1,0:T(8,128)} %get-tuple-element.92.second_ref, f32[8,512]{1,0:T(8,128)} %get-tuple-element.97.ab_ref, f32[32,8,128]{2,1,0:T(8,128)} %copy-done.40, ...), custom_call_target="tpu_custom_call" | custom-call | flops 20000000000 | bytes 60000000 | tf_op jit(solution)/shard_map/conv_back/pallas_call | solution.py:1675
  215.5 6.1 %all-to-all-start.9 = ((f32[32,8,128]{2,1,0:T(8,128)}), f32[32,8,128]{2,1,0:T(8,128)S(1)}, u32[]{:S(2)}, u32[]{:S(2)}) async-start(f32[32,8,128]{2,1,0:T(8,128)} %get-tuple-element.135), calls=%async_computation.9 | async-start | bytes 262144 | tf_op jit(solution)/shard_map/all_to_all | solution.py:23
  221.6 9.5 %conv_grad.1 = (bf16[16,144,128]{2,1,0:T(8,128)(2,1)}, bf16[16,144,128]{2,1,0:T(8,128)(2,1)}) custom-call(s32[1]{0:T(128)} %bitcast.odd.refs_1_, bf16[4096,256]{1,0:T(8,128)(2,1)} %get-tuple-element.145.act_ref, bf16[4096,512]{1,0:T(8,128)(2,1)} %get-tuple-element.146.dsecond_ref, bf16[96,128]{1,0:T(8,128)(2,1)} %copy-done.28), custom_call_target="tpu_custom_call" | custom-call | flops 15000000512 | bytes 45000000 | tf_op jit(solution)/shard_map/conv_grad/pallas_call | solution.py:1741
  235.4 6.6 %all-to-all-start.10 = ((bf16[16,208,128]{2,1,0:T(8,128)(2,1)}), bf16[16,208,128]{2,1,0:T(8,128)(2,1)S(1)}, u32[]{:S(2)}, u32[]{:S(2)}) async-start(bf16[16,208,128]{2,1,0:T(8,128)(2,1)} %last_merge.1), calls=%async_computation.10 | async-start | bytes 1703936 | tf_op jit(solution)/shard_map/all_to_all | solution.py:54
  242.1 13.1 %last.1 = (f32[4096,1024]{1,0:T(8,128)}, f32[8,128]{1,0:T(8,128)}) custom-call(s32[16]{0:T(128)} %sides.19, f32[4096,256]{1,0:T(8,128)} %get-tuple-element.126.dfirst_ref, f32[4096,256]{1,0:T(8,128)} %get-tuple-element.89.first_ref, f32[8,256]{1,0:T(8,128)} %copy-done.4, bf16[1024,256]{1,0:T(8,128)(2,1)} %get-tuple-element.140.w_ref, ...), custom_call_target="tpu_custom_call" | custom-call | flops 15000000512 | bytes 45000000 | tf_op jit(solution)/shard_map/last/pallas_call | solution.py:1773
  255.2 8.1 %all-to-all-done.10.part_ref = bf16[16,208,128]{2,1,0:T(8,128)(2,1)S(1)} async-done(((bf16[16,208,128]{2,1,0:T(8,128)(2,1)}), bf16[16,208,128]{2,1,0:T(8,128)(2,1)S(1)}, u32[]{:S(2)}, u32[]{:S(2)}) %all-to-all-start.10) | async-done | bytes 852000 | tf_op jit(solution)/shard_map/all_to_all | solution.py:54
  266.8 2.5 collective-permute-done.10.refs_2_
  (143 shorter events, 31.7 us)
Async XLA Ops:
  2.5 10.7 %collective-permute-start = (bf16[1,528,128]{2,1,0:T(8,128)(2,1)}, bf16[1,528,128]{2,1,0:T(8,128)(2,1)S(1)}, u32[]{:S(2)}, u32[]{:S(2)}) collective-permute-start(bf16[1,528,128]{2,1,0:T(8,128)(2,1)} %bitcast.73), channel_id=1, source_target_pairs={{0,16},{4,20},{8,24},{12,28},{16,0},{20,4},{24,8},{28,12},{1,17},{... | collective-permute-start | bytes 405512 | tf_op jit(solution)/shard_map/ppermute | solution.py:40
  14.0 15.8 %all-to-all-start = ((bf16[8,128,128]{2,1,0:T(8,128)(2,1)}), bf16[8,128,128]{2,1,0:T(8,128)(2,1)S(1)}, u32[]{:S(2)}, u32[]{:S(2)}) async-start(bf16[8,128,128]{2,1,0:T(8,128)(2,1)} %broadcast_in_dim.15), calls=%async_computation | async-start | bytes 524288 | tf_op jit(solution)/shard_map/all_to_all | solution.py:23
  20.6 11.7 %collective-permute-start.2 = (bf16[2,528,128]{2,1,0:T(8,128)(2,1)S(1)}, bf16[2,528,128]{2,1,0:T(8,128)(2,1)S(1)}, u32[]{:S(2)}, u32[]{:S(2)}) collective-permute-start(bf16[2,528,128]{2,1,0:T(8,128)(2,1)S(1)} %pad_maximum_fusion.1), channel_id=1, source_target_pairs={{0,8},{4,12},{8,0},{12,4},{16,24},{20,28},{24,16},{28,20},{1,9},{5... | collective-permute-start | bytes 811016 | tf_op jit(solution)/shard_map/ppermute | solution.py:40
  29.7 5.2 %collective-permute-start.1 = (bf16[1024,128]{1,0:T(8,128)(2,1)S(1)}, bf16[1024,128]{1,0:T(8,128)(2,1)S(1)}, u32[]{:S(2)}, u32[]{:S(2)}) collective-permute-start(bf16[1024,128]{1,0:T(8,128)(2,1)S(1)} %bitcast.77), channel_id=1, source_target_pairs={{0,1},{1,0},{2,3},{3,2},{4,5},{5,4},{6,7},{7,6},{8,9},{9,8},{10,11... | collective-permute-start | bytes 786440 | tf_op jit(solution)/shard_map/ppermute | solution.py:32
  33.3 13.6 %collective-permute-start.3 = (bf16[4,528,128]{2,1,0:T(8,128)(2,1)S(1)}, bf16[4,528,128]{2,1,0:T(8,128)(2,1)S(1)}, u32[]{:S(2)}, u32[]{:S(2)}) collective-permute-start(bf16[4,528,128]{2,1,0:T(8,128)(2,1)S(1)} %pad_maximum_fusion.refs_2_.refs_0_), channel_id=1, source_target_pairs={{0,4},{4,0},{8,12},{12,8},{16,20},{20,16},{24,28},{28,24},{1,5},{5... | collective-permute-start | bytes 1622024 | tf_op jit(solution)/shard_map/ppermute | solution.py:40
  34.9 21.0 %collective-permute-start.4 = (bf16[4,528,128]{2,1,0:T(8,128)(2,1)S(1)}, bf16[4,528,128]{2,1,0:T(8,128)(2,1)S(1)}, u32[]{:S(2)}, u32[]{:S(2)}) collective-permute-start(bf16[4,528,128]{2,1,0:T(8,128)(2,1)S(1)} %pad_maximum_fusion.refs_2_.refs_0_), channel_id=1, source_target_pairs={{0,1},{1,0},{2,3},{3,2},{4,5},{5,4},{6,7},{7,6},{8,9},{9,8},{10,11... | collective-permute-start | bytes 1622024 | tf_op jit(solution)/shard_map/ppermute | solution.py:32
  43.3 12.6 %all-to-all-start.1 = ((f32[32,8,128]{2,1,0:T(8,128)}), f32[32,8,128]{2,1,0:T(8,128)S(1)}, u32[]{:S(2)}, u32[]{:S(2)}) async-start(f32[32,8,128]{2,1,0:T(8,128)} %get-tuple-element.90), calls=%async_computation.1 | async-start | bytes 262144 | tf_op jit(solution)/shard_map/all_to_all | solution.py:23
  47.0 9.0 %collective-permute-start.5 = (bf16[4,528,128]{2,1,0:T(8,128)(2,1)S(1)}, bf16[4,528,128]{2,1,0:T(8,128)(2,1)S(1)}, u32[]{:S(2)}, u32[]{:S(2)}) collective-permute-start(bf16[4,528,128]{2,1,0:T(8,128)(2,1)S(1)} %collective-permute-done.3.refs_3_.refs_1_), channel_id=1, source_target_pairs={{0,1},{1,0},{2,3},{3,2},{4,5},{5,4},{6,7},{7,6},{8,9},{9,8},{10,11... | collective-permute-start | bytes 1622024 | tf_op jit(solution)/shard_map/ppermute | solution.py:32
  89.3 10.8 %all-to-all-start.3 = ((f32[32,8,128]{2,1,0:T(8,128)}), f32[32,8,128]{2,1,0:T(8,128)S(1)}, u32[]{:S(2)}, u32[]{:S(2)}) async-start(f32[32,8,128]{2,1,0:T(8,128)} %get-tuple-element.99), calls=%async_computation.3 | async-start | bytes 262144 | tf_op jit(solution)/shard_map/all_to_all | solution.py:23
  143.8 10.8 %all-to-all-start.5 = ((bf16[32,16,128]{2,1,0:T(8,128)(2,1)}), bf16[32,16,128]{2,1,0:T(8,128)(2,1)S(1)}, u32[]{:S(2)}, u32[]{:S(2)}) async-start(bf16[32,16,128]{2,1,0:T(8,128)(2,1)} %get-tuple-element.111), calls=%async_computation.5 | async-start | bytes 262144 | tf_op jit(solution)/shard_map/all_to_all | solution.py:23
  155.3 18.2 %copy-start.36 = (f32[256,1024]{1,0:T(8,128)S(1)}, f32[256,1024]{1,0:T(8,128)}, u32[]{:S(2)}) copy-start(f32[256,1024]{1,0:T(8,128)} %get-tuple-element.130) | copy-start | bytes 3145732
  155.3 18.2 %copy-start.37 = (f32[256,1024]{1,0:T(8,128)S(1)}, f32[256,1024]{1,0:T(8,128)}, u32[]{:S(2)}) copy-start(f32[256,1024]{1,0:T(8,128)} %get-tuple-element.127) | copy-start | bytes 3145732
  167.5 11.9 %copy-start.11 = (s32[16]{0:T(128)S(1)}, s32[16]{0:T(128)}, u32[]{:S(2)}) copy-start(s32[16]{0:T(128)} %sides.19) | copy-start | bytes 196
  167.6 11.9 %copy-start.17 = (f32[5,16,512]{2,1,0:T(8,128)S(1)}, f32[5,16,512]{2,1,0:T(8,128)}, u32[]{:S(2)}) copy-start(f32[5,16,512]{2,1,0:T(8,128)} %get-tuple-element.120.sums_ref) | copy-start | bytes 491524
  167.6 11.9 %copy-start.18 = (bf16[256,128]{1,0:T(8,128)(2,1)S(1)}, bf16[256,128]{1,0:T(8,128)(2,1)}, u32[]{:S(2)}) copy-start(bf16[256,128]{1,0:T(8,128)(2,1)} %get-tuple-element.96.down_ref) | copy-start | bytes 196612
  167.6 11.9 %copy-start.20 = (bf16[16,256]{1,0:T(8,128)(2,1)S(1)}, bf16[16,256]{1,0:T(8,128)(2,1)}, u32[]{:S(2)}) copy-start(bf16[16,256]{1,0:T(8,128)(2,1)} %get-tuple-element.103._.pooled_ref) | copy-start | bytes 24580
  167.6 11.9 %copy-start.21 = (f32[8,1024]{1,0:T(8,128)S(1)}, f32[8,1024]{1,0:T(8,128)}, u32[]{:S(2)}) copy-start(f32[8,1024]{1,0:T(8,128)} %get-tuple-element.112.terms_ref) | copy-start | bytes 98308
  167.6 11.9 %copy-start.22 = (f32[16,512]{1,0:T(8,128)S(1)}, f32[16,512]{1,0:T(8,128)}, u32[]{:S(2)}) copy-start(f32[16,512]{1,0:T(8,128)} %get-tuple-element.113.weights_ref) | copy-start | bytes 98308
  167.6 11.9 %copy-start.23 = (f32[8,512]{1,0:T(8,128)S(1)}, f32[8,512]{1,0:T(8,128)}, u32[]{:S(2)}) copy-start(f32[8,512]{1,0:T(8,128)} %get-tuple-element.94.param_ref) | copy-start | bytes 49156
  167.6 11.9 %copy-start.26 = (f32[16,128]{1,0:T(8,128)S(1)}, f32[16,128]{1,0:T(8,128)}, u32[]{:S(2)}) copy-start(f32[16,128]{1,0:T(8,128)} %get-tuple-element.98.squeeze_ref) | copy-start | bytes 24580
  168.6 10.8 %all-to-all-start.6 = ((f32[32,8,128]{2,1,0:T(8,128)}), f32[32,8,128]{2,1,0:T(8,128)S(1)}, u32[]{:S(2)}, u32[]{:S(2)}) async-start(f32[32,8,128]{2,1,0:T(8,128)} %get-tuple-element.119), calls=%async_computation.6 | async-start | bytes 262144 | tf_op jit(solution)/shard_map/all_to_all | solution.py:23
  181.5 10.8 %all-to-all-start.7 = ((f32[32,8,128]{2,1,0:T(8,128)}), f32[32,8,128]{2,1,0:T(8,128)S(1)}, u32[]{:S(2)}, u32[]{:S(2)}) async-start(f32[32,8,128]{2,1,0:T(8,128)} %get-tuple-element.121), calls=%async_computation.7 | async-start | bytes 262144 | tf_op jit(solution)/shard_map/all_to_all | solution.py:23
  184.3 1.8 collective-permute-start.6
  192.3 21.2 %all-to-all-start.8 = ((bf16[16,96,128]{2,1,0:T(8,128)(2,1)}), bf16[16,96,128]{2,1,0:T(8,128)(2,1)S(1)}, u32[]{:S(2)}, u32[]{:S(2)}) async-start(bf16[16,96,128]{2,1,0:T(8,128)(2,1)} %fusion.7), calls=%async_computation.8 | async-start | bytes 786432 | tf_op jit(solution)/shard_map/all_to_all | solution.py:54
  215.5 16.3 %all-to-all-start.9 = ((f32[32,8,128]{2,1,0:T(8,128)}), f32[32,8,128]{2,1,0:T(8,128)S(1)}, u32[]{:S(2)}, u32[]{:S(2)}) async-start(f32[32,8,128]{2,1,0:T(8,128)} %get-tuple-element.135), calls=%async_computation.9 | async-start | bytes 262144 | tf_op jit(solution)/shard_map/all_to_all | solution.py:23
  231.2 3.1 %collective-permute-start.7 = (bf16[16,144,128]{2,1,0:T(8,128)(2,1)}, bf16[16,144,128]{2,1,0:T(8,128)(2,1)S(1)}, u32[]{:S(2)}, u32[]{:S(2)}) collective-permute-start(bf16[16,144,128]{2,1,0:T(8,128)(2,1)} %get-tuple-element.148), channel_id=1, source_target_pairs={{0,1},{1,0},{2,3},{3,2},{4,5},{5,4},{6,7},{7,6},{8,9},{9,8},{10,11... | collective-permute-start | bytes 1769480 | tf_op jit(solution)/shard_map/ppermute | solution.py:32
  232.4 1.9 collective-permute-start.8
  235.4 27.8 %all-to-all-start.10 = ((bf16[16,208,128]{2,1,0:T(8,128)(2,1)}), bf16[16,208,128]{2,1,0:T(8,128)(2,1)S(1)}, u32[]{:S(2)}, u32[]{:S(2)}) async-start(bf16[16,208,128]{2,1,0:T(8,128)(2,1)} %last_merge.1), calls=%async_computation.10 | async-start | bytes 1703936 | tf_op jit(solution)/shard_map/all_to_all | solution.py:54
  242.1 21.1 %copy-start.29 = (bf16[96,128]{1,0:T(8,128)(2,1)S(1)}, bf16[96,128]{1,0:T(8,128)(2,1)}, u32[]{:S(2)}) copy-start(bf16[96,128]{1,0:T(8,128)(2,1)} %copy-done.28) | copy-start | bytes 73732
  264.0 5.3 %collective-permute-start.10 = (bf16[304,128]{1,0:T(8,128)(2,1)S(1)}, bf16[304,128]{1,0:T(8,128)(2,1)S(1)}, u32[]{:S(2)}, u32[]{:S(2)}) collective-permute-start(bf16[304,128]{1,0:T(8,128)(2,1)S(1)} %last_total.1.refs_0_), channel_id=1, source_target_pairs={{0,2},{1,3},{2,0},{3,1},{4,6},{5,7},{6,4},{7,5},{8,10},{9,11},{10,... | collective-permute-start | bytes 233480 | tf_op jit(solution)/shard_map/ppermute | solution.py:1828
  264.7 4.7 %collective-permute-start.11 = (bf16[304,128]{1,0:T(8,128)(2,1)S(1)}, bf16[304,128]{1,0:T(8,128)(2,1)S(1)}, u32[]{:S(2)}, u32[]{:S(2)}) collective-permute-start(bf16[304,128]{1,0:T(8,128)(2,1)S(1)} %last_total.1.refs_0_), channel_id=1, source_target_pairs={{0,3},{1,2},{2,1},{3,0},{4,7},{5,6},{6,5},{7,4},{8,11},{9,10},{10,... | collective-permute-start | bytes 233480 | tf_op jit(solution)/shard_map/ppermute | solution.py:1828
  264.7 4.7 %collective-permute-start.9 = (bf16[304,128]{1,0:T(8,128)(2,1)S(1)}, bf16[304,128]{1,0:T(8,128)(2,1)S(1)}, u32[]{:S(2)}, u32[]{:S(2)}) collective-permute-start(bf16[304,128]{1,0:T(8,128)(2,1)S(1)} %last_total.1.refs_0_), channel_id=1, source_target_pairs={{0,1},{1,0},{2,3},{3,2},{4,5},{5,4},{6,7},{7,6},{8,9},{9,8},{10,11... | collective-permute-start | bytes 233480 | tf_op jit(solution)/shard_map/ppermute | solution.py:1828
  (33 other events, 177.9 us)
